TPU v7x, 32 devices: a whole 2x2x4 slice. The times are simulated.
32 devices in a mesh: dp: 2 (over y), expert: 16 (over z, x, core).
Axes of the slice: x: 2, y: 2, z: 4, core: 2. Of those that a mesh axis runs over, the one named last changes fastest.
Arguments:
- tokens: bfloat16 [4096, 2048], P(('dp', 'expert')), may hold values from -6 to 6
- cotangent: bfloat16 [4096, 2048], P(('dp', 'expert')), may hold values from -6 to 6
- routes: int32 [4096, 2], P(('dp', 'expert')), may hold values from 0 to 15, all different within a row; in each aligned block of 128 rows (0 to 127, 128 to 255, ...) at most 24 rows name the same one
- gates: float32 [4096, 2], P(('dp', 'expert')), may hold values from 0.1 to 1
- w_gate: bfloat16 [16, 2048, 768], P('expert', None, 'dp'), may hold values from -0.125 to 0.125
- w_up: bfloat16 [16, 2048, 768], P('expert', None, 'dp'), may hold values from -0.125 to 0.125
- w_down: bfloat16 [16, 768, 2048], P('expert', 'dp'), may hold values from -0.21875 to 0.21875
Outputs:
- mixed: bfloat16 [4096, 2048], P(('dp', 'expert'))
- token_grad: bfloat16 [4096, 2048], P(('dp', 'expert'))
- gate_grad: float32 [4096, 2], P(('dp', 'expert'))
Inputs may be any that keep to these rules, and one draw needn't show every extreme that they name: `routes`: each row names 2 different experts. In each aligned block of 128 rows (the rows of one device), no expert is named by more than 24 rows, a bound that some block reaches.
All inputs are finite; a program needn't handle non-finite values.
Results may differ from a plain program's by a relative error of at most 0.014.
Values may be sent and summed in bfloat16 or wider, within the bound.
No kernel may reach another device: no remote copies, remote signals or barrier semaphores. Data moves between devices by JAX's collectives and lax.ppermute only.
A program may use at most 64 MiB of HBM per device.

v0:
```python
import jax
import jax.numpy as jnp
from jax import lax
from jax.sharding import PartitionSpec as P


def forward_rows(rows, weight_rows, gate_w, up_w, down_w):
    pre_gate = jnp.dot(rows, gate_w, preferred_element_type=jnp.float32)
    pre_up = jnp.dot(rows, up_w, preferred_element_type=jnp.float32)
    sig = jax.nn.sigmoid(pre_gate)
    act = pre_gate * sig
    hidden = (act * pre_up).astype(jnp.bfloat16)
    raw_out = jnp.dot(hidden, down_w, preferred_element_type=jnp.float32)
    slot_out = (weight_rows[:, None] * raw_out).astype(jnp.bfloat16)
    return (slot_out, pre_gate, pre_up, hidden)


def backward_rows(back_rows, weight_rows, pre_gate, pre_up, hidden, gate_w, up_w, down_w):
    sig = jax.nn.sigmoid(pre_gate)
    act = pre_gate * sig
    back_hidden = jnp.dot(back_rows, down_w.T, preferred_element_type=jnp.float32)
    gate_part = jnp.sum(hidden.astype(jnp.float32) * back_hidden, axis=1)
    scaled = weight_rows[:, None] * back_hidden
    back_gate = (scaled * pre_up * sig * (1.0 + pre_gate * (1.0 - sig))).astype(jnp.bfloat16)
    back_up = (scaled * act).astype(jnp.bfloat16)
    slot_grad = jnp.dot(back_gate, gate_w.T, preferred_element_type=jnp.float32)
    slot_grad = (slot_grad + jnp.dot(back_up, up_w.T, preferred_element_type=jnp.float32)).astype(
        jnp.bfloat16
    )
    return (slot_grad, gate_part)


def body(tokens, cotangent, routes, gates, w_gate, w_up, w_down):
    tok_rows = tokens.shape[0]
    top_count = routes.shape[1]
    width = tokens.shape[1]
    experts = lax.axis_size("expert")
    capacity = max(2, 3 * tok_rows * top_count // (2 * experts))
    slots = tok_rows * top_count
    expert_ids = routes.reshape(slots)
    onehot = (expert_ids[:, None] == jnp.arange(experts, dtype=jnp.int32)[None, :]).astype(
        jnp.int32
    )
    slot_rank = jnp.sum(onehot * (jnp.cumsum(onehot, axis=0) - onehot), axis=1)
    slot_index = expert_ids * capacity + slot_rank
    table = (
        jnp.full((experts * capacity,), slots, jnp.int32)
        .at[slot_index]
        .set(jnp.arange(slots, dtype=jnp.int32))
    )
    live = table < slots
    source = jnp.where(live, table // top_count, 0)
    zero_rows = jnp.zeros((), jnp.bfloat16)
    x_slots = jnp.where(live[:, None], tokens[source], zero_rows).reshape(experts, capacity, width)
    dy_slots = jnp.where(live[:, None], cotangent[source], zero_rows).reshape(
        experts, capacity, width
    )
    gate_slots = jnp.where(live, gates.reshape(slots)[jnp.minimum(table, slots - 1)], 0.0).reshape(
        experts, capacity
    )
    gate_full, up_full, down_full = (
        lax.all_gather(w_gate, "dp", axis=2, tiled=True),
        lax.all_gather(w_up, "dp", axis=2, tiled=True),
        lax.all_gather(w_down, "dp", axis=1, tiled=True),
    )
    gate_w = gate_full[0]
    up_w = up_full[0]
    down_w = down_full[0]
    rows, weight_rows = (
        lax.all_to_all(x_slots, "expert", split_axis=0, concat_axis=0, tiled=True),
        lax.all_to_all(
            gate_slots.astype(jnp.bfloat16), "expert", split_axis=0, concat_axis=0, tiled=True
        ).astype(gate_slots.dtype),
    )
    flat_w = weight_rows.reshape(-1)
    slot_out, pre_gate, pre_up, hidden = forward_rows(
        rows.reshape(-1, width), flat_w, gate_w, up_w, down_w
    )
    out_back = lax.all_to_all(
        slot_out.reshape(experts, capacity, width),
        "expert",
        split_axis=0,
        concat_axis=0,
        tiled=True,
    )
    back_rows = lax.all_to_all(dy_slots, "expert", split_axis=0, concat_axis=0, tiled=True)
    slot_grad, gate_part = backward_rows(
        back_rows.reshape(-1, width), flat_w, pre_gate, pre_up, hidden, gate_w, up_w, down_w
    )
    grad_back, gate_back = (
        lax.all_to_all(
            slot_grad.reshape(experts, capacity, width),
            "expert",
            split_axis=0,
            concat_axis=0,
            tiled=True,
        ),
        lax.all_to_all(
            gate_part.reshape(experts, capacity).astype(jnp.bfloat16),
            "expert",
            split_axis=0,
            concat_axis=0,
            tiled=True,
        ).astype(jnp.float32),
    )
    out_rows = out_back.reshape(experts * capacity, width)[slot_index].reshape(
        tok_rows, top_count, width
    )
    mixed = jnp.sum(out_rows.astype(jnp.float32), axis=1).astype(jnp.bfloat16)
    grad_rows = grad_back.reshape(experts * capacity, width)[slot_index].reshape(
        tok_rows, top_count, width
    )
    token_grad = jnp.sum(grad_rows.astype(jnp.float32), axis=1).astype(jnp.bfloat16)
    gate_grad = gate_back.reshape(experts * capacity)[slot_index].reshape(tok_rows, top_count)
    return (mixed, token_grad, gate_grad)


def solution(mesh):
    return jax.shard_map(
        body,
        mesh=mesh,
        in_specs=(
            P(("dp", "expert"), None),
            P(("dp", "expert"), None),
            P(("dp", "expert"), None),
            P(("dp", "expert"), None),
            P("expert", None, "dp"),
            P("expert", None, "dp"),
            P("expert", "dp", None),
        ),
        out_specs=(P(("dp", "expert"), None), P(("dp", "expert"), None), P(("dp", "expert"), None)),
        check_vma=False,
    )
```

profile of v0, /device:TPU:0, one launch (start us, length us, event | category | flops | bytes accessed | tf_op | source)
XLA Modules:
  0.0 264.8 jit_solution(989866741604857193)
XLA Ops:
  7.2 0.0 copy-start
  7.2 0.0 copy-start.4
  7.2 0.0 copy-start.5
  7.2 0.0 all-gather.6.cloned.1.call-start
  7.2 0.7 all-gather.6.cloned.1.call-update
  7.9 0.0 copy-done.4
  7.9 0.1 copy.17
  8.1 0.1 eq.25
  8.2 0.1 eq.29
  8.3 0.0 copy-done.5
  8.3 0.1 copy.20
  8.5 0.1 reshape.136
  8.6 0.1 copy.16
  8.8 0.1 mul.62
  8.9 0.6 reduce-window.6
  9.5 0.2 slice_reduce_fusion
  9.7 0.1 fusion.23
  9.8 1.4 scatter_custom_fusion
  11.3 2.7 %gather_fusion = bf16[384]{0:T(512)(128)(2,1)S(1)} fusion(bf16[256]{0:T(256)(128)(2,1)S(1)} %reshape.136, s32[1024]{0:T(1024)S(1)} %pad_clamp_fusion.2), kind=kCustom, calls=%fused_computation | custom fusion | bytes 3072 | tf_op jit(solution)/shard_map/gather | solution.py:58
  14.0 0.7 convert_element_type.90
  14.7 7.4 %all-to-all-start = ((bf16[16,1,24]{2,1,0:T(2,128)(2,1)}), bf16[16,1,24]{2,1,0:T(2,128)(2,1)S(1)}, u32[]{:S(2)}, u32[]{:S(2)}) async-start(bf16[16,1,24]{2,1,0:T(2,128)(2,1)} %convert_element_type.90), calls=%async_computation | async-start | bytes 16384 | tf_op jit(solution)/shard_map/all_to_all | solution.py:71
  22.0 0.0 all-gather.4.cloned.1.call-start
  22.1 0.7 all-gather.4.cloned.1.call-update
  22.8 0.1 broadcast_in_dim.40
  22.9 0.0 copy-done
  22.9 0.0 copy-start.1
  23.0 2.5 gather_fusion.1
  25.4 0.0 copy-done.1
  25.4 3.1 %gather_fusion.3 = bf16[384,2048]{1,0:T(8,128)(2,1)} fusion(bf16[128,2048]{1,0:T(8,128)(2,1)S(1)} %copy-done.1, s32[1024]{0:T(1024)S(1)} %pad_clamp_fusion.1), kind=kCustom, calls=%fused_computation.3 | custom fusion | bytes 3147264 | tf_op jit(solution)/shard_map/gather | solution.py:55
  28.5 3.3 %broadcast_select_fusion.1 = (bf16[16,24,2048]{2,1,0:T(8,128)(2,1)}, bf16[16,24,2048]{2,1,0:T(8,128)(2,1)}) fusion(bf16[16,24,2048]{2,1,0:T(8,128)(2,1)S(1)} %bitcast.55, pred[16,24]{1,0:T(8,128)(4,1)S(1)} %broadcast_in_dim.40, bf16[16,24,2048]{2,1,0:T(8,128)(2,1)} %bitcast.56), kind=kLoop, calls=%fused_computation.22 | loop fusion | flops 1572864 | bytes 6291840 | tf_op jit(solution)/shard_map/jit(_where)/select_n | solution.py:54
  31.9 0.0 all-to-all-done
  31.9 6.0 %all-to-all-start.1 = ((bf16[16,24,2048]{2,1,0:T(8,128)(2,1)}), bf16[16,24,2048]{2,1,0:T(8,128)(2,1)S(1)}, u32[]{:S(2)}, u32[]{:S(2)}) async-start(bf16[16,24,2048]{2,1,0:T(8,128)(2,1)} %get-tuple-element.13), calls=%async_computation.1 | async-start | bytes 3145728 | tf_op jit(solution)/shard_map/all_to_all | solution.py:70
  37.9 0.0 all-gather.8.cloned.1.call-start
  37.9 0.7 all-gather.8.cloned.1.call-update
  38.6 31.2 %all-to-all-done.1 = bf16[16,24,2048]{2,1,0:T(8,128)(2,1)S(1)} async-done(((bf16[16,24,2048]{2,1,0:T(8,128)(2,1)}), bf16[16,24,2048]{2,1,0:T(8,128)(2,1)S(1)}, u32[]{:S(2)}, u32[]{:S(2)}) %all-to-all-start.1) | async-done | bytes 1572896 | tf_op jit(solution)/shard_map/all_to_all | solution.py:70
  69.9 9.2 %all-to-all-start.3 = ((bf16[16,24,2048]{2,1,0:T(8,128)(2,1)}), bf16[16,24,2048]{2,1,0:T(8,128)(2,1)}, u32[]{:S(2)}, u32[]{:S(2)}) async-start(bf16[16,24,2048]{2,1,0:T(8,128)(2,1)} %get-tuple-element.14), calls=%async_computation.3 | async-start | bytes 3145728 | tf_op jit(solution)/shard_map/all_to_all | solution.py:86
  79.0 0.1 reshape.146
  79.1 0.0 all-gather.6.cloned.1.call-done
  79.2 3.3 %fusion.6 = f32[384,768]{1,0:T(8,128)S(1)} fusion(bf16[384,2048]{1,0:T(8,128)(2,1)S(1)} %bitcast.57, bf16[1,2048,768]{2,1,0:T(8,128)(2,1)} %all-gather.6.cloned.1.call-done), kind=kOutput, calls=%fused_computation.13 | convolution fusion | flops 1207959552 | bytes 5898240 | tf_op jit(solution)/shard_map/dot_general | solution.py:9
  82.4 21.3 %all-gather.4.cloned.1.call-done = bf16[1,2048,768]{2,1,0:T(8,128)(2,1)} async-done(((bf16[1,2048,384]{2,1,0:T(8,128)(2,1)}), bf16[1,2048,768]{2,1,0:T(8,128)(2,1)}) %all-gather.4.cloned.1.call-update) | async-done | bytes 3145744 | tf_op jit(solution)/shard_map/all_gather | solution.py:62
  103.8 4.4 %fusion.10 = f32[384,768]{1,0:T(8,128)} fusion(bf16[384,2048]{1,0:T(8,128)(2,1)S(1)} %bitcast.58, bf16[1,2048,768]{2,1,0:T(8,128)(2,1)} %all-gather.4.cloned.1.call-done), kind=kOutput, calls=%fused_computation.17 | convolution fusion | flops 1207959552 | bytes 5898240 | tf_op jit(solution)/shard_map/dot_general | solution.py:8
  108.1 2.9 %all-to-all-done.3 = bf16[16,24,2048]{2,1,0:T(8,128)(2,1)} async-done(((bf16[16,24,2048]{2,1,0:T(8,128)(2,1)}), bf16[16,24,2048]{2,1,0:T(8,128)(2,1)}, u32[]{:S(2)}, u32[]{:S(2)}) %all-to-all-start.3) | async-done | bytes 1572896 | tf_op jit(solution)/shard_map/all_to_all | solution.py:86
  111.0 39.2 %all-gather.8.cloned.1.call-done = bf16[1,768,2048]{2,1,0:T(8,128)(2,1)} async-done(((bf16[1,384,2048]{2,1,0:T(8,128)(2,1)}), bf16[1,768,2048]{2,1,0:T(8,128)(2,1)}) %all-gather.8.cloned.1.call-update) | async-done | bytes 3145744 | tf_op jit(solution)/shard_map/all_gather | solution.py:64
  150.3 5.2 %multiply_reduce_fusion = (bf16[384]{0:T(512)(128)(2,1)S(1)}, bf16[384,768]{1,0:T(8,128)(2,1)S(1)}, f32[384,768]{1,0:T(8,128)}) fusion(f32[384,768]{1,0:T(8,128)S(1)} %fusion.6, f32[384,768]{1,0:T(8,128)} %fusion.10, bf16[384,2048]{1,0:T(8,128)(2,1)} %bitcast.11, bf16[1,768,2048]{2,1,0:T(8,128)(2,1)} %all-gather.8.cloned.1.call-done), kind=kOutput, calls=%fused_computation.23 | convolution fusion | flops 1210613376 | bytes 8848128 | tf_op jit(solution)/shard_map/dot_general | solution.py:21
  155.4 0.7 convert_element_type.91
  156.1 5.6 %all-to-all-start.5 = ((bf16[16,1,24]{2,1,0:T(2,128)(2,1)}), bf16[16,1,24]{2,1,0:T(2,128)(2,1)S(1)}, u32[]{:S(2)}, u32[]{:S(2)}) async-start(bf16[16,1,24]{2,1,0:T(2,128)(2,1)} %convert_element_type.91), calls=%async_computation.5 | async-start | bytes 16384 | tf_op jit(solution)/shard_map/all_to_all | solution.py:98
  161.8 4.4 %multiply_convert_fusion = bf16[384,2048]{1,0:T(8,128)(2,1)} fusion(bf16[384,768]{1,0:T(8,128)(2,1)S(1)} %get-tuple-element.10, bf16[1,768,2048]{2,1,0:T(8,128)(2,1)} %all-gather.8.cloned.1.call-done, f32[384]{0:T(512)S(1)} %reshape.146), kind=kOutput, calls=%fused_computation.20 | convolution fusion | flops 1209532416 | bytes 5309952 | tf_op jit(solution)/shard_map/dot_general | solution.py:13
  166.2 1.9 all-to-all-done.5
  168.1 4.1 %all-to-all-start.2 = ((bf16[16,24,2048]{2,1,0:T(8,128)(2,1)}), bf16[16,24,2048]{2,1,0:T(8,128)(2,1)S(1)}, u32[]{:S(2)}, u32[]{:S(2)}) async-start(bf16[16,24,2048]{2,1,0:T(8,128)(2,1)} %bitcast.60), calls=%async_computation.2 | async-start | bytes 3145728 | tf_op jit(solution)/shard_map/all_to_all | solution.py:79
  172.3 4.4 %fusion.4 = f32[384,2048]{1,0:T(8,128)S(1)} fusion(bf16[1,2048,768]{2,1,0:T(8,128)(2,1)} %all-gather.6.cloned.1.call-done, f32[384,768]{1,0:T(8,128)} %get-tuple-element.15, f32[384]{0:T(512)S(1)} %reshape.146, f32[384,768]{1,0:T(8,128)} %fusion.10), kind=kOutput, calls=%fused_computation.11 | convolution fusion | flops 1210023936 | bytes 8652288 | tf_op jit(solution)/shard_map/dot_general | solution.py:27
  176.7 2.9 %add_convert_fusion = bf16[384,2048]{1,0:T(8,128)(2,1)} fusion(f32[384,2048]{1,0:T(8,128)S(1)} %fusion.4, bf16[1,2048,768]{2,1,0:T(8,128)(2,1)S(1)} %copy-done.6, f32[384,768]{1,0:T(8,128)S(1)} %copy-done.7, f32[384,768]{1,0:T(8,128)S(1)} %fusion.6, f32[384,768]{1,0:T(8,128)S(1)} %copy-done.8, f32[384]{0:T(512)S(1)} %reshape.146), kind=kOutput, calls=%fused_computation.19 | convolution fusion | flops 1212776448 | bytes 11404800 | tf_op jit(solution)/shard_map/dot_general | solution.py:26
  179.6 24.6 %all-to-all-done.2 = bf16[16,24,2048]{2,1,0:T(8,128)(2,1)S(1)} async-done(((bf16[16,24,2048]{2,1,0:T(8,128)(2,1)}), bf16[16,24,2048]{2,1,0:T(8,128)(2,1)S(1)}, u32[]{:S(2)}, u32[]{:S(2)}) %all-to-all-start.2) | async-done | bytes 1572896 | tf_op jit(solution)/shard_map/all_to_all | solution.py:79
  204.2 9.2 %all-to-all-start.4 = ((bf16[16,24,2048]{2,1,0:T(8,128)(2,1)}), bf16[16,24,2048]{2,1,0:T(8,128)(2,1)}, u32[]{:S(2)}, u32[]{:S(2)}) async-start(bf16[16,24,2048]{2,1,0:T(8,128)(2,1)} %bitcast.59), calls=%async_computation.4 | async-start | bytes 3145728 | tf_op jit(solution)/shard_map/all_to_all | solution.py:91
  213.4 0.1 reshape.147
  213.5 1.9 gather_fusion.5
  215.5 0.1 reshape.145
  215.6 0.6 copy.23
  216.2 1.4 gather_fusion.2
  217.6 1.5 reshape.140
  219.1 26.3 %all-to-all-done.4 = bf16[16,24,2048]{2,1,0:T(8,128)(2,1)} async-done(((bf16[16,24,2048]{2,1,0:T(8,128)(2,1)}), bf16[16,24,2048]{2,1,0:T(8,128)(2,1)}, u32[]{:S(2)}, u32[]{:S(2)}) %all-to-all-start.4) | async-done | bytes 1572896 | tf_op jit(solution)/shard_map/all_to_all | solution.py:91
  245.4 4.0 %gather_fusion.4 = bf16[256,2048]{1,0:T(8,128)(2,1)S(1)} fusion(bf16[384,2048]{1,0:T(8,128)(2,1)} %bitcast.13, s32[1024]{0:T(1024)S(1)} %pad_clamp_fusion), kind=kCustom, calls=%fused_computation.4 | custom fusion | bytes 2098176 | tf_op jit(solution)/shard_map/gather | solution.py:110
  249.4 1.5 reshape.144
  250.9 3.8 %reduce_sum.46 = bf16[128,2048]{1,0:T(8,128)(2,1)} reduce(bf16[128,2,2048]{2,1,0:T(2,128)(2,1)S(1)} %copy-done.2, bf16[]{:T(256)} %constant.37.clone.1), dimensions={1}, to_apply=%region_4.5 | reduce | flops 262144 | bytes 1572866 | tf_op jit(solution)/shard_map/reduce_sum | solution.py:109
  254.7 3.6 %reduce_sum.47 = bf16[128,2048]{1,0:T(8,128)(2,1)} reduce(bf16[128,2,2048]{2,1,0:T(2,128)(2,1)S(1)} %copy-done.3, bf16[]{:T(256)} %constant.37.clone.1), dimensions={1}, to_apply=%region_5.6 | reduce | flops 262144 | bytes 1572866 | tf_op jit(solution)/shard_map/reduce_sum | solution.py:113
  (24 shorter events, 0.2 us)
Async XLA Ops:
  7.2 15.8 %copy-start = (bf16[128,2048]{1,0:T(8,128)(2,1)S(1)}, bf16[128,2048]{1,0:T(8,128)(2,1)}, u32[]{:S(2)}) copy-start(bf16[128,2048]{1,0:T(8,128)(2,1)} %param.7) | copy-start | bytes 1572868
  7.2 0.8 copy-start.4
  7.2 1.2 copy-start.5
  7.2 72.0 %all-gather.6.cloned.1.call-start = ((), (), s32[]{:S(2)}) async-start(), calls=%async_computation.7 | async-start | bytes 4718592 | tf_op jit(solution)/shard_map/all_gather | solution.py:63
  14.7 17.2 %all-to-all-start = ((bf16[16,1,24]{2,1,0:T(2,128)(2,1)}), bf16[16,1,24]{2,1,0:T(2,128)(2,1)S(1)}, u32[]{:S(2)}, u32[]{:S(2)}) async-start(bf16[16,1,24]{2,1,0:T(2,128)(2,1)} %convert_element_type.90), calls=%async_computation | async-start | bytes 16384 | tf_op jit(solution)/shard_map/all_to_all | solution.py:71
  22.0 81.7 %all-gather.4.cloned.1.call-start = ((), (), s32[]{:S(2)}) async-start(), calls=%async_computation.6 | async-start | bytes 4718592 | tf_op jit(solution)/shard_map/all_gather | solution.py:62
  22.9 2.5 copy-start.1
  31.9 38.0 %all-to-all-start.1 = ((bf16[16,24,2048]{2,1,0:T(8,128)(2,1)}), bf16[16,24,2048]{2,1,0:T(8,128)(2,1)S(1)}, u32[]{:S(2)}, u32[]{:S(2)}) async-start(bf16[16,24,2048]{2,1,0:T(8,128)(2,1)} %get-tuple-element.13), calls=%async_computation.1 | async-start | bytes 3145728 | tf_op jit(solution)/shard_map/all_to_all | solution.py:70
  37.9 112.4 %all-gather.8.cloned.1.call-start = ((), (), s32[]{:S(2)}) async-start(), calls=%async_computation.8 | async-start | bytes 4718592 | tf_op jit(solution)/shard_map/all_gather | solution.py:64
  69.9 41.2 %all-to-all-start.3 = ((bf16[16,24,2048]{2,1,0:T(8,128)(2,1)}), bf16[16,24,2048]{2,1,0:T(8,128)(2,1)}, u32[]{:S(2)}, u32[]{:S(2)}) async-start(bf16[16,24,2048]{2,1,0:T(8,128)(2,1)} %get-tuple-element.14), calls=%async_computation.3 | async-start | bytes 3145728 | tf_op jit(solution)/shard_map/all_to_all | solution.py:86
  156.1 12.0 %all-to-all-start.5 = ((bf16[16,1,24]{2,1,0:T(2,128)(2,1)}), bf16[16,1,24]{2,1,0:T(2,128)(2,1)S(1)}, u32[]{:S(2)}, u32[]{:S(2)}) async-start(bf16[16,1,24]{2,1,0:T(2,128)(2,1)} %convert_element_type.91), calls=%async_computation.5 | async-start | bytes 16384 | tf_op jit(solution)/shard_map/all_to_all | solution.py:98
  168.1 36.1 %all-to-all-start.2 = ((bf16[16,24,2048]{2,1,0:T(8,128)(2,1)}), bf16[16,24,2048]{2,1,0:T(8,128)(2,1)S(1)}, u32[]{:S(2)}, u32[]{:S(2)}) async-start(bf16[16,24,2048]{2,1,0:T(8,128)(2,1)} %bitcast.60), calls=%async_computation.2 | async-start | bytes 3145728 | tf_op jit(solution)/shard_map/all_to_all | solution.py:79
  172.2 4.4 %copy-start.6 = (bf16[1,2048,768]{2,1,0:T(8,128)(2,1)S(1)}, bf16[1,2048,768]{2,1,0:T(8,128)(2,1)}, u32[]{:S(2)}) copy-start(bf16[1,2048,768]{2,1,0:T(8,128)(2,1)} %all-gather.4.cloned.1.call-done) | copy-start | bytes 9437188
  172.2 4.4 %copy-start.7 = (f32[384,768]{1,0:T(8,128)S(1)}, f32[384,768]{1,0:T(8,128)}, u32[]{:S(2)}) copy-start(f32[384,768]{1,0:T(8,128)} %fusion.10) | copy-start | bytes 3538948
  172.3 4.4 %copy-start.8 = (f32[384,768]{1,0:T(8,128)S(1)}, f32[384,768]{1,0:T(8,128)}, u32[]{:S(2)}) copy-start(f32[384,768]{1,0:T(8,128)} %get-tuple-element.15) | copy-start | bytes 3538948
  204.2 41.2 %all-to-all-start.4 = ((bf16[16,24,2048]{2,1,0:T(8,128)(2,1)}), bf16[16,24,2048]{2,1,0:T(8,128)(2,1)}, u32[]{:S(2)}, u32[]{:S(2)}) async-start(bf16[16,24,2048]{2,1,0:T(8,128)(2,1)} %bitcast.59), calls=%async_computation.4 | async-start | bytes 3145728 | tf_op jit(solution)/shard_map/all_to_all | solution.py:91
  249.4 1.5 copy-start.2
  250.9 3.8 %copy-start.3 = (bf16[128,2,2048]{2,1,0:T(2,128)(2,1)S(1)}, bf16[128,2,2048]{2,1,0:T(2,128)(2,1)}, u32[]{:S(2)}) copy-start(bf16[128,2,2048]{2,1,0:T(2,128)(2,1)} %reshape.144) | copy-start | bytes 3145732
Sparse Core Ops, SparseCore 0:
  9.6 47.6 all-gather.5
  58.8 44.9 all-gather.3
  105.3 44.9 all-gather.7
where the time goes:
time: 269 us; the launch traced here: 265 us
  waiting for transfers between devices  150 us (56%)
  starting transfers between devices  41.5 us (15%)
  matrix products  24.6 us (9%)
  local copies, waits for them, and re-layouts  23.5 us (9%)
  between operations  14.1 us (5%)
  other arithmetic  11.6 us (4%)
    all_gather x1, waiting for transfers between devices, body(): lax.all_gather(w_down, 'dp', axis=1, tiled=True)  39.2 us
    all_to_all x1, waiting for transfers between devices, body(): lax.all_to_all(x_slots, 'expert', split_axis=0, concat_axis=0, tiled=True)  31.2 us
    all_to_all x1, waiting for transfers between devices, body(): lax.all_to_all(slot_grad.reshape(experts, capacity, width), 'expert', spl...  26.3 us
    all_to_all x1, waiting for transfers between devices, body(): lax.all_to_all(slot_out.reshape(experts, capacity, width), 'expert', spli...  24.6 us
    all_gather x1, waiting for transfers between devices, body(): lax.all_gather(w_gate, 'dp', axis=2, tiled=True)  21.3 us
    all_to_all x1, starting transfers between devices, body(): lax.all_to_all(slot_grad.reshape(experts, capacity, width), 'expert', spl...  9.15 us
    all_to_all x1, starting transfers between devices, body(): lax.all_to_all(dy_slots, 'expert', split_axis=0, concat_axis=0, tiled=True)  9.15 us
    all_to_all x1, starting transfers between devices, body(): lax.all_to_all(gate_slots.astype(jnp.bfloat16), 'expert', split_axis=0, c...  7.36 us
  transfers between devices with their start and end apart: 9, of which 7 were waited for; matrix products, arithmetic and copies ran while one was open for 15% of the time, Pallas kernels for 0%

commit v1 on v0

v1 whole, which is shorter than its diff:
```python
import functools

import jax
import jax.numpy as jnp
from jax import lax
from jax.experimental import pallas as pl
from jax.experimental.pallas import tpu as pltpu
from jax.sharding import PartitionSpec as P

BF16 = jnp.bfloat16
F32 = jnp.float32
VMEM_BYTES = 48 << 20


def dot(a, b, dims):
    return lax.dot_general(a, b, ((dims[:1], dims[1:]), ((), ())), preferred_element_type=F32)


def place_kernel(experts, capacity, routes_ref, tokens_ref, slots_ref, place_ref):
    tok_rows, top_count = routes_ref.shape
    routes = routes_ref[...]
    lanes = lax.broadcasted_iota(jnp.int32, (tok_rows, experts), 1)
    named = [lanes == routes[:, k : k + 1] for k in range(top_count)]
    chosen = sum(n.astype(F32) for n in named)
    earlier = (
        lax.broadcasted_iota(jnp.int32, (tok_rows, tok_rows), 1)
        < lax.broadcasted_iota(jnp.int32, (tok_rows, tok_rows), 0)
    ).astype(F32)
    rank = dot(earlier.astype(BF16), chosen.astype(BF16), (1, 0))
    slot_lanes = lax.broadcasted_iota(jnp.int32, (tok_rows, experts * capacity), 1)
    total = None
    for k in range(top_count):
        own = jnp.sum(jnp.where(named[k], rank, 0.0), axis=1, keepdims=True)
        slot = routes[:, k : k + 1] * capacity + own.astype(jnp.int32)
        mark = (slot_lanes == slot).astype(F32)
        place_ref[k * tok_rows : (k + 1) * tok_rows, :] = mark.astype(BF16)
        total = mark if total is None else total + mark
    slots_ref[...] = dot(total.astype(BF16), tokens_ref[...], (0, 0)).astype(BF16)


def spread_kernel(top_count, place_ref, rows_ref, slots_ref):
    tok_rows = rows_ref.shape[0]
    total = sum(
        place_ref[k * tok_rows : (k + 1) * tok_rows, :].astype(F32) for k in range(top_count)
    )
    slots_ref[...] = dot(total.astype(BF16), rows_ref[...], (0, 0)).astype(BF16)


def forward_kernel(parts, *refs):
    rows_ref = refs[0]
    gate_refs, up_refs, down_refs = (refs[1 + i * parts : 1 + (i + 1) * parts] for i in range(3))
    out_ref, by_gate_ref, by_up_ref, hidden_ref = refs[1 + 3 * parts :]
    width = rows_ref.shape[1]
    for i in range(parts):
        rows = rows_ref[...]
        pre_gate = dot(rows, gate_refs[i][...], (1, 0))
        pre_up = dot(rows, up_refs[i][...], (1, 0))
        sig = jax.nn.sigmoid(pre_gate)
        act = pre_gate * sig
        hidden_ref[i] = (act * pre_up).astype(BF16)
        by_gate_ref[i] = pre_up * sig * (1.0 + pre_gate * (1.0 - sig))
        by_up_ref[i] = act
    tile = min(512, width)
    for d in range(0, width, tile):
        out_ref[:, d : d + tile] = sum(
            dot(hidden_ref[i], down_refs[i][:, d : d + tile], (1, 0)) for i in range(parts)
        ).astype(BF16)


def backward_kernel(parts, *refs):
    rows_ref = refs[0]
    gate_refs, up_refs, down_refs = (refs[1 + i * parts : 1 + (i + 1) * parts] for i in range(3))
    by_gate_ref, by_up_ref, out_ref, back_gate_ref, back_up_ref = refs[1 + 3 * parts :]
    width = rows_ref.shape[1]
    for i in range(parts):
        back_hidden = dot(rows_ref[...], down_refs[i][...], (1, 1))
        back_gate_ref[i] = (back_hidden * by_gate_ref[i]).astype(BF16)
        back_up_ref[i] = (back_hidden * by_up_ref[i]).astype(BF16)
    tile = min(512, width)
    for d in range(0, width, tile):
        out_ref[:, d : d + tile] = sum(
            dot(back_gate_ref[i], gate_refs[i][d : d + tile, :], (1, 1))
            + dot(back_up_ref[i], up_refs[i][d : d + tile, :], (1, 1))
            for i in range(parts)
        ).astype(BF16)


def mix_kernel(place_ref, gates_ref, slots_ref, cotangent_ref, mixed_ref, gate_grad_ref):
    tok_rows, top_count = gates_ref.shape
    total, grads = None, []
    for k in range(top_count):
        raw = dot(place_ref[k * tok_rows : (k + 1) * tok_rows, :], slots_ref[...], (1, 0))
        grads.append(jnp.sum(raw * cotangent_ref[...].astype(F32), axis=1, keepdims=True))
        part = raw * gates_ref[:, k : k + 1]
        total = part if total is None else total + part
    mixed_ref[...] = total.astype(BF16)
    gate_grad_ref[...] = jnp.concatenate(grads, axis=1)


def sum_kernel(place_ref, gates_ref, slots_ref, out_ref):
    tok_rows, top_count = gates_ref.shape
    total = None
    for k in range(top_count):
        raw = dot(place_ref[k * tok_rows : (k + 1) * tok_rows, :], slots_ref[...], (1, 0))
        part = raw * gates_ref[:, k : k + 1]
        total = part if total is None else total + part
    out_ref[...] = total.astype(BF16)


def call(kernel, outs, flops, scratch=()):
    def run(*args):
        moved = sum(a.size * a.dtype.itemsize for a in (*args, *outs))
        return pl.pallas_call(
            kernel,
            out_shape=outs,
            scratch_shapes=scratch,
            compiler_params=pltpu.CompilerParams(vmem_limit_bytes=VMEM_BYTES),
            cost_estimate=pl.CostEstimate(flops=flops, bytes_accessed=moved, transcendentals=0),
        )(*args)

    return run


def body(tokens, cotangent, routes, gates, w_gate, w_up, w_down):
    tok_rows, width = tokens.shape
    top_count = routes.shape[1]
    parts, experts = lax.axis_size("dp"), lax.axis_size("expert")
    hidden = w_gate.shape[2]
    capacity = max(2, 3 * tok_rows * top_count // (2 * experts))
    slots = experts * capacity
    axes = ("dp", "expert")

    def device(g, j):
        return g * experts + j

    swap = [
        (device(g, parts * q + r), device(r, parts * q + g))
        for g in range(parts)
        for q in range(experts // parts)
        for r in range(parts)
    ]
    groups = [
        [device(e % parts, e // parts * parts + c) for e in range(experts)] for c in range(parts)
    ]

    def whole_expert(weight):
        own = lax.ppermute(weight[0], axes, swap)
        shares = [own]
        for step in range(1, parts):
            turn = [(j, j // parts * parts + (j + step) % parts) for j in range(experts)]
            shares.append(lax.ppermute(own, "expert", turn))
        return shares

    def exchange(rows):
        return lax.all_to_all(
            rows.reshape(experts, capacity, width),
            axes,
            split_axis=0,
            concat_axis=0,
            axis_index_groups=groups,
            tiled=True,
        ).reshape(slots, width)

    spread_flops = 2 * slots * tok_rows * width
    dot_flops = 2 * slots * width * hidden * parts
    slot_shape = jax.ShapeDtypeStruct((slots, width), BF16)
    unit_shape = jax.ShapeDtypeStruct((parts, slots, hidden), F32)
    token_shape = jax.ShapeDtypeStruct((tok_rows, width), BF16)
    unit_scratch = pltpu.VMEM((parts, slots, hidden), BF16)

    gate_w, up_w, down_w = whole_expert(w_gate), whole_expert(w_up), whole_expert(w_down)
    x_slots, place = call(
        functools.partial(place_kernel, experts, capacity),
        (slot_shape, jax.ShapeDtypeStruct((top_count * tok_rows, slots), BF16)),
        spread_flops,
    )(routes, tokens)
    x_rows = exchange(x_slots)
    (dy_slots,) = call(functools.partial(spread_kernel, top_count), (slot_shape,), spread_flops)(
        place, cotangent
    )
    dy_rows = exchange(dy_slots)
    out_rows, by_gate, by_up = call(
        functools.partial(forward_kernel, parts),
        (slot_shape, unit_shape, unit_shape),
        3 * dot_flops,
        [unit_scratch],
    )(x_rows, *gate_w, *up_w, *down_w)
    out_slots = exchange(out_rows)
    (grad_rows,) = call(
        functools.partial(backward_kernel, parts),
        (slot_shape,),
        3 * dot_flops,
        [unit_scratch, unit_scratch],
    )(dy_rows, *gate_w, *up_w, *down_w, by_gate, by_up)
    grad_slots = exchange(grad_rows)
    mixed, gate_grad = call(
        mix_kernel,
        (token_shape, jax.ShapeDtypeStruct(gates.shape, F32)),
        2 * spread_flops,
    )(place, gates, out_slots, cotangent)
    (token_grad,) = call(sum_kernel, (token_shape,), 2 * spread_flops)(place, gates, grad_slots)
    return (mixed, token_grad, gate_grad)


def solution(mesh):
    rows, weights = P(("dp", "expert"), None), P("expert", None, "dp")
    return jax.shard_map(
        body,
        mesh=mesh,
        in_specs=(rows, rows, rows, rows, weights, weights, P("expert", "dp", None)),
        out_specs=(rows, rows, rows),
        check_vma=False,
    )
```

time: 269 us -> 204 us (0.76)
  the two profiles are of different devices: /device:TPU:0 before, /device:TPU:10 now
where the time goes in v1:
time: 204 us; the launch traced here: 201 us
  starting transfers between devices  101 us (50%)
  waiting for transfers between devices  62 us (30%)
  Pallas kernels  23.7 us (12%)
  local copies, waits for them, and re-layouts  12.9 us (6%)
    all_to_all x4, waiting for transfers between devices, exchange(): lax.all_to_all(rows.reshape(experts, capacity, width), axes, split_axis=0...  58.8 us
    ppermute x3, starting transfers between devices, whole_expert(): own = lax.ppermute(weight[0], axes, swap)  40 us
    ppermute x3, starting transfers between devices, whole_expert(): shares.append(lax.ppermute(own, 'expert', turn))  32.9 us
    all_to_all x4, starting transfers between devices, exchange(): lax.all_to_all(rows.reshape(experts, capacity, width), axes, split_axis=0...  28.5 us
    pallas_call x6, Pallas kernels, run(): pl.pallas_call(kernel, out_shape=outs, scratch_shapes=scratch, compiler_p...  23.7 us
    unnamed x31, local copies, waits for them, and re-layouts  12.9 us
  transfers between devices with their start and end apart: 10, of which 3 were waited for; matrix products, arithmetic and copies ran while one was open for 0% of the time, Pallas kernels for 11%

profile of v1, /device:TPU:10, one launch (start us, length us, event | category | flops | bytes accessed | tf_op | source)
XLA Modules:
  0.0 200.8 jit_solution(8401078647438868710)
XLA Ops:
  0.6 0.8 copy.10.routes_ref
  1.4 0.0 copy-start.9
  1.4 1.0 copy-done.9
  2.5 1.0 shard_map.94
  3.5 0.0 copy-start.4
  3.5 1.2 copy-done.4
  4.7 0.0 copy-start.1
  4.7 7.3 %all-to-all-start = ((bf16[16,24,2048]{2,1,0:T(8,128)(2,1)}), bf16[16,24,2048]{2,1,0:T(8,128)(2,1)S(1)}, u32[]{:S(2)}, u32[]{:S(2)}) async-start(bf16[16,24,2048]{2,1,0:T(8,128)(2,1)} %bitcast.17), calls=%async_computation | async-start | bytes 3145728 | tf_op jit(solution)/shard_map/all_to_all | solution.py:155
  12.0 13.3 %collective-permute-start = (bf16[2048,384]{1,0:T(8,128)(2,1)}, bf16[2048,384]{1,0:T(8,128)(2,1)}, u32[]{:S(2)}, u32[]{:S(2)}) collective-permute-start(bf16[2048,384]{1,0:T(8,128)(2,1)} %bitcast.18), channel_id=1, source_target_pairs={{0,0},{1,16},{2,2},{3,18},{4,4},{5,20},{6,6},{7,22},{8,8},{9,24},{... | collective-permute-start | bytes 4718600 | tf_op jit(solution)/shard_map/ppermute | solution.py:147
  25.4 13.3 %collective-permute-start.2 = (bf16[2048,384]{1,0:T(8,128)(2,1)}, bf16[2048,384]{1,0:T(8,128)(2,1)}, u32[]{:S(2)}, u32[]{:S(2)}) collective-permute-start(bf16[2048,384]{1,0:T(8,128)(2,1)} %bitcast.19), channel_id=1, source_target_pairs={{0,0},{1,16},{2,2},{3,18},{4,4},{5,20},{6,6},{7,22},{8,8},{9,24},{... | collective-permute-start | bytes 4718600 | tf_op jit(solution)/shard_map/ppermute | solution.py:147
  38.7 13.3 %collective-permute-start.4 = (bf16[384,2048]{1,0:T(8,128)(2,1)}, bf16[384,2048]{1,0:T(8,128)(2,1)}, u32[]{:S(2)}, u32[]{:S(2)}) collective-permute-start(bf16[384,2048]{1,0:T(8,128)(2,1)} %bitcast.20), channel_id=1, source_target_pairs={{0,0},{1,16},{2,2},{3,18},{4,4},{5,20},{6,6},{7,22},{8,8},{9,24},{... | collective-permute-start | bytes 4718600 | tf_op jit(solution)/shard_map/ppermute | solution.py:147
  52.0 0.0 copy-done.1
  52.0 1.8 shard_map.97
  53.8 0.0 all-to-all-done
  53.8 6.0 %all-to-all-start.2 = ((bf16[16,24,2048]{2,1,0:T(8,128)(2,1)}), bf16[16,24,2048]{2,1,0:T(8,128)(2,1)S(1)}, u32[]{:S(2)}, u32[]{:S(2)}) async-start(bf16[16,24,2048]{2,1,0:T(8,128)(2,1)} %bitcast.7), calls=%async_computation.2 | async-start | bytes 3145728 | tf_op jit(solution)/shard_map/all_to_all | solution.py:155
  59.8 0.0 collective-permute-done.refs_1_
  59.8 0.1 collective-permute-start.1
  59.9 0.0 collective-permute-done.2.refs_3_
  59.9 7.6 %collective-permute-start.3 = (bf16[2048,384]{1,0:T(8,128)(2,1)}, bf16[2048,384]{1,0:T(8,128)(2,1)S(1)}, u32[]{:S(2)}, u32[]{:S(2)}) collective-permute-start(bf16[2048,384]{1,0:T(8,128)(2,1)} %collective-permute-done.2.refs_3_), channel_id=1, source_target_pairs={{0,1},{1,0},{2,3},{3,2},{4,5},{5,4},{6,7},{7,6},{8,9},{9,8},{10,11... | collective-permute-start | bytes 4718600 | tf_op jit(solution)/shard_map/ppermute | solution.py:151
  67.5 0.0 collective-permute-done.4.refs_5_
  67.5 25.2 %collective-permute-start.5 = (bf16[384,2048]{1,0:T(8,128)(2,1)}, bf16[384,2048]{1,0:T(8,128)(2,1)S(1)}, u32[]{:S(2)}, u32[]{:S(2)}) collective-permute-start(bf16[384,2048]{1,0:T(8,128)(2,1)} %collective-permute-done.4.refs_5_), channel_id=1, source_target_pairs={{0,1},{1,0},{2,3},{3,2},{4,5},{5,4},{6,7},{7,6},{8,9},{9,8},{10,11... | collective-permute-start | bytes 4718600 | tf_op jit(solution)/shard_map/ppermute | solution.py:151
  92.7 0.0 collective-permute-done.1.refs_2_
  92.7 0.0 copy-start.10
  92.7 0.0 collective-permute-done.3.refs_4_
  92.7 0.0 copy-start.11
  92.7 3.2 %collective-permute-done.5.refs_6_ = bf16[384,2048]{1,0:T(8,128)(2,1)S(1)} collective-permute-done((bf16[384,2048]{1,0:T(8,128)(2,1)}, bf16[384,2048]{1,0:T(8,128)(2,1)S(1)}, u32[]{:S(2)}, u32[]{:S(2)}) %collective-permute-start.5) | collective-permute-done | bytes 1572896 | tf_op jit(solution)/shard_map/ppermute | solution.py:151
  96.0 0.0 copy-start.12
  96.0 0.0 copy-done.10
  96.0 0.0 copy-done.11
  96.0 1.1 copy-done.12
  97.1 8.9 %shard_map.95 = (bf16[384,2048]{1,0:T(8,128)(2,1)S(1)}, f32[2,384,384]{2,1,0:T(8,128)S(1)}, f32[2,384,384]{2,1,0:T(8,128)S(1)}) custom-call(bf16[384,2048]{1,0:T(8,128)(2,1)S(1)} %bitcast.15, bf16[2048,384]{1,0:T(8,128)(2,1)} %collective-permute-done.refs_1_, bf16[2048,384]{1,0:T(8,128)(2,1)} %copy-done.10, ...), custom_call_target="tpu_custom_call" | custom-call | flops 3623878656 | bytes 14942208 | tf_op jit(solution)/shard_map/pallas_call | solution.py:113
  106.0 0.0 copy-start.3
  106.1 1.2 copy-done.3
  107.2 0.0 copy-start.5
  107.3 1.0 copy-done.5
  108.3 0.0 copy-start.7
  108.3 1.0 copy-done.7
  109.3 0.0 all-to-all-done.2
  109.3 10.8 %all-to-all-start.1 = ((bf16[16,24,2048]{2,1,0:T(8,128)(2,1)}), bf16[16,24,2048]{2,1,0:T(8,128)(2,1)S(1)}, u32[]{:S(2)}, u32[]{:S(2)}) async-start(bf16[16,24,2048]{2,1,0:T(8,128)(2,1)} %bitcast.16), calls=%async_computation.1 | async-start | bytes 3145728 | tf_op jit(solution)/shard_map/all_to_all | solution.py:155
  120.1 0.0 copy-start.6
  120.1 1.3 copy-done.6
  121.4 0.0 copy-start.8
  121.4 1.3 copy-done.8
  122.7 8.8 %shard_map.98 = bf16[384,2048]{1,0:T(8,128)(2,1)S(1)} custom-call(bf16[384,2048]{1,0:T(8,128)(2,1)S(1)} %bitcast.11, bf16[2048,384]{1,0:T(8,128)(2,1)} %collective-permute-done.refs_1_, bf16[2048,384]{1,0:T(8,128)(2,1)} %copy-done.10, bf16[2048,384]{1,0:T(8,128)(2,1)} %collective-permute-done.2.refs_3_, bf16[2048,384]{1,0:T(8,128)(2,1)} %copy-done.11, ...), custom_call_target="tpu_custom_call" | custom-call | flops 3623878656 | bytes 14942208 | tf_op jit(solution)/shard_map/pallas_call | solution.py:113
  131.4 0.0 copy-start
  131.5 1.2 copy-done
  132.6 25.3 %all-to-all-done.1 = bf16[16,24,2048]{2,1,0:T(8,128)(2,1)S(1)} async-done(((bf16[16,24,2048]{2,1,0:T(8,128)(2,1)}), bf16[16,24,2048]{2,1,0:T(8,128)(2,1)S(1)}, u32[]{:S(2)}, u32[]{:S(2)}) %all-to-all-start.1) | async-done | bytes 1572896 | tf_op jit(solution)/shard_map/all_to_all | solution.py:155
  158.0 0.0 copy-start.13
  158.0 4.3 %all-to-all-start.3 = ((bf16[16,24,2048]{2,1,0:T(8,128)(2,1)}), bf16[16,24,2048]{2,1,0:T(8,128)(2,1)S(1)}, u32[]{:S(2)}, u32[]{:S(2)}) async-start(bf16[16,24,2048]{2,1,0:T(8,128)(2,1)} %bitcast.13), calls=%async_computation.3 | async-start | bytes 3145728 | tf_op jit(solution)/shard_map/all_to_all | solution.py:155
  162.3 0.0 copy-done.13
  162.4 0.1 copy.11.gates_ref
  162.5 0.0 copy-start.2
  162.5 1.0 copy-done.2
  163.5 1.7 shard_map.96
  165.2 33.4 %all-to-all-done.3 = bf16[16,24,2048]{2,1,0:T(8,128)(2,1)S(1)} async-done(((bf16[16,24,2048]{2,1,0:T(8,128)(2,1)}), bf16[16,24,2048]{2,1,0:T(8,128)(2,1)S(1)}, u32[]{:S(2)}, u32[]{:S(2)}) %all-to-all-start.3) | async-done | bytes 1572896 | tf_op jit(solution)/shard_map/all_to_all | solution.py:155
  198.6 1.5 shard_map.99
  200.1 0.6 copy.13
Async XLA Ops:
  1.4 1.0 copy-start.9
  3.5 1.2 copy-start.4
  4.7 47.3 %copy-start.1 = (bf16[128,2048]{1,0:T(8,128)(2,1)S(1)}, bf16[128,2048]{1,0:T(8,128)(2,1)}, u32[]{:S(2)}) copy-start(bf16[128,2048]{1,0:T(8,128)(2,1)} %rows_ref.1) | copy-start | bytes 1572868
  4.7 49.1 %all-to-all-start = ((bf16[16,24,2048]{2,1,0:T(8,128)(2,1)}), bf16[16,24,2048]{2,1,0:T(8,128)(2,1)S(1)}, u32[]{:S(2)}, u32[]{:S(2)}) async-start(bf16[16,24,2048]{2,1,0:T(8,128)(2,1)} %bitcast.17), calls=%async_computation | async-start | bytes 3145728 | tf_op jit(solution)/shard_map/all_to_all | solution.py:155
  12.0 47.8 %collective-permute-start = (bf16[2048,384]{1,0:T(8,128)(2,1)}, bf16[2048,384]{1,0:T(8,128)(2,1)}, u32[]{:S(2)}, u32[]{:S(2)}) collective-permute-start(bf16[2048,384]{1,0:T(8,128)(2,1)} %bitcast.18), channel_id=1, source_target_pairs={{0,0},{1,16},{2,2},{3,18},{4,4},{5,20},{6,6},{7,22},{8,8},{9,24},{... | collective-permute-start | bytes 4718600 | tf_op jit(solution)/shard_map/ppermute | solution.py:147
  25.4 34.6 %collective-permute-start.2 = (bf16[2048,384]{1,0:T(8,128)(2,1)}, bf16[2048,384]{1,0:T(8,128)(2,1)}, u32[]{:S(2)}, u32[]{:S(2)}) collective-permute-start(bf16[2048,384]{1,0:T(8,128)(2,1)} %bitcast.19), channel_id=1, source_target_pairs={{0,0},{1,16},{2,2},{3,18},{4,4},{5,20},{6,6},{7,22},{8,8},{9,24},{... | collective-permute-start | bytes 4718600 | tf_op jit(solution)/shard_map/ppermute | solution.py:147
  38.7 28.9 %collective-permute-start.4 = (bf16[384,2048]{1,0:T(8,128)(2,1)}, bf16[384,2048]{1,0:T(8,128)(2,1)}, u32[]{:S(2)}, u32[]{:S(2)}) collective-permute-start(bf16[384,2048]{1,0:T(8,128)(2,1)} %bitcast.20), channel_id=1, source_target_pairs={{0,0},{1,16},{2,2},{3,18},{4,4},{5,20},{6,6},{7,22},{8,8},{9,24},{... | collective-permute-start | bytes 4718600 | tf_op jit(solution)/shard_map/ppermute | solution.py:147
  53.8 55.5 %all-to-all-start.2 = ((bf16[16,24,2048]{2,1,0:T(8,128)(2,1)}), bf16[16,24,2048]{2,1,0:T(8,128)(2,1)S(1)}, u32[]{:S(2)}, u32[]{:S(2)}) async-start(bf16[16,24,2048]{2,1,0:T(8,128)(2,1)} %bitcast.7), calls=%async_computation.2 | async-start | bytes 3145728 | tf_op jit(solution)/shard_map/all_to_all | solution.py:155
  59.8 32.9 %collective-permute-start.1 = (bf16[2048,384]{1,0:T(8,128)(2,1)}, bf16[2048,384]{1,0:T(8,128)(2,1)S(1)}, u32[]{:S(2)}, u32[]{:S(2)}) collective-permute-start(bf16[2048,384]{1,0:T(8,128)(2,1)} %collective-permute-done.refs_1_), channel_id=1, source_target_pairs={{0,1},{1,0},{2,3},{3,2},{4,5},{5,4},{6,7},{7,6},{8,9},{9,8},{10,11... | collective-permute-start | bytes 4718600 | tf_op jit(solution)/shard_map/ppermute | solution.py:151
  59.9 32.8 %collective-permute-start.3 = (bf16[2048,384]{1,0:T(8,128)(2,1)}, bf16[2048,384]{1,0:T(8,128)(2,1)S(1)}, u32[]{:S(2)}, u32[]{:S(2)}) collective-permute-start(bf16[2048,384]{1,0:T(8,128)(2,1)} %collective-permute-done.2.refs_3_), channel_id=1, source_target_pairs={{0,1},{1,0},{2,3},{3,2},{4,5},{5,4},{6,7},{7,6},{8,9},{9,8},{10,11... | collective-permute-start | bytes 4718600 | tf_op jit(solution)/shard_map/ppermute | solution.py:151
  67.5 28.4 %collective-permute-start.5 = (bf16[384,2048]{1,0:T(8,128)(2,1)}, bf16[384,2048]{1,0:T(8,128)(2,1)S(1)}, u32[]{:S(2)}, u32[]{:S(2)}) collective-permute-start(bf16[384,2048]{1,0:T(8,128)(2,1)} %collective-permute-done.4.refs_5_), channel_id=1, source_target_pairs={{0,1},{1,0},{2,3},{3,2},{4,5},{5,4},{6,7},{7,6},{8,9},{9,8},{10,11... | collective-permute-start | bytes 4718600 | tf_op jit(solution)/shard_map/ppermute | solution.py:151
  92.7 3.2 %copy-start.10 = (bf16[2048,384]{1,0:T(8,128)(2,1)}, bf16[2048,384]{1,0:T(8,128)(2,1)S(1)}, u32[]{:S(2)}) copy-start(bf16[2048,384]{1,0:T(8,128)(2,1)S(1)} %collective-permute-done.1.refs_2_) | copy-start | bytes 4718596
  92.7 3.2 %copy-start.11 = (bf16[2048,384]{1,0:T(8,128)(2,1)}, bf16[2048,384]{1,0:T(8,128)(2,1)S(1)}, u32[]{:S(2)}) copy-start(bf16[2048,384]{1,0:T(8,128)(2,1)S(1)} %collective-permute-done.3.refs_4_) | copy-start | bytes 4718596
  96.0 1.2 copy-start.12
  106.0 1.2 copy-start.3
  107.2 1.0 copy-start.5
  108.3 1.0 copy-start.7
  109.3 48.7 %all-to-all-start.1 = ((bf16[16,24,2048]{2,1,0:T(8,128)(2,1)}), bf16[16,24,2048]{2,1,0:T(8,128)(2,1)S(1)}, u32[]{:S(2)}, u32[]{:S(2)}) async-start(bf16[16,24,2048]{2,1,0:T(8,128)(2,1)} %bitcast.16), calls=%async_computation.1 | async-start | bytes 3145728 | tf_op jit(solution)/shard_map/all_to_all | solution.py:155
  120.1 1.3 copy-start.6
  121.4 1.3 copy-start.8
  131.4 1.2 copy-start
  158.0 4.4 %copy-start.13 = (f32[128,2]{0,1:T(2,128)S(1)}, f32[128,2]{0,1:T(2,128)}, u32[]{:S(2)}) copy-start(f32[128,2]{0,1:T(2,128)} %param.10) | copy-start | bytes 3076
  158.0 40.6 %all-to-all-start.3 = ((bf16[16,24,2048]{2,1,0:T(8,128)(2,1)}), bf16[16,24,2048]{2,1,0:T(8,128)(2,1)S(1)}, u32[]{:S(2)}, u32[]{:S(2)}) async-start(bf16[16,24,2048]{2,1,0:T(8,128)(2,1)} %bitcast.13), calls=%async_computation.3 | async-start | bytes 3145728 | tf_op jit(solution)/shard_map/all_to_all | solution.py:155
  162.5 1.0 copy-start.2

commit v2 on v1

v2 whole, which is shorter than its diff:
```python
import functools

import jax
import jax.numpy as jnp
from jax import lax
from jax.experimental import pallas as pl
from jax.experimental.pallas import tpu as pltpu
from jax.sharding import PartitionSpec as P

BF16 = jnp.bfloat16
F32 = jnp.float32
VMEM_BYTES = 48 << 20


def dot(a, b, dims):
    return lax.dot_general(a, b, ((dims[:1], dims[1:]), ((), ())), preferred_element_type=F32)


def tiles(width):
    tile = min(512, width)
    return [slice(d, d + tile) for d in range(0, width, tile)]


def join(lane_refs, rows_ref):
    capacity = lane_refs[0].shape[0]
    for b in range(0, len(lane_refs), 2):
        pair = [ref[...].astype(F32) for ref in lane_refs[b : b + 2]]
        rows_ref[b * capacity : (b + 2) * capacity, :] = jnp.concatenate(pair, axis=0).astype(BF16)


def part(rows, lane_refs, columns):
    capacity = lane_refs[0].shape[0]
    for b, ref in enumerate(lane_refs):
        ref[:, columns] = rows[b * capacity : (b + 1) * capacity, :].astype(BF16)


def place_kernel(lanes, capacity, routes_ref, tokens_ref, *refs):
    lane_refs, place_ref = refs[:lanes], refs[lanes]
    tok_rows, top_count = routes_ref.shape
    routes = routes_ref[...]
    numbers = lax.broadcasted_iota(jnp.int32, (tok_rows, lanes), 1)
    named = [numbers == routes[:, k : k + 1] for k in range(top_count)]
    chosen = sum(n.astype(F32) for n in named)
    earlier = (
        lax.broadcasted_iota(jnp.int32, (tok_rows, tok_rows), 1)
        < lax.broadcasted_iota(jnp.int32, (tok_rows, tok_rows), 0)
    ).astype(F32)
    rank = dot(earlier.astype(BF16), chosen.astype(BF16), (1, 0))
    slot_numbers = lax.broadcasted_iota(jnp.int32, (tok_rows, lanes * capacity), 1)
    total = None
    for k in range(top_count):
        own = jnp.sum(jnp.where(named[k], rank, 0.0), axis=1, keepdims=True)
        slot = routes[:, k : k + 1] * capacity + own.astype(jnp.int32)
        mark = (slot_numbers == slot).astype(F32)
        place_ref[k * tok_rows : (k + 1) * tok_rows, :] = mark.astype(BF16)
        total = mark if total is None else total + mark
    total = total.astype(BF16)
    for columns in tiles(tokens_ref.shape[1]):
        part(dot(total, tokens_ref[:, columns], (0, 0)), lane_refs, columns)


def spread_kernel(top_count, place_ref, rows_ref, *lane_refs):
    tok_rows = rows_ref.shape[0]
    total = sum(
        place_ref[k * tok_rows : (k + 1) * tok_rows, :].astype(F32) for k in range(top_count)
    ).astype(BF16)
    for columns in tiles(rows_ref.shape[1]):
        part(dot(total, rows_ref[:, columns], (0, 0)), lane_refs, columns)


def forward_kernel(lanes, parts, *refs):
    lane_refs, refs = refs[:lanes], refs[lanes:]
    gate_refs, up_refs, down_refs = (refs[i * parts : (i + 1) * parts] for i in range(3))
    out_refs, refs = refs[3 * parts : 3 * parts + lanes], refs[3 * parts + lanes :]
    by_gate_ref, by_up_ref, rows_ref, hidden_ref = refs
    join(lane_refs, rows_ref)
    for i in range(parts):
        pre_gate = dot(rows_ref[...], gate_refs[i][...], (1, 0))
        pre_up = dot(rows_ref[...], up_refs[i][...], (1, 0))
        sig = jax.nn.sigmoid(pre_gate)
        act = pre_gate * sig
        hidden_ref[i] = (act * pre_up).astype(BF16)
        by_gate_ref[i] = pre_up * sig * (1.0 + pre_gate * (1.0 - sig))
        by_up_ref[i] = act
    for columns in tiles(rows_ref.shape[1]):
        rows = sum(dot(hidden_ref[i], down_refs[i][:, columns], (1, 0)) for i in range(parts))
        part(rows, out_refs, columns)


def backward_kernel(lanes, parts, *refs):
    lane_refs, refs = refs[:lanes], refs[lanes:]
    gate_refs, up_refs, down_refs = (refs[i * parts : (i + 1) * parts] for i in range(3))
    by_gate_ref, by_up_ref = refs[3 * parts : 3 * parts + 2]
    out_refs, refs = refs[3 * parts + 2 : 3 * parts + 2 + lanes], refs[3 * parts + 2 + lanes :]
    rows_ref, back_gate_ref, back_up_ref = refs
    join(lane_refs, rows_ref)
    for i in range(parts):
        back_hidden = dot(rows_ref[...], down_refs[i][...], (1, 1))
        back_gate_ref[i] = (back_hidden * by_gate_ref[i]).astype(BF16)
        back_up_ref[i] = (back_hidden * by_up_ref[i]).astype(BF16)
    for columns in tiles(rows_ref.shape[1]):
        rows = sum(
            dot(back_gate_ref[i], gate_refs[i][columns, :], (1, 1))
            + dot(back_up_ref[i], up_refs[i][columns, :], (1, 1))
            for i in range(parts)
        )
        part(rows, out_refs, columns)


def mix_kernel(lanes, place_ref, gates_ref, cotangent_ref, *refs):
    mixed_ref, gate_grad_ref, rows_ref = refs[lanes:]
    tok_rows, top_count = gates_ref.shape
    join(refs[:lanes], rows_ref)
    total, grads = None, []
    for k in range(top_count):
        raw = dot(place_ref[k * tok_rows : (k + 1) * tok_rows, :], rows_ref[...], (1, 0))
        grads.append(jnp.sum(raw * cotangent_ref[...].astype(F32), axis=1, keepdims=True))
        term = raw * gates_ref[:, k : k + 1]
        total = term if total is None else total + term
    mixed_ref[...] = total.astype(BF16)
    gate_grad_ref[...] = jnp.concatenate(grads, axis=1)


def sum_kernel(lanes, place_ref, gates_ref, *refs):
    out_ref, rows_ref = refs[lanes:]
    tok_rows, top_count = gates_ref.shape
    join(refs[:lanes], rows_ref)
    total = None
    for k in range(top_count):
        raw = dot(place_ref[k * tok_rows : (k + 1) * tok_rows, :], rows_ref[...], (1, 0))
        term = raw * gates_ref[:, k : k + 1]
        total = term if total is None else total + term
    out_ref[...] = total.astype(BF16)


def call(kernel, outs, flops, scratch=()):
    def run(*args):
        moved = sum(a.size * a.dtype.itemsize for a in (*args, *outs))
        return pl.pallas_call(
            kernel,
            out_shape=tuple(outs),
            scratch_shapes=scratch,
            compiler_params=pltpu.CompilerParams(vmem_limit_bytes=VMEM_BYTES),
            cost_estimate=pl.CostEstimate(flops=flops, bytes_accessed=moved, transcendentals=0),
        )(*args)

    return run


def body(tokens, cotangent, routes, gates, w_gate, w_up, w_down):
    tok_rows, width = tokens.shape
    top_count = routes.shape[1]
    parts, experts = lax.axis_size("dp"), lax.axis_size("expert")
    hidden = w_gate.shape[2]
    capacity = max(2, 3 * tok_rows * top_count // (2 * experts))
    capacity = -(-capacity // 8) * 8
    slots = experts * capacity
    axes = ("dp", "expert")

    def device(g, j):
        return g * experts + j

    def home(e, c):
        return device((e + 1) % parts, e // parts * parts + c)

    swap = [(device(g, e), home(e, g)) for g in range(parts) for e in range(experts)]

    def whole_expert(weight):
        own = lax.ppermute(weight[0], axes, swap)
        shares = [own]
        for step in range(1, parts):
            turn = [(j, j // parts * parts + (j + step) % parts) for j in range(experts)]
            shares.append(lax.ppermute(own, "expert", turn))
        return shares

    def exchange(lane_rows):
        received = [lane_rows[0]]
        for b in range(1, experts):
            pairs = [(home(e, c), home(e ^ b, c)) for c in range(parts) for e in range(experts)]
            received.append(lax.ppermute(lane_rows[b], axes, pairs))
        return received

    spread_flops = 2 * slots * tok_rows * width
    dot_flops = 2 * slots * width * hidden * parts
    lane_shapes = [jax.ShapeDtypeStruct((capacity, width), BF16)] * experts
    place_shape = jax.ShapeDtypeStruct((top_count * tok_rows, slots), BF16)
    unit_shape = jax.ShapeDtypeStruct((parts, slots, hidden), F32)
    token_shape = jax.ShapeDtypeStruct((tok_rows, width), BF16)
    unit_scratch = pltpu.VMEM((parts, slots, hidden), BF16)
    row_scratch = pltpu.VMEM((slots, width), BF16)

    gate_w, up_w, down_w = whole_expert(w_gate), whole_expert(w_up), whole_expert(w_down)
    column = lax.axis_index("expert")
    place_here = column // parts * parts + (lax.axis_index("dp") + parts - 1) % parts
    *x_lanes, place = call(
        functools.partial(place_kernel, experts, capacity),
        [*lane_shapes, place_shape],
        spread_flops,
    )(routes ^ place_here, tokens)
    x_rows = exchange(x_lanes)
    dy_lanes = call(functools.partial(spread_kernel, top_count), lane_shapes, spread_flops)(
        place, cotangent
    )
    dy_rows = exchange(dy_lanes)
    *out_rows, by_gate, by_up = call(
        functools.partial(forward_kernel, experts, parts),
        [*lane_shapes, unit_shape, unit_shape],
        3 * dot_flops,
        [row_scratch, unit_scratch],
    )(*x_rows, *gate_w, *up_w, *down_w)
    out_lanes = exchange(out_rows)
    grad_rows = call(
        functools.partial(backward_kernel, experts, parts),
        lane_shapes,
        3 * dot_flops,
        [row_scratch, unit_scratch, unit_scratch],
    )(*dy_rows, *gate_w, *up_w, *down_w, by_gate, by_up)
    grad_lanes = exchange(grad_rows)
    mixed, gate_grad = call(
        functools.partial(mix_kernel, experts),
        [token_shape, jax.ShapeDtypeStruct(gates.shape, F32)],
        2 * spread_flops,
        [row_scratch],
    )(place, gates, cotangent, *out_lanes)
    (token_grad,) = call(
        functools.partial(sum_kernel, experts), [token_shape], 2 * spread_flops, [row_scratch]
    )(place, gates, *grad_lanes)
    return (mixed, token_grad, gate_grad)


def solution(mesh):
    rows, weights = P(("dp", "expert"), None), P("expert", None, "dp")
    return jax.shard_map(
        body,
        mesh=mesh,
        in_specs=(rows, rows, rows, rows, weights, weights, P("expert", "dp", None)),
        out_specs=(rows, rows, rows),
        check_vma=False,
    )
```

time: 204 us -> 248 us (1.22)
  the two profiles are of different devices: /device:TPU:10 before, /device:TPU:0 now
where the time goes in v2:
time: 248 us
  waiting for transfers between devices  117 us (47%)
  starting transfers between devices  100 us (40%)
  Pallas kernels  24.5 us (10%)
  local copies, waits for them, and re-layouts  5.07 us (2%)
    ppermute x60, starting transfers between devices, exchange(): received.append(lax.ppermute(lane_rows[b], axes, pairs))  97.3 us
    ppermute x60, waiting for transfers between devices, exchange(): received.append(lax.ppermute(lane_rows[b], axes, pairs))  65.2 us
    ppermute x3, waiting for transfers between devices, whole_expert(): own = lax.ppermute(weight[0], axes, swap)  51.9 us
    pallas_call x6, Pallas kernels, run(): pl.pallas_call(kernel, out_shape=tuple(outs), scratch_shapes=scratch, com...  24.5 us
    unnamed x13, local copies, waits for them, and re-layouts  5.07 us
  transfers between devices with their start and end apart: 66, of which 25 were waited for; matrix products, arithmetic and copies ran while one was open for 1% of the time, Pallas kernels for 9%

profile of v2, /device:TPU:0, one launch (start us, length us, event | category | flops | bytes accessed | tf_op | source)
XLA Modules:
  0.0 247.9 jit_solution(13841101514140729422)
XLA Ops:
  0.6 3.0 %collective-permute-start.15 = (bf16[2048,384]{1,0:T(8,128)(2,1)}, bf16[2048,384]{1,0:T(8,128)(2,1)}, u32[]{:S(2)}, u32[]{:S(2)}) collective-permute-start(bf16[2048,384]{1,0:T(8,128)(2,1)} %bitcast.3), channel_id=1, source_target_pairs={{0,16},{1,0},{2,18},{3,2},{4,20},{5,4},{6,22},{7,6},{8,24},{9,8},{... | collective-permute-start | bytes 4718600 | tf_op jit(solution)/shard_map/ppermute | solution.py:169
  3.7 18.2 %collective-permute-done.15.refs_16_ = bf16[2048,384]{1,0:T(8,128)(2,1)} collective-permute-done((bf16[2048,384]{1,0:T(8,128)(2,1)}, bf16[2048,384]{1,0:T(8,128)(2,1)}, u32[]{:S(2)}, u32[]{:S(2)}) %collective-permute-start.15) | collective-permute-done | bytes 1572896 | tf_op jit(solution)/shard_map/ppermute | solution.py:169
  21.9 16.8 %collective-permute-done.17.refs_18_ = bf16[2048,384]{1,0:T(8,128)(2,1)} collective-permute-done((bf16[2048,384]{1,0:T(8,128)(2,1)}, bf16[2048,384]{1,0:T(8,128)(2,1)}, u32[]{:S(2)}, u32[]{:S(2)}) %collective-permute-start.17) | collective-permute-done | bytes 1572896 | tf_op jit(solution)/shard_map/ppermute | solution.py:169
  38.7 16.8 %collective-permute-done.19.refs_20_ = bf16[384,2048]{1,0:T(8,128)(2,1)} collective-permute-done((bf16[384,2048]{1,0:T(8,128)(2,1)}, bf16[384,2048]{1,0:T(8,128)(2,1)}, u32[]{:S(2)}, u32[]{:S(2)}) %collective-permute-start.19) | collective-permute-done | bytes 1572896 | tf_op jit(solution)/shard_map/ppermute | solution.py:169
  56.4 1.0 copy-done.3
  57.4 1.0 shard_map.94
  58.5 2.5 %collective-permute-start = (bf16[24,2048]{1,0:T(8,128)(2,1)S(1)}, bf16[24,2048]{1,0:T(8,128)(2,1)S(1)}, u32[]{:S(2)}, u32[]{:S(2)}) collective-permute-start(bf16[24,2048]{1,0:T(8,128)(2,1)S(1)} %get-tuple-element.74), channel_id=1, source_target_pairs={{16,0},{0,16},{18,2},{2,18},{20,4},{4,20},{22,6},{6,22},{24,8},{8,... | collective-permute-start | bytes 294920 | tf_op jit(solution)/shard_map/ppermute | solution.py:180
  61.0 1.5 collective-permute-start.1
  62.5 2.0 collective-permute-done.refs_1_
  64.5 2.7 %collective-permute-start.2 = (bf16[24,2048]{1,0:T(8,128)(2,1)S(1)}, bf16[24,2048]{1,0:T(8,128)(2,1)S(1)}, u32[]{:S(2)}, u32[]{:S(2)}) collective-permute-start(bf16[24,2048]{1,0:T(8,128)(2,1)S(1)} %get-tuple-element.76), channel_id=1, source_target_pairs={{16,2},{0,18},{18,0},{2,16},{20,6},{4,22},{22,4},{6,20},{24,10},{8... | collective-permute-start | bytes 294920 | tf_op jit(solution)/shard_map/ppermute | solution.py:180
  67.1 1.6 collective-permute-start.3
  68.7 1.3 collective-permute-done.2.refs_3_
  70.0 2.7 %collective-permute-start.4 = (bf16[24,2048]{1,0:T(8,128)(2,1)S(1)}, bf16[24,2048]{1,0:T(8,128)(2,1)S(1)}, u32[]{:S(2)}, u32[]{:S(2)}) collective-permute-start(bf16[24,2048]{1,0:T(8,128)(2,1)S(1)} %get-tuple-element.78), channel_id=1, source_target_pairs={{16,4},{0,20},{18,6},{2,22},{20,0},{4,16},{22,2},{6,18},{24,12},{8... | collective-permute-start | bytes 294920 | tf_op jit(solution)/shard_map/ppermute | solution.py:180
  72.7 1.4 collective-permute-start.5
  74.1 2.2 collective-permute-done.4.refs_5_
  76.3 2.9 %collective-permute-start.6 = (bf16[24,2048]{1,0:T(8,128)(2,1)S(1)}, bf16[24,2048]{1,0:T(8,128)(2,1)S(1)}, u32[]{:S(2)}, u32[]{:S(2)}) collective-permute-start(bf16[24,2048]{1,0:T(8,128)(2,1)S(1)} %get-tuple-element.80), channel_id=1, source_target_pairs={{16,6},{0,22},{18,4},{2,20},{20,2},{4,18},{22,0},{6,16},{24,14},{8... | collective-permute-start | bytes 294920 | tf_op jit(solution)/shard_map/ppermute | solution.py:180
  79.2 2.6 %collective-permute-start.7 = (bf16[24,2048]{1,0:T(8,128)(2,1)S(1)}, bf16[24,2048]{1,0:T(8,128)(2,1)S(1)}, u32[]{:S(2)}, u32[]{:S(2)}) collective-permute-start(bf16[24,2048]{1,0:T(8,128)(2,1)S(1)} %get-tuple-element.81), channel_id=1, source_target_pairs={{16,24},{0,8},{18,26},{2,10},{20,28},{4,12},{22,30},{6,14},{24,16}... | collective-permute-start | bytes 294920 | tf_op jit(solution)/shard_map/ppermute | solution.py:180
  81.8 3.4 %collective-permute-done.6.refs_7_ = bf16[24,2048]{1,0:T(8,128)(2,1)S(1)} collective-permute-done((bf16[24,2048]{1,0:T(8,128)(2,1)S(1)}, bf16[24,2048]{1,0:T(8,128)(2,1)S(1)}, u32[]{:S(2)}, u32[]{:S(2)}) %collective-permute-start.6) | collective-permute-done | bytes 98336 | tf_op jit(solution)/shard_map/ppermute | solution.py:180
  85.2 1.7 collective-permute-start.8
  86.9 2.0 collective-permute-done.7.refs_8_
  89.3 2.6 %collective-permute-done.8.refs_9_ = bf16[24,2048]{1,0:T(8,128)(2,1)S(1)} collective-permute-done((bf16[24,2048]{1,0:T(8,128)(2,1)S(1)}, bf16[24,2048]{1,0:T(8,128)(2,1)S(1)}, u32[]{:S(2)}, u32[]{:S(2)}) %collective-permute-start.8) | collective-permute-done | bytes 98336 | tf_op jit(solution)/shard_map/ppermute | solution.py:180
  91.9 1.5 collective-permute-start.10
  93.4 5.1 %collective-permute-done.9.refs_10_ = bf16[24,2048]{1,0:T(8,128)(2,1)S(1)} collective-permute-done((bf16[24,2048]{1,0:T(8,128)(2,1)S(1)}, bf16[24,2048]{1,0:T(8,128)(2,1)S(1)}, u32[]{:S(2)}, u32[]{:S(2)}) %collective-permute-start.9) | collective-permute-done | bytes 98336 | tf_op jit(solution)/shard_map/ppermute | solution.py:180
  98.5 1.0 collective-permute-start.11
  99.5 5.0 %collective-permute-done.10.refs_11_ = bf16[24,2048]{1,0:T(8,128)(2,1)S(1)} collective-permute-done((bf16[24,2048]{1,0:T(8,128)(2,1)S(1)}, bf16[24,2048]{1,0:T(8,128)(2,1)S(1)}, u32[]{:S(2)}, u32[]{:S(2)}) %collective-permute-start.10) | collective-permute-done | bytes 98336 | tf_op jit(solution)/shard_map/ppermute | solution.py:180
  105.7 2.3 collective-permute-start.13
  108.0 4.9 %collective-permute-done.12.refs_13_ = bf16[24,2048]{1,0:T(8,128)(2,1)S(1)} collective-permute-done((bf16[24,2048]{1,0:T(8,128)(2,1)S(1)}, bf16[24,2048]{1,0:T(8,128)(2,1)S(1)}, u32[]{:S(2)}, u32[]{:S(2)}) %collective-permute-start.12) | collective-permute-done | bytes 98336 | tf_op jit(solution)/shard_map/ppermute | solution.py:180
  113.4 1.0 copy-done
  115.1 1.0 collective-permute-start.36
  116.1 5.1 %collective-permute-done.14.refs_15_ = bf16[24,2048]{1,0:T(8,128)(2,1)S(1)} collective-permute-done((bf16[24,2048]{1,0:T(8,128)(2,1)S(1)}, bf16[24,2048]{1,0:T(8,128)(2,1)S(1)}, u32[]{:S(2)}, u32[]{:S(2)}) %collective-permute-start.14) | collective-permute-done | bytes 98336 | tf_op jit(solution)/shard_map/ppermute | solution.py:180
  121.2 2.7 %collective-permute-start.38 = (bf16[24,2048]{1,0:T(8,128)(2,1)S(1)}, bf16[24,2048]{1,0:T(8,128)(2,1)S(1)}, u32[]{:S(2)}, u32[]{:S(2)}) collective-permute-start(bf16[24,2048]{1,0:T(8,128)(2,1)S(1)} %get-tuple-element.109), channel_id=1, source_target_pairs={{16,2},{0,18},{18,0},{2,16},{20,6},{4,22},{22,4},{6,20},{24,10},{8... | collective-permute-start | bytes 294920 | tf_op jit(solution)/shard_map/ppermute | solution.py:180
  123.8 2.4 collective-permute-done.37.refs_2_
  126.7 4.9 %collective-permute-done.39.refs_4_ = bf16[24,2048]{1,0:T(8,128)(2,1)S(1)} collective-permute-done((bf16[24,2048]{1,0:T(8,128)(2,1)S(1)}, bf16[24,2048]{1,0:T(8,128)(2,1)S(1)}, u32[]{:S(2)}, u32[]{:S(2)}) %collective-permute-start.39) | collective-permute-done | bytes 98336 | tf_op jit(solution)/shard_map/ppermute | solution.py:180
  132.5 2.5 %collective-permute-start.42 = (bf16[24,2048]{1,0:T(8,128)(2,1)S(1)}, bf16[24,2048]{1,0:T(8,128)(2,1)S(1)}, u32[]{:S(2)}, u32[]{:S(2)}) collective-permute-start(bf16[24,2048]{1,0:T(8,128)(2,1)S(1)} %get-tuple-element.113), channel_id=1, source_target_pairs={{16,6},{0,22},{18,4},{2,20},{20,2},{4,18},{22,0},{6,16},{24,14},{8... | collective-permute-start | bytes 294920 | tf_op jit(solution)/shard_map/ppermute | solution.py:180
  135.1 3.0 %collective-permute-done.41.refs_6_ = bf16[24,2048]{1,0:T(8,128)(2,1)S(1)} collective-permute-done((bf16[24,2048]{1,0:T(8,128)(2,1)S(1)}, bf16[24,2048]{1,0:T(8,128)(2,1)S(1)}, u32[]{:S(2)}, u32[]{:S(2)}) %collective-permute-start.41) | collective-permute-done | bytes 98336 | tf_op jit(solution)/shard_map/ppermute | solution.py:180
  138.6 1.8 collective-permute-done.42.refs_7_
  140.4 1.1 collective-permute-start.44
  141.5 8.0 %collective-permute-done.43.refs_8_ = bf16[24,2048]{1,0:T(8,128)(2,1)S(1)} collective-permute-done((bf16[24,2048]{1,0:T(8,128)(2,1)S(1)}, bf16[24,2048]{1,0:T(8,128)(2,1)S(1)}, u32[]{:S(2)}, u32[]{:S(2)}) %collective-permute-start.43) | collective-permute-done | bytes 98336 | tf_op jit(solution)/shard_map/ppermute | solution.py:180
  149.9 3.5 %collective-permute-done.44.refs_9_ = bf16[24,2048]{1,0:T(8,128)(2,1)S(1)} collective-permute-done((bf16[24,2048]{1,0:T(8,128)(2,1)S(1)}, bf16[24,2048]{1,0:T(8,128)(2,1)S(1)}, u32[]{:S(2)}, u32[]{:S(2)}) %collective-permute-start.44) | collective-permute-done | bytes 98336 | tf_op jit(solution)/shard_map/ppermute | solution.py:180
  154.1 4.7 %collective-permute-done.45.refs_10_ = bf16[24,2048]{1,0:T(8,128)(2,1)S(1)} collective-permute-done((bf16[24,2048]{1,0:T(8,128)(2,1)S(1)}, bf16[24,2048]{1,0:T(8,128)(2,1)S(1)}, u32[]{:S(2)}, u32[]{:S(2)}) %collective-permute-start.45) | collective-permute-done | bytes 98336 | tf_op jit(solution)/shard_map/ppermute | solution.py:180
  158.9 1.7 collective-permute-start.48
  160.5 1.8 collective-permute-start.49
  162.3 6.0 %collective-permute-start.50 = (bf16[24,2048]{1,0:T(8,128)(2,1)S(1)}, bf16[24,2048]{1,0:T(8,128)(2,1)S(1)}, u32[]{:S(2)}, u32[]{:S(2)}) collective-permute-start(bf16[24,2048]{1,0:T(8,128)(2,1)S(1)} %get-tuple-element.121), channel_id=1, source_target_pairs={{16,14},{0,30},{18,12},{2,28},{20,10},{4,26},{22,8},{6,24},{24,6},... | collective-permute-start | bytes 294920 | tf_op jit(solution)/shard_map/ppermute | solution.py:180
  168.3 8.9 %shard_map.95 = (bf16[24,2048]{1,0:T(8,128)(2,1)S(1)}, bf16[24,2048]{1,0:T(8,128)(2,1)S(1)}, bf16[24,2048]{1,0:T(8,128)(2,1)S(1)}, bf16[24,2048]{1,0:T(8,128)(2,...) custom-call(bf16[24,2048]{1,0:T(8,128)(2,1)S(1)} %get-tuple-element., ...), custom_call_target="tpu_custom_call" | custom-call | flops 3623878656 | bytes 14942208 | tf_op jit(solution)/shard_map/pallas_call | solution.py:139
  177.5 3.3 %collective-permute-start.23 = (bf16[24,2048]{1,0:T(8,128)(2,1)S(1)}, bf16[24,2048]{1,0:T(8,128)(2,1)S(1)}, u32[]{:S(2)}, u32[]{:S(2)}) collective-permute-start(bf16[24,2048]{1,0:T(8,128)(2,1)S(1)} %get-tuple-element.92), channel_id=1, source_target_pairs={{16,2},{0,18},{18,0},{2,16},{20,6},{4,22},{22,4},{6,20},{24,10},{8... | collective-permute-start | bytes 294920 | tf_op jit(solution)/shard_map/ppermute | solution.py:180
  180.8 1.5 collective-permute-start.25
  183.0 3.7 %collective-permute-start.27 = (bf16[24,2048]{1,0:T(8,128)(2,1)S(1)}, bf16[24,2048]{1,0:T(8,128)(2,1)S(1)}, u32[]{:S(2)}, u32[]{:S(2)}) collective-permute-start(bf16[24,2048]{1,0:T(8,128)(2,1)S(1)} %get-tuple-element.96), channel_id=1, source_target_pairs={{16,6},{0,22},{18,4},{2,20},{20,2},{4,18},{22,0},{6,16},{24,14},{8... | collective-permute-start | bytes 294920 | tf_op jit(solution)/shard_map/ppermute | solution.py:180
  186.7 3.1 %collective-permute-start.29 = (bf16[24,2048]{1,0:T(8,128)(2,1)S(1)}, bf16[24,2048]{1,0:T(8,128)(2,1)S(1)}, u32[]{:S(2)}, u32[]{:S(2)}) collective-permute-start(bf16[24,2048]{1,0:T(8,128)(2,1)S(1)} %get-tuple-element.98), channel_id=1, source_target_pairs={{16,8},{0,24},{18,10},{2,26},{20,12},{4,28},{22,14},{6,30},{24,0},... | collective-permute-start | bytes 294920 | tf_op jit(solution)/shard_map/ppermute | solution.py:180
  189.8 4.6 %collective-permute-start.31 = (bf16[24,2048]{1,0:T(8,128)(2,1)S(1)}, bf16[24,2048]{1,0:T(8,128)(2,1)S(1)}, u32[]{:S(2)}, u32[]{:S(2)}) collective-permute-start(bf16[24,2048]{1,0:T(8,128)(2,1)S(1)} %get-tuple-element.100), channel_id=1, source_target_pairs={{16,10},{0,26},{18,8},{2,24},{20,14},{4,30},{22,12},{6,28},{24,2},... | collective-permute-start | bytes 294920 | tf_op jit(solution)/shard_map/ppermute | solution.py:180
  194.9 3.4 %collective-permute-start.33 = (bf16[24,2048]{1,0:T(8,128)(2,1)S(1)}, bf16[24,2048]{1,0:T(8,128)(2,1)S(1)}, u32[]{:S(2)}, u32[]{:S(2)}) collective-permute-start(bf16[24,2048]{1,0:T(8,128)(2,1)S(1)} %get-tuple-element.102), channel_id=1, source_target_pairs={{16,12},{0,28},{18,14},{2,30},{20,8},{4,24},{22,10},{6,26},{24,4},... | collective-permute-start | bytes 294920 | tf_op jit(solution)/shard_map/ppermute | solution.py:180
  198.3 1.2 collective-permute-start.34
  199.5 4.3 %collective-permute-start.35 = (bf16[24,2048]{1,0:T(8,128)(2,1)S(1)}, bf16[24,2048]{1,0:T(8,128)(2,1)S(1)}, u32[]{:S(2)}, u32[]{:S(2)}) collective-permute-start(bf16[24,2048]{1,0:T(8,128)(2,1)S(1)} %get-tuple-element.104), channel_id=1, source_target_pairs={{16,14},{0,30},{18,12},{2,28},{20,10},{4,26},{22,8},{6,24},{24,6},... | collective-permute-start | bytes 294920 | tf_op jit(solution)/shard_map/ppermute | solution.py:180
  203.8 9.7 %shard_map.98 = (bf16[24,2048]{1,0:T(8,128)(2,1)S(1)}, bf16[24,2048]{1,0:T(8,128)(2,1)S(1)}, bf16[24,2048]{1,0:T(8,128)(2,1)S(1)}, bf16[24,2048]{1,0:T(8,128)(2,...) custom-call(bf16[24,2048]{1,0:T(8,128)(2,1)S(1)} %get-tuple-element., ...), custom_call_target="tpu_custom_call" | custom-call | flops 3623878656 | bytes 14942208 | tf_op jit(solution)/shard_map/pallas_call | solution.py:139
  214.3 2.8 %collective-permute-start.53 = (bf16[24,2048]{1,0:T(8,128)(2,1)S(1)}, bf16[24,2048]{1,0:T(8,128)(2,1)S(1)}, u32[]{:S(2)}, u32[]{:S(2)}) collective-permute-start(bf16[24,2048]{1,0:T(8,128)(2,1)S(1)} %get-tuple-element.127), channel_id=1, source_target_pairs={{16,2},{0,18},{18,0},{2,16},{20,6},{4,22},{22,4},{6,20},{24,10},{8... | collective-permute-start | bytes 294920 | tf_op jit(solution)/shard_map/ppermute | solution.py:180
  217.1 2.2 collective-permute-start.55
  219.2 5.0 %collective-permute-start.57 = (bf16[24,2048]{1,0:T(8,128)(2,1)S(1)}, bf16[24,2048]{1,0:T(8,128)(2,1)S(1)}, u32[]{:S(2)}, u32[]{:S(2)}) collective-permute-start(bf16[24,2048]{1,0:T(8,128)(2,1)S(1)} %get-tuple-element.131), channel_id=1, source_target_pairs={{16,6},{0,22},{18,4},{2,20},{20,2},{4,18},{22,0},{6,16},{24,14},{8... | collective-permute-start | bytes 294920 | tf_op jit(solution)/shard_map/ppermute | solution.py:180
  224.2 1.7 collective-permute-start.59
  226.7 5.2 %collective-permute-start.61 = (bf16[24,2048]{1,0:T(8,128)(2,1)}, bf16[24,2048]{1,0:T(8,128)(2,1)S(1)}, u32[]{:S(2)}, u32[]{:S(2)}) collective-permute-start(bf16[24,2048]{1,0:T(8,128)(2,1)} %get-tuple-element.135), channel_id=1, source_target_pairs={{16,10},{0,26},{18,8},{2,24},{20,14},{4,30},{22,12},{6,28},{24,2},... | collective-permute-start | bytes 294920 | tf_op jit(solution)/shard_map/ppermute | solution.py:180
  231.9 2.6 %collective-permute-start.63 = (bf16[24,2048]{1,0:T(8,128)(2,1)}, bf16[24,2048]{1,0:T(8,128)(2,1)}, u32[]{:S(2)}, u32[]{:S(2)}) collective-permute-start(bf16[24,2048]{1,0:T(8,128)(2,1)} %get-tuple-element.137), channel_id=1, source_target_pairs={{16,12},{0,28},{18,14},{2,30},{20,8},{4,24},{22,10},{6,26},{24,4},... | collective-permute-start | bytes 294920 | tf_op jit(solution)/shard_map/ppermute | solution.py:180
  234.6 1.2 collective-permute-start.64
  235.7 5.6 %collective-permute-start.65 = (bf16[24,2048]{1,0:T(8,128)(2,1)}, bf16[24,2048]{1,0:T(8,128)(2,1)}, u32[]{:S(2)}, u32[]{:S(2)}) collective-permute-start(bf16[24,2048]{1,0:T(8,128)(2,1)} %get-tuple-element.139), channel_id=1, source_target_pairs={{16,14},{0,30},{18,12},{2,28},{20,10},{4,26},{22,8},{6,24},{24,6},... | collective-permute-start | bytes 294920 | tf_op jit(solution)/shard_map/ppermute | solution.py:180
  241.5 1.7 shard_map.96
  243.8 1.5 copy.18
  245.3 2.5 %shard_map.99 = bf16[128,2048]{1,0:T(8,128)(2,1)} custom-call(bf16[256,384]{1,0:T(8,128)(2,1)S(1)} %get-tuple-element.72.place_ref, f32[128,2]{1,0:T(8,128)S(1)} %copy.16.gates_ref, bf16[24,2048]{1,0:T(8,128)(2,1)S(1)} %get-tuple-element.124.refs_0_, bf16[24,2048]{1,0:T(8,128)(2,1)S(1)} %collective-permute-done.51.refs_1_, ...), custom_call_target="tpu_custom_call" | custom-call | flops 402653184 | bytes 2294784 | tf_op jit(solution)/shard_map/pallas_call | solution.py:139
  (88 shorter events, 10.2 us)
Async XLA Ops:
  0.6 21.2 %collective-permute-start.15 = (bf16[2048,384]{1,0:T(8,128)(2,1)}, bf16[2048,384]{1,0:T(8,128)(2,1)}, u32[]{:S(2)}, u32[]{:S(2)}) collective-permute-start(bf16[2048,384]{1,0:T(8,128)(2,1)} %bitcast.3), channel_id=1, source_target_pairs={{0,16},{1,0},{2,18},{3,2},{4,20},{5,4},{6,22},{7,6},{8,24},{9,8},{... | collective-permute-start | bytes 4718600 | tf_op jit(solution)/shard_map/ppermute | solution.py:169
  3.6 35.1 %collective-permute-start.17 = (bf16[2048,384]{1,0:T(8,128)(2,1)}, bf16[2048,384]{1,0:T(8,128)(2,1)}, u32[]{:S(2)}, u32[]{:S(2)}) collective-permute-start(bf16[2048,384]{1,0:T(8,128)(2,1)} %bitcast.4), channel_id=1, source_target_pairs={{0,16},{1,0},{2,18},{3,2},{4,20},{5,4},{6,22},{7,6},{8,24},{9,8},{... | collective-permute-start | bytes 4718600 | tf_op jit(solution)/shard_map/ppermute | solution.py:169
  3.7 51.9 %collective-permute-start.19 = (bf16[384,2048]{1,0:T(8,128)(2,1)}, bf16[384,2048]{1,0:T(8,128)(2,1)}, u32[]{:S(2)}, u32[]{:S(2)}) collective-permute-start(bf16[384,2048]{1,0:T(8,128)(2,1)} %bitcast.5), channel_id=1, source_target_pairs={{0,16},{1,0},{2,18},{3,2},{4,20},{5,4},{6,22},{7,6},{8,24},{9,8},{... | collective-permute-start | bytes 4718600 | tf_op jit(solution)/shard_map/ppermute | solution.py:169
  21.9 137.0 %collective-permute-start.16 = (bf16[2048,384]{1,0:T(8,128)(2,1)}, bf16[2048,384]{1,0:T(8,128)(2,1)}, u32[]{:S(2)}, u32[]{:S(2)}) collective-permute-start(bf16[2048,384]{1,0:T(8,128)(2,1)} %collective-permute-done.15.refs_16_), channel_id=1, source_target_pairs={{0,1},{1,0},{2,3},{3,2},{4,5},{5,4},{6,7},{7,6},{8,9},{9,8},{10,11... | collective-permute-start | bytes 4718600 | tf_op jit(solution)/shard_map/ppermute | solution.py:173
  38.7 121.8 %collective-permute-start.18 = (bf16[2048,384]{1,0:T(8,128)(2,1)}, bf16[2048,384]{1,0:T(8,128)(2,1)}, u32[]{:S(2)}, u32[]{:S(2)}) collective-permute-start(bf16[2048,384]{1,0:T(8,128)(2,1)} %collective-permute-done.17.refs_18_), channel_id=1, source_target_pairs={{0,1},{1,0},{2,3},{3,2},{4,5},{5,4},{6,7},{7,6},{8,9},{9,8},{10,11... | collective-permute-start | bytes 4718600 | tf_op jit(solution)/shard_map/ppermute | solution.py:173
  55.6 106.8 %collective-permute-start.20 = (bf16[384,2048]{1,0:T(8,128)(2,1)}, bf16[384,2048]{1,0:T(8,128)(2,1)}, u32[]{:S(2)}, u32[]{:S(2)}) collective-permute-start(bf16[384,2048]{1,0:T(8,128)(2,1)} %collective-permute-done.19.refs_20_), channel_id=1, source_target_pairs={{0,1},{1,0},{2,3},{3,2},{4,5},{5,4},{6,7},{7,6},{8,9},{9,8},{10,11... | collective-permute-start | bytes 4718600 | tf_op jit(solution)/shard_map/ppermute | solution.py:173
  58.5 6.0 %collective-permute-start = (bf16[24,2048]{1,0:T(8,128)(2,1)S(1)}, bf16[24,2048]{1,0:T(8,128)(2,1)S(1)}, u32[]{:S(2)}, u32[]{:S(2)}) collective-permute-start(bf16[24,2048]{1,0:T(8,128)(2,1)S(1)} %get-tuple-element.74), channel_id=1, source_target_pairs={{16,0},{0,16},{18,2},{2,18},{20,4},{4,20},{22,6},{6,22},{24,8},{8,... | collective-permute-start | bytes 294920 | tf_op jit(solution)/shard_map/ppermute | solution.py:180
  61.0 6.1 %collective-permute-start.1 = (bf16[24,2048]{1,0:T(8,128)(2,1)S(1)}, bf16[24,2048]{1,0:T(8,128)(2,1)S(1)}, u32[]{:S(2)}, u32[]{:S(2)}) collective-permute-start(bf16[24,2048]{1,0:T(8,128)(2,1)S(1)} %get-tuple-element.75), channel_id=1, source_target_pairs={{16,18},{0,2},{18,16},{2,0},{20,22},{4,6},{22,20},{6,4},{24,26},{8... | collective-permute-start | bytes 294920 | tf_op jit(solution)/shard_map/ppermute | solution.py:180
  64.5 5.5 %collective-permute-start.2 = (bf16[24,2048]{1,0:T(8,128)(2,1)S(1)}, bf16[24,2048]{1,0:T(8,128)(2,1)S(1)}, u32[]{:S(2)}, u32[]{:S(2)}) collective-permute-start(bf16[24,2048]{1,0:T(8,128)(2,1)S(1)} %get-tuple-element.76), channel_id=1, source_target_pairs={{16,2},{0,18},{18,0},{2,16},{20,6},{4,22},{22,4},{6,20},{24,10},{8... | collective-permute-start | bytes 294920 | tf_op jit(solution)/shard_map/ppermute | solution.py:180
  67.1 5.6 %collective-permute-start.3 = (bf16[24,2048]{1,0:T(8,128)(2,1)S(1)}, bf16[24,2048]{1,0:T(8,128)(2,1)S(1)}, u32[]{:S(2)}, u32[]{:S(2)}) collective-permute-start(bf16[24,2048]{1,0:T(8,128)(2,1)S(1)} %get-tuple-element.77), channel_id=1, source_target_pairs={{16,20},{0,4},{18,22},{2,6},{20,16},{4,0},{22,18},{6,2},{24,28},{8... | collective-permute-start | bytes 294920 | tf_op jit(solution)/shard_map/ppermute | solution.py:180
  70.0 6.3 %collective-permute-start.4 = (bf16[24,2048]{1,0:T(8,128)(2,1)S(1)}, bf16[24,2048]{1,0:T(8,128)(2,1)S(1)}, u32[]{:S(2)}, u32[]{:S(2)}) collective-permute-start(bf16[24,2048]{1,0:T(8,128)(2,1)S(1)} %get-tuple-element.78), channel_id=1, source_target_pairs={{16,4},{0,20},{18,6},{2,22},{20,0},{4,16},{22,2},{6,18},{24,12},{8... | collective-permute-start | bytes 294920 | tf_op jit(solution)/shard_map/ppermute | solution.py:180
  72.7 6.5 %collective-permute-start.5 = (bf16[24,2048]{1,0:T(8,128)(2,1)S(1)}, bf16[24,2048]{1,0:T(8,128)(2,1)S(1)}, u32[]{:S(2)}, u32[]{:S(2)}) collective-permute-start(bf16[24,2048]{1,0:T(8,128)(2,1)S(1)} %get-tuple-element.79), channel_id=1, source_target_pairs={{16,22},{0,6},{18,20},{2,4},{20,18},{4,2},{22,16},{6,0},{24,30},{8... | collective-permute-start | bytes 294920 | tf_op jit(solution)/shard_map/ppermute | solution.py:180
  76.3 8.9 %collective-permute-start.6 = (bf16[24,2048]{1,0:T(8,128)(2,1)S(1)}, bf16[24,2048]{1,0:T(8,128)(2,1)S(1)}, u32[]{:S(2)}, u32[]{:S(2)}) collective-permute-start(bf16[24,2048]{1,0:T(8,128)(2,1)S(1)} %get-tuple-element.80), channel_id=1, source_target_pairs={{16,6},{0,22},{18,4},{2,20},{20,2},{4,18},{22,0},{6,16},{24,14},{8... | collective-permute-start | bytes 294920 | tf_op jit(solution)/shard_map/ppermute | solution.py:180
  79.2 9.7 %collective-permute-start.7 = (bf16[24,2048]{1,0:T(8,128)(2,1)S(1)}, bf16[24,2048]{1,0:T(8,128)(2,1)S(1)}, u32[]{:S(2)}, u32[]{:S(2)}) collective-permute-start(bf16[24,2048]{1,0:T(8,128)(2,1)S(1)} %get-tuple-element.81), channel_id=1, source_target_pairs={{16,24},{0,8},{18,26},{2,10},{20,28},{4,12},{22,30},{6,14},{24,16}... | collective-permute-start | bytes 294920 | tf_op jit(solution)/shard_map/ppermute | solution.py:180
  85.2 6.7 %collective-permute-start.8 = (bf16[24,2048]{1,0:T(8,128)(2,1)S(1)}, bf16[24,2048]{1,0:T(8,128)(2,1)S(1)}, u32[]{:S(2)}, u32[]{:S(2)}) collective-permute-start(bf16[24,2048]{1,0:T(8,128)(2,1)S(1)} %get-tuple-element.82), channel_id=1, source_target_pairs={{16,8},{0,24},{18,10},{2,26},{20,12},{4,28},{22,14},{6,30},{24,0},... | collective-permute-start | bytes 294920 | tf_op jit(solution)/shard_map/ppermute | solution.py:180
  88.9 9.6 %collective-permute-start.9 = (bf16[24,2048]{1,0:T(8,128)(2,1)S(1)}, bf16[24,2048]{1,0:T(8,128)(2,1)S(1)}, u32[]{:S(2)}, u32[]{:S(2)}) collective-permute-start(bf16[24,2048]{1,0:T(8,128)(2,1)S(1)} %get-tuple-element.83), channel_id=1, source_target_pairs={{16,26},{0,10},{18,24},{2,8},{20,30},{4,14},{22,28},{6,12},{24,18}... | collective-permute-start | bytes 294920 | tf_op jit(solution)/shard_map/ppermute | solution.py:180
  91.9 12.6 %collective-permute-start.10 = (bf16[24,2048]{1,0:T(8,128)(2,1)S(1)}, bf16[24,2048]{1,0:T(8,128)(2,1)S(1)}, u32[]{:S(2)}, u32[]{:S(2)}) collective-permute-start(bf16[24,2048]{1,0:T(8,128)(2,1)S(1)} %get-tuple-element.84), channel_id=1, source_target_pairs={{16,10},{0,26},{18,8},{2,24},{20,14},{4,30},{22,12},{6,28},{24,2},... | collective-permute-start | bytes 294920 | tf_op jit(solution)/shard_map/ppermute | solution.py:180
  98.5 7.2 %collective-permute-start.11 = (bf16[24,2048]{1,0:T(8,128)(2,1)S(1)}, bf16[24,2048]{1,0:T(8,128)(2,1)S(1)}, u32[]{:S(2)}, u32[]{:S(2)}) collective-permute-start(bf16[24,2048]{1,0:T(8,128)(2,1)S(1)} %get-tuple-element.85), channel_id=1, source_target_pairs={{16,28},{0,12},{18,30},{2,14},{20,24},{4,8},{22,26},{6,10},{24,20}... | collective-permute-start | bytes 294920 | tf_op jit(solution)/shard_map/ppermute | solution.py:180
  104.5 8.4 %collective-permute-start.12 = (bf16[24,2048]{1,0:T(8,128)(2,1)S(1)}, bf16[24,2048]{1,0:T(8,128)(2,1)S(1)}, u32[]{:S(2)}, u32[]{:S(2)}) collective-permute-start(bf16[24,2048]{1,0:T(8,128)(2,1)S(1)} %get-tuple-element.86), channel_id=1, source_target_pairs={{16,12},{0,28},{18,14},{2,30},{20,8},{4,24},{22,10},{6,26},{24,4},... | collective-permute-start | bytes 294920 | tf_op jit(solution)/shard_map/ppermute | solution.py:180
  105.7 9.3 %collective-permute-start.13 = (bf16[24,2048]{1,0:T(8,128)(2,1)S(1)}, bf16[24,2048]{1,0:T(8,128)(2,1)S(1)}, u32[]{:S(2)}, u32[]{:S(2)}) collective-permute-start(bf16[24,2048]{1,0:T(8,128)(2,1)S(1)} %get-tuple-element.87), channel_id=1, source_target_pairs={{16,30},{0,14},{18,28},{2,12},{20,26},{4,10},{22,24},{6,8},{24,22}... | collective-permute-start | bytes 294920 | tf_op jit(solution)/shard_map/ppermute | solution.py:180
  112.9 8.2 %collective-permute-start.14 = (bf16[24,2048]{1,0:T(8,128)(2,1)S(1)}, bf16[24,2048]{1,0:T(8,128)(2,1)S(1)}, u32[]{:S(2)}, u32[]{:S(2)}) collective-permute-start(bf16[24,2048]{1,0:T(8,128)(2,1)S(1)} %get-tuple-element.88), channel_id=1, source_target_pairs={{16,14},{0,30},{18,12},{2,28},{20,10},{4,26},{22,8},{6,24},{24,6},... | collective-permute-start | bytes 294920 | tf_op jit(solution)/shard_map/ppermute | solution.py:180
  115.1 6.1 %collective-permute-start.36 = (bf16[24,2048]{1,0:T(8,128)(2,1)S(1)}, bf16[24,2048]{1,0:T(8,128)(2,1)S(1)}, u32[]{:S(2)}, u32[]{:S(2)}) collective-permute-start(bf16[24,2048]{1,0:T(8,128)(2,1)S(1)} %get-tuple-element.107), channel_id=1, source_target_pairs={{16,0},{0,16},{18,2},{2,18},{20,4},{4,20},{22,6},{6,22},{24,8},{8,... | collective-permute-start | bytes 294920 | tf_op jit(solution)/shard_map/ppermute | solution.py:180
  121.2 5.5 %collective-permute-start.38 = (bf16[24,2048]{1,0:T(8,128)(2,1)S(1)}, bf16[24,2048]{1,0:T(8,128)(2,1)S(1)}, u32[]{:S(2)}, u32[]{:S(2)}) collective-permute-start(bf16[24,2048]{1,0:T(8,128)(2,1)S(1)} %get-tuple-element.109), channel_id=1, source_target_pairs={{16,2},{0,18},{18,0},{2,16},{20,6},{4,22},{22,4},{6,20},{24,10},{8... | collective-permute-start | bytes 294920 | tf_op jit(solution)/shard_map/ppermute | solution.py:180
  126.2 5.4 %collective-permute-start.39 = (bf16[24,2048]{1,0:T(8,128)(2,1)S(1)}, bf16[24,2048]{1,0:T(8,128)(2,1)S(1)}, u32[]{:S(2)}, u32[]{:S(2)}) collective-permute-start(bf16[24,2048]{1,0:T(8,128)(2,1)S(1)} %get-tuple-element.110), channel_id=1, source_target_pairs={{16,20},{0,4},{18,22},{2,6},{20,16},{4,0},{22,18},{6,2},{24,28},{8... | collective-permute-start | bytes 294920 | tf_op jit(solution)/shard_map/ppermute | solution.py:180
  126.7 5.9 %collective-permute-start.40 = (bf16[24,2048]{1,0:T(8,128)(2,1)S(1)}, bf16[24,2048]{1,0:T(8,128)(2,1)S(1)}, u32[]{:S(2)}, u32[]{:S(2)}) collective-permute-start(bf16[24,2048]{1,0:T(8,128)(2,1)S(1)} %get-tuple-element.111), channel_id=1, source_target_pairs={{16,4},{0,20},{18,6},{2,22},{20,0},{4,16},{22,2},{6,18},{24,12},{8... | collective-permute-start | bytes 294920 | tf_op jit(solution)/shard_map/ppermute | solution.py:180
  131.6 6.5 %collective-permute-start.41 = (bf16[24,2048]{1,0:T(8,128)(2,1)S(1)}, bf16[24,2048]{1,0:T(8,128)(2,1)S(1)}, u32[]{:S(2)}, u32[]{:S(2)}) collective-permute-start(bf16[24,2048]{1,0:T(8,128)(2,1)S(1)} %get-tuple-element.112), channel_id=1, source_target_pairs={{16,22},{0,6},{18,20},{2,4},{20,18},{4,2},{22,16},{6,0},{24,30},{8... | collective-permute-start | bytes 294920 | tf_op jit(solution)/shard_map/ppermute | solution.py:180
  132.5 7.9 %collective-permute-start.42 = (bf16[24,2048]{1,0:T(8,128)(2,1)S(1)}, bf16[24,2048]{1,0:T(8,128)(2,1)S(1)}, u32[]{:S(2)}, u32[]{:S(2)}) collective-permute-start(bf16[24,2048]{1,0:T(8,128)(2,1)S(1)} %get-tuple-element.113), channel_id=1, source_target_pairs={{16,6},{0,22},{18,4},{2,20},{20,2},{4,18},{22,0},{6,16},{24,14},{8... | collective-permute-start | bytes 294920 | tf_op jit(solution)/shard_map/ppermute | solution.py:180
  138.1 11.4 %collective-permute-start.43 = (bf16[24,2048]{1,0:T(8,128)(2,1)S(1)}, bf16[24,2048]{1,0:T(8,128)(2,1)S(1)}, u32[]{:S(2)}, u32[]{:S(2)}) collective-permute-start(bf16[24,2048]{1,0:T(8,128)(2,1)S(1)} %get-tuple-element.114), channel_id=1, source_target_pairs={{16,24},{0,8},{18,26},{2,10},{20,28},{4,12},{22,30},{6,14},{24,16}... | collective-permute-start | bytes 294920 | tf_op jit(solution)/shard_map/ppermute | solution.py:180
  140.4 13.1 %collective-permute-start.44 = (bf16[24,2048]{1,0:T(8,128)(2,1)S(1)}, bf16[24,2048]{1,0:T(8,128)(2,1)S(1)}, u32[]{:S(2)}, u32[]{:S(2)}) collective-permute-start(bf16[24,2048]{1,0:T(8,128)(2,1)S(1)} %get-tuple-element.115), channel_id=1, source_target_pairs={{16,8},{0,24},{18,10},{2,26},{20,12},{4,28},{22,14},{6,30},{24,0},... | collective-permute-start | bytes 294920 | tf_op jit(solution)/shard_map/ppermute | solution.py:180
  149.5 9.4 %collective-permute-start.45 = (bf16[24,2048]{1,0:T(8,128)(2,1)S(1)}, bf16[24,2048]{1,0:T(8,128)(2,1)S(1)}, u32[]{:S(2)}, u32[]{:S(2)}) collective-permute-start(bf16[24,2048]{1,0:T(8,128)(2,1)S(1)} %get-tuple-element.116), channel_id=1, source_target_pairs={{16,26},{0,10},{18,24},{2,8},{20,30},{4,14},{22,28},{6,12},{24,18}... | collective-permute-start | bytes 294920 | tf_op jit(solution)/shard_map/ppermute | solution.py:180
  153.5 23.8 %collective-permute-start.46 = (bf16[24,2048]{1,0:T(8,128)(2,1)S(1)}, bf16[24,2048]{1,0:T(8,128)(2,1)S(1)}, u32[]{:S(2)}, u32[]{:S(2)}) collective-permute-start(bf16[24,2048]{1,0:T(8,128)(2,1)S(1)} %get-tuple-element.117), channel_id=1, source_target_pairs={{16,10},{0,26},{18,8},{2,24},{20,14},{4,30},{22,12},{6,28},{24,2},... | collective-permute-start | bytes 294920 | tf_op jit(solution)/shard_map/ppermute | solution.py:180
  158.9 18.5 %collective-permute-start.47 = (bf16[24,2048]{1,0:T(8,128)(2,1)S(1)}, bf16[24,2048]{1,0:T(8,128)(2,1)S(1)}, u32[]{:S(2)}, u32[]{:S(2)}) collective-permute-start(bf16[24,2048]{1,0:T(8,128)(2,1)S(1)} %get-tuple-element.118), channel_id=1, source_target_pairs={{16,28},{0,12},{18,30},{2,14},{20,24},{4,8},{22,26},{6,10},{24,20}... | collective-permute-start | bytes 294920 | tf_op jit(solution)/shard_map/ppermute | solution.py:180
  158.9 18.7 %collective-permute-start.48 = (bf16[24,2048]{1,0:T(8,128)(2,1)S(1)}, bf16[24,2048]{1,0:T(8,128)(2,1)S(1)}, u32[]{:S(2)}, u32[]{:S(2)}) collective-permute-start(bf16[24,2048]{1,0:T(8,128)(2,1)S(1)} %get-tuple-element.119), channel_id=1, source_target_pairs={{16,12},{0,28},{18,14},{2,30},{20,8},{4,24},{22,10},{6,26},{24,4},... | collective-permute-start | bytes 294920 | tf_op jit(solution)/shard_map/ppermute | solution.py:180
  160.5 20.3 %collective-permute-start.49 = (bf16[24,2048]{1,0:T(8,128)(2,1)S(1)}, bf16[24,2048]{1,0:T(8,128)(2,1)S(1)}, u32[]{:S(2)}, u32[]{:S(2)}) collective-permute-start(bf16[24,2048]{1,0:T(8,128)(2,1)S(1)} %get-tuple-element.120), channel_id=1, source_target_pairs={{16,30},{0,14},{18,28},{2,12},{20,26},{4,10},{22,24},{6,8},{24,22}... | collective-permute-start | bytes 294920 | tf_op jit(solution)/shard_map/ppermute | solution.py:180
  162.3 18.5 %collective-permute-start.50 = (bf16[24,2048]{1,0:T(8,128)(2,1)S(1)}, bf16[24,2048]{1,0:T(8,128)(2,1)S(1)}, u32[]{:S(2)}, u32[]{:S(2)}) collective-permute-start(bf16[24,2048]{1,0:T(8,128)(2,1)S(1)} %get-tuple-element.121), channel_id=1, source_target_pairs={{16,14},{0,30},{18,12},{2,28},{20,10},{4,26},{22,8},{6,24},{24,6},... | collective-permute-start | bytes 294920 | tf_op jit(solution)/shard_map/ppermute | solution.py:180
  177.2 5.7 %collective-permute-start.21 = (bf16[24,2048]{1,0:T(8,128)(2,1)S(1)}, bf16[24,2048]{1,0:T(8,128)(2,1)S(1)}, u32[]{:S(2)}, u32[]{:S(2)}) collective-permute-start(bf16[24,2048]{1,0:T(8,128)(2,1)S(1)} %get-tuple-element.90), channel_id=1, source_target_pairs={{16,0},{0,16},{18,2},{2,18},{20,4},{4,20},{22,6},{6,22},{24,8},{8,... | collective-permute-start | bytes 294920 | tf_op jit(solution)/shard_map/ppermute | solution.py:180
  177.3 5.7 %collective-permute-start.22 = (bf16[24,2048]{1,0:T(8,128)(2,1)S(1)}, bf16[24,2048]{1,0:T(8,128)(2,1)S(1)}, u32[]{:S(2)}, u32[]{:S(2)}) collective-permute-start(bf16[24,2048]{1,0:T(8,128)(2,1)S(1)} %get-tuple-element.91), channel_id=1, source_target_pairs={{16,18},{0,2},{18,16},{2,0},{20,22},{4,6},{22,20},{6,4},{24,26},{8... | collective-permute-start | bytes 294920 | tf_op jit(solution)/shard_map/ppermute | solution.py:180
  177.5 9.1 %collective-permute-start.23 = (bf16[24,2048]{1,0:T(8,128)(2,1)S(1)}, bf16[24,2048]{1,0:T(8,128)(2,1)S(1)}, u32[]{:S(2)}, u32[]{:S(2)}) collective-permute-start(bf16[24,2048]{1,0:T(8,128)(2,1)S(1)} %get-tuple-element.92), channel_id=1, source_target_pairs={{16,2},{0,18},{18,0},{2,16},{20,6},{4,22},{22,4},{6,20},{24,10},{8... | collective-permute-start | bytes 294920 | tf_op jit(solution)/shard_map/ppermute | solution.py:180
  180.8 5.9 %collective-permute-start.24 = (bf16[24,2048]{1,0:T(8,128)(2,1)S(1)}, bf16[24,2048]{1,0:T(8,128)(2,1)S(1)}, u32[]{:S(2)}, u32[]{:S(2)}) collective-permute-start(bf16[24,2048]{1,0:T(8,128)(2,1)S(1)} %get-tuple-element.93), channel_id=1, source_target_pairs={{16,20},{0,4},{18,22},{2,6},{20,16},{4,0},{22,18},{6,2},{24,28},{8... | collective-permute-start | bytes 294920 | tf_op jit(solution)/shard_map/ppermute | solution.py:180
  180.8 8.9 %collective-permute-start.25 = (bf16[24,2048]{1,0:T(8,128)(2,1)S(1)}, bf16[24,2048]{1,0:T(8,128)(2,1)S(1)}, u32[]{:S(2)}, u32[]{:S(2)}) collective-permute-start(bf16[24,2048]{1,0:T(8,128)(2,1)S(1)} %get-tuple-element.94), channel_id=1, source_target_pairs={{16,4},{0,20},{18,6},{2,22},{20,0},{4,16},{22,2},{6,18},{24,12},{8... | collective-permute-start | bytes 294920 | tf_op jit(solution)/shard_map/ppermute | solution.py:180
  183.0 6.8 %collective-permute-start.26 = (bf16[24,2048]{1,0:T(8,128)(2,1)S(1)}, bf16[24,2048]{1,0:T(8,128)(2,1)S(1)}, u32[]{:S(2)}, u32[]{:S(2)}) collective-permute-start(bf16[24,2048]{1,0:T(8,128)(2,1)S(1)} %get-tuple-element.95), channel_id=1, source_target_pairs={{16,22},{0,6},{18,20},{2,4},{20,18},{4,2},{22,16},{6,0},{24,30},{8... | collective-permute-start | bytes 294920 | tf_op jit(solution)/shard_map/ppermute | solution.py:180
  183.0 11.4 %collective-permute-start.27 = (bf16[24,2048]{1,0:T(8,128)(2,1)S(1)}, bf16[24,2048]{1,0:T(8,128)(2,1)S(1)}, u32[]{:S(2)}, u32[]{:S(2)}) collective-permute-start(bf16[24,2048]{1,0:T(8,128)(2,1)S(1)} %get-tuple-element.96), channel_id=1, source_target_pairs={{16,6},{0,22},{18,4},{2,20},{20,2},{4,18},{22,0},{6,16},{24,14},{8... | collective-permute-start | bytes 294920 | tf_op jit(solution)/shard_map/ppermute | solution.py:180
  186.7 8.2 %collective-permute-start.28 = (bf16[24,2048]{1,0:T(8,128)(2,1)S(1)}, bf16[24,2048]{1,0:T(8,128)(2,1)S(1)}, u32[]{:S(2)}, u32[]{:S(2)}) collective-permute-start(bf16[24,2048]{1,0:T(8,128)(2,1)S(1)} %get-tuple-element.97), channel_id=1, source_target_pairs={{16,24},{0,8},{18,26},{2,10},{20,28},{4,12},{22,30},{6,14},{24,16}... | collective-permute-start | bytes 294920 | tf_op jit(solution)/shard_map/ppermute | solution.py:180
  186.7 11.6 %collective-permute-start.29 = (bf16[24,2048]{1,0:T(8,128)(2,1)S(1)}, bf16[24,2048]{1,0:T(8,128)(2,1)S(1)}, u32[]{:S(2)}, u32[]{:S(2)}) collective-permute-start(bf16[24,2048]{1,0:T(8,128)(2,1)S(1)} %get-tuple-element.98), channel_id=1, source_target_pairs={{16,8},{0,24},{18,10},{2,26},{20,12},{4,28},{22,14},{6,30},{24,0},... | collective-permute-start | bytes 294920 | tf_op jit(solution)/shard_map/ppermute | solution.py:180
  189.8 9.7 %collective-permute-start.30 = (bf16[24,2048]{1,0:T(8,128)(2,1)S(1)}, bf16[24,2048]{1,0:T(8,128)(2,1)S(1)}, u32[]{:S(2)}, u32[]{:S(2)}) collective-permute-start(bf16[24,2048]{1,0:T(8,128)(2,1)S(1)} %get-tuple-element.99), channel_id=1, source_target_pairs={{16,26},{0,10},{18,24},{2,8},{20,30},{4,14},{22,28},{6,12},{24,18}... | collective-permute-start | bytes 294920 | tf_op jit(solution)/shard_map/ppermute | solution.py:180
  189.8 23.8 %collective-permute-start.31 = (bf16[24,2048]{1,0:T(8,128)(2,1)S(1)}, bf16[24,2048]{1,0:T(8,128)(2,1)S(1)}, u32[]{:S(2)}, u32[]{:S(2)}) collective-permute-start(bf16[24,2048]{1,0:T(8,128)(2,1)S(1)} %get-tuple-element.100), channel_id=1, source_target_pairs={{16,10},{0,26},{18,8},{2,24},{20,14},{4,30},{22,12},{6,28},{24,2},... | collective-permute-start | bytes 294920 | tf_op jit(solution)/shard_map/ppermute | solution.py:180
  194.3 19.9 %collective-permute-start.32 = (bf16[24,2048]{1,0:T(8,128)(2,1)S(1)}, bf16[24,2048]{1,0:T(8,128)(2,1)S(1)}, u32[]{:S(2)}, u32[]{:S(2)}) collective-permute-start(bf16[24,2048]{1,0:T(8,128)(2,1)S(1)} %get-tuple-element.101), channel_id=1, source_target_pairs={{16,28},{0,12},{18,30},{2,14},{20,24},{4,8},{22,26},{6,10},{24,20}... | collective-permute-start | bytes 294920 | tf_op jit(solution)/shard_map/ppermute | solution.py:180
  194.9 19.4 %collective-permute-start.33 = (bf16[24,2048]{1,0:T(8,128)(2,1)S(1)}, bf16[24,2048]{1,0:T(8,128)(2,1)S(1)}, u32[]{:S(2)}, u32[]{:S(2)}) collective-permute-start(bf16[24,2048]{1,0:T(8,128)(2,1)S(1)} %get-tuple-element.102), channel_id=1, source_target_pairs={{16,12},{0,28},{18,14},{2,30},{20,8},{4,24},{22,10},{6,26},{24,4},... | collective-permute-start | bytes 294920 | tf_op jit(solution)/shard_map/ppermute | solution.py:180
  198.3 18.7 %collective-permute-start.34 = (bf16[24,2048]{1,0:T(8,128)(2,1)S(1)}, bf16[24,2048]{1,0:T(8,128)(2,1)S(1)}, u32[]{:S(2)}, u32[]{:S(2)}) collective-permute-start(bf16[24,2048]{1,0:T(8,128)(2,1)S(1)} %get-tuple-element.103), channel_id=1, source_target_pairs={{16,30},{0,14},{18,28},{2,12},{20,26},{4,10},{22,24},{6,8},{24,22}... | collective-permute-start | bytes 294920 | tf_op jit(solution)/shard_map/ppermute | solution.py:180
  199.5 17.6 %collective-permute-start.35 = (bf16[24,2048]{1,0:T(8,128)(2,1)S(1)}, bf16[24,2048]{1,0:T(8,128)(2,1)S(1)}, u32[]{:S(2)}, u32[]{:S(2)}) collective-permute-start(bf16[24,2048]{1,0:T(8,128)(2,1)S(1)} %get-tuple-element.104), channel_id=1, source_target_pairs={{16,14},{0,30},{18,12},{2,28},{20,10},{4,26},{22,8},{6,24},{24,6},... | collective-permute-start | bytes 294920 | tf_op jit(solution)/shard_map/ppermute | solution.py:180
  213.6 5.7 %collective-permute-start.51 = (bf16[24,2048]{1,0:T(8,128)(2,1)S(1)}, bf16[24,2048]{1,0:T(8,128)(2,1)S(1)}, u32[]{:S(2)}, u32[]{:S(2)}) collective-permute-start(bf16[24,2048]{1,0:T(8,128)(2,1)S(1)} %get-tuple-element.125), channel_id=1, source_target_pairs={{16,0},{0,16},{18,2},{2,18},{20,4},{4,20},{22,6},{6,22},{24,8},{8,... | collective-permute-start | bytes 294920 | tf_op jit(solution)/shard_map/ppermute | solution.py:180
  214.3 10.0 %collective-permute-start.53 = (bf16[24,2048]{1,0:T(8,128)(2,1)S(1)}, bf16[24,2048]{1,0:T(8,128)(2,1)S(1)}, u32[]{:S(2)}, u32[]{:S(2)}) collective-permute-start(bf16[24,2048]{1,0:T(8,128)(2,1)S(1)} %get-tuple-element.127), channel_id=1, source_target_pairs={{16,2},{0,18},{18,0},{2,16},{20,6},{4,22},{22,4},{6,20},{24,10},{8... | collective-permute-start | bytes 294920 | tf_op jit(solution)/shard_map/ppermute | solution.py:180
  217.1 7.2 %collective-permute-start.54 = (bf16[24,2048]{1,0:T(8,128)(2,1)S(1)}, bf16[24,2048]{1,0:T(8,128)(2,1)S(1)}, u32[]{:S(2)}, u32[]{:S(2)}) collective-permute-start(bf16[24,2048]{1,0:T(8,128)(2,1)S(1)} %get-tuple-element.128), channel_id=1, source_target_pairs={{16,20},{0,4},{18,22},{2,6},{20,16},{4,0},{22,18},{6,2},{24,28},{8... | collective-permute-start | bytes 294920 | tf_op jit(solution)/shard_map/ppermute | solution.py:180
  217.1 8.9 %collective-permute-start.55 = (bf16[24,2048]{1,0:T(8,128)(2,1)S(1)}, bf16[24,2048]{1,0:T(8,128)(2,1)S(1)}, u32[]{:S(2)}, u32[]{:S(2)}) collective-permute-start(bf16[24,2048]{1,0:T(8,128)(2,1)S(1)} %get-tuple-element.129), channel_id=1, source_target_pairs={{16,4},{0,20},{18,6},{2,22},{20,0},{4,16},{22,2},{6,18},{24,12},{8... | collective-permute-start | bytes 294920 | tf_op jit(solution)/shard_map/ppermute | solution.py:180
  219.2 7.5 %collective-permute-start.56 = (bf16[24,2048]{1,0:T(8,128)(2,1)S(1)}, bf16[24,2048]{1,0:T(8,128)(2,1)S(1)}, u32[]{:S(2)}, u32[]{:S(2)}) collective-permute-start(bf16[24,2048]{1,0:T(8,128)(2,1)S(1)} %get-tuple-element.130), channel_id=1, source_target_pairs={{16,22},{0,6},{18,20},{2,4},{20,18},{4,2},{22,16},{6,0},{24,30},{8... | collective-permute-start | bytes 294920 | tf_op jit(solution)/shard_map/ppermute | solution.py:180
  219.2 12.7 %collective-permute-start.57 = (bf16[24,2048]{1,0:T(8,128)(2,1)S(1)}, bf16[24,2048]{1,0:T(8,128)(2,1)S(1)}, u32[]{:S(2)}, u32[]{:S(2)}) collective-permute-start(bf16[24,2048]{1,0:T(8,128)(2,1)S(1)} %get-tuple-element.131), channel_id=1, source_target_pairs={{16,6},{0,22},{18,4},{2,20},{20,2},{4,18},{22,0},{6,16},{24,14},{8... | collective-permute-start | bytes 294920 | tf_op jit(solution)/shard_map/ppermute | solution.py:180
  224.2 7.7 %collective-permute-start.58 = (bf16[24,2048]{1,0:T(8,128)(2,1)S(1)}, bf16[24,2048]{1,0:T(8,128)(2,1)S(1)}, u32[]{:S(2)}, u32[]{:S(2)}) collective-permute-start(bf16[24,2048]{1,0:T(8,128)(2,1)S(1)} %get-tuple-element.132), channel_id=1, source_target_pairs={{16,24},{0,8},{18,26},{2,10},{20,28},{4,12},{22,30},{6,14},{24,16}... | collective-permute-start | bytes 294920 | tf_op jit(solution)/shard_map/ppermute | solution.py:180
  224.2 10.3 %collective-permute-start.59 = (bf16[24,2048]{1,0:T(8,128)(2,1)S(1)}, bf16[24,2048]{1,0:T(8,128)(2,1)S(1)}, u32[]{:S(2)}, u32[]{:S(2)}) collective-permute-start(bf16[24,2048]{1,0:T(8,128)(2,1)S(1)} %get-tuple-element.133), channel_id=1, source_target_pairs={{16,8},{0,24},{18,10},{2,26},{20,12},{4,28},{22,14},{6,30},{24,0},... | collective-permute-start | bytes 294920 | tf_op jit(solution)/shard_map/ppermute | solution.py:180
  226.0 9.7 %collective-permute-start.60 = (bf16[24,2048]{1,0:T(8,128)(2,1)S(1)}, bf16[24,2048]{1,0:T(8,128)(2,1)S(1)}, u32[]{:S(2)}, u32[]{:S(2)}) collective-permute-start(bf16[24,2048]{1,0:T(8,128)(2,1)S(1)} %get-tuple-element.134), channel_id=1, source_target_pairs={{16,26},{0,10},{18,24},{2,8},{20,30},{4,14},{22,28},{6,12},{24,18}... | collective-permute-start | bytes 294920 | tf_op jit(solution)/shard_map/ppermute | solution.py:180
  226.7 18.6 %collective-permute-start.61 = (bf16[24,2048]{1,0:T(8,128)(2,1)}, bf16[24,2048]{1,0:T(8,128)(2,1)S(1)}, u32[]{:S(2)}, u32[]{:S(2)}) collective-permute-start(bf16[24,2048]{1,0:T(8,128)(2,1)} %get-tuple-element.135), channel_id=1, source_target_pairs={{16,10},{0,26},{18,8},{2,24},{20,14},{4,30},{22,12},{6,28},{24,2},... | collective-permute-start | bytes 294920 | tf_op jit(solution)/shard_map/ppermute | solution.py:180
  231.9 13.4 %collective-permute-start.62 = (bf16[24,2048]{1,0:T(8,128)(2,1)}, bf16[24,2048]{1,0:T(8,128)(2,1)}, u32[]{:S(2)}, u32[]{:S(2)}) collective-permute-start(bf16[24,2048]{1,0:T(8,128)(2,1)} %get-tuple-element.136), channel_id=1, source_target_pairs={{16,28},{0,12},{18,30},{2,14},{20,24},{4,8},{22,26},{6,10},{24,20}... | collective-permute-start | bytes 294920 | tf_op jit(solution)/shard_map/ppermute | solution.py:180
  231.9 13.3 %collective-permute-start.63 = (bf16[24,2048]{1,0:T(8,128)(2,1)}, bf16[24,2048]{1,0:T(8,128)(2,1)}, u32[]{:S(2)}, u32[]{:S(2)}) collective-permute-start(bf16[24,2048]{1,0:T(8,128)(2,1)} %get-tuple-element.137), channel_id=1, source_target_pairs={{16,12},{0,28},{18,14},{2,30},{20,8},{4,24},{22,10},{6,26},{24,4},... | collective-permute-start | bytes 294920 | tf_op jit(solution)/shard_map/ppermute | solution.py:180
  234.6 10.7 %collective-permute-start.64 = (bf16[24,2048]{1,0:T(8,128)(2,1)}, bf16[24,2048]{1,0:T(8,128)(2,1)}, u32[]{:S(2)}, u32[]{:S(2)}) collective-permute-start(bf16[24,2048]{1,0:T(8,128)(2,1)} %get-tuple-element.138), channel_id=1, source_target_pairs={{16,30},{0,14},{18,28},{2,12},{20,26},{4,10},{22,24},{6,8},{24,22}... | collective-permute-start | bytes 294920 | tf_op jit(solution)/shard_map/ppermute | solution.py:180
  235.7 9.6 %collective-permute-start.65 = (bf16[24,2048]{1,0:T(8,128)(2,1)}, bf16[24,2048]{1,0:T(8,128)(2,1)}, u32[]{:S(2)}, u32[]{:S(2)}) collective-permute-start(bf16[24,2048]{1,0:T(8,128)(2,1)} %get-tuple-element.139), channel_id=1, source_target_pairs={{16,14},{0,30},{18,12},{2,28},{20,10},{4,26},{22,8},{6,24},{24,6},... | collective-permute-start | bytes 294920 | tf_op jit(solution)/shard_map/ppermute | solution.py:180
  (7 other events, 87.9 us)

commit v3 on v2

--- a/solution.py
+++ b/solution.py
@@ -21,23 +21,27 @@
     return [slice(d, d + tile) for d in range(0, width, tile)]
 
 
-def join(lane_refs, rows_ref):
-    capacity = lane_refs[0].shape[0]
-    for b in range(0, len(lane_refs), 2):
-        pair = [ref[...].astype(F32) for ref in lane_refs[b : b + 2]]
-        rows_ref[b * capacity : (b + 2) * capacity, :] = jnp.concatenate(pair, axis=0).astype(BF16)
-
-
-def part(rows, lane_refs, columns):
-    capacity = lane_refs[0].shape[0]
-    for b, ref in enumerate(lane_refs):
-        ref[:, columns] = rows[b * capacity : (b + 1) * capacity, :].astype(BF16)
-
-
-def place_kernel(lanes, capacity, routes_ref, tokens_ref, *refs):
-    lane_refs, place_ref = refs[:lanes], refs[lanes]
+def join(lanes, rows_ref):
+    for b in range(0, len(lanes), 2):
+        pair = jnp.concatenate([lane[...].astype(F32) for lane in lanes[b : b + 2]], axis=0)
+        start = b * pair.shape[0] // 2
+        rows_ref[start : start + pair.shape[0], :] = pair.astype(BF16)
+
+
+def part(rows, lanes, columns):
+    capacity = lanes[0].shape[0]
+    for b, lane in enumerate(lanes):
+        lane[:, columns] = rows[b * capacity : (b + 1) * capacity, :].astype(BF16)
+
+
+def by_difference(rows_ref, here_ref):
+    return [rows_ref.at[here_ref[0] ^ b] for b in range(rows_ref.shape[0])]
+
+
+def place_kernel(here_ref, routes_ref, tokens_ref, slots_ref, place_ref):
+    lanes, capacity, width = slots_ref.shape
     tok_rows, top_count = routes_ref.shape
-    routes = routes_ref[...]
+    routes = routes_ref[...] ^ here_ref[0]
     numbers = lax.broadcasted_iota(jnp.int32, (tok_rows, lanes), 1)
     named = [numbers == routes[:, k : k + 1] for k in range(top_count)]
     chosen = sum(n.astype(F32) for n in named)
@@ -55,25 +59,27 @@
         place_ref[k * tok_rows : (k + 1) * tok_rows, :] = mark.astype(BF16)
         total = mark if total is None else total + mark
     total = total.astype(BF16)
-    for columns in tiles(tokens_ref.shape[1]):
-        part(dot(total, tokens_ref[:, columns], (0, 0)), lane_refs, columns)
-
-
-def spread_kernel(top_count, place_ref, rows_ref, *lane_refs):
+    slot_lanes = by_difference(slots_ref, here_ref)
+    for columns in tiles(width):
+        part(dot(total, tokens_ref[:, columns], (0, 0)), slot_lanes, columns)
+
+
+def spread_kernel(top_count, here_ref, place_ref, rows_ref, slots_ref):
     tok_rows = rows_ref.shape[0]
+    slot_lanes = by_difference(slots_ref, here_ref)
     total = sum(
         place_ref[k * tok_rows : (k + 1) * tok_rows, :].astype(F32) for k in range(top_count)
     ).astype(BF16)
     for columns in tiles(rows_ref.shape[1]):
-        part(dot(total, rows_ref[:, columns], (0, 0)), lane_refs, columns)
-
-
-def forward_kernel(lanes, parts, *refs):
-    lane_refs, refs = refs[:lanes], refs[lanes:]
+        part(dot(total, rows_ref[:, columns], (0, 0)), slot_lanes, columns)
+
+
+def forward_kernel(parts, here_ref, lanes_ref, *refs):
+    lanes = lanes_ref.shape[0]
     gate_refs, up_refs, down_refs = (refs[i * parts : (i + 1) * parts] for i in range(3))
     out_refs, refs = refs[3 * parts : 3 * parts + lanes], refs[3 * parts + lanes :]
     by_gate_ref, by_up_ref, rows_ref, hidden_ref = refs
-    join(lane_refs, rows_ref)
+    join(by_difference(lanes_ref, here_ref), rows_ref)
     for i in range(parts):
         pre_gate = dot(rows_ref[...], gate_refs[i][...], (1, 0))
         pre_up = dot(rows_ref[...], up_refs[i][...], (1, 0))
@@ -87,13 +93,13 @@
         part(rows, out_refs, columns)
 
 
-def backward_kernel(lanes, parts, *refs):
-    lane_refs, refs = refs[:lanes], refs[lanes:]
+def backward_kernel(parts, here_ref, lanes_ref, *refs):
+    lanes = lanes_ref.shape[0]
     gate_refs, up_refs, down_refs = (refs[i * parts : (i + 1) * parts] for i in range(3))
     by_gate_ref, by_up_ref = refs[3 * parts : 3 * parts + 2]
     out_refs, refs = refs[3 * parts + 2 : 3 * parts + 2 + lanes], refs[3 * parts + 2 + lanes :]
     rows_ref, back_gate_ref, back_up_ref = refs
-    join(lane_refs, rows_ref)
+    join(by_difference(lanes_ref, here_ref), rows_ref)
     for i in range(parts):
         back_hidden = dot(rows_ref[...], down_refs[i][...], (1, 1))
         back_gate_ref[i] = (back_hidden * by_gate_ref[i]).astype(BF16)
@@ -136,9 +142,11 @@
 def call(kernel, outs, flops, scratch=()):
     def run(*args):
         moved = sum(a.size * a.dtype.itemsize for a in (*args, *outs))
+        spaces = [pltpu.SMEM if a.shape == (1,) else pltpu.VMEM for a in args]
         return pl.pallas_call(
             kernel,
             out_shape=tuple(outs),
+            in_specs=[pl.BlockSpec(memory_space=space) for space in spaces],
             scratch_shapes=scratch,
             compiler_params=pltpu.CompilerParams(vmem_limit_bytes=VMEM_BYTES),
             cost_estimate=pl.CostEstimate(flops=flops, bytes_accessed=moved, transcendentals=0),
@@ -173,7 +181,11 @@
             shares.append(lax.ppermute(own, "expert", turn))
         return shares
 
-    def exchange(lane_rows):
+    def send(slot_rows):
+        groups = [[home(e, c) for e in range(experts)] for c in range(parts)]
+        return lax.all_to_all(slot_rows, axes, 0, 0, axis_index_groups=groups, tiled=True)
+
+    def send_back(lane_rows):
         received = [lane_rows[0]]
         for b in range(1, experts):
             pairs = [(home(e, c), home(e ^ b, c)) for c in range(parts) for e in range(experts)]
@@ -183,6 +195,7 @@
     spread_flops = 2 * slots * tok_rows * width
     dot_flops = 2 * slots * width * hidden * parts
     lane_shapes = [jax.ShapeDtypeStruct((capacity, width), BF16)] * experts
+    slot_shape = jax.ShapeDtypeStruct((experts, capacity, width), BF16)
     place_shape = jax.ShapeDtypeStruct((top_count * tok_rows, slots), BF16)
     unit_shape = jax.ShapeDtypeStruct((parts, slots, hidden), F32)
     token_shape = jax.ShapeDtypeStruct((tok_rows, width), BF16)
@@ -191,31 +204,30 @@
 
     gate_w, up_w, down_w = whole_expert(w_gate), whole_expert(w_up), whole_expert(w_down)
     column = lax.axis_index("expert")
-    place_here = column // parts * parts + (lax.axis_index("dp") + parts - 1) % parts
-    *x_lanes, place = call(
-        functools.partial(place_kernel, experts, capacity),
-        [*lane_shapes, place_shape],
-        spread_flops,
-    )(routes ^ place_here, tokens)
-    x_rows = exchange(x_lanes)
-    dy_lanes = call(functools.partial(spread_kernel, top_count), lane_shapes, spread_flops)(
-        place, cotangent
+    here = column // parts * parts + (lax.axis_index("dp") + parts - 1) % parts
+    here = here.astype(jnp.int32).reshape(1)
+    x_slots, place = call(place_kernel, [slot_shape, place_shape], spread_flops)(
+        here, routes, tokens
     )
-    dy_rows = exchange(dy_lanes)
+    x_rows = send(x_slots)
+    (dy_slots,) = call(
+        functools.partial(spread_kernel, top_count), [slot_shape], spread_flops
+    )(here, place, cotangent)
+    dy_rows = send(dy_slots)
     *out_rows, by_gate, by_up = call(
-        functools.partial(forward_kernel, experts, parts),
+        functools.partial(forward_kernel, parts),
         [*lane_shapes, unit_shape, unit_shape],
         3 * dot_flops,
         [row_scratch, unit_scratch],
-    )(*x_rows, *gate_w, *up_w, *down_w)
-    out_lanes = exchange(out_rows)
+    )(here, x_rows, *gate_w, *up_w, *down_w)
+    out_lanes = send_back(out_rows)
     grad_rows = call(
-        functools.partial(backward_kernel, experts, parts),
+        functools.partial(backward_kernel, parts),
         lane_shapes,
         3 * dot_flops,
         [row_scratch, unit_scratch, unit_scratch],
-    )(*dy_rows, *gate_w, *up_w, *down_w, by_gate, by_up)
-    grad_lanes = exchange(grad_rows)
+    )(here, dy_rows, *gate_w, *up_w, *down_w, by_gate, by_up)
+    grad_lanes = send_back(grad_rows)
     mixed, gate_grad = call(
         functools.partial(mix_kernel, experts),
         [token_shape, jax.ShapeDtypeStruct(gates.shape, F32)],

time: 248 us -> 209 us (0.84)
  waiting for transfers between devices: 117 us -> 84.6 us
  starting transfers between devices: 100 us -> 83 us
  local copies, waits for them, and re-layouts: 5.07 us -> 12.8 us
  Pallas kernels: 24.5 us -> 27.1 us
    ppermute x60 -> x30, waiting for transfers between devices: 65.2 us -> 12 us  [send_back(): received.append(lax.ppermute(lane_rows[b], axes, pairs))]
    ppermute x60 -> x30, starting transfers between devices: 97.3 us -> 62.6 us  [send_back(): received.append(lax.ppermute(lane_rows[b], axes, pairs))]
    all_to_all x0 -> x2, waiting for transfers between devices: none -> 29.4 us  [send(): lax.all_to_all(slot_rows, axes, 0, 0, axis_index_groups=groups, tiled=True)]
    all_to_all x0 -> x2, starting transfers between devices: none -> 18.6 us  [send(): lax.all_to_all(slot_rows, axes, 0, 0, axis_index_groups=groups, tiled=True)]
    ppermute x3, waiting for transfers between devices: 51.9 us -> 40 us  [whole_expert(): own = lax.ppermute(weight[0], axes, swap)]
    unnamed x13 -> x33, local copies, waits for them, and re-layouts: 5.07 us -> 12.8 us
    ppermute x3, waiting for transfers between devices: 0.01 us -> 3.3 us  [whole_expert(): shares.append(lax.ppermute(own, 'expert', turn))]
    pallas_call x6, Pallas kernels: 24.5 us -> 27.1 us  [run(): pl.pallas_call(kernel, out_shape=tuple(outs), in_specs=[pl.BlockSpec(memo...]
  transfers between devices with their start and end apart: 66 -> 38, of which waited for: 25 -> 10; matrix products, arithmetic and copies ran while one was open for 1% -> 0% of each run, Pallas kernels for 9% -> 11%
where the time goes in v3:
time: 209 us; the launch traced here: 208 us
  waiting for transfers between devices  84.6 us (40%)
  starting transfers between devices  83 us (40%)
  Pallas kernels  27.1 us (13%)
  local copies, waits for them, and re-layouts  12.8 us (6%)
    ppermute x30, starting transfers between devices, send_back(): received.append(lax.ppermute(lane_rows[b], axes, pairs))  62.6 us
    ppermute x3, waiting for transfers between devices, whole_expert(): own = lax.ppermute(weight[0], axes, swap)  40 us
    all_to_all x2, waiting for transfers between devices, send(): lax.all_to_all(slot_rows, axes, 0, 0, axis_index_groups=groups, tiled=True)  29.4 us
    pallas_call x6, Pallas kernels, run(): pl.pallas_call(kernel, out_shape=tuple(outs), in_specs=[pl.BlockSpec(memo...  27.1 us
    all_to_all x2, starting transfers between devices, send(): lax.all_to_all(slot_rows, axes, 0, 0, axis_index_groups=groups, tiled=True)  18.6 us
    unnamed x33, local copies, waits for them, and re-layouts  12.8 us
    ppermute x30, waiting for transfers between devices, send_back(): received.append(lax.ppermute(lane_rows[b], axes, pairs))  12 us
  transfers between devices with their start and end apart: 38, of which 10 were waited for; matrix products, arithmetic and copies ran while one was open for 0% of the time, Pallas kernels for 11%

profile of v3, /device:TPU:0, one launch (start us, length us, event | category | flops | bytes accessed | tf_op | source)
XLA Modules:
  0.0 208.4 jit_solution(9599902163263526609)
XLA Ops:
  0.6 0.8 copy.10.routes_ref
  1.5 1.0 copy-done.6
  2.5 1.0 shard_map.94
  3.5 1.2 copy-done.3
  4.7 8.9 %all-to-all-start = ((bf16[16,24,2048]{2,1,0:T(8,128)(2,1)}), bf16[16,24,2048]{2,1,0:T(8,128)(2,1)S(1)}, u32[]{:S(2)}, u32[]{:S(2)}) async-start(bf16[16,24,2048]{2,1,0:T(8,128)(2,1)} %copy-done.3), calls=%async_computation | async-start | bytes 3145728 | tf_op jit(solution)/shard_map/all_to_all | solution.py:186
  13.6 0.1 collective-permute-start
  13.8 0.9 collective-permute-start.4
  14.6 1.8 shard_map.97
  16.4 29.3 %all-to-all-done.lanes_ref = bf16[16,24,2048]{2,1,0:T(8,128)(2,1)S(1)} async-done(((bf16[16,24,2048]{2,1,0:T(8,128)(2,1)}), bf16[16,24,2048]{2,1,0:T(8,128)(2,1)S(1)}, u32[]{:S(2)}, u32[]{:S(2)}) %all-to-all-start) | async-done | bytes 1572896 | tf_op jit(solution)/shard_map/all_to_all | solution.py:186
  45.7 1.2 copy-done.1
  47.0 9.7 %all-to-all-start.1 = ((bf16[16,24,2048]{2,1,0:T(8,128)(2,1)}), bf16[16,24,2048]{2,1,0:T(8,128)(2,1)S(1)}, u32[]{:S(2)}, u32[]{:S(2)}) async-start(bf16[16,24,2048]{2,1,0:T(8,128)(2,1)} %shard_map.97), calls=%async_computation.1 | async-start | bytes 3145728 | tf_op jit(solution)/shard_map/all_to_all | solution.py:186
  56.7 19.4 %collective-permute-done.2.refs_2_ = bf16[2048,384]{1,0:T(8,128)(2,1)} collective-permute-done((bf16[2048,384]{1,0:T(8,128)(2,1)}, bf16[2048,384]{1,0:T(8,128)(2,1)}, u32[]{:S(2)}, u32[]{:S(2)}) %collective-permute-start.2) | collective-permute-done | bytes 1572896 | tf_op jit(solution)/shard_map/ppermute | solution.py:177
  76.1 0.4 collective-permute-start.3
  76.5 20.6 %collective-permute-done.4.refs_4_ = bf16[384,2048]{1,0:T(8,128)(2,1)} collective-permute-done((bf16[384,2048]{1,0:T(8,128)(2,1)}, bf16[384,2048]{1,0:T(8,128)(2,1)}, u32[]{:S(2)}, u32[]{:S(2)}) %collective-permute-start.4) | collective-permute-done | bytes 1572896 | tf_op jit(solution)/shard_map/ppermute | solution.py:177
  97.1 0.3 collective-permute-start.5
  97.5 3.3 %collective-permute-done.5.refs_5_ = bf16[384,2048]{1,0:T(8,128)(2,1)S(1)} collective-permute-done((bf16[384,2048]{1,0:T(8,128)(2,1)}, bf16[384,2048]{1,0:T(8,128)(2,1)S(1)}, u32[]{:S(2)}, u32[]{:S(2)}) %collective-permute-start.5) | collective-permute-done | bytes 1572896 | tf_op jit(solution)/shard_map/ppermute | solution.py:181
  100.8 1.2 copy-done.14
  102.0 1.4 copy-done.2
  103.4 9.7 %shard_map.95 = (bf16[24,2048]{1,0:T(8,128)(2,1)S(1)}, bf16[24,2048]{1,0:T(8,128)(2,1)S(1)}, bf16[24,2048]{1,0:T(8,128)(2,1)S(1)}, bf16[24,2048]{1,0:T(8,128)(2,...) custom-call(s32[1]{0:T(128)} %bitcast.here_ref, ...), custom_call_target="tpu_custom_call" | custom-call | flops 3623878656 | bytes 14942212 | tf_op jit(solution)/shard_map/pallas_call | solution.py:146
  113.0 1.0 copy-done.7
  114.1 1.0 copy-done.9
  115.1 2.5 %collective-permute-start.6 = (bf16[24,2048]{1,0:T(8,128)(2,1)S(1)}, bf16[24,2048]{1,0:T(8,128)(2,1)S(1)}, u32[]{:S(2)}, u32[]{:S(2)}) collective-permute-start(bf16[24,2048]{1,0:T(8,128)(2,1)S(1)} %get-tuple-element.44), channel_id=1, source_target_pairs={{16,0},{0,16},{18,2},{2,18},{20,4},{4,20},{22,6},{6,22},{24,8},{8,... | collective-permute-start | bytes 294920 | tf_op jit(solution)/shard_map/ppermute | solution.py:192
  117.6 1.1 collective-permute-start.7
  118.7 0.4 collective-permute-start.8
  119.1 1.5 collective-permute-start.9
  120.5 2.0 collective-permute-start.10
  122.5 2.0 collective-permute-start.11
  124.5 0.4 collective-permute-start.12
  124.9 2.4 %collective-permute-start.13 = (bf16[24,2048]{1,0:T(8,128)(2,1)S(1)}, bf16[24,2048]{1,0:T(8,128)(2,1)S(1)}, u32[]{:S(2)}, u32[]{:S(2)}) collective-permute-start(bf16[24,2048]{1,0:T(8,128)(2,1)S(1)} %get-tuple-element.51), channel_id=1, source_target_pairs={{16,24},{0,8},{18,26},{2,10},{20,28},{4,12},{22,30},{6,14},{24,16}... | collective-permute-start | bytes 294920 | tf_op jit(solution)/shard_map/ppermute | solution.py:192
  127.3 2.0 collective-permute-start.14
  129.3 0.1 collective-permute-done.10.refs_5_
  129.4 2.8 %collective-permute-start.15 = (bf16[24,2048]{1,0:T(8,128)(2,1)S(1)}, bf16[24,2048]{1,0:T(8,128)(2,1)S(1)}, u32[]{:S(2)}, u32[]{:S(2)}) collective-permute-start(bf16[24,2048]{1,0:T(8,128)(2,1)S(1)} %get-tuple-element.53), channel_id=1, source_target_pairs={{16,26},{0,10},{18,24},{2,8},{20,30},{4,14},{22,28},{6,12},{24,18}... | collective-permute-start | bytes 294920 | tf_op jit(solution)/shard_map/ppermute | solution.py:192
  132.2 2.0 collective-permute-start.16
  134.2 0.9 collective-permute-done.12.refs_7_
  135.1 2.3 %collective-permute-start.17 = (bf16[24,2048]{1,0:T(8,128)(2,1)}, bf16[24,2048]{1,0:T(8,128)(2,1)}, u32[]{:S(2)}, u32[]{:S(2)}) collective-permute-start(bf16[24,2048]{1,0:T(8,128)(2,1)} %get-tuple-element.55), channel_id=1, source_target_pairs={{16,28},{0,12},{18,30},{2,14},{20,24},{4,8},{22,26},{6,10},{24,20}... | collective-permute-start | bytes 294920 | tf_op jit(solution)/shard_map/ppermute | solution.py:192
  137.5 10.6 %collective-permute-start.18 = (bf16[24,2048]{1,0:T(8,128)(2,1)}, bf16[24,2048]{1,0:T(8,128)(2,1)}, u32[]{:S(2)}, u32[]{:S(2)}) collective-permute-start(bf16[24,2048]{1,0:T(8,128)(2,1)} %get-tuple-element.56), channel_id=1, source_target_pairs={{16,12},{0,28},{18,14},{2,30},{20,8},{4,24},{22,10},{6,26},{24,4},... | collective-permute-start | bytes 294920 | tf_op jit(solution)/shard_map/ppermute | solution.py:192
  148.1 2.6 %collective-permute-start.19 = (bf16[24,2048]{1,0:T(8,128)(2,1)}, bf16[24,2048]{1,0:T(8,128)(2,1)}, u32[]{:S(2)}, u32[]{:S(2)}) collective-permute-start(bf16[24,2048]{1,0:T(8,128)(2,1)} %get-tuple-element.57), channel_id=1, source_target_pairs={{16,30},{0,14},{18,28},{2,12},{20,26},{4,10},{22,24},{6,8},{24,22}... | collective-permute-start | bytes 294920 | tf_op jit(solution)/shard_map/ppermute | solution.py:192
  150.7 2.5 %collective-permute-start.20 = (bf16[24,2048]{1,0:T(8,128)(2,1)}, bf16[24,2048]{1,0:T(8,128)(2,1)}, u32[]{:S(2)}, u32[]{:S(2)}) collective-permute-start(bf16[24,2048]{1,0:T(8,128)(2,1)} %get-tuple-element.58), channel_id=1, source_target_pairs={{16,14},{0,30},{18,12},{2,28},{20,10},{4,26},{22,8},{6,24},{24,6},... | collective-permute-start | bytes 294920 | tf_op jit(solution)/shard_map/ppermute | solution.py:192
  153.2 1.3 copy-done.8
  154.4 1.3 copy-done.10
  155.7 9.6 %shard_map.98 = (bf16[24,2048]{1,0:T(8,128)(2,1)S(1)}, bf16[24,2048]{1,0:T(8,128)(2,1)S(1)}, bf16[24,2048]{1,0:T(8,128)(2,1)S(1)}, bf16[24,2048]{1,0:T(8,128)(2,...) custom-call(s32[1]{0:T(128)} %bitcast.here_ref, ...), custom_call_target="tpu_custom_call" | custom-call | flops 3623878656 | bytes 14942212 | tf_op jit(solution)/shard_map/pallas_call | solution.py:146
  165.3 0.7 copy-done.4
  165.9 1.1 collective-permute-start.21
  167.0 1.1 collective-permute-start.22
  168.1 1.3 collective-permute-start.23
  169.5 2.5 %collective-permute-start.25 = (bf16[24,2048]{1,0:T(8,128)(2,1)S(1)}, bf16[24,2048]{1,0:T(8,128)(2,1)S(1)}, u32[]{:S(2)}, u32[]{:S(2)}) collective-permute-start(bf16[24,2048]{1,0:T(8,128)(2,1)S(1)} %get-tuple-element.67), channel_id=1, source_target_pairs={{16,4},{0,20},{18,6},{2,22},{20,0},{4,16},{22,2},{6,18},{24,12},{8... | collective-permute-start | bytes 294920 | tf_op jit(solution)/shard_map/ppermute | solution.py:192
  172.0 0.6 collective-permute-start.26
  172.6 0.7 collective-permute-done.22.refs_2_
  173.3 2.0 collective-permute-start.27
  175.3 1.0 collective-permute-start.28
  176.3 2.4 %collective-permute-start.29 = (bf16[24,2048]{1,0:T(8,128)(2,1)S(1)}, bf16[24,2048]{1,0:T(8,128)(2,1)S(1)}, u32[]{:S(2)}, u32[]{:S(2)}) collective-permute-start(bf16[24,2048]{1,0:T(8,128)(2,1)S(1)} %get-tuple-element.71), channel_id=1, source_target_pairs={{16,8},{0,24},{18,10},{2,26},{20,12},{4,28},{22,14},{6,30},{24,0},... | collective-permute-start | bytes 294920 | tf_op jit(solution)/shard_map/ppermute | solution.py:192
  178.8 1.7 collective-permute-start.30
  180.4 2.5 %collective-permute-start.31 = (bf16[24,2048]{1,0:T(8,128)(2,1)}, bf16[24,2048]{1,0:T(8,128)(2,1)S(1)}, u32[]{:S(2)}, u32[]{:S(2)}) collective-permute-start(bf16[24,2048]{1,0:T(8,128)(2,1)} %get-tuple-element.73), channel_id=1, source_target_pairs={{16,10},{0,26},{18,8},{2,24},{20,14},{4,30},{22,12},{6,28},{24,2},... | collective-permute-start | bytes 294920 | tf_op jit(solution)/shard_map/ppermute | solution.py:192
  183.0 1.3 collective-permute-start.32
  184.3 7.5 %collective-permute-done.28.refs_8_ = bf16[24,2048]{1,0:T(8,128)(2,1)S(1)} collective-permute-done((bf16[24,2048]{1,0:T(8,128)(2,1)S(1)}, bf16[24,2048]{1,0:T(8,128)(2,1)S(1)}, u32[]{:S(2)}, u32[]{:S(2)}) %collective-permute-start.28) | collective-permute-done | bytes 98336 | tf_op jit(solution)/shard_map/ppermute | solution.py:192
  191.9 3.0 %collective-permute-start.33 = (bf16[24,2048]{1,0:T(8,128)(2,1)}, bf16[24,2048]{1,0:T(8,128)(2,1)S(1)}, u32[]{:S(2)}, u32[]{:S(2)}) collective-permute-start(bf16[24,2048]{1,0:T(8,128)(2,1)} %get-tuple-element.75), channel_id=1, source_target_pairs={{16,12},{0,28},{18,14},{2,30},{20,8},{4,24},{22,10},{6,26},{24,4},... | collective-permute-start | bytes 294920 | tf_op jit(solution)/shard_map/ppermute | solution.py:192
  194.8 0.1 collective-permute-done.29.refs_9_
  194.9 2.4 %collective-permute-start.34 = (bf16[24,2048]{1,0:T(8,128)(2,1)}, bf16[24,2048]{1,0:T(8,128)(2,1)S(1)}, u32[]{:S(2)}, u32[]{:S(2)}) collective-permute-start(bf16[24,2048]{1,0:T(8,128)(2,1)} %get-tuple-element.76), channel_id=1, source_target_pairs={{16,30},{0,14},{18,28},{2,12},{20,26},{4,10},{22,24},{6,8},{24,22}... | collective-permute-start | bytes 294920 | tf_op jit(solution)/shard_map/ppermute | solution.py:192
  197.4 2.6 %collective-permute-start.35 = (bf16[24,2048]{1,0:T(8,128)(2,1)}, bf16[24,2048]{1,0:T(8,128)(2,1)}, u32[]{:S(2)}, u32[]{:S(2)}) collective-permute-start(bf16[24,2048]{1,0:T(8,128)(2,1)} %get-tuple-element.77), channel_id=1, source_target_pairs={{16,14},{0,30},{18,12},{2,28},{20,10},{4,26},{22,8},{6,24},{24,6},... | collective-permute-start | bytes 294920 | tf_op jit(solution)/shard_map/ppermute | solution.py:192
  199.9 0.1 copy.11.gates_ref
  200.0 2.7 %shard_map.96 = (bf16[128,2048]{1,0:T(8,128)(2,1)}, f32[128,2]{1,0:T(8,128)S(1)}) custom-call(bf16[256,384]{1,0:T(8,128)(2,1)S(1)} %get-tuple-element.41.place_ref, f32[128,2]{1,0:T(8,128)S(1)} %copy.11.gates_ref, bf16[128,2048]{1,0:T(8,128)(2,1)S(1)} %copy-done, bf16[24,2048]{1,0:T(8,128)(2,1)S(1)} %get-tuple-element.43.refs_0_, ...), custom_call_target="tpu_custom_call" | custom-call | flops 402653184 | bytes 2820096 | tf_op jit(solution)/shard_map/pallas_call | solution.py:146
  202.7 0.6 copy.13
  203.4 2.6 %collective-permute-done.35.refs_15_ = bf16[24,2048]{1,0:T(8,128)(2,1)} collective-permute-done((bf16[24,2048]{1,0:T(8,128)(2,1)}, bf16[24,2048]{1,0:T(8,128)(2,1)}, u32[]{:S(2)}, u32[]{:S(2)}) %collective-permute-start.35) | collective-permute-done | bytes 98336 | tf_op jit(solution)/shard_map/ppermute | solution.py:192
  206.0 2.4 %shard_map.99 = bf16[128,2048]{1,0:T(8,128)(2,1)} custom-call(bf16[256,384]{1,0:T(8,128)(2,1)S(1)} %get-tuple-element.41.place_ref, f32[128,2]{1,0:T(8,128)S(1)} %copy.11.gates_ref, bf16[24,2048]{1,0:T(8,128)(2,1)S(1)} %copy-done.5, bf16[24,2048]{1,0:T(8,128)(2,1)S(1)} %collective-permute-done.21.refs_1_, ...), custom_call_target="tpu_custom_call" | custom-call | flops 402653184 | bytes 2294784 | tf_op jit(solution)/shard_map/pallas_call | solution.py:146
  (51 shorter events, 0.2 us)
Async XLA Ops:
  1.4 1.0 copy-start.6
  3.5 1.2 copy-start.3
  4.7 9.9 %copy-start = (bf16[128,2048]{1,0:T(8,128)(2,1)S(1)}, bf16[128,2048]{1,0:T(8,128)(2,1)}, u32[]{:S(2)}) copy-start(bf16[128,2048]{1,0:T(8,128)(2,1)} %rows_ref.1) | copy-start | bytes 1572868
  4.7 41.0 %all-to-all-start = ((bf16[16,24,2048]{2,1,0:T(8,128)(2,1)}), bf16[16,24,2048]{2,1,0:T(8,128)(2,1)S(1)}, u32[]{:S(2)}, u32[]{:S(2)}) async-start(bf16[16,24,2048]{2,1,0:T(8,128)(2,1)} %copy-done.3), calls=%async_computation | async-start | bytes 3145728 | tf_op jit(solution)/shard_map/all_to_all | solution.py:186
  13.6 43.1 %collective-permute-start = (bf16[2048,384]{1,0:T(8,128)(2,1)}, bf16[2048,384]{1,0:T(8,128)(2,1)}, u32[]{:S(2)}, u32[]{:S(2)}) collective-permute-start(bf16[2048,384]{1,0:T(8,128)(2,1)} %bitcast.4), channel_id=1, source_target_pairs={{0,16},{1,0},{2,18},{3,2},{4,20},{5,4},{6,22},{7,6},{8,24},{9,8},{... | collective-permute-start | bytes 4718600 | tf_op jit(solution)/shard_map/ppermute | solution.py:177
  13.7 62.4 %collective-permute-start.2 = (bf16[2048,384]{1,0:T(8,128)(2,1)}, bf16[2048,384]{1,0:T(8,128)(2,1)}, u32[]{:S(2)}, u32[]{:S(2)}) collective-permute-start(bf16[2048,384]{1,0:T(8,128)(2,1)} %bitcast.5), channel_id=1, source_target_pairs={{0,16},{1,0},{2,18},{3,2},{4,20},{5,4},{6,22},{7,6},{8,24},{9,8},{... | collective-permute-start | bytes 4718600 | tf_op jit(solution)/shard_map/ppermute | solution.py:177
  13.8 83.4 %collective-permute-start.4 = (bf16[384,2048]{1,0:T(8,128)(2,1)}, bf16[384,2048]{1,0:T(8,128)(2,1)}, u32[]{:S(2)}, u32[]{:S(2)}) collective-permute-start(bf16[384,2048]{1,0:T(8,128)(2,1)} %bitcast.6), channel_id=1, source_target_pairs={{0,16},{1,0},{2,18},{3,2},{4,20},{5,4},{6,22},{7,6},{8,24},{9,8},{... | collective-permute-start | bytes 4718600 | tf_op jit(solution)/shard_map/ppermute | solution.py:177
  45.7 1.2 copy-start.1
  47.0 106.2 %all-to-all-start.1 = ((bf16[16,24,2048]{2,1,0:T(8,128)(2,1)}), bf16[16,24,2048]{2,1,0:T(8,128)(2,1)S(1)}, u32[]{:S(2)}, u32[]{:S(2)}) async-start(bf16[16,24,2048]{2,1,0:T(8,128)(2,1)} %shard_map.97), calls=%async_computation.1 | async-start | bytes 3145728 | tf_op jit(solution)/shard_map/all_to_all | solution.py:186
  56.7 40.8 %collective-permute-start.1 = (bf16[2048,384]{1,0:T(8,128)(2,1)}, bf16[2048,384]{1,0:T(8,128)(2,1)S(1)}, u32[]{:S(2)}, u32[]{:S(2)}) collective-permute-start(bf16[2048,384]{1,0:T(8,128)(2,1)} %collective-permute-done.refs_0_), channel_id=1, source_target_pairs={{0,1},{1,0},{2,3},{3,2},{4,5},{5,4},{6,7},{7,6},{8,9},{9,8},{10,11... | collective-permute-start | bytes 4718600 | tf_op jit(solution)/shard_map/ppermute | solution.py:181
  76.1 21.3 %collective-permute-start.3 = (bf16[2048,384]{1,0:T(8,128)(2,1)}, bf16[2048,384]{1,0:T(8,128)(2,1)S(1)}, u32[]{:S(2)}, u32[]{:S(2)}) collective-permute-start(bf16[2048,384]{1,0:T(8,128)(2,1)} %collective-permute-done.2.refs_2_), channel_id=1, source_target_pairs={{0,1},{1,0},{2,3},{3,2},{4,5},{5,4},{6,7},{7,6},{8,9},{9,8},{10,11... | collective-permute-start | bytes 4718600 | tf_op jit(solution)/shard_map/ppermute | solution.py:181
  97.1 3.6 %collective-permute-start.5 = (bf16[384,2048]{1,0:T(8,128)(2,1)}, bf16[384,2048]{1,0:T(8,128)(2,1)S(1)}, u32[]{:S(2)}, u32[]{:S(2)}) collective-permute-start(bf16[384,2048]{1,0:T(8,128)(2,1)} %collective-permute-done.4.refs_4_), channel_id=1, source_target_pairs={{0,1},{1,0},{2,3},{3,2},{4,5},{5,4},{6,7},{7,6},{8,9},{9,8},{10,11... | collective-permute-start | bytes 4718600 | tf_op jit(solution)/shard_map/ppermute | solution.py:181
  97.5 3.3 %copy-start.12 = (bf16[2048,384]{1,0:T(8,128)(2,1)}, bf16[2048,384]{1,0:T(8,128)(2,1)S(1)}, u32[]{:S(2)}) copy-start(bf16[2048,384]{1,0:T(8,128)(2,1)S(1)} %collective-permute-done.1.refs_1_) | copy-start | bytes 4718596
  97.5 3.3 %copy-start.13 = (bf16[2048,384]{1,0:T(8,128)(2,1)}, bf16[2048,384]{1,0:T(8,128)(2,1)S(1)}, u32[]{:S(2)}) copy-start(bf16[2048,384]{1,0:T(8,128)(2,1)S(1)} %collective-permute-done.3.refs_3_) | copy-start | bytes 4718596
  100.8 1.2 copy-start.14
  102.0 1.4 copy-start.2
  113.0 1.1 copy-start.7
  114.1 1.0 copy-start.9
  115.1 7.4 %collective-permute-start.6 = (bf16[24,2048]{1,0:T(8,128)(2,1)S(1)}, bf16[24,2048]{1,0:T(8,128)(2,1)S(1)}, u32[]{:S(2)}, u32[]{:S(2)}) collective-permute-start(bf16[24,2048]{1,0:T(8,128)(2,1)S(1)} %get-tuple-element.44), channel_id=1, source_target_pairs={{16,0},{0,16},{18,2},{2,18},{20,4},{4,20},{22,6},{6,22},{24,8},{8,... | collective-permute-start | bytes 294920 | tf_op jit(solution)/shard_map/ppermute | solution.py:192
  117.6 7.0 %collective-permute-start.7 = (bf16[24,2048]{1,0:T(8,128)(2,1)S(1)}, bf16[24,2048]{1,0:T(8,128)(2,1)S(1)}, u32[]{:S(2)}, u32[]{:S(2)}) collective-permute-start(bf16[24,2048]{1,0:T(8,128)(2,1)S(1)} %get-tuple-element.45), channel_id=1, source_target_pairs={{16,18},{0,2},{18,16},{2,0},{20,22},{4,6},{22,20},{6,4},{24,26},{8... | collective-permute-start | bytes 294920 | tf_op jit(solution)/shard_map/ppermute | solution.py:192
  118.7 6.2 %collective-permute-start.8 = (bf16[24,2048]{1,0:T(8,128)(2,1)S(1)}, bf16[24,2048]{1,0:T(8,128)(2,1)S(1)}, u32[]{:S(2)}, u32[]{:S(2)}) collective-permute-start(bf16[24,2048]{1,0:T(8,128)(2,1)S(1)} %get-tuple-element.46), channel_id=1, source_target_pairs={{16,2},{0,18},{18,0},{2,16},{20,6},{4,22},{22,4},{6,20},{24,10},{8... | collective-permute-start | bytes 294920 | tf_op jit(solution)/shard_map/ppermute | solution.py:192
  119.1 8.2 %collective-permute-start.9 = (bf16[24,2048]{1,0:T(8,128)(2,1)S(1)}, bf16[24,2048]{1,0:T(8,128)(2,1)S(1)}, u32[]{:S(2)}, u32[]{:S(2)}) collective-permute-start(bf16[24,2048]{1,0:T(8,128)(2,1)S(1)} %get-tuple-element.47), channel_id=1, source_target_pairs={{16,20},{0,4},{18,22},{2,6},{20,16},{4,0},{22,18},{6,2},{24,28},{8... | collective-permute-start | bytes 294920 | tf_op jit(solution)/shard_map/ppermute | solution.py:192
  120.5 8.9 %collective-permute-start.10 = (bf16[24,2048]{1,0:T(8,128)(2,1)S(1)}, bf16[24,2048]{1,0:T(8,128)(2,1)S(1)}, u32[]{:S(2)}, u32[]{:S(2)}) collective-permute-start(bf16[24,2048]{1,0:T(8,128)(2,1)S(1)} %get-tuple-element.48), channel_id=1, source_target_pairs={{16,4},{0,20},{18,6},{2,22},{20,0},{4,16},{22,2},{6,18},{24,12},{8... | collective-permute-start | bytes 294920 | tf_op jit(solution)/shard_map/ppermute | solution.py:192
  122.5 9.7 %collective-permute-start.11 = (bf16[24,2048]{1,0:T(8,128)(2,1)S(1)}, bf16[24,2048]{1,0:T(8,128)(2,1)S(1)}, u32[]{:S(2)}, u32[]{:S(2)}) collective-permute-start(bf16[24,2048]{1,0:T(8,128)(2,1)S(1)} %get-tuple-element.49), channel_id=1, source_target_pairs={{16,22},{0,6},{18,20},{2,4},{20,18},{4,2},{22,16},{6,0},{24,30},{8... | collective-permute-start | bytes 294920 | tf_op jit(solution)/shard_map/ppermute | solution.py:192
  124.5 10.6 %collective-permute-start.12 = (bf16[24,2048]{1,0:T(8,128)(2,1)S(1)}, bf16[24,2048]{1,0:T(8,128)(2,1)S(1)}, u32[]{:S(2)}, u32[]{:S(2)}) collective-permute-start(bf16[24,2048]{1,0:T(8,128)(2,1)S(1)} %get-tuple-element.50), channel_id=1, source_target_pairs={{16,6},{0,22},{18,4},{2,20},{20,2},{4,18},{22,0},{6,16},{24,14},{8... | collective-permute-start | bytes 294920 | tf_op jit(solution)/shard_map/ppermute | solution.py:192
  124.9 12.6 %collective-permute-start.13 = (bf16[24,2048]{1,0:T(8,128)(2,1)S(1)}, bf16[24,2048]{1,0:T(8,128)(2,1)S(1)}, u32[]{:S(2)}, u32[]{:S(2)}) collective-permute-start(bf16[24,2048]{1,0:T(8,128)(2,1)S(1)} %get-tuple-element.51), channel_id=1, source_target_pairs={{16,24},{0,8},{18,26},{2,10},{20,28},{4,12},{22,30},{6,14},{24,16}... | collective-permute-start | bytes 294920 | tf_op jit(solution)/shard_map/ppermute | solution.py:192
  127.3 20.8 %collective-permute-start.14 = (bf16[24,2048]{1,0:T(8,128)(2,1)S(1)}, bf16[24,2048]{1,0:T(8,128)(2,1)S(1)}, u32[]{:S(2)}, u32[]{:S(2)}) collective-permute-start(bf16[24,2048]{1,0:T(8,128)(2,1)S(1)} %get-tuple-element.52), channel_id=1, source_target_pairs={{16,8},{0,24},{18,10},{2,26},{20,12},{4,28},{22,14},{6,30},{24,0},... | collective-permute-start | bytes 294920 | tf_op jit(solution)/shard_map/ppermute | solution.py:192
  129.4 21.3 %collective-permute-start.15 = (bf16[24,2048]{1,0:T(8,128)(2,1)S(1)}, bf16[24,2048]{1,0:T(8,128)(2,1)S(1)}, u32[]{:S(2)}, u32[]{:S(2)}) collective-permute-start(bf16[24,2048]{1,0:T(8,128)(2,1)S(1)} %get-tuple-element.53), channel_id=1, source_target_pairs={{16,26},{0,10},{18,24},{2,8},{20,30},{4,14},{22,28},{6,12},{24,18}... | collective-permute-start | bytes 294920 | tf_op jit(solution)/shard_map/ppermute | solution.py:192
  132.2 33.7 %collective-permute-start.16 = (bf16[24,2048]{1,0:T(8,128)(2,1)}, bf16[24,2048]{1,0:T(8,128)(2,1)S(1)}, u32[]{:S(2)}, u32[]{:S(2)}) collective-permute-start(bf16[24,2048]{1,0:T(8,128)(2,1)} %get-tuple-element.54), channel_id=1, source_target_pairs={{16,10},{0,26},{18,8},{2,24},{20,14},{4,30},{22,12},{6,28},{24,2},... | collective-permute-start | bytes 294920 | tf_op jit(solution)/shard_map/ppermute | solution.py:192
  135.1 31.9 %collective-permute-start.17 = (bf16[24,2048]{1,0:T(8,128)(2,1)}, bf16[24,2048]{1,0:T(8,128)(2,1)}, u32[]{:S(2)}, u32[]{:S(2)}) collective-permute-start(bf16[24,2048]{1,0:T(8,128)(2,1)} %get-tuple-element.55), channel_id=1, source_target_pairs={{16,28},{0,12},{18,30},{2,14},{20,24},{4,8},{22,26},{6,10},{24,20}... | collective-permute-start | bytes 294920 | tf_op jit(solution)/shard_map/ppermute | solution.py:192
  137.5 30.6 %collective-permute-start.18 = (bf16[24,2048]{1,0:T(8,128)(2,1)}, bf16[24,2048]{1,0:T(8,128)(2,1)}, u32[]{:S(2)}, u32[]{:S(2)}) collective-permute-start(bf16[24,2048]{1,0:T(8,128)(2,1)} %get-tuple-element.56), channel_id=1, source_target_pairs={{16,12},{0,28},{18,14},{2,30},{20,8},{4,24},{22,10},{6,26},{24,4},... | collective-permute-start | bytes 294920 | tf_op jit(solution)/shard_map/ppermute | solution.py:192
  148.1 21.4 %collective-permute-start.19 = (bf16[24,2048]{1,0:T(8,128)(2,1)}, bf16[24,2048]{1,0:T(8,128)(2,1)}, u32[]{:S(2)}, u32[]{:S(2)}) collective-permute-start(bf16[24,2048]{1,0:T(8,128)(2,1)} %get-tuple-element.57), channel_id=1, source_target_pairs={{16,30},{0,14},{18,28},{2,12},{20,26},{4,10},{22,24},{6,8},{24,22}... | collective-permute-start | bytes 294920 | tf_op jit(solution)/shard_map/ppermute | solution.py:192
  150.7 18.8 %collective-permute-start.20 = (bf16[24,2048]{1,0:T(8,128)(2,1)}, bf16[24,2048]{1,0:T(8,128)(2,1)}, u32[]{:S(2)}, u32[]{:S(2)}) collective-permute-start(bf16[24,2048]{1,0:T(8,128)(2,1)} %get-tuple-element.58), channel_id=1, source_target_pairs={{16,14},{0,30},{18,12},{2,28},{20,10},{4,26},{22,8},{6,24},{24,6},... | collective-permute-start | bytes 294920 | tf_op jit(solution)/shard_map/ppermute | solution.py:192
  153.2 1.3 copy-start.8
  154.4 1.3 copy-start.10
  155.7 44.2 %copy-start.11 = (f32[128,2]{0,1:T(2,128)S(1)}, f32[128,2]{0,1:T(2,128)}, u32[]{:S(2)}) copy-start(f32[128,2]{0,1:T(2,128)} %param.10) | copy-start | bytes 3076
  165.3 0.7 copy-start.4
  165.9 40.1 %copy-start.5 = (bf16[24,2048]{1,0:T(8,128)(2,1)S(1)}, bf16[24,2048]{1,0:T(8,128)(2,1)}, u32[]{:S(2)}) copy-start(bf16[24,2048]{1,0:T(8,128)(2,1)} %copy-done.4) | copy-start | bytes 294916
  165.9 6.1 %collective-permute-start.21 = (bf16[24,2048]{1,0:T(8,128)(2,1)S(1)}, bf16[24,2048]{1,0:T(8,128)(2,1)S(1)}, u32[]{:S(2)}, u32[]{:S(2)}) collective-permute-start(bf16[24,2048]{1,0:T(8,128)(2,1)S(1)} %get-tuple-element.63), channel_id=1, source_target_pairs={{16,0},{0,16},{18,2},{2,18},{20,4},{4,20},{22,6},{6,22},{24,8},{8,... | collective-permute-start | bytes 294920 | tf_op jit(solution)/shard_map/ppermute | solution.py:192
  167.0 6.2 %collective-permute-start.22 = (bf16[24,2048]{1,0:T(8,128)(2,1)S(1)}, bf16[24,2048]{1,0:T(8,128)(2,1)S(1)}, u32[]{:S(2)}, u32[]{:S(2)}) collective-permute-start(bf16[24,2048]{1,0:T(8,128)(2,1)S(1)} %get-tuple-element.64), channel_id=1, source_target_pairs={{16,18},{0,2},{18,16},{2,0},{20,22},{4,6},{22,20},{6,4},{24,26},{8... | collective-permute-start | bytes 294920 | tf_op jit(solution)/shard_map/ppermute | solution.py:192
  168.1 7.2 %collective-permute-start.23 = (bf16[24,2048]{1,0:T(8,128)(2,1)S(1)}, bf16[24,2048]{1,0:T(8,128)(2,1)S(1)}, u32[]{:S(2)}, u32[]{:S(2)}) collective-permute-start(bf16[24,2048]{1,0:T(8,128)(2,1)S(1)} %get-tuple-element.65), channel_id=1, source_target_pairs={{16,2},{0,18},{18,0},{2,16},{20,6},{4,22},{22,4},{6,20},{24,10},{8... | collective-permute-start | bytes 294920 | tf_op jit(solution)/shard_map/ppermute | solution.py:192
  169.4 6.9 %collective-permute-start.24 = (bf16[24,2048]{1,0:T(8,128)(2,1)S(1)}, bf16[24,2048]{1,0:T(8,128)(2,1)S(1)}, u32[]{:S(2)}, u32[]{:S(2)}) collective-permute-start(bf16[24,2048]{1,0:T(8,128)(2,1)S(1)} %get-tuple-element.66), channel_id=1, source_target_pairs={{16,20},{0,4},{18,22},{2,6},{20,16},{4,0},{22,18},{6,2},{24,28},{8... | collective-permute-start | bytes 294920 | tf_op jit(solution)/shard_map/ppermute | solution.py:192
  169.5 9.3 %collective-permute-start.25 = (bf16[24,2048]{1,0:T(8,128)(2,1)S(1)}, bf16[24,2048]{1,0:T(8,128)(2,1)S(1)}, u32[]{:S(2)}, u32[]{:S(2)}) collective-permute-start(bf16[24,2048]{1,0:T(8,128)(2,1)S(1)} %get-tuple-element.67), channel_id=1, source_target_pairs={{16,4},{0,20},{18,6},{2,22},{20,0},{4,16},{22,2},{6,18},{24,12},{8... | collective-permute-start | bytes 294920 | tf_op jit(solution)/shard_map/ppermute | solution.py:192
  172.0 8.4 %collective-permute-start.26 = (bf16[24,2048]{1,0:T(8,128)(2,1)S(1)}, bf16[24,2048]{1,0:T(8,128)(2,1)S(1)}, u32[]{:S(2)}, u32[]{:S(2)}) collective-permute-start(bf16[24,2048]{1,0:T(8,128)(2,1)S(1)} %get-tuple-element.68), channel_id=1, source_target_pairs={{16,22},{0,6},{18,20},{2,4},{20,18},{4,2},{22,16},{6,0},{24,30},{8... | collective-permute-start | bytes 294920 | tf_op jit(solution)/shard_map/ppermute | solution.py:192
  173.3 9.7 %collective-permute-start.27 = (bf16[24,2048]{1,0:T(8,128)(2,1)S(1)}, bf16[24,2048]{1,0:T(8,128)(2,1)S(1)}, u32[]{:S(2)}, u32[]{:S(2)}) collective-permute-start(bf16[24,2048]{1,0:T(8,128)(2,1)S(1)} %get-tuple-element.69), channel_id=1, source_target_pairs={{16,6},{0,22},{18,4},{2,20},{20,2},{4,18},{22,0},{6,16},{24,14},{8... | collective-permute-start | bytes 294920 | tf_op jit(solution)/shard_map/ppermute | solution.py:192
  175.3 16.5 %collective-permute-start.28 = (bf16[24,2048]{1,0:T(8,128)(2,1)S(1)}, bf16[24,2048]{1,0:T(8,128)(2,1)S(1)}, u32[]{:S(2)}, u32[]{:S(2)}) collective-permute-start(bf16[24,2048]{1,0:T(8,128)(2,1)S(1)} %get-tuple-element.70), channel_id=1, source_target_pairs={{16,24},{0,8},{18,26},{2,10},{20,28},{4,12},{22,30},{6,14},{24,16}... | collective-permute-start | bytes 294920 | tf_op jit(solution)/shard_map/ppermute | solution.py:192
  176.3 18.6 %collective-permute-start.29 = (bf16[24,2048]{1,0:T(8,128)(2,1)S(1)}, bf16[24,2048]{1,0:T(8,128)(2,1)S(1)}, u32[]{:S(2)}, u32[]{:S(2)}) collective-permute-start(bf16[24,2048]{1,0:T(8,128)(2,1)S(1)} %get-tuple-element.71), channel_id=1, source_target_pairs={{16,8},{0,24},{18,10},{2,26},{20,12},{4,28},{22,14},{6,30},{24,0},... | collective-permute-start | bytes 294920 | tf_op jit(solution)/shard_map/ppermute | solution.py:192
  178.8 18.6 %collective-permute-start.30 = (bf16[24,2048]{1,0:T(8,128)(2,1)S(1)}, bf16[24,2048]{1,0:T(8,128)(2,1)S(1)}, u32[]{:S(2)}, u32[]{:S(2)}) collective-permute-start(bf16[24,2048]{1,0:T(8,128)(2,1)S(1)} %get-tuple-element.72), channel_id=1, source_target_pairs={{16,26},{0,10},{18,24},{2,8},{20,30},{4,14},{22,28},{6,12},{24,18}... | collective-permute-start | bytes 294920 | tf_op jit(solution)/shard_map/ppermute | solution.py:192
  180.4 23.0 %collective-permute-start.31 = (bf16[24,2048]{1,0:T(8,128)(2,1)}, bf16[24,2048]{1,0:T(8,128)(2,1)S(1)}, u32[]{:S(2)}, u32[]{:S(2)}) collective-permute-start(bf16[24,2048]{1,0:T(8,128)(2,1)} %get-tuple-element.73), channel_id=1, source_target_pairs={{16,10},{0,26},{18,8},{2,24},{20,14},{4,30},{22,12},{6,28},{24,2},... | collective-permute-start | bytes 294920 | tf_op jit(solution)/shard_map/ppermute | solution.py:192
  183.0 20.4 %collective-permute-start.32 = (bf16[24,2048]{1,0:T(8,128)(2,1)}, bf16[24,2048]{1,0:T(8,128)(2,1)S(1)}, u32[]{:S(2)}, u32[]{:S(2)}) collective-permute-start(bf16[24,2048]{1,0:T(8,128)(2,1)} %get-tuple-element.74), channel_id=1, source_target_pairs={{16,28},{0,12},{18,30},{2,14},{20,24},{4,8},{22,26},{6,10},{24,20}... | collective-permute-start | bytes 294920 | tf_op jit(solution)/shard_map/ppermute | solution.py:192
  191.9 11.5 %collective-permute-start.33 = (bf16[24,2048]{1,0:T(8,128)(2,1)}, bf16[24,2048]{1,0:T(8,128)(2,1)S(1)}, u32[]{:S(2)}, u32[]{:S(2)}) collective-permute-start(bf16[24,2048]{1,0:T(8,128)(2,1)} %get-tuple-element.75), channel_id=1, source_target_pairs={{16,12},{0,28},{18,14},{2,30},{20,8},{4,24},{22,10},{6,26},{24,4},... | collective-permute-start | bytes 294920 | tf_op jit(solution)/shard_map/ppermute | solution.py:192
  194.9 8.5 %collective-permute-start.34 = (bf16[24,2048]{1,0:T(8,128)(2,1)}, bf16[24,2048]{1,0:T(8,128)(2,1)S(1)}, u32[]{:S(2)}, u32[]{:S(2)}) collective-permute-start(bf16[24,2048]{1,0:T(8,128)(2,1)} %get-tuple-element.76), channel_id=1, source_target_pairs={{16,30},{0,14},{18,28},{2,12},{20,26},{4,10},{22,24},{6,8},{24,22}... | collective-permute-start | bytes 294920 | tf_op jit(solution)/shard_map/ppermute | solution.py:192
  197.4 8.6 %collective-permute-start.35 = (bf16[24,2048]{1,0:T(8,128)(2,1)}, bf16[24,2048]{1,0:T(8,128)(2,1)}, u32[]{:S(2)}, u32[]{:S(2)}) collective-permute-start(bf16[24,2048]{1,0:T(8,128)(2,1)} %get-tuple-element.77), channel_id=1, source_target_pairs={{16,14},{0,30},{18,12},{2,28},{20,10},{4,26},{22,8},{6,24},{24,6},... | collective-permute-start | bytes 294920 | tf_op jit(solution)/shard_map/ppermute | solution.py:192

commit v4 on v1

v4 whole, which is shorter than its diff:
```python
import functools

import jax
import jax.numpy as jnp
from jax import lax
from jax.experimental import pallas as pl
from jax.experimental.pallas import tpu as pltpu
from jax.sharding import PartitionSpec as P

BF16 = jnp.bfloat16
F32 = jnp.float32
VMEM_BYTES = 40 << 20


def dot(a, b, dims):
    return lax.dot_general(a, b, ((dims[:1], dims[1:]), ((), ())), preferred_element_type=F32)


def tiles(width):
    tile = min(512, width)
    return [slice(d, d + tile) for d in range(0, width, tile)]


def fetch(sources, targets, sems):
    copies = [pltpu.make_async_copy(s, t, sems.at[i]) for i, (s, t) in enumerate(zip(sources, targets))]
    for copy in copies:
        copy.start()
    return copies


def store(columns, index, stage_ref, out_ref, sems):
    copy = pltpu.make_async_copy(stage_ref.at[:, columns], out_ref.at[:, columns], sems.at[index])
    copy.start()
    return copy


def place_kernel(experts, routes_ref, tokens_ref, slots_ref, place_ref):
    slots, width = slots_ref.shape
    tok_rows, top_count = routes_ref.shape
    routes = routes_ref[...]
    numbers = lax.broadcasted_iota(jnp.int32, (tok_rows, experts), 1)
    named = [numbers == routes[:, k : k + 1] for k in range(top_count)]
    chosen = sum(n.astype(F32) for n in named)
    earlier = (
        lax.broadcasted_iota(jnp.int32, (tok_rows, tok_rows), 1)
        < lax.broadcasted_iota(jnp.int32, (tok_rows, tok_rows), 0)
    ).astype(F32)
    rank = dot(earlier.astype(BF16), chosen.astype(BF16), (1, 0))
    slot_numbers = lax.broadcasted_iota(jnp.int32, (tok_rows, slots), 1)
    total = None
    for k in range(top_count):
        own = jnp.sum(jnp.where(named[k], rank, 0.0), axis=1, keepdims=True)
        slot = routes[:, k : k + 1] * (slots // experts) + own.astype(jnp.int32)
        mark = (slot_numbers == slot).astype(F32)
        place_ref[k * tok_rows : (k + 1) * tok_rows, :] = mark.astype(BF16)
        total = mark if total is None else total + mark
    total = total.astype(BF16)
    for columns in tiles(width):
        slots_ref[:, columns] = dot(total, tokens_ref[:, columns], (0, 0)).astype(BF16)


def spread_kernel(top_count, place_ref, rows_ref, slots_ref):
    tok_rows = rows_ref.shape[0]
    total = sum(
        place_ref[k * tok_rows : (k + 1) * tok_rows, :].astype(F32) for k in range(top_count)
    ).astype(BF16)
    for columns in tiles(rows_ref.shape[1]):
        slots_ref[:, columns] = dot(total, rows_ref[:, columns], (0, 0)).astype(BF16)


def hidden_kernel(parts, rows_ref, *refs):
    sources, refs = [rows_ref, *refs[: 2 * parts]], refs[2 * parts :]
    hidden_ref, by_gate_ref, by_up_ref, sems, *targets = refs
    copies = fetch(sources, targets, sems)
    rows_ref, weights = targets[0], targets[1:]
    copies[0].wait()
    for i in range(parts):
        copies[1 + 2 * i].wait()
        pre_gate = dot(rows_ref[...], weights[2 * i][...], (1, 0))
        copies[2 + 2 * i].wait()
        pre_up = dot(rows_ref[...], weights[2 * i + 1][...], (1, 0))
        sig = jax.nn.sigmoid(pre_gate)
        act = pre_gate * sig
        hidden_ref[i] = (act * pre_up).astype(BF16)
        by_gate_ref[i] = pre_up * sig * (1.0 + pre_gate * (1.0 - sig))
        by_up_ref[i] = act


def out_kernel(parts, hidden_ref, *refs):
    sources, refs = refs[:parts], refs[parts:]
    out_ref, sems, out_sems, stage_ref, *weights = refs
    copies = fetch(sources, weights, sems)
    for copy in copies:
        copy.wait()
    sent = []
    for d, columns in enumerate(tiles(out_ref.shape[1])):
        stage_ref[:, columns] = sum(
            dot(hidden_ref[i], weights[i][:, columns], (1, 0)) for i in range(parts)
        ).astype(BF16)
        sent.append(store(columns, d, stage_ref, out_ref, out_sems))
    for copy in sent:
        copy.wait()


def backward_kernel(parts, by_gate_ref, by_up_ref, rows_ref, *refs):
    sources, refs = [rows_ref, *refs[: 3 * parts]], refs[3 * parts :]
    out_ref, sems, out_sems, back_gate_ref, back_up_ref, stage_ref, *targets = refs
    copies = fetch(sources, targets, sems)
    rows_ref, down, gate, up = targets[0], *(targets[1 + i * parts : 1 + (i + 1) * parts] for i in range(3))
    copies[0].wait()
    for i in range(parts):
        copies[1 + i].wait()
        back_hidden = dot(rows_ref[...], down[i][...], (1, 1))
        back_gate_ref[i] = (back_hidden * by_gate_ref[i]).astype(BF16)
        back_up_ref[i] = (back_hidden * by_up_ref[i]).astype(BF16)
    for copy in copies[1 + parts :]:
        copy.wait()
    sent = []
    for d, columns in enumerate(tiles(out_ref.shape[1])):
        stage_ref[:, columns] = sum(
            dot(back_gate_ref[i], gate[i][columns, :], (1, 1))
            + dot(back_up_ref[i], up[i][columns, :], (1, 1))
            for i in range(parts)
        ).astype(BF16)
        sent.append(store(columns, d, stage_ref, out_ref, out_sems))
    for copy in sent:
        copy.wait()


def mix_kernel(place_ref, gates_ref, cotangent_ref, slots_ref, mixed_ref, gate_grad_ref):
    tok_rows, top_count = gates_ref.shape
    total, grads = None, []
    for k in range(top_count):
        raw = dot(place_ref[k * tok_rows : (k + 1) * tok_rows, :], slots_ref[...], (1, 0))
        grads.append(jnp.sum(raw * cotangent_ref[...].astype(F32), axis=1, keepdims=True))
        term = raw * gates_ref[:, k : k + 1]
        total = term if total is None else total + term
    mixed_ref[...] = total.astype(BF16)
    gate_grad_ref[...] = jnp.concatenate(grads, axis=1)


def sum_kernel(place_ref, gates_ref, slots_ref, out_ref):
    tok_rows, top_count = gates_ref.shape
    total = None
    for k in range(top_count):
        raw = dot(place_ref[k * tok_rows : (k + 1) * tok_rows, :], slots_ref[...], (1, 0))
        term = raw * gates_ref[:, k : k + 1]
        total = term if total is None else total + term
    out_ref[...] = total.astype(BF16)


def call(kernel, outs, flops, scratch=(), far=(), far_out=False):
    def run(*args):
        moved = sum(a.size * a.dtype.itemsize for a in (*args, *outs))
        spaces = [pl.ANY if i in far else pltpu.VMEM for i in range(len(args))]
        return pl.pallas_call(
            kernel,
            out_shape=tuple(outs),
            in_specs=[pl.BlockSpec(memory_space=space) for space in spaces],
            out_specs=tuple(
                pl.BlockSpec(memory_space=pl.ANY if far_out else pltpu.VMEM) for _ in outs
            ),
            scratch_shapes=scratch,
            compiler_params=pltpu.CompilerParams(vmem_limit_bytes=VMEM_BYTES),
            cost_estimate=pl.CostEstimate(flops=flops, bytes_accessed=moved, transcendentals=0),
        )(*args)

    return run


def body(tokens, cotangent, routes, gates, w_gate, w_up, w_down):
    tok_rows, width = tokens.shape
    top_count = routes.shape[1]
    parts, experts = lax.axis_size("dp"), lax.axis_size("expert")
    hidden = w_gate.shape[2]
    capacity = max(2, 3 * tok_rows * top_count // (2 * experts))
    slots = experts * capacity
    axes = ("dp", "expert")

    def device(g, j):
        return g * experts + j

    def home(e, c):
        return device((e + 1) % parts, e // parts * parts + c)

    swap = [(device(g, e), home(e, g)) for g in range(parts) for e in range(experts)]
    groups = [[home(e, c) for e in range(experts)] for c in range(parts)]

    def whole_expert(weight):
        own = lax.ppermute(weight[0], axes, swap)
        shares = [own]
        for step in range(1, parts):
            turn = [(j, j // parts * parts + (j + step) % parts) for j in range(experts)]
            shares.append(lax.ppermute(own, "expert", turn))
        return shares

    def exchange(rows):
        return lax.all_to_all(
            rows.reshape(experts, capacity, width), axes, 0, 0, axis_index_groups=groups, tiled=True
        ).reshape(slots, width)

    spread_flops = 2 * slots * tok_rows * width
    dot_flops = 2 * slots * width * hidden * parts
    slot_shape = jax.ShapeDtypeStruct((slots, width), BF16)
    place_shape = jax.ShapeDtypeStruct((top_count * tok_rows, slots), BF16)
    unit_shape = jax.ShapeDtypeStruct((parts, slots, hidden), F32)
    hidden_shape = jax.ShapeDtypeStruct((parts, slots, hidden), BF16)
    token_shape = jax.ShapeDtypeStruct((tok_rows, width), BF16)
    hidden_scratch = pltpu.VMEM((parts, slots, hidden), BF16)
    row_scratch = pltpu.VMEM((slots, width), BF16)
    in_scratch = pltpu.VMEM((width, hidden), BF16)
    down_scratch = pltpu.VMEM((hidden, width), BF16)
    out_sems = pltpu.SemaphoreType.DMA((len(tiles(width)),))

    gate_w, up_w, down_w = whole_expert(w_gate), whole_expert(w_up), whole_expert(w_down)
    x_slots, place = call(
        functools.partial(place_kernel, experts), [slot_shape, place_shape], spread_flops
    )(routes, tokens)
    x_rows = exchange(x_slots)
    (dy_slots,) = call(
        functools.partial(spread_kernel, top_count), [slot_shape], spread_flops
    )(place, cotangent)
    dy_rows = exchange(dy_slots)
    hidden_rows, by_gate, by_up = call(
        functools.partial(hidden_kernel, parts),
        [hidden_shape, unit_shape, unit_shape],
        2 * dot_flops,
        [pltpu.SemaphoreType.DMA((1 + 2 * parts,)), row_scratch] + [in_scratch] * (2 * parts),
        far=range(1 + 2 * parts),
    )(x_rows, *(w for pair in zip(gate_w, up_w) for w in pair))
    (out_rows,) = call(
        functools.partial(out_kernel, parts),
        [slot_shape],
        dot_flops,
        [pltpu.SemaphoreType.DMA((parts,)), out_sems, row_scratch] + [down_scratch] * parts,
        far=range(1, 1 + parts),
        far_out=True,
    )(hidden_rows, *down_w)
    out_slots = exchange(out_rows)
    (grad_rows,) = call(
        functools.partial(backward_kernel, parts),
        [slot_shape],
        3 * dot_flops,
        [pltpu.SemaphoreType.DMA((1 + 3 * parts,)), out_sems, hidden_scratch, hidden_scratch]
        + [row_scratch] * 2
        + [down_scratch] * parts
        + [in_scratch] * (2 * parts),
        far=range(2, 3 + 3 * parts),
        far_out=True,
    )(by_gate, by_up, dy_rows, *down_w, *gate_w, *up_w)
    grad_slots = exchange(grad_rows)
    mixed, gate_grad = call(
        mix_kernel, [token_shape, jax.ShapeDtypeStruct(gates.shape, F32)], 2 * spread_flops
    )(place, gates, cotangent, out_slots)
    (token_grad,) = call(sum_kernel, [token_shape], 2 * spread_flops)(place, gates, grad_slots)
    return (mixed, token_grad, gate_grad)


def solution(mesh):
    rows, weights = P(("dp", "expert"), None), P("expert", None, "dp")
    return jax.shard_map(
        body,
        mesh=mesh,
        in_specs=(rows, rows, rows, rows, weights, weights, P("expert", "dp", None)),
        out_specs=(rows, rows, rows),
        check_vma=False,
    )
```

time: 204 us -> 209 us (1.025)
  the two profiles are of different devices: /device:TPU:10 before, /device:TPU:0 now
where the time goes in v4:
time: 209 us; the launch traced here: 205 us
  waiting for transfers between devices  127 us (61%)
  starting transfers between devices  38.1 us (18%)
  Pallas kernels  24.5 us (12%)
  local copies, waits for them, and re-layouts  15.1 us (7%)
    all_to_all x4, waiting for transfers between devices, exchange(): lax.all_to_all(rows.reshape(experts, capacity, width), axes, 0, 0, axis_i...  85.7 us
    ppermute x3, waiting for transfers between devices, whole_expert(): own = lax.ppermute(weight[0], axes, swap)  41.2 us
    all_to_all x4, starting transfers between devices, exchange(): lax.all_to_all(rows.reshape(experts, capacity, width), axes, 0, 0, axis_i...  36.5 us
    pallas_call x7, Pallas kernels, run(): pl.pallas_call(kernel, out_shape=tuple(outs), in_specs=[pl.BlockSpec(memo...  24.5 us
    unnamed x31, local copies, waits for them, and re-layouts  15.1 us
  transfers between devices with their start and end apart: 10, of which 5 were waited for; matrix products, arithmetic and copies ran while one was open for 0% of the time, Pallas kernels for 6%

profile of v4, /device:TPU:0, one launch (start us, length us, event | category | flops | bytes accessed | tf_op | source)
XLA Modules:
  0.0 205.4 jit_solution(16508965079686916409)
XLA Ops:
  0.6 0.8 copy.10.routes_ref
  1.4 0.0 copy-start.12
  1.4 1.0 copy-done.12
  2.5 2.2 %shard_map.94 = (bf16[384,2048]{1,0:T(8,128)(2,1)}, bf16[256,384]{1,0:T(8,128)(2,1)S(1)}) custom-call(s32[128,2]{1,0:T(8,128)S(1)} %copy.10.routes_ref, bf16[128,2048]{1,0:T(8,128)(2,1)S(1)} %copy-done.12), custom_call_target="tpu_custom_call" | custom-call | flops 201326592 | bytes 2294784 | tf_op jit(solution)/shard_map/pallas_call | solution.py:156
  4.7 0.0 copy-start.1
  4.7 8.9 %all-to-all-start = ((bf16[16,24,2048]{2,1,0:T(8,128)(2,1)}), bf16[16,24,2048]{2,1,0:T(8,128)(2,1)}, u32[]{:S(2)}, u32[]{:S(2)}) async-start(bf16[16,24,2048]{2,1,0:T(8,128)(2,1)} %bitcast), calls=%async_computation | async-start | bytes 3145728 | tf_op jit(solution)/shard_map/all_to_all | solution.py:198
  13.6 0.2 collective-permute-start
  13.7 0.0 collective-permute-start.1
  13.8 0.8 collective-permute-start.4
  14.6 0.0 copy-done.1
  14.6 1.7 shard_map.98
  16.3 29.5 %all-to-all-done = bf16[16,24,2048]{2,1,0:T(8,128)(2,1)} async-done(((bf16[16,24,2048]{2,1,0:T(8,128)(2,1)}), bf16[16,24,2048]{2,1,0:T(8,128)(2,1)}, u32[]{:S(2)}, u32[]{:S(2)}) %all-to-all-start) | async-done | bytes 1572896 | tf_op jit(solution)/shard_map/all_to_all | solution.py:198
  45.8 9.7 %all-to-all-start.2 = ((bf16[16,24,2048]{2,1,0:T(8,128)(2,1)}), bf16[16,24,2048]{2,1,0:T(8,128)(2,1)S(1)}, u32[]{:S(2)}, u32[]{:S(2)}) async-start(bf16[16,24,2048]{2,1,0:T(8,128)(2,1)} %bitcast.7), calls=%async_computation.2 | async-start | bytes 3145728 | tf_op jit(solution)/shard_map/all_to_all | solution.py:198
  55.5 0.0 collective-permute-done.refs_0_.refs_2_
  55.5 0.1 collective-permute-start.2
  55.6 20.5 %collective-permute-done.1.refs_1_.refs_4_ = bf16[2048,384]{1,0:T(8,128)(2,1)} collective-permute-done((bf16[2048,384]{1,0:T(8,128)(2,1)}, bf16[2048,384]{1,0:T(8,128)(2,1)}, u32[]{:S(2)}, u32[]{:S(2)}) %collective-permute-start.1) | collective-permute-done | bytes 1572896 | tf_op jit(solution)/shard_map/ppermute | solution.py:190
  76.1 0.3 collective-permute-start.3
  76.4 20.7 %collective-permute-done.4.refs_0_ = bf16[384,2048]{1,0:T(8,128)(2,1)S(1)} collective-permute-done((bf16[384,2048]{1,0:T(8,128)(2,1)}, bf16[384,2048]{1,0:T(8,128)(2,1)S(1)}, u32[]{:S(2)}, u32[]{:S(2)}) %collective-permute-start.4) | collective-permute-done | bytes 1572896 | tf_op jit(solution)/shard_map/ppermute | solution.py:190
  97.1 0.2 collective-permute-start.5
  97.3 0.0 collective-permute-done.2.refs_2_.refs_3_
  97.3 0.0 collective-permute-done.3.refs_3_.refs_5_
  97.4 6.0 %shard_map.95 = (bf16[2,384,384]{2,1,0:T(8,128)(2,1)S(1)}, f32[2,384,384]{2,1,0:T(8,128)S(1)}, f32[2,384,384]{2,1,0:T(8,128)S(1)}) custom-call(bf16[384,2048]{1,0:T(8,128)(2,1)} %bitcast.1.rows_ref, bf16[2048,384]{1,0:T(8,128)(2,1)} %collective-permute-done.refs_0_.refs_2_, bf16[2048,384]{1,0:T(8,128)(2,1)} %collective-permute-done.1.refs_1_.refs_4_, ...), custom_call_target="tpu_custom_call" | custom-call | flops 2415919104 | bytes 10813440 | tf_op jit(solution)/shard_map/pallas_call | solution.py:156
  103.3 0.0 copy-start.3
  103.3 1.2 copy-done.3
  104.6 0.0 copy-start.5
  104.6 1.2 copy-done.5
  105.8 0.0 copy-start.6
  105.8 1.0 copy-done.6
  106.8 0.0 copy-start.8
  106.8 1.0 copy-done.8
  107.8 0.0 copy-start.10
  107.8 0.8 copy-done.10
  108.7 0.0 all-to-all-done.2
  108.7 0.0 collective-permute-done.5.refs_1_
  108.7 0.0 copy-start.4
  108.7 1.4 copy-done.4
  110.1 0.0 copy-start.7
  110.1 1.3 copy-done.7
  111.3 0.0 copy-start.9
  111.3 1.3 copy-done.9
  112.6 7.4 %shard_map.99 = bf16[384,2048]{1,0:T(8,128)(2,1)} custom-call(f32[2,384,384]{2,1,0:T(8,128)S(1)} %copy-done.7, f32[2,384,384]{2,1,0:T(8,128)S(1)} %copy-done.9, bf16[384,2048]{1,0:T(8,128)(2,1)S(1)} %bitcast.11, bf16[384,2048]{1,0:T(8,128)(2,1)S(1)} %collective-permute-done.4.refs_0_, bf16[384,2048]{1,0:T(8,128)(2,1)} %collective-permute-done.5.refs_1_, ...), custom_call_target="tpu_custom_call" | custom-call | flops 3623878656 | bytes 14942208 | tf_op jit(solution)/shard_map/pallas_call | solution.py:156
  120.0 7.3 %all-to-all-start.3 = ((bf16[16,24,2048]{2,1,0:T(8,128)(2,1)}), bf16[16,24,2048]{2,1,0:T(8,128)(2,1)S(1)}, u32[]{:S(2)}, u32[]{:S(2)}) async-start(bf16[16,24,2048]{2,1,0:T(8,128)(2,1)} %bitcast.9), calls=%async_computation.3 | async-start | bytes 3145728 | tf_op jit(solution)/shard_map/all_to_all | solution.py:198
  127.3 0.0 copy-start.11
  127.3 1.1 copy-done.11
  128.4 4.0 %shard_map.96 = bf16[384,2048]{1,0:T(8,128)(2,1)S(1)} custom-call(bf16[2,384,384]{2,1,0:T(8,128)(2,1)S(1)} %copy-done.11, bf16[384,2048]{1,0:T(8,128)(2,1)S(1)} %collective-permute-done.4.refs_0_, bf16[384,2048]{1,0:T(8,128)(2,1)} %collective-permute-done.5.refs_1_), custom_call_target="tpu_custom_call" | custom-call | flops 1207959552 | bytes 5308416 | tf_op jit(solution)/shard_map/pallas_call | solution.py:156
  132.4 0.0 copy-start
  132.4 1.2 copy-done
  133.6 26.2 %all-to-all-done.3 = bf16[16,24,2048]{2,1,0:T(8,128)(2,1)S(1)} async-done(((bf16[16,24,2048]{2,1,0:T(8,128)(2,1)}), bf16[16,24,2048]{2,1,0:T(8,128)(2,1)S(1)}, u32[]{:S(2)}, u32[]{:S(2)}) %all-to-all-start.3) | async-done | bytes 1572896 | tf_op jit(solution)/shard_map/all_to_all | solution.py:198
  159.8 0.0 copy-start.13
  159.8 10.6 %all-to-all-start.1 = ((bf16[16,24,2048]{2,1,0:T(8,128)(2,1)}), bf16[16,24,2048]{2,1,0:T(8,128)(2,1)S(1)}, u32[]{:S(2)}, u32[]{:S(2)}) async-start(bf16[16,24,2048]{2,1,0:T(8,128)(2,1)} %bitcast.14), calls=%async_computation.1 | async-start | bytes 3145728 | tf_op jit(solution)/shard_map/all_to_all | solution.py:198
  170.4 0.0 copy-done.13
  170.4 0.1 copy.11.gates_ref
  170.5 1.5 shard_map.100
  172.1 30.1 %all-to-all-done.1 = bf16[16,24,2048]{2,1,0:T(8,128)(2,1)S(1)} async-done(((bf16[16,24,2048]{2,1,0:T(8,128)(2,1)}), bf16[16,24,2048]{2,1,0:T(8,128)(2,1)S(1)}, u32[]{:S(2)}, u32[]{:S(2)}) %all-to-all-start.1) | async-done | bytes 1572896 | tf_op jit(solution)/shard_map/all_to_all | solution.py:198
  202.1 0.0 copy-start.2
  202.1 1.0 copy-done.2
  203.2 1.7 shard_map.97
  204.8 0.6 copy.13
Async XLA Ops:
  1.4 1.0 copy-start.12
  4.7 9.9 %copy-start.1 = (bf16[128,2048]{1,0:T(8,128)(2,1)S(1)}, bf16[128,2048]{1,0:T(8,128)(2,1)}, u32[]{:S(2)}) copy-start(bf16[128,2048]{1,0:T(8,128)(2,1)} %rows_ref.1) | copy-start | bytes 1572868
  4.7 41.1 %all-to-all-start = ((bf16[16,24,2048]{2,1,0:T(8,128)(2,1)}), bf16[16,24,2048]{2,1,0:T(8,128)(2,1)}, u32[]{:S(2)}, u32[]{:S(2)}) async-start(bf16[16,24,2048]{2,1,0:T(8,128)(2,1)} %bitcast), calls=%async_computation | async-start | bytes 3145728 | tf_op jit(solution)/shard_map/all_to_all | solution.py:198
  13.6 41.9 %collective-permute-start = (bf16[2048,384]{1,0:T(8,128)(2,1)}, bf16[2048,384]{1,0:T(8,128)(2,1)}, u32[]{:S(2)}, u32[]{:S(2)}) collective-permute-start(bf16[2048,384]{1,0:T(8,128)(2,1)} %bitcast.2), channel_id=1, source_target_pairs={{0,16},{1,0},{2,18},{3,2},{4,20},{5,4},{6,22},{7,6},{8,24},{9,8},{... | collective-permute-start | bytes 4718600 | tf_op jit(solution)/shard_map/ppermute | solution.py:190
  13.7 62.3 %collective-permute-start.1 = (bf16[2048,384]{1,0:T(8,128)(2,1)}, bf16[2048,384]{1,0:T(8,128)(2,1)}, u32[]{:S(2)}, u32[]{:S(2)}) collective-permute-start(bf16[2048,384]{1,0:T(8,128)(2,1)} %bitcast.3), channel_id=1, source_target_pairs={{0,16},{1,0},{2,18},{3,2},{4,20},{5,4},{6,22},{7,6},{8,24},{9,8},{... | collective-permute-start | bytes 4718600 | tf_op jit(solution)/shard_map/ppermute | solution.py:190
  13.8 83.3 %collective-permute-start.4 = (bf16[384,2048]{1,0:T(8,128)(2,1)}, bf16[384,2048]{1,0:T(8,128)(2,1)S(1)}, u32[]{:S(2)}, u32[]{:S(2)}) collective-permute-start(bf16[384,2048]{1,0:T(8,128)(2,1)} %bitcast.15), channel_id=1, source_target_pairs={{0,16},{1,0},{2,18},{3,2},{4,20},{5,4},{6,22},{7,6},{8,24},{9,8},{... | collective-permute-start | bytes 4718600 | tf_op jit(solution)/shard_map/ppermute | solution.py:190
  45.8 62.9 %all-to-all-start.2 = ((bf16[16,24,2048]{2,1,0:T(8,128)(2,1)}), bf16[16,24,2048]{2,1,0:T(8,128)(2,1)S(1)}, u32[]{:S(2)}, u32[]{:S(2)}) async-start(bf16[16,24,2048]{2,1,0:T(8,128)(2,1)} %bitcast.7), calls=%async_computation.2 | async-start | bytes 3145728 | tf_op jit(solution)/shard_map/all_to_all | solution.py:198
  55.5 41.8 %collective-permute-start.2 = (bf16[2048,384]{1,0:T(8,128)(2,1)}, bf16[2048,384]{1,0:T(8,128)(2,1)S(1)}, u32[]{:S(2)}, u32[]{:S(2)}) collective-permute-start(bf16[2048,384]{1,0:T(8,128)(2,1)} %collective-permute-done.refs_0_.refs_2_), channel_id=1, source_target_pairs={{0,1},{1,0},{2,3},{3,2},{4,5},{5,4},{6,7},{7,6},{8,9},{9,8},{10,11... | collective-permute-start | bytes 4718600 | tf_op jit(solution)/shard_map/ppermute | solution.py:194
  76.1 21.3 %collective-permute-start.3 = (bf16[2048,384]{1,0:T(8,128)(2,1)}, bf16[2048,384]{1,0:T(8,128)(2,1)S(1)}, u32[]{:S(2)}, u32[]{:S(2)}) collective-permute-start(bf16[2048,384]{1,0:T(8,128)(2,1)} %collective-permute-done.1.refs_1_.refs_4_), channel_id=1, source_target_pairs={{0,1},{1,0},{2,3},{3,2},{4,5},{5,4},{6,7},{7,6},{8,9},{9,8},{10,11... | collective-permute-start | bytes 4718600 | tf_op jit(solution)/shard_map/ppermute | solution.py:194
  97.1 11.5 %collective-permute-start.5 = (bf16[384,2048]{1,0:T(8,128)(2,1)S(1)}, bf16[384,2048]{1,0:T(8,128)(2,1)}, u32[]{:S(2)}, u32[]{:S(2)}) collective-permute-start(bf16[384,2048]{1,0:T(8,128)(2,1)S(1)} %collective-permute-done.4.refs_0_), channel_id=1, source_target_pairs={{0,1},{1,0},{2,3},{3,2},{4,5},{5,4},{6,7},{7,6},{8,9},{9,8},{10,11... | collective-permute-start | bytes 4718600 | tf_op jit(solution)/shard_map/ppermute | solution.py:194
  103.3 1.2 copy-start.3
  104.6 1.2 copy-start.5
  105.8 1.0 copy-start.6
  106.8 1.0 copy-start.8
  107.8 0.8 copy-start.10
  108.7 1.4 copy-start.4
  110.1 1.3 copy-start.7
  111.3 1.3 copy-start.9
  120.0 39.8 %all-to-all-start.3 = ((bf16[16,24,2048]{2,1,0:T(8,128)(2,1)}), bf16[16,24,2048]{2,1,0:T(8,128)(2,1)S(1)}, u32[]{:S(2)}, u32[]{:S(2)}) async-start(bf16[16,24,2048]{2,1,0:T(8,128)(2,1)} %bitcast.9), calls=%async_computation.3 | async-start | bytes 3145728 | tf_op jit(solution)/shard_map/all_to_all | solution.py:198
  127.3 1.1 copy-start.11
  132.4 1.2 copy-start
  159.8 10.6 %copy-start.13 = (f32[128,2]{0,1:T(2,128)S(1)}, f32[128,2]{0,1:T(2,128)}, u32[]{:S(2)}) copy-start(f32[128,2]{0,1:T(2,128)} %param.10) | copy-start | bytes 3076
  159.8 42.3 %all-to-all-start.1 = ((bf16[16,24,2048]{2,1,0:T(8,128)(2,1)}), bf16[16,24,2048]{2,1,0:T(8,128)(2,1)S(1)}, u32[]{:S(2)}, u32[]{:S(2)}) async-start(bf16[16,24,2048]{2,1,0:T(8,128)(2,1)} %bitcast.14), calls=%async_computation.1 | async-start | bytes 3145728 | tf_op jit(solution)/shard_map/all_to_all | solution.py:198
  202.1 1.0 copy-start.2

commit v5 on v4

--- a/solution.py
+++ b/solution.py
@@ -28,8 +28,8 @@
     return copies
 
 
-def store(columns, index, stage_ref, out_ref, sems):
-    copy = pltpu.make_async_copy(stage_ref.at[:, columns], out_ref.at[:, columns], sems.at[index])
+def store(stage_ref, out_ref, sem):
+    copy = pltpu.make_async_copy(stage_ref, out_ref, sem)
     copy.start()
     return copy
 
@@ -59,7 +59,7 @@
         slots_ref[:, columns] = dot(total, tokens_ref[:, columns], (0, 0)).astype(BF16)
 
 
-def spread_kernel(top_count, place_ref, rows_ref, slots_ref):
+def spread_kernel(top_count, place_ref, rows_ref, _, slots_ref):
     tok_rows = rows_ref.shape[0]
     total = sum(
         place_ref[k * tok_rows : (k + 1) * tok_rows, :].astype(F32) for k in range(top_count)
@@ -68,11 +68,13 @@
         slots_ref[:, columns] = dot(total, rows_ref[:, columns], (0, 0)).astype(BF16)
 
 
-def hidden_kernel(parts, rows_ref, *refs):
-    sources, refs = [rows_ref, *refs[: 2 * parts]], refs[2 * parts :]
-    hidden_ref, by_gate_ref, by_up_ref, sems, *targets = refs
+def forward_kernel(parts, *refs):
+    sources, refs = refs[: 1 + 3 * parts], refs[1 + 3 * parts :]
+    out_ref, by_gate_ref, by_up_ref, sems, out_sems = refs[:5]
+    stage_ref, by_gate_stage, by_up_stage, hidden_ref, *targets = refs[5:]
     copies = fetch(sources, targets, sems)
     rows_ref, weights = targets[0], targets[1:]
+    sent = []
     copies[0].wait()
     for i in range(parts):
         copies[1 + 2 * i].wait()
@@ -82,47 +84,47 @@
         sig = jax.nn.sigmoid(pre_gate)
         act = pre_gate * sig
         hidden_ref[i] = (act * pre_up).astype(BF16)
-        by_gate_ref[i] = pre_up * sig * (1.0 + pre_gate * (1.0 - sig))
-        by_up_ref[i] = act
-
-
-def out_kernel(parts, hidden_ref, *refs):
-    sources, refs = refs[:parts], refs[parts:]
-    out_ref, sems, out_sems, stage_ref, *weights = refs
-    copies = fetch(sources, weights, sems)
-    for copy in copies:
-        copy.wait()
-    sent = []
-    for d, columns in enumerate(tiles(out_ref.shape[1])):
+        by_gate_stage[i] = pre_up * sig * (1.0 + pre_gate * (1.0 - sig))
+        by_up_stage[i] = act
+    sent.append(store(by_gate_stage, by_gate_ref, out_sems.at[0]))
+    sent.append(store(by_up_stage, by_up_ref, out_sems.at[1]))
+    for copy in copies[1 + 2 * parts :]:
+        copy.wait()
+    down = weights[2 * parts :]
+    for columns in tiles(out_ref.shape[1]):
         stage_ref[:, columns] = sum(
-            dot(hidden_ref[i], weights[i][:, columns], (1, 0)) for i in range(parts)
+            dot(hidden_ref[i], down[i][:, columns], (1, 0)) for i in range(parts)
         ).astype(BF16)
-        sent.append(store(columns, d, stage_ref, out_ref, out_sems))
+        sem = out_sems.at[len(sent)]
+        sent.append(store(stage_ref.at[:, columns], out_ref.at[:, columns], sem))
     for copy in sent:
         copy.wait()
 
 
-def backward_kernel(parts, by_gate_ref, by_up_ref, rows_ref, *refs):
-    sources, refs = [rows_ref, *refs[: 3 * parts]], refs[3 * parts :]
+def backward_kernel(parts, *refs):
+    sources, refs = refs[: 3 + 3 * parts], refs[3 + 3 * parts :]
     out_ref, sems, out_sems, back_gate_ref, back_up_ref, stage_ref, *targets = refs
     copies = fetch(sources, targets, sems)
-    rows_ref, down, gate, up = targets[0], *(targets[1 + i * parts : 1 + (i + 1) * parts] for i in range(3))
-    copies[0].wait()
+    rows_ref, targets = targets[0], targets[1:]
+    down, (by_gate_ref, by_up_ref) = targets[:parts], targets[parts : parts + 2]
+    gate, up = targets[parts + 2 : 2 * parts + 2], targets[2 * parts + 2 :]
+    for copy in copies[: 3 + parts]:
+        copy.wait()
     for i in range(parts):
-        copies[1 + i].wait()
         back_hidden = dot(rows_ref[...], down[i][...], (1, 1))
         back_gate_ref[i] = (back_hidden * by_gate_ref[i]).astype(BF16)
         back_up_ref[i] = (back_hidden * by_up_ref[i]).astype(BF16)
-    for copy in copies[1 + parts :]:
+    for copy in copies[3 + parts :]:
         copy.wait()
     sent = []
-    for d, columns in enumerate(tiles(out_ref.shape[1])):
+    for columns in tiles(out_ref.shape[1]):
         stage_ref[:, columns] = sum(
             dot(back_gate_ref[i], gate[i][columns, :], (1, 1))
             + dot(back_up_ref[i], up[i][columns, :], (1, 1))
             for i in range(parts)
         ).astype(BF16)
-        sent.append(store(columns, d, stage_ref, out_ref, out_sems))
+        sem = out_sems.at[len(sent)]
+        sent.append(store(stage_ref.at[:, columns], out_ref.at[:, columns], sem))
     for copy in sent:
         copy.wait()
 
@@ -152,13 +154,13 @@
 def call(kernel, outs, flops, scratch=(), far=(), far_out=False):
     def run(*args):
         moved = sum(a.size * a.dtype.itemsize for a in (*args, *outs))
-        spaces = [pl.ANY if i in far else pltpu.VMEM for i in range(len(args))]
+        spaces = [pltpu.HBM if i in far else pltpu.VMEM for i in range(len(args))]
         return pl.pallas_call(
             kernel,
             out_shape=tuple(outs),
             in_specs=[pl.BlockSpec(memory_space=space) for space in spaces],
             out_specs=tuple(
-                pl.BlockSpec(memory_space=pl.ANY if far_out else pltpu.VMEM) for _ in outs
+                pl.BlockSpec(memory_space=pltpu.HBM if far_out else pltpu.VMEM) for _ in outs
             ),
             scratch_shapes=scratch,
             compiler_params=pltpu.CompilerParams(vmem_limit_bytes=VMEM_BYTES),
@@ -204,13 +206,15 @@
     slot_shape = jax.ShapeDtypeStruct((slots, width), BF16)
     place_shape = jax.ShapeDtypeStruct((top_count * tok_rows, slots), BF16)
     unit_shape = jax.ShapeDtypeStruct((parts, slots, hidden), F32)
-    hidden_shape = jax.ShapeDtypeStruct((parts, slots, hidden), BF16)
     token_shape = jax.ShapeDtypeStruct((tok_rows, width), BF16)
     hidden_scratch = pltpu.VMEM((parts, slots, hidden), BF16)
     row_scratch = pltpu.VMEM((slots, width), BF16)
     in_scratch = pltpu.VMEM((width, hidden), BF16)
     down_scratch = pltpu.VMEM((hidden, width), BF16)
-    out_sems = pltpu.SemaphoreType.DMA((len(tiles(width)),))
+    unit_stage = pltpu.VMEM((parts, slots, hidden), F32)
+
+    def sems(number):
+        return pltpu.SemaphoreType.DMA((number,))
 
     gate_w, up_w, down_w = whole_expert(w_gate), whole_expert(w_up), whole_expert(w_down)
     x_slots, place = call(
@@ -218,36 +222,33 @@
     )(routes, tokens)
     x_rows = exchange(x_slots)
     (dy_slots,) = call(
-        functools.partial(spread_kernel, top_count), [slot_shape], spread_flops
-    )(place, cotangent)
+        functools.partial(spread_kernel, top_count), [slot_shape], spread_flops, far=(2,)
+    )(place, cotangent, gate_w[0])
     dy_rows = exchange(dy_slots)
-    hidden_rows, by_gate, by_up = call(
-        functools.partial(hidden_kernel, parts),
-        [hidden_shape, unit_shape, unit_shape],
-        2 * dot_flops,
-        [pltpu.SemaphoreType.DMA((1 + 2 * parts,)), row_scratch] + [in_scratch] * (2 * parts),
-        far=range(1 + 2 * parts),
-    )(x_rows, *(w for pair in zip(gate_w, up_w) for w in pair))
-    (out_rows,) = call(
-        functools.partial(out_kernel, parts),
-        [slot_shape],
-        dot_flops,
-        [pltpu.SemaphoreType.DMA((parts,)), out_sems, row_scratch] + [down_scratch] * parts,
-        far=range(1, 1 + parts),
+    out_rows, by_gate, by_up = call(
+        functools.partial(forward_kernel, parts),
+        [slot_shape, unit_shape, unit_shape],
+        3 * dot_flops,
+        [sems(1 + 3 * parts), sems(2 + len(tiles(width))), row_scratch, unit_stage, unit_stage]
+        + [hidden_scratch, row_scratch]
+        + [in_scratch] * (2 * parts)
+        + [down_scratch] * parts,
+        far=range(1 + 3 * parts),
         far_out=True,
-    )(hidden_rows, *down_w)
+    )(x_rows, *(w for pair in zip(gate_w, up_w) for w in pair), *down_w)
     out_slots = exchange(out_rows)
     (grad_rows,) = call(
         functools.partial(backward_kernel, parts),
         [slot_shape],
         3 * dot_flops,
-        [pltpu.SemaphoreType.DMA((1 + 3 * parts,)), out_sems, hidden_scratch, hidden_scratch]
+        [sems(3 + 3 * parts), sems(len(tiles(width))), hidden_scratch, hidden_scratch]
         + [row_scratch] * 2
         + [down_scratch] * parts
+        + [unit_stage] * 2
         + [in_scratch] * (2 * parts),
-        far=range(2, 3 + 3 * parts),
+        far=range(3 + 3 * parts),
         far_out=True,
-    )(by_gate, by_up, dy_rows, *down_w, *gate_w, *up_w)
+    )(dy_rows, *down_w, by_gate, by_up, *gate_w, *up_w)
     grad_slots = exchange(grad_rows)
     mixed, gate_grad = call(
         mix_kernel, [token_shape, jax.ShapeDtypeStruct(gates.shape, F32)], 2 * spread_flops

time: 209 us -> 202 us (0.967)
  waiting for transfers between devices: 127 us -> 123 us
  starting transfers between devices: 38.1 us -> 34.6 us
    all_to_all x4, waiting for transfers between devices: 85.7 us -> 45.4 us  [exchange(): lax.all_to_all(rows.reshape(experts, capacity, width), axes, 0, 0, axis_i...]
    ppermute x3, waiting for transfers between devices: 41.2 us -> 73.8 us  [whole_expert(): own = lax.ppermute(weight[0], axes, swap)]
    ppermute x3, waiting for transfers between devices: 0.01 us -> 3.3 us  [whole_expert(): shares.append(lax.ppermute(own, 'expert', turn))]
    all_to_all x4, starting transfers between devices: 36.5 us -> 33.2 us  [exchange(): lax.all_to_all(rows.reshape(experts, capacity, width), axes, 0, 0, axis_i...]
    unnamed x31 -> x35, local copies, waits for them, and re-layouts: 15.1 us -> 17.1 us
    pallas_call x7 -> x6, Pallas kernels: 24.5 us -> 23.6 us  [run(): pl.pallas_call(kernel, out_shape=tuple(outs), in_specs=[pl.BlockSpec(memo...]
  transfers between devices with their start and end apart: 10 -> 10, of which waited for: 5 -> 6; matrix products, arithmetic and copies ran while one was open for 0% -> 0% of each run, Pallas kernels for 6% -> 10%
where the time goes in v5:
time: 202 us; the launch traced here: 199 us
  waiting for transfers between devices  123 us (61%)
  starting transfers between devices  34.6 us (17%)
  Pallas kernels  23.6 us (12%)
  local copies, waits for them, and re-layouts  17.1 us (8%)
    ppermute x3, waiting for transfers between devices, whole_expert(): own = lax.ppermute(weight[0], axes, swap)  73.8 us
    all_to_all x4, waiting for transfers between devices, exchange(): lax.all_to_all(rows.reshape(experts, capacity, width), axes, 0, 0, axis_i...  45.4 us
    all_to_all x4, starting transfers between devices, exchange(): lax.all_to_all(rows.reshape(experts, capacity, width), axes, 0, 0, axis_i...  33.2 us
    pallas_call x6, Pallas kernels, run(): pl.pallas_call(kernel, out_shape=tuple(outs), in_specs=[pl.BlockSpec(memo...  23.6 us
    unnamed x35, local copies, waits for them, and re-layouts  17.1 us
  transfers between devices with their start and end apart: 10, of which 6 were waited for; matrix products, arithmetic and copies ran while one was open for 0% of the time, Pallas kernels for 10%

profile of v5, /device:TPU:0, one launch (start us, length us, event | category | flops | bytes accessed | tf_op | source)
XLA Modules:
  0.0 198.6 jit_solution(9737096856609344337)
XLA Ops:
  0.6 0.8 copy.10.routes_ref
  1.4 0.0 copy-start.14
  1.4 1.0 copy-done.14
  2.5 2.2 %shard_map.94 = (bf16[384,2048]{1,0:T(8,128)(2,1)}, bf16[256,384]{1,0:T(8,128)(2,1)S(1)}) custom-call(s32[128,2]{1,0:T(8,128)S(1)} %copy.10.routes_ref, bf16[128,2048]{1,0:T(8,128)(2,1)S(1)} %copy-done.14), custom_call_target="tpu_custom_call" | custom-call | flops 201326592 | bytes 2294784 | tf_op jit(solution)/shard_map/pallas_call | solution.py:158
  4.7 0.0 copy-start.2
  4.7 8.9 %all-to-all-start = ((bf16[16,24,2048]{2,1,0:T(8,128)(2,1)}), bf16[16,24,2048]{2,1,0:T(8,128)(2,1)}, u32[]{:S(2)}, u32[]{:S(2)}) async-start(bf16[16,24,2048]{2,1,0:T(8,128)(2,1)} %bitcast), calls=%async_computation | async-start | bytes 3145728 | tf_op jit(solution)/shard_map/all_to_all | solution.py:200
  13.6 0.2 collective-permute-start
  13.8 0.0 collective-permute-start.1
  13.8 0.8 collective-permute-start.4
  14.6 33.0 %collective-permute-done.refs_1_._.refs_5_ = bf16[2048,384]{1,0:T(8,128)(2,1)S(1)} collective-permute-done((bf16[2048,384]{1,0:T(8,128)(2,1)}, bf16[2048,384]{1,0:T(8,128)(2,1)S(1)}, u32[]{:S(2)}, u32[]{:S(2)}) %collective-permute-start) | collective-permute-done | bytes 1572896 | tf_op jit(solution)/shard_map/ppermute | solution.py:192
  47.7 0.0 copy-done.2
  47.7 0.6 shard_map.97
  48.3 0.0 copy-start.1
  48.3 1.1 copy-done.1
  49.4 0.0 all-to-all-done
  49.4 6.9 %all-to-all-start.2 = ((bf16[16,24,2048]{2,1,0:T(8,128)(2,1)}), bf16[16,24,2048]{2,1,0:T(8,128)(2,1)S(1)}, u32[]{:S(2)}, u32[]{:S(2)}) async-start(bf16[16,24,2048]{2,1,0:T(8,128)(2,1)} %bitcast.14), calls=%async_computation.2 | async-start | bytes 3145728 | tf_op jit(solution)/shard_map/all_to_all | solution.py:200
  56.3 0.0 collective-permute-start.2
  56.3 19.6 %collective-permute-done.1.refs_2_.refs_7_ = bf16[2048,384]{1,0:T(8,128)(2,1)} collective-permute-done((bf16[2048,384]{1,0:T(8,128)(2,1)}, bf16[2048,384]{1,0:T(8,128)(2,1)}, u32[]{:S(2)}, u32[]{:S(2)}) %collective-permute-start.1) | collective-permute-done | bytes 1572896 | tf_op jit(solution)/shard_map/ppermute | solution.py:192
  75.9 0.0 collective-permute-start.3
  75.9 21.2 %collective-permute-done.4.refs_5_.refs_1_ = bf16[384,2048]{1,0:T(8,128)(2,1)} collective-permute-done((bf16[384,2048]{1,0:T(8,128)(2,1)}, bf16[384,2048]{1,0:T(8,128)(2,1)}, u32[]{:S(2)}, u32[]{:S(2)}) %collective-permute-start.4) | collective-permute-done | bytes 1572896 | tf_op jit(solution)/shard_map/ppermute | solution.py:192
  97.2 0.3 collective-permute-start.5
  97.5 0.0 collective-permute-done.2.refs_3_.refs_6_
  97.5 0.0 collective-permute-done.3.refs_4_.refs_8_
  97.5 3.3 %collective-permute-done.5.refs_6_.refs_2_ = bf16[384,2048]{1,0:T(8,128)(2,1)S(1)} collective-permute-done((bf16[384,2048]{1,0:T(8,128)(2,1)}, bf16[384,2048]{1,0:T(8,128)(2,1)S(1)}, u32[]{:S(2)}, u32[]{:S(2)}) %collective-permute-start.5) | collective-permute-done | bytes 1572896 | tf_op jit(solution)/shard_map/ppermute | solution.py:196
  100.8 0.0 copy-start.7
  100.8 1.2 copy-done.7
  102.0 8.5 %shard_map.95 = (bf16[384,2048]{1,0:T(8,128)(2,1)S(1)}, f32[2,384,384]{2,1,0:T(8,128)S(1)}, f32[2,384,384]{2,1,0:T(8,128)S(1)}) custom-call(bf16[384,2048]{1,0:T(8,128)(2,1)} %bitcast.1.refs_0_, bf16[2048,384]{1,0:T(8,128)(2,1)S(1)} %collective-permute-done.refs_1_._.refs_5_, bf16[2048,384]{1,0:T(8,128)(2,1)} %collective-permute-done.1.refs_2_.refs_7_, ...), custom_call_target="tpu_custom_call" | custom-call | flops 3623878656 | bytes 14942208 | tf_op jit(solution)/shard_map/pallas_call | solution.py:158
  110.5 0.0 copy-start.4
  110.5 1.2 copy-done.4
  111.7 0.0 copy-start.6
  111.7 1.2 copy-done.6
  112.9 0.0 copy-start.9
  112.9 1.2 copy-done.9
  114.1 0.0 copy-start.10
  114.1 1.0 copy-done.10
  115.1 0.0 copy-start.12
  115.1 1.1 copy-done.12
  116.2 0.0 all-to-all-done.2
  116.2 7.6 %all-to-all-start.1 = ((bf16[16,24,2048]{2,1,0:T(8,128)(2,1)}), bf16[16,24,2048]{2,1,0:T(8,128)(2,1)}, u32[]{:S(2)}, u32[]{:S(2)}) async-start(bf16[16,24,2048]{2,1,0:T(8,128)(2,1)} %bitcast.15), calls=%async_computation.1 | async-start | bytes 3145728 | tf_op jit(solution)/shard_map/all_to_all | solution.py:200
  123.8 0.0 copy-start.5
  123.8 1.4 copy-done.5
  125.2 0.0 copy-start.8
  125.2 1.4 copy-done.8
  126.6 0.0 copy-start.11
  126.6 1.3 copy-done.11
  127.8 0.0 copy-start.13
  127.8 1.3 copy-done.13
  129.1 7.7 %shard_map.98 = bf16[384,2048]{1,0:T(8,128)(2,1)S(1)} custom-call(bf16[384,2048]{1,0:T(8,128)(2,1)S(1)} %bitcast.11, bf16[384,2048]{1,0:T(8,128)(2,1)} %collective-permute-done.4.refs_5_.refs_1_, bf16[384,2048]{1,0:T(8,128)(2,1)S(1)} %copy-done.8, f32[2,384,384]{2,1,0:T(8,128)S(1)} %copy-done.11, f32[2,384,384]{2,1,0:T(8,128)S(1)} %copy-done.13, ...), custom_call_target="tpu_custom_call" | custom-call | flops 3623878656 | bytes 14942208 | tf_op jit(solution)/shard_map/pallas_call | solution.py:158
  136.8 0.0 copy-start
  136.8 1.2 copy-done
  138.0 18.3 %all-to-all-done.1 = bf16[16,24,2048]{2,1,0:T(8,128)(2,1)} async-done(((bf16[16,24,2048]{2,1,0:T(8,128)(2,1)}), bf16[16,24,2048]{2,1,0:T(8,128)(2,1)}, u32[]{:S(2)}, u32[]{:S(2)}) %all-to-all-start.1) | async-done | bytes 1572896 | tf_op jit(solution)/shard_map/all_to_all | solution.py:200
  156.3 0.0 copy-start.15
  156.3 0.0 copy-start.3
  156.3 9.8 %all-to-all-start.3 = ((bf16[16,24,2048]{2,1,0:T(8,128)(2,1)}), bf16[16,24,2048]{2,1,0:T(8,128)(2,1)S(1)}, u32[]{:S(2)}, u32[]{:S(2)}) async-start(bf16[16,24,2048]{2,1,0:T(8,128)(2,1)} %bitcast.12), calls=%async_computation.3 | async-start | bytes 3145728 | tf_op jit(solution)/shard_map/all_to_all | solution.py:200
  166.1 0.0 copy-done.15
  166.1 0.1 copy.11.gates_ref
  166.2 0.0 copy-done.3
  166.2 3.1 %shard_map.96 = (bf16[128,2048]{1,0:T(8,128)(2,1)}, f32[128,2]{1,0:T(8,128)S(1)}) custom-call(bf16[256,384]{1,0:T(8,128)(2,1)S(1)} %get-tuple-element.10.place_ref, f32[128,2]{1,0:T(8,128)S(1)} %copy.11.gates_ref, bf16[128,2048]{1,0:T(8,128)(2,1)S(1)} %copy-done.3, bf16[384,2048]{1,0:T(8,128)(2,1)} %bitcast.6.slots_ref), custom_call_target="tpu_custom_call" | custom-call | flops 402653184 | bytes 2820096 | tf_op jit(solution)/shard_map/pallas_call | solution.py:158
  169.3 0.6 copy.13
  169.9 27.1 %all-to-all-done.3 = bf16[16,24,2048]{2,1,0:T(8,128)(2,1)S(1)} async-done(((bf16[16,24,2048]{2,1,0:T(8,128)(2,1)}), bf16[16,24,2048]{2,1,0:T(8,128)(2,1)S(1)}, u32[]{:S(2)}, u32[]{:S(2)}) %all-to-all-start.3) | async-done | bytes 1572896 | tf_op jit(solution)/shard_map/all_to_all | solution.py:200
  197.1 1.5 shard_map.99
Async XLA Ops:
  1.4 1.0 copy-start.14
  4.7 43.0 %copy-start.2 = (bf16[128,2048]{1,0:T(8,128)(2,1)S(1)}, bf16[128,2048]{1,0:T(8,128)(2,1)}, u32[]{:S(2)}) copy-start(bf16[128,2048]{1,0:T(8,128)(2,1)} %rows_ref.1) | copy-start | bytes 1572868
  4.7 44.7 %all-to-all-start = ((bf16[16,24,2048]{2,1,0:T(8,128)(2,1)}), bf16[16,24,2048]{2,1,0:T(8,128)(2,1)}, u32[]{:S(2)}, u32[]{:S(2)}) async-start(bf16[16,24,2048]{2,1,0:T(8,128)(2,1)} %bitcast), calls=%async_computation | async-start | bytes 3145728 | tf_op jit(solution)/shard_map/all_to_all | solution.py:200
  13.6 34.0 %collective-permute-start = (bf16[2048,384]{1,0:T(8,128)(2,1)}, bf16[2048,384]{1,0:T(8,128)(2,1)S(1)}, u32[]{:S(2)}, u32[]{:S(2)}) collective-permute-start(bf16[2048,384]{1,0:T(8,128)(2,1)} %bitcast.16), channel_id=1, source_target_pairs={{0,16},{1,0},{2,18},{3,2},{4,20},{5,4},{6,22},{7,6},{8,24},{9,8},{... | collective-permute-start | bytes 4718600 | tf_op jit(solution)/shard_map/ppermute | solution.py:192
  13.8 62.2 %collective-permute-start.1 = (bf16[2048,384]{1,0:T(8,128)(2,1)}, bf16[2048,384]{1,0:T(8,128)(2,1)}, u32[]{:S(2)}, u32[]{:S(2)}) collective-permute-start(bf16[2048,384]{1,0:T(8,128)(2,1)} %bitcast.17), channel_id=1, source_target_pairs={{0,16},{1,0},{2,18},{3,2},{4,20},{5,4},{6,22},{7,6},{8,24},{9,8},{... | collective-permute-start | bytes 4718600 | tf_op jit(solution)/shard_map/ppermute | solution.py:192
  13.8 83.3 %collective-permute-start.4 = (bf16[384,2048]{1,0:T(8,128)(2,1)}, bf16[384,2048]{1,0:T(8,128)(2,1)}, u32[]{:S(2)}, u32[]{:S(2)}) collective-permute-start(bf16[384,2048]{1,0:T(8,128)(2,1)} %bitcast.18), channel_id=1, source_target_pairs={{0,16},{1,0},{2,18},{3,2},{4,20},{5,4},{6,22},{7,6},{8,24},{9,8},{... | collective-permute-start | bytes 4718600 | tf_op jit(solution)/shard_map/ppermute | solution.py:192
  48.3 1.1 copy-start.1
  49.4 66.8 %all-to-all-start.2 = ((bf16[16,24,2048]{2,1,0:T(8,128)(2,1)}), bf16[16,24,2048]{2,1,0:T(8,128)(2,1)S(1)}, u32[]{:S(2)}, u32[]{:S(2)}) async-start(bf16[16,24,2048]{2,1,0:T(8,128)(2,1)} %bitcast.14), calls=%async_computation.2 | async-start | bytes 3145728 | tf_op jit(solution)/shard_map/all_to_all | solution.py:200
  56.3 41.1 %collective-permute-start.2 = (bf16[2048,384]{1,0:T(8,128)(2,1)S(1)}, bf16[2048,384]{1,0:T(8,128)(2,1)S(1)}, u32[]{:S(2)}, u32[]{:S(2)}) collective-permute-start(bf16[2048,384]{1,0:T(8,128)(2,1)S(1)} %collective-permute-done.refs_1_._.refs_5_), channel_id=1, source_target_pairs={{0,1},{1,0},{2,3},{3,2},{4,5},{5,4},{6,7},{7,6},{8,9},{9,8},{10,11... | collective-permute-start | bytes 4718600 | tf_op jit(solution)/shard_map/ppermute | solution.py:196
  75.9 21.6 %collective-permute-start.3 = (bf16[2048,384]{1,0:T(8,128)(2,1)}, bf16[2048,384]{1,0:T(8,128)(2,1)S(1)}, u32[]{:S(2)}, u32[]{:S(2)}) collective-permute-start(bf16[2048,384]{1,0:T(8,128)(2,1)} %collective-permute-done.1.refs_2_.refs_7_), channel_id=1, source_target_pairs={{0,1},{1,0},{2,3},{3,2},{4,5},{5,4},{6,7},{7,6},{8,9},{9,8},{10,11... | collective-permute-start | bytes 4718600 | tf_op jit(solution)/shard_map/ppermute | solution.py:196
  97.2 3.6 %collective-permute-start.5 = (bf16[384,2048]{1,0:T(8,128)(2,1)}, bf16[384,2048]{1,0:T(8,128)(2,1)S(1)}, u32[]{:S(2)}, u32[]{:S(2)}) collective-permute-start(bf16[384,2048]{1,0:T(8,128)(2,1)} %collective-permute-done.4.refs_5_.refs_1_), channel_id=1, source_target_pairs={{0,1},{1,0},{2,3},{3,2},{4,5},{5,4},{6,7},{7,6},{8,9},{9,8},{10,11... | collective-permute-start | bytes 4718600 | tf_op jit(solution)/shard_map/ppermute | solution.py:196
  100.8 1.2 copy-start.7
  110.5 1.2 copy-start.4
  111.7 1.2 copy-start.6
  112.9 1.2 copy-start.9
  114.1 1.0 copy-start.10
  115.1 1.1 copy-start.12
  116.2 40.1 %all-to-all-start.1 = ((bf16[16,24,2048]{2,1,0:T(8,128)(2,1)}), bf16[16,24,2048]{2,1,0:T(8,128)(2,1)}, u32[]{:S(2)}, u32[]{:S(2)}) async-start(bf16[16,24,2048]{2,1,0:T(8,128)(2,1)} %bitcast.15), calls=%async_computation.1 | async-start | bytes 3145728 | tf_op jit(solution)/shard_map/all_to_all | solution.py:200
  123.8 1.4 copy-start.5
  125.2 1.4 copy-start.8
  126.6 1.3 copy-start.11
  127.8 1.3 copy-start.13
  136.8 1.2 copy-start
  156.3 9.8 %copy-start.15 = (f32[128,2]{0,1:T(2,128)S(1)}, f32[128,2]{0,1:T(2,128)}, u32[]{:S(2)}) copy-start(f32[128,2]{0,1:T(2,128)} %param.10) | copy-start | bytes 3076
  156.3 9.9 %copy-start.3 = (bf16[128,2048]{1,0:T(8,128)(2,1)S(1)}, bf16[128,2048]{1,0:T(8,128)(2,1)}, u32[]{:S(2)}) copy-start(bf16[128,2048]{1,0:T(8,128)(2,1)} %rows_ref.1) | copy-start | bytes 1572868
  156.3 40.8 %all-to-all-start.3 = ((bf16[16,24,2048]{2,1,0:T(8,128)(2,1)}), bf16[16,24,2048]{2,1,0:T(8,128)(2,1)S(1)}, u32[]{:S(2)}, u32[]{:S(2)}) async-start(bf16[16,24,2048]{2,1,0:T(8,128)(2,1)} %bitcast.12), calls=%async_computation.3 | async-start | bytes 3145728 | tf_op jit(solution)/shard_map/all_to_all | solution.py:200

commit v6 on v5

--- a/solution.py
+++ b/solution.py
@@ -9,7 +9,7 @@
 
 BF16 = jnp.bfloat16
 F32 = jnp.float32
-VMEM_BYTES = 40 << 20
+VMEM_BYTES = 60 << 20
 
 
 def dot(a, b, dims):
@@ -222,7 +222,7 @@
     )(routes, tokens)
     x_rows = exchange(x_slots)
     (dy_slots,) = call(
-        functools.partial(spread_kernel, top_count), [slot_shape], spread_flops, far=(2,)
+        functools.partial(spread_kernel, top_count), [slot_shape], 256 * spread_flops, far=(2,)
     )(place, cotangent, gate_w[0])
     dy_rows = exchange(dy_slots)
     out_rows, by_gate, by_up = call(

time: 202 us -> 192 us (0.950)
  waiting for transfers between devices: 123 us -> 107 us
  Pallas kernels: 23.6 us -> 30.5 us
  local copies, waits for them, and re-layouts: 17.1 us -> 13.1 us
  starting transfers between devices: 34.6 us -> 37.7 us
    ppermute x3, waiting for transfers between devices: 73.8 us -> 40.4 us  [whole_expert(): own = lax.ppermute(weight[0], axes, swap)]
    all_to_all x4, waiting for transfers between devices: 45.4 us -> 65 us  [exchange(): lax.all_to_all(rows.reshape(experts, capacity, width), axes, 0, 0, axis_i...]
    pallas_call x6, Pallas kernels: 23.6 us -> 30.5 us  [run(): pl.pallas_call(kernel, out_shape=tuple(outs), in_specs=[pl.BlockSpec(memo...]
    unnamed x35 -> x23, local copies, waits for them, and re-layouts: 17.1 us -> 13.1 us
    ppermute x3, starting transfers between devices: 1.01 us -> 3.14 us  [whole_expert(): own = lax.ppermute(weight[0], axes, swap)]
    ppermute x3, waiting for transfers between devices: 3.3 us -> 1.2 us  [whole_expert(): shares.append(lax.ppermute(own, 'expert', turn))]
  transfers between devices with their start and end apart: 10 -> 10, of which waited for: 6 -> 6; matrix products, arithmetic and copies ran while one was open for 0% -> 2% of each run, Pallas kernels for 10% -> 15%
where the time goes in v6:
time: 192 us; the launch traced here: 189 us
  waiting for transfers between devices  107 us (56%)
  starting transfers between devices  37.7 us (20%)
  Pallas kernels  30.5 us (16%)
  local copies, waits for them, and re-layouts  13.1 us (7%)
    all_to_all x4, waiting for transfers between devices, exchange(): lax.all_to_all(rows.reshape(experts, capacity, width), axes, 0, 0, axis_i...  65 us
    ppermute x3, waiting for transfers between devices, whole_expert(): own = lax.ppermute(weight[0], axes, swap)  40.4 us
    all_to_all x4, starting transfers between devices, exchange(): lax.all_to_all(rows.reshape(experts, capacity, width), axes, 0, 0, axis_i...  33.9 us
    pallas_call x6, Pallas kernels, run(): pl.pallas_call(kernel, out_shape=tuple(outs), in_specs=[pl.BlockSpec(memo...  30.5 us
    unnamed x23, local copies, waits for them, and re-layouts  13.1 us
  transfers between devices with their start and end apart: 10, of which 6 were waited for; matrix products, arithmetic and copies ran while one was open for 2% of the time, Pallas kernels for 15%

profile of v6, /device:TPU:0, one launch (start us, length us, event | category | flops | bytes accessed | tf_op | source)
XLA Modules:
  0.0 188.6 jit_solution(5607734693988185785)
XLA Ops:
  0.6 3.0 %collective-permute-start = (bf16[2048,384]{1,0:T(8,128)(2,1)}, bf16[2048,384]{1,0:T(8,128)(2,1)S(1)}, u32[]{:S(2)}, u32[]{:S(2)}) collective-permute-start(bf16[2048,384]{1,0:T(8,128)(2,1)} %bitcast.19), channel_id=1, source_target_pairs={{0,16},{1,0},{2,18},{3,2},{4,20},{5,4},{6,22},{7,6},{8,24},{9,8},{... | collective-permute-start | bytes 4718600 | tf_op jit(solution)/shard_map/ppermute | solution.py:192
  3.6 1.4 copy.10.routes_ref
  5.0 3.3 %shard_map.94 = (bf16[384,2048]{1,0:T(8,128)(2,1)}, bf16[256,384]{1,0:T(8,128)(2,1)}) custom-call(s32[128,2]{1,0:T(8,128)} %copy.10.routes_ref, bf16[128,2048]{1,0:T(8,128)(2,1)} %tokens_ref.1), custom_call_target="tpu_custom_call" | custom-call | flops 201326592 | bytes 2294784 | tf_op jit(solution)/shard_map/pallas_call | solution.py:158
  8.3 7.3 %all-to-all-start = ((bf16[16,24,2048]{2,1,0:T(8,128)(2,1)}), bf16[16,24,2048]{2,1,0:T(8,128)(2,1)S(1)}, u32[]{:S(2)}, u32[]{:S(2)}) async-start(bf16[16,24,2048]{2,1,0:T(8,128)(2,1)} %bitcast.18), calls=%async_computation | async-start | bytes 3145728 | tf_op jit(solution)/shard_map/all_to_all | solution.py:200
  15.6 0.1 collective-permute-start.1
  15.7 0.0 collective-permute-start.4
  15.8 10.5 %collective-permute-done.refs_1_._.refs_5_ = bf16[2048,384]{1,0:T(8,128)(2,1)S(1)} collective-permute-done((bf16[2048,384]{1,0:T(8,128)(2,1)}, bf16[2048,384]{1,0:T(8,128)(2,1)S(1)}, u32[]{:S(2)}, u32[]{:S(2)}) %collective-permute-start) | collective-permute-done | bytes 1572896 | tf_op jit(solution)/shard_map/ppermute | solution.py:192
  26.3 0.0 copy-start.3
  26.3 1.2 copy-done.3
  27.5 2.9 %shard_map.97 = bf16[384,2048]{1,0:T(8,128)(2,1)} custom-call(bf16[256,384]{1,0:T(8,128)(2,1)} %get-tuple-element.10.place_ref, bf16[128,2048]{1,0:T(8,128)(2,1)} %rows_ref.1, bf16[2048,384]{1,0:T(8,128)(2,1)} %copy-done.3), custom_call_target="tpu_custom_call" | custom-call | flops 51539607552 | bytes 3866624 | tf_op jit(solution)/shard_map/pallas_call | solution.py:158
  30.4 16.5 %all-to-all-done = bf16[16,24,2048]{2,1,0:T(8,128)(2,1)S(1)} async-done(((bf16[16,24,2048]{2,1,0:T(8,128)(2,1)}), bf16[16,24,2048]{2,1,0:T(8,128)(2,1)S(1)}, u32[]{:S(2)}, u32[]{:S(2)}) %all-to-all-start) | async-done | bytes 1572896 | tf_op jit(solution)/shard_map/all_to_all | solution.py:200
  46.9 0.0 copy-start.8
  46.9 0.0 copy-start.4
  46.9 1.2 copy-done.8
  48.1 9.7 %all-to-all-start.2 = ((bf16[16,24,2048]{2,1,0:T(8,128)(2,1)}), bf16[16,24,2048]{2,1,0:T(8,128)(2,1)S(1)}, u32[]{:S(2)}, u32[]{:S(2)}) async-start(bf16[16,24,2048]{2,1,0:T(8,128)(2,1)} %bitcast.16), calls=%async_computation.2 | async-start | bytes 3145728 | tf_op jit(solution)/shard_map/all_to_all | solution.py:200
  57.8 0.0 copy-done.4
  57.8 0.1 collective-permute-start.2
  57.9 0.0 collective-permute-done.1.refs_2_.refs_7_
  57.9 0.5 collective-permute-start.3
  58.4 29.9 %collective-permute-done.4.refs_5_.refs_1_ = bf16[384,2048]{1,0:T(8,128)(2,1)} collective-permute-done((bf16[384,2048]{1,0:T(8,128)(2,1)}, bf16[384,2048]{1,0:T(8,128)(2,1)}, u32[]{:S(2)}, u32[]{:S(2)}) %collective-permute-start.4) | collective-permute-done | bytes 1572896 | tf_op jit(solution)/shard_map/ppermute | solution.py:192
  88.2 0.0 collective-permute-start.5
  88.2 0.0 collective-permute-done.2.refs_3_.refs_6_
  88.2 0.0 copy-start.5
  88.2 1.3 copy-done.5
  89.5 0.0 collective-permute-done.3.refs_4_.refs_8_
  89.5 0.0 copy-start.6
  89.5 1.2 copy-done.6
  90.7 1.2 collective-permute-done.5.refs_6_.refs_2_
  91.8 0.0 copy-start.7
  91.8 1.2 copy-done.7
  93.0 8.6 %shard_map.95 = (bf16[384,2048]{1,0:T(8,128)(2,1)}, f32[2,384,384]{2,1,0:T(8,128)}, f32[2,384,384]{2,1,0:T(8,128)}) custom-call(bf16[384,2048]{1,0:T(8,128)(2,1)} %bitcast.15, bf16[2048,384]{1,0:T(8,128)(2,1)} %copy-done.3, bf16[2048,384]{1,0:T(8,128)(2,1)} %collective-permute-done.1.refs_2_.refs_7_, bf16[2048,384]{1,0:T(8,128)(2,1)} %copy-done.5, ...), custom_call_target="tpu_custom_call" | custom-call | flops 3623878656 | bytes 14942208 | tf_op jit(solution)/shard_map/pallas_call | solution.py:158
  101.6 0.0 all-to-all-done.2
  101.7 0.0 copy-start
  101.7 1.2 copy-done
  102.8 7.3 %all-to-all-start.1 = ((bf16[16,24,2048]{2,1,0:T(8,128)(2,1)}), bf16[16,24,2048]{2,1,0:T(8,128)(2,1)S(1)}, u32[]{:S(2)}, u32[]{:S(2)}) async-start(bf16[16,24,2048]{2,1,0:T(8,128)(2,1)} %bitcast.17), calls=%async_computation.1 | async-start | bytes 3145728 | tf_op jit(solution)/shard_map/all_to_all | solution.py:200
  110.1 9.2 %shard_map.98 = bf16[384,2048]{1,0:T(8,128)(2,1)} custom-call(bf16[384,2048]{1,0:T(8,128)(2,1)} %bitcast.11, bf16[384,2048]{1,0:T(8,128)(2,1)} %collective-permute-done.4.refs_5_.refs_1_, bf16[384,2048]{1,0:T(8,128)(2,1)} %copy-done.7, f32[2,384,384]{2,1,0:T(8,128)} %get-tuple-element.14.refs_3_, f32[2,384,384]{2,1,0:T(8,128)} %get-tuple-element.15.refs_4_, ...), custom_call_target="tpu_custom_call" | custom-call | flops 3623878656 | bytes 14942208 | tf_op jit(solution)/shard_map/pallas_call | solution.py:158
  119.4 23.2 %all-to-all-done.1 = bf16[16,24,2048]{2,1,0:T(8,128)(2,1)S(1)} async-done(((bf16[16,24,2048]{2,1,0:T(8,128)(2,1)}), bf16[16,24,2048]{2,1,0:T(8,128)(2,1)S(1)}, u32[]{:S(2)}, u32[]{:S(2)}) %all-to-all-start.1) | async-done | bytes 1572896 | tf_op jit(solution)/shard_map/all_to_all | solution.py:200
  142.6 0.0 copy-start.1
  142.6 0.0 copy-start.9
  142.6 1.2 copy-done.1
  143.7 9.7 %all-to-all-start.3 = ((bf16[16,24,2048]{2,1,0:T(8,128)(2,1)}), bf16[16,24,2048]{2,1,0:T(8,128)(2,1)S(1)}, u32[]{:S(2)}, u32[]{:S(2)}) async-start(bf16[16,24,2048]{2,1,0:T(8,128)(2,1)} %bitcast.13), calls=%async_computation.3 | async-start | bytes 3145728 | tf_op jit(solution)/shard_map/all_to_all | solution.py:200
  153.4 0.0 copy-done.9
  153.4 0.7 copy.11.gates_ref
  154.2 3.4 %shard_map.96 = (bf16[128,2048]{1,0:T(8,128)(2,1)}, f32[128,2]{1,0:T(8,128)}) custom-call(bf16[256,384]{1,0:T(8,128)(2,1)} %get-tuple-element.10.place_ref, f32[128,2]{1,0:T(8,128)} %copy.11.gates_ref, bf16[128,2048]{1,0:T(8,128)(2,1)} %rows_ref.1, bf16[384,2048]{1,0:T(8,128)(2,1)} %bitcast.12), custom_call_target="tpu_custom_call" | custom-call | flops 402653184 | bytes 2820096 | tf_op jit(solution)/shard_map/pallas_call | solution.py:158
  157.6 1.5 copy.13
  159.0 25.3 %all-to-all-done.3 = bf16[16,24,2048]{2,1,0:T(8,128)(2,1)S(1)} async-done(((bf16[16,24,2048]{2,1,0:T(8,128)(2,1)}), bf16[16,24,2048]{2,1,0:T(8,128)(2,1)S(1)}, u32[]{:S(2)}, u32[]{:S(2)}) %all-to-all-start.3) | async-done | bytes 1572896 | tf_op jit(solution)/shard_map/all_to_all | solution.py:200
  184.3 0.0 copy-start.2
  184.3 1.2 copy-done.2
  185.5 3.1 %shard_map.99 = bf16[128,2048]{1,0:T(8,128)(2,1)} custom-call(bf16[256,384]{1,0:T(8,128)(2,1)} %get-tuple-element.10.place_ref, f32[128,2]{1,0:T(8,128)} %copy.11.gates_ref, bf16[384,2048]{1,0:T(8,128)(2,1)} %bitcast.14), custom_call_target="tpu_custom_call" | custom-call | flops 402653184 | bytes 2294784 | tf_op jit(solution)/shard_map/pallas_call | solution.py:158
Async XLA Ops:
  0.6 25.7 %collective-permute-start = (bf16[2048,384]{1,0:T(8,128)(2,1)}, bf16[2048,384]{1,0:T(8,128)(2,1)S(1)}, u32[]{:S(2)}, u32[]{:S(2)}) collective-permute-start(bf16[2048,384]{1,0:T(8,128)(2,1)} %bitcast.19), channel_id=1, source_target_pairs={{0,16},{1,0},{2,18},{3,2},{4,20},{5,4},{6,22},{7,6},{8,24},{9,8},{... | collective-permute-start | bytes 4718600 | tf_op jit(solution)/shard_map/ppermute | solution.py:192
  8.3 38.6 %all-to-all-start = ((bf16[16,24,2048]{2,1,0:T(8,128)(2,1)}), bf16[16,24,2048]{2,1,0:T(8,128)(2,1)S(1)}, u32[]{:S(2)}, u32[]{:S(2)}) async-start(bf16[16,24,2048]{2,1,0:T(8,128)(2,1)} %bitcast.18), calls=%async_computation | async-start | bytes 3145728 | tf_op jit(solution)/shard_map/all_to_all | solution.py:200
  15.6 42.3 %collective-permute-start.1 = (bf16[2048,384]{1,0:T(8,128)(2,1)}, bf16[2048,384]{1,0:T(8,128)(2,1)}, u32[]{:S(2)}, u32[]{:S(2)}) collective-permute-start(bf16[2048,384]{1,0:T(8,128)(2,1)} %bitcast.20), channel_id=1, source_target_pairs={{0,16},{1,0},{2,18},{3,2},{4,20},{5,4},{6,22},{7,6},{8,24},{9,8},{... | collective-permute-start | bytes 4718600 | tf_op jit(solution)/shard_map/ppermute | solution.py:192
  15.7 72.5 %collective-permute-start.4 = (bf16[384,2048]{1,0:T(8,128)(2,1)}, bf16[384,2048]{1,0:T(8,128)(2,1)}, u32[]{:S(2)}, u32[]{:S(2)}) collective-permute-start(bf16[384,2048]{1,0:T(8,128)(2,1)} %bitcast.21), channel_id=1, source_target_pairs={{0,16},{1,0},{2,18},{3,2},{4,20},{5,4},{6,22},{7,6},{8,24},{9,8},{... | collective-permute-start | bytes 4718600 | tf_op jit(solution)/shard_map/ppermute | solution.py:192
  26.3 1.2 copy-start.3
  46.9 1.2 copy-start.8
  46.9 10.9 %copy-start.4 = (bf16[2048,384]{1,0:T(8,128)(2,1)S(1)}, bf16[2048,384]{1,0:T(8,128)(2,1)}, u32[]{:S(2)}) copy-start(bf16[2048,384]{1,0:T(8,128)(2,1)} %copy-done.3) | copy-start | bytes 4718596
  48.1 53.6 %all-to-all-start.2 = ((bf16[16,24,2048]{2,1,0:T(8,128)(2,1)}), bf16[16,24,2048]{2,1,0:T(8,128)(2,1)S(1)}, u32[]{:S(2)}, u32[]{:S(2)}) async-start(bf16[16,24,2048]{2,1,0:T(8,128)(2,1)} %bitcast.16), calls=%async_computation.2 | async-start | bytes 3145728 | tf_op jit(solution)/shard_map/all_to_all | solution.py:200
  57.8 30.4 %collective-permute-start.2 = (bf16[2048,384]{1,0:T(8,128)(2,1)S(1)}, bf16[2048,384]{1,0:T(8,128)(2,1)S(1)}, u32[]{:S(2)}, u32[]{:S(2)}) collective-permute-start(bf16[2048,384]{1,0:T(8,128)(2,1)S(1)} %copy-done.4), channel_id=1, source_target_pairs={{0,1},{1,0},{2,3},{3,2},{4,5},{5,4},{6,7},{7,6},{8,9},{9,8},{10,11... | collective-permute-start | bytes 4718600 | tf_op jit(solution)/shard_map/ppermute | solution.py:196
  57.9 31.6 %collective-permute-start.3 = (bf16[2048,384]{1,0:T(8,128)(2,1)}, bf16[2048,384]{1,0:T(8,128)(2,1)S(1)}, u32[]{:S(2)}, u32[]{:S(2)}) collective-permute-start(bf16[2048,384]{1,0:T(8,128)(2,1)} %collective-permute-done.1.refs_2_.refs_7_), channel_id=1, source_target_pairs={{0,1},{1,0},{2,3},{3,2},{4,5},{5,4},{6,7},{7,6},{8,9},{9,8},{10,11... | collective-permute-start | bytes 4718600 | tf_op jit(solution)/shard_map/ppermute | solution.py:196
  88.2 3.6 %collective-permute-start.5 = (bf16[384,2048]{1,0:T(8,128)(2,1)}, bf16[384,2048]{1,0:T(8,128)(2,1)S(1)}, u32[]{:S(2)}, u32[]{:S(2)}) collective-permute-start(bf16[384,2048]{1,0:T(8,128)(2,1)} %collective-permute-done.4.refs_5_.refs_1_), channel_id=1, source_target_pairs={{0,1},{1,0},{2,3},{3,2},{4,5},{5,4},{6,7},{7,6},{8,9},{9,8},{10,11... | collective-permute-start | bytes 4718600 | tf_op jit(solution)/shard_map/ppermute | solution.py:196
  88.2 1.3 copy-start.5
  89.5 1.2 copy-start.6
  91.8 1.2 copy-start.7
  101.7 1.2 copy-start
  102.8 39.7 %all-to-all-start.1 = ((bf16[16,24,2048]{2,1,0:T(8,128)(2,1)}), bf16[16,24,2048]{2,1,0:T(8,128)(2,1)S(1)}, u32[]{:S(2)}, u32[]{:S(2)}) async-start(bf16[16,24,2048]{2,1,0:T(8,128)(2,1)} %bitcast.17), calls=%async_computation.1 | async-start | bytes 3145728 | tf_op jit(solution)/shard_map/all_to_all | solution.py:200
  142.6 1.2 copy-start.1
  142.6 10.9 %copy-start.9 = (f32[128,2]{0,1:T(2,128)S(1)}, f32[128,2]{0,1:T(2,128)}, u32[]{:S(2)}) copy-start(f32[128,2]{0,1:T(2,128)} %param.10) | copy-start | bytes 3076
  143.7 40.6 %all-to-all-start.3 = ((bf16[16,24,2048]{2,1,0:T(8,128)(2,1)}), bf16[16,24,2048]{2,1,0:T(8,128)(2,1)S(1)}, u32[]{:S(2)}, u32[]{:S(2)}) async-start(bf16[16,24,2048]{2,1,0:T(8,128)(2,1)} %bitcast.13), calls=%async_computation.3 | async-start | bytes 3145728 | tf_op jit(solution)/shard_map/all_to_all | solution.py:200
  184.3 1.2 copy-start.2

commit v7 on v6

--- a/solution.py
+++ b/solution.py
@@ -9,7 +9,7 @@
 
 BF16 = jnp.bfloat16
 F32 = jnp.float32
-VMEM_BYTES = 60 << 20
+VMEM_BYTES = 28 << 20
 
 
 def dot(a, b, dims):
@@ -34,10 +34,14 @@
     return copy
 
 
-def place_kernel(experts, routes_ref, tokens_ref, slots_ref, place_ref):
+def place_kernel(experts, parts, plane_ref, routes_ref, tokens_ref, slots_ref, place_ref, near_ref):
     slots, width = slots_ref.shape
+    capacity = slots // experts
     tok_rows, top_count = routes_ref.shape
     routes = routes_ref[...]
+    home_plane, home_set = lax.rem(routes + 1, parts), lax.div(routes, parts)
+    lanes = home_plane * (experts // parts) + home_set
+    near_lanes = home_set * parts + lax.rem(home_plane + (parts - plane_ref[0]), parts)
     numbers = lax.broadcasted_iota(jnp.int32, (tok_rows, experts), 1)
     named = [numbers == routes[:, k : k + 1] for k in range(top_count)]
     chosen = sum(n.astype(F32) for n in named)
@@ -47,39 +51,37 @@
     ).astype(F32)
     rank = dot(earlier.astype(BF16), chosen.astype(BF16), (1, 0))
     slot_numbers = lax.broadcasted_iota(jnp.int32, (tok_rows, slots), 1)
-    total = None
+    total, near = None, None
     for k in range(top_count):
-        own = jnp.sum(jnp.where(named[k], rank, 0.0), axis=1, keepdims=True)
-        slot = routes[:, k : k + 1] * (slots // experts) + own.astype(jnp.int32)
-        mark = (slot_numbers == slot).astype(F32)
+        own = jnp.sum(jnp.where(named[k], rank, 0.0), axis=1, keepdims=True).astype(jnp.int32)
+        mark, near_mark = (
+            (slot_numbers == order[:, k : k + 1] * capacity + own).astype(F32)
+            for order in (lanes, near_lanes)
+        )
         place_ref[k * tok_rows : (k + 1) * tok_rows, :] = mark.astype(BF16)
         total = mark if total is None else total + mark
+        near = near_mark if near is None else near + near_mark
+    near_ref[...] = near.astype(BF16)
     total = total.astype(BF16)
     for columns in tiles(width):
         slots_ref[:, columns] = dot(total, tokens_ref[:, columns], (0, 0)).astype(BF16)
 
 
-def spread_kernel(top_count, place_ref, rows_ref, _, slots_ref):
-    tok_rows = rows_ref.shape[0]
-    total = sum(
-        place_ref[k * tok_rows : (k + 1) * tok_rows, :].astype(F32) for k in range(top_count)
-    ).astype(BF16)
+def spread_kernel(near_ref, rows_ref, _, slots_ref):
     for columns in tiles(rows_ref.shape[1]):
-        slots_ref[:, columns] = dot(total, rows_ref[:, columns], (0, 0)).astype(BF16)
-
-
-def forward_kernel(parts, *refs):
-    sources, refs = refs[: 1 + 3 * parts], refs[1 + 3 * parts :]
+        slots_ref[:, columns] = dot(near_ref[...], rows_ref[:, columns], (0, 0)).astype(BF16)
+
+
+def forward_kernel(parts, rows_ref, *refs):
+    sources, refs = refs[: 3 * parts], refs[3 * parts :]
     out_ref, by_gate_ref, by_up_ref, sems, out_sems = refs[:5]
-    stage_ref, by_gate_stage, by_up_stage, hidden_ref, *targets = refs[5:]
-    copies = fetch(sources, targets, sems)
-    rows_ref, weights = targets[0], targets[1:]
+    stage_ref, by_gate_stage, by_up_stage, hidden_ref, *weights = refs[5:]
+    copies = fetch(sources, weights, sems)
     sent = []
-    copies[0].wait()
     for i in range(parts):
+        copies[2 * i].wait()
+        pre_gate = dot(rows_ref[...], weights[2 * i][...], (1, 0))
         copies[1 + 2 * i].wait()
-        pre_gate = dot(rows_ref[...], weights[2 * i][...], (1, 0))
-        copies[2 + 2 * i].wait()
         pre_up = dot(rows_ref[...], weights[2 * i + 1][...], (1, 0))
         sig = jax.nn.sigmoid(pre_gate)
         act = pre_gate * sig
@@ -88,7 +90,7 @@
         by_up_stage[i] = act
     sent.append(store(by_gate_stage, by_gate_ref, out_sems.at[0]))
     sent.append(store(by_up_stage, by_up_ref, out_sems.at[1]))
-    for copy in copies[1 + 2 * parts :]:
+    for copy in copies[2 * parts :]:
         copy.wait()
     down = weights[2 * parts :]
     for columns in tiles(out_ref.shape[1]):
@@ -101,20 +103,24 @@
         copy.wait()
 
 
-def backward_kernel(parts, *refs):
-    sources, refs = refs[: 3 + 3 * parts], refs[3 + 3 * parts :]
-    out_ref, sems, out_sems, back_gate_ref, back_up_ref, stage_ref, *targets = refs
-    copies = fetch(sources, targets, sems)
-    rows_ref, targets = targets[0], targets[1:]
+def backward_kernel(parts, plane_ref, *refs):
+    sources, refs = refs[: 2 + 4 * parts], refs[2 + 4 * parts :]
+    out_ref, sems, out_sems, back_gate_ref, back_up_ref, stage_ref, rows_ref, *targets = refs
+    share = rows_ref.shape[0] // parts
+    places = [
+        rows_ref.at[pl.ds(pl.multiple_of((plane_ref[0] + parts - i) % parts * share, share), share)]
+        for i in range(parts)
+    ]
+    copies = fetch(sources, [*places, *targets], sems)
     down, (by_gate_ref, by_up_ref) = targets[:parts], targets[parts : parts + 2]
     gate, up = targets[parts + 2 : 2 * parts + 2], targets[2 * parts + 2 :]
-    for copy in copies[: 3 + parts]:
+    for copy in copies[: 2 + 2 * parts]:
         copy.wait()
     for i in range(parts):
         back_hidden = dot(rows_ref[...], down[i][...], (1, 1))
         back_gate_ref[i] = (back_hidden * by_gate_ref[i]).astype(BF16)
         back_up_ref[i] = (back_hidden * by_up_ref[i]).astype(BF16)
-    for copy in copies[3 + parts :]:
+    for copy in copies[2 + 2 * parts :]:
         copy.wait()
     sent = []
     for columns in tiles(out_ref.shape[1]):
@@ -154,13 +160,16 @@
 def call(kernel, outs, flops, scratch=(), far=(), far_out=False):
     def run(*args):
         moved = sum(a.size * a.dtype.itemsize for a in (*args, *outs))
-        spaces = [pltpu.HBM if i in far else pltpu.VMEM for i in range(len(args))]
+        spaces = [
+            pltpu.SMEM if a.shape == (1,) else pl.ANY if i in far else pltpu.VMEM
+            for i, a in enumerate(args)
+        ]
         return pl.pallas_call(
             kernel,
             out_shape=tuple(outs),
             in_specs=[pl.BlockSpec(memory_space=space) for space in spaces],
             out_specs=tuple(
-                pl.BlockSpec(memory_space=pltpu.HBM if far_out else pltpu.VMEM) for _ in outs
+                pl.BlockSpec(memory_space=pl.ANY if far_out else pltpu.VMEM) for _ in outs
             ),
             scratch_shapes=scratch,
             compiler_params=pltpu.CompilerParams(vmem_limit_bytes=VMEM_BYTES),
@@ -182,11 +191,17 @@
     def device(g, j):
         return g * experts + j
 
+    sets = experts // parts
+
     def home(e, c):
         return device((e + 1) % parts, e // parts * parts + c)
 
     swap = [(device(g, e), home(e, g)) for g in range(parts) for e in range(experts)]
-    groups = [[home(e, c) for e in range(experts)] for c in range(parts)]
+    planes = [
+        [[device(g, parts * q + c) for q in range(sets)] for g in range(parts)] for c in range(parts)
+    ]
+    everywhere = [[d for plane in planes[c] for d in plane] for c in range(parts)]
+    in_plane = [plane for c in range(parts) for plane in planes[c]]
 
     def whole_expert(weight):
         own = lax.ppermute(weight[0], axes, swap)
@@ -197,9 +212,22 @@
         return shares
 
     def exchange(rows):
+        rows = rows.reshape(experts, capacity, width)
         return lax.all_to_all(
-            rows.reshape(experts, capacity, width), axes, 0, 0, axis_index_groups=groups, tiled=True
+            rows, axes, 0, 0, axis_index_groups=everywhere, tiled=True
         ).reshape(slots, width)
+
+    def exchange_late(rows):
+        rows = rows.reshape(sets, parts * capacity, width)
+        rows = lax.all_to_all(rows, axes, 0, 0, axis_index_groups=in_plane, tiled=True)
+        rows = rows.reshape(sets, parts, capacity, width)
+        shares = []
+        for i in range(parts):
+            share = rows[:, i].reshape(sets * capacity, width)
+            if i > 0:
+                share = lax.ppermute(share, "dp", [(g, (g + i) % parts) for g in range(parts)])
+            shares.append(share)
+        return shares
 
     spread_flops = 2 * slots * tok_rows * width
     dot_flops = 2 * slots * width * hidden * parts
@@ -217,23 +245,26 @@
         return pltpu.SemaphoreType.DMA((number,))
 
     gate_w, up_w, down_w = whole_expert(w_gate), whole_expert(w_up), whole_expert(w_down)
-    x_slots, place = call(
-        functools.partial(place_kernel, experts), [slot_shape, place_shape], spread_flops
-    )(routes, tokens)
+    plane = lax.axis_index("dp").astype(jnp.int32).reshape(1)
+    x_slots, place, near = call(
+        functools.partial(place_kernel, experts, parts),
+        [slot_shape, place_shape, jax.ShapeDtypeStruct((tok_rows, slots), BF16)],
+        spread_flops,
+    )(plane, routes, tokens)
     x_rows = exchange(x_slots)
-    (dy_slots,) = call(
-        functools.partial(spread_kernel, top_count), [slot_shape], 256 * spread_flops, far=(2,)
-    )(place, cotangent, gate_w[0])
-    dy_rows = exchange(dy_slots)
+    (dy_slots,) = call(spread_kernel, [slot_shape], 256 * spread_flops, far=(2,))(
+        near, cotangent, gate_w[0]
+    )
+    dy_shares = exchange_late(dy_slots)
     out_rows, by_gate, by_up = call(
         functools.partial(forward_kernel, parts),
         [slot_shape, unit_shape, unit_shape],
         3 * dot_flops,
-        [sems(1 + 3 * parts), sems(2 + len(tiles(width))), row_scratch, unit_stage, unit_stage]
-        + [hidden_scratch, row_scratch]
+        [sems(3 * parts), sems(2 + len(tiles(width))), row_scratch, unit_stage, unit_stage]
+        + [hidden_scratch]
         + [in_scratch] * (2 * parts)
         + [down_scratch] * parts,
-        far=range(1 + 3 * parts),
+        far=range(1, 1 + 3 * parts),
         far_out=True,
     )(x_rows, *(w for pair in zip(gate_w, up_w) for w in pair), *down_w)
     out_slots = exchange(out_rows)
@@ -241,14 +272,14 @@
         functools.partial(backward_kernel, parts),
         [slot_shape],
         3 * dot_flops,
-        [sems(3 + 3 * parts), sems(len(tiles(width))), hidden_scratch, hidden_scratch]
+        [sems(2 + 4 * parts), sems(len(tiles(width))), hidden_scratch, hidden_scratch]
         + [row_scratch] * 2
         + [down_scratch] * parts
         + [unit_stage] * 2
         + [in_scratch] * (2 * parts),
-        far=range(3 + 3 * parts),
+        far=range(1, 3 + 4 * parts),
         far_out=True,
-    )(dy_rows, *down_w, by_gate, by_up, *gate_w, *up_w)
+    )(plane, *dy_shares, *down_w, by_gate, by_up, *gate_w, *up_w)
     grad_slots = exchange(grad_rows)
     mixed, gate_grad = call(
         mix_kernel, [token_shape, jax.ShapeDtypeStruct(gates.shape, F32)], 2 * spread_flops

time: 192 us -> 194 us (1.010); the launches traced: 189 us -> 194 us
  waiting for transfers between devices: 107 us -> 120 us
  Pallas kernels: 30.5 us -> 22.8 us
  starting transfers between devices: 37.7 us -> 30.6 us
  local copies, waits for them, and re-layouts: 13.1 us -> 19.6 us
    ppermute x0 -> x1, waiting for transfers between devices: none -> 32.6 us  [exchange_late(): lax.ppermute(share, 'dp', [(g, (g + i) % parts) for g in range(parts)])]
    all_to_all x4, waiting for transfers between devices: 65 us -> 48.4 us  [the longest x3 48.4 us: exchange(): lax.all_to_all(rows, axes, 0, 0, axis_index_groups=everywhere, tiled=True)]
    all_to_all x4, starting transfers between devices: 33.9 us -> 23.6 us  [the longest x3 19.3 us: exchange(): lax.all_to_all(rows, axes, 0, 0, axis_index_groups=everywhere, tiled=True)]
    pallas_call x6, Pallas kernels: 30.5 us -> 22.8 us  [run(): pl.pallas_call(kernel, out_shape=tuple(outs), in_specs=[pl.BlockSpec(memo...]
    ppermute x3, waiting for transfers between devices: 40.4 us -> 35.2 us  [whole_expert(): own = lax.ppermute(weight[0], axes, swap)]
    unnamed x23 -> x39, local copies, waits for them, and re-layouts: 13.1 us -> 17.9 us
    ppermute x3, waiting for transfers between devices: 1.2 us -> 3.61 us  [whole_expert(): shares.append(lax.ppermute(own, 'expert', turn))]
    ppermute x0 -> x1, starting transfers between devices: none -> 1.99 us  [exchange_late(): lax.ppermute(share, 'dp', [(g, (g + i) % parts) for g in range(parts)])]
  transfers between devices with their start and end apart: 10 -> 11, of which waited for: 6 -> 7; matrix products, arithmetic and copies ran while one was open for 2% -> 2% of each run, Pallas kernels for 15% -> 11%
where the time goes in v7:
time: 194 us
  waiting for transfers between devices  120 us (62%)
  starting transfers between devices  30.6 us (16%)
  Pallas kernels  22.8 us (12%)
  local copies, waits for them, and re-layouts  19.6 us (10%)
    all_to_all x3, waiting for transfers between devices, exchange(): lax.all_to_all(rows, axes, 0, 0, axis_index_groups=everywhere, tiled=True)  48.4 us
    ppermute x3, waiting for transfers between devices, whole_expert(): own = lax.ppermute(weight[0], axes, swap)  35.2 us
    ppermute x1, waiting for transfers between devices, exchange_late(): lax.ppermute(share, 'dp', [(g, (g + i) % parts) for g in range(parts)])  32.6 us
    pallas_call x6, Pallas kernels, run(): pl.pallas_call(kernel, out_shape=tuple(outs), in_specs=[pl.BlockSpec(memo...  22.8 us
    all_to_all x3, starting transfers between devices, exchange(): lax.all_to_all(rows, axes, 0, 0, axis_index_groups=everywhere, tiled=True)  19.3 us
    unnamed x39, local copies, waits for them, and re-layouts  17.9 us
    ppermute x3, starting transfers between devices, whole_expert(): own = lax.ppermute(weight[0], axes, swap)  4.91 us
    all_to_all x1, starting transfers between devices, exchange_late(): lax.all_to_all(rows, axes, 0, 0, axis_index_groups=in_plane, tiled=True)  4.31 us
  transfers between devices with their start and end apart: 11, of which 7 were waited for; matrix products, arithmetic and copies ran while one was open for 2% of the time, Pallas kernels for 11%

profile of v7, /device:TPU:0, one launch (start us, length us, event | category | flops | bytes accessed | tf_op | source)
XLA Modules:
  0.0 193.6 jit_solution(4596129135132139314)
XLA Ops:
  0.6 3.0 %collective-permute-start = (bf16[2048,384]{1,0:T(8,128)(2,1)}, bf16[2048,384]{1,0:T(8,128)(2,1)S(1)}, u32[]{:S(2)}, u32[]{:S(2)}) collective-permute-start(bf16[2048,384]{1,0:T(8,128)(2,1)} %bitcast.20), channel_id=1, source_target_pairs={{0,16},{1,0},{2,18},{3,2},{4,20},{5,4},{6,22},{7,6},{8,24},{9,8},{... | collective-permute-start | bytes 4718600 | tf_op jit(solution)/shard_map/ppermute | solution.py:207
  3.6 0.8 copy.14.routes_ref
  4.4 0.0 copy-start.16
  4.4 1.0 copy-done.16
  5.4 2.3 %shard_map.94 = (bf16[384,2048]{1,0:T(8,128)(2,1)}, bf16[256,384]{1,0:T(8,128)(2,1)S(1)}, bf16[128,384]{1,0:T(8,128)(2,1)S(1)}) custom-call(s32[1]{0:T(128)} %bitcast.plane_ref, s32[128,2]{1,0:T(8,128)S(1)} %copy.14.routes_ref, bf16[128,2048]{1,0:T(8,128)(2,1)S(1)} %copy-done.16), custom_call_target="tpu_custom_call" | custom-call | flops 201326592 | bytes 2393092 | tf_op jit(solution)/shard_map/pallas_call | solution.py:167
  7.7 6.0 %all-to-all-start = ((bf16[16,24,2048]{2,1,0:T(8,128)(2,1)}), bf16[16,24,2048]{2,1,0:T(8,128)(2,1)}, u32[]{:S(2)}, u32[]{:S(2)}) async-start(bf16[16,24,2048]{2,1,0:T(8,128)(2,1)} %bitcast.1), calls=%async_computation | async-start | bytes 3145728 | tf_op jit(solution)/shard_map/all_to_all | solution.py:216
  13.7 1.9 collective-permute-start.1
  15.5 0.0 collective-permute-start.4
  15.6 17.9 %collective-permute-done.refs_0_._.refs_6_ = bf16[2048,384]{1,0:T(8,128)(2,1)S(1)} collective-permute-done((bf16[2048,384]{1,0:T(8,128)(2,1)}, bf16[2048,384]{1,0:T(8,128)(2,1)S(1)}, u32[]{:S(2)}, u32[]{:S(2)}) %collective-permute-start) | collective-permute-done | bytes 1572896 | tf_op jit(solution)/shard_map/ppermute | solution.py:207
  33.5 0.0 copy-start.14
  33.5 1.0 copy-done.14
  34.5 0.6 shard_map.97
  35.1 0.0 copy-start.8
  35.1 1.1 copy-done.8
  36.2 14.4 %all-to-all-done = bf16[16,24,2048]{2,1,0:T(8,128)(2,1)} async-done(((bf16[16,24,2048]{2,1,0:T(8,128)(2,1)}), bf16[16,24,2048]{2,1,0:T(8,128)(2,1)}, u32[]{:S(2)}, u32[]{:S(2)}) %all-to-all-start) | async-done | bytes 1572896 | tf_op jit(solution)/shard_map/all_to_all | solution.py:216
  50.7 4.3 %all-to-all-start.2 = ((bf16[8,48,2048]{2,1,0:T(8,128)(2,1)}), bf16[8,48,2048]{2,1,0:T(8,128)(2,1)}, u32[]{:S(2)}, u32[]{:S(2)}) async-start(bf16[8,48,2048]{2,1,0:T(8,128)(2,1)} %bitcast.17), calls=%async_computation.2 | async-start | bytes 3145728 | tf_op jit(solution)/shard_map/all_to_all | solution.py:222
  55.0 0.1 collective-permute-start.2
  55.0 0.5 collective-permute-done.1.refs_1_.refs_8_
  55.6 0.0 collective-permute-start.3
  55.6 16.8 %collective-permute-done.4.refs_4_.refs_2_ = bf16[384,2048]{1,0:T(8,128)(2,1)} collective-permute-done((bf16[384,2048]{1,0:T(8,128)(2,1)}, bf16[384,2048]{1,0:T(8,128)(2,1)}, u32[]{:S(2)}, u32[]{:S(2)}) %collective-permute-start.4) | collective-permute-done | bytes 1572896 | tf_op jit(solution)/shard_map/ppermute | solution.py:207
  72.4 0.0 collective-permute-start.5
  72.4 0.0 collective-permute-done.2.refs_2_.refs_7_
  72.4 0.0 collective-permute-done.3.refs_3_.refs_9_
  72.4 3.6 %collective-permute-done.5.refs_5_.refs_3_ = bf16[384,2048]{1,0:T(8,128)(2,1)S(1)} collective-permute-done((bf16[384,2048]{1,0:T(8,128)(2,1)}, bf16[384,2048]{1,0:T(8,128)(2,1)S(1)}, u32[]{:S(2)}, u32[]{:S(2)}) %collective-permute-start.5) | collective-permute-done | bytes 1572896 | tf_op jit(solution)/shard_map/ppermute | solution.py:211
  76.0 9.0 %shard_map.95 = (bf16[384,2048]{1,0:T(8,128)(2,1)S(1)}, f32[2,384,384]{2,1,0:T(8,128)S(1)}, f32[2,384,384]{2,1,0:T(8,128)S(1)}) custom-call(bf16[384,2048]{1,0:T(8,128)(2,1)} %bitcast.2.rows_ref, bf16[2048,384]{1,0:T(8,128)(2,1)S(1)} %collective-permute-done.refs_0_._.refs_6_, bf16[2048,384]{1,0:T(8,128)(2,1)S(1)} %collective-permute-done.1.refs_1_.refs_8_, ...), custom_call_target="tpu_custom_call" | custom-call | flops 3623878656 | bytes 14942208 | tf_op jit(solution)/shard_map/pallas_call | solution.py:167
  85.1 0.0 copy-done
  85.1 0.0 copy-start.2
  85.1 1.1 copy-done.2
  86.2 0.0 copy-start.4
  86.2 1.2 copy-done.4
  87.4 0.0 copy-start.6
  87.4 1.2 copy-done.6
  88.7 0.0 copy-start.9
  88.7 1.1 copy-done.9
  89.8 0.0 copy-start.10
  89.8 1.0 copy-done.10
  90.8 0.0 copy-start.12
  90.8 1.0 copy-done.12
  91.8 0.0 all-to-all-done.2
  91.8 7.8 %all-to-all-start.1 = ((bf16[16,24,2048]{2,1,0:T(8,128)(2,1)}), bf16[16,24,2048]{2,1,0:T(8,128)(2,1)S(1)}, u32[]{:S(2)}, u32[]{:S(2)}) async-start(bf16[16,24,2048]{2,1,0:T(8,128)(2,1)} %bitcast.18), calls=%async_computation.1 | async-start | bytes 3145728 | tf_op jit(solution)/shard_map/all_to_all | solution.py:216
  99.7 0.0 copy-start.1
  99.7 0.0 copy-start.3
  99.7 1.7 fusion
  101.4 2.0 %collective-permute-start.6 = (bf16[192,2048]{1,0:T(8,128)(2,1)S(1)}, bf16[192,2048]{1,0:T(8,128)(2,1)S(1)}, u32[]{:S(2)}, u32[]{:S(2)}) collective-permute-start(bf16[192,2048]{1,0:T(8,128)(2,1)S(1)} %bitcast.19), channel_id=1, source_target_pairs={{0,16},{16,0},{1,17},{17,1},{2,18},{18,2},{3,19},{19,3},{4,20},{20... | collective-permute-start | bytes 2359304 | tf_op jit(solution)/shard_map/ppermute | solution.py:228
  103.4 32.6 %collective-permute-done.6.refs_1_ = bf16[192,2048]{1,0:T(8,128)(2,1)S(1)} collective-permute-done((bf16[192,2048]{1,0:T(8,128)(2,1)S(1)}, bf16[192,2048]{1,0:T(8,128)(2,1)S(1)}, u32[]{:S(2)}, u32[]{:S(2)}) %collective-permute-start.6) | collective-permute-done | bytes 786464 | tf_op jit(solution)/shard_map/ppermute | solution.py:228
  135.9 0.0 copy-done.1
  135.9 0.0 copy-done.3
  135.9 0.0 copy-start.5
  135.9 1.4 copy-done.5
  137.3 0.0 copy-start.7
  137.3 1.4 copy-done.7
  138.8 1.3 copy-done.11
  140.0 1.3 copy-done.13
  141.3 7.7 %shard_map.98 = bf16[384,2048]{1,0:T(8,128)(2,1)} custom-call(s32[1]{0:T(128)} %bitcast.plane_ref, bf16[192,2048]{1,0:T(8,128)(2,1)S(1)} %bitcast.16, bf16[192,2048]{1,0:T(8,128)(2,1)S(1)} %collective-permute-done.6.refs_1_, bf16[384,2048]{1,0:T(8,128)(2,1)} %collective-permute-done.4.refs_4_.refs_2_, bf16[384,2048]{1,0:T(8,128)(2,1)S(1)} %copy-done.7, ...), custom_call_target="tpu_custom_call" | custom-call | flops 3623878656 | bytes 14942212 | tf_op jit(solution)/shard_map/pallas_call | solution.py:167
  149.0 0.0 all-to-all-done.1
  149.0 0.0 copy-start.17
  149.0 5.6 %all-to-all-start.3 = ((bf16[16,24,2048]{2,1,0:T(8,128)(2,1)}), bf16[16,24,2048]{2,1,0:T(8,128)(2,1)S(1)}, u32[]{:S(2)}, u32[]{:S(2)}) async-start(bf16[16,24,2048]{2,1,0:T(8,128)(2,1)} %bitcast.12), calls=%async_computation.3 | async-start | bytes 3145728 | tf_op jit(solution)/shard_map/all_to_all | solution.py:216
  154.6 0.0 copy-done.17
  154.6 0.1 copy.15.gates_ref
  154.7 1.0 copy-done.15
  155.8 1.7 shard_map.96
  157.4 0.6 copy.17
  158.1 34.0 %all-to-all-done.3 = bf16[16,24,2048]{2,1,0:T(8,128)(2,1)S(1)} async-done(((bf16[16,24,2048]{2,1,0:T(8,128)(2,1)}), bf16[16,24,2048]{2,1,0:T(8,128)(2,1)S(1)}, u32[]{:S(2)}, u32[]{:S(2)}) %all-to-all-start.3) | async-done | bytes 1572896 | tf_op jit(solution)/shard_map/all_to_all | solution.py:216
  192.1 1.5 shard_map.99
  (4 shorter events, 0.0 us)
Async XLA Ops:
  0.6 32.8 %collective-permute-start = (bf16[2048,384]{1,0:T(8,128)(2,1)}, bf16[2048,384]{1,0:T(8,128)(2,1)S(1)}, u32[]{:S(2)}, u32[]{:S(2)}) collective-permute-start(bf16[2048,384]{1,0:T(8,128)(2,1)} %bitcast.20), channel_id=1, source_target_pairs={{0,16},{1,0},{2,18},{3,2},{4,20},{5,4},{6,22},{7,6},{8,24},{9,8},{... | collective-permute-start | bytes 4718600 | tf_op jit(solution)/shard_map/ppermute | solution.py:207
  4.4 1.0 copy-start.16
  7.7 43.0 %all-to-all-start = ((bf16[16,24,2048]{2,1,0:T(8,128)(2,1)}), bf16[16,24,2048]{2,1,0:T(8,128)(2,1)}, u32[]{:S(2)}, u32[]{:S(2)}) async-start(bf16[16,24,2048]{2,1,0:T(8,128)(2,1)} %bitcast.1), calls=%async_computation | async-start | bytes 3145728 | tf_op jit(solution)/shard_map/all_to_all | solution.py:216
  13.7 41.9 %collective-permute-start.1 = (bf16[2048,384]{1,0:T(8,128)(2,1)}, bf16[2048,384]{1,0:T(8,128)(2,1)S(1)}, u32[]{:S(2)}, u32[]{:S(2)}) collective-permute-start(bf16[2048,384]{1,0:T(8,128)(2,1)} %bitcast.21), channel_id=1, source_target_pairs={{0,16},{1,0},{2,18},{3,2},{4,20},{5,4},{6,22},{7,6},{8,24},{9,8},{... | collective-permute-start | bytes 4718600 | tf_op jit(solution)/shard_map/ppermute | solution.py:207
  15.5 56.9 %collective-permute-start.4 = (bf16[384,2048]{1,0:T(8,128)(2,1)}, bf16[384,2048]{1,0:T(8,128)(2,1)}, u32[]{:S(2)}, u32[]{:S(2)}) collective-permute-start(bf16[384,2048]{1,0:T(8,128)(2,1)} %bitcast.22), channel_id=1, source_target_pairs={{0,16},{1,0},{2,18},{3,2},{4,20},{5,4},{6,22},{7,6},{8,24},{9,8},{... | collective-permute-start | bytes 4718600 | tf_op jit(solution)/shard_map/ppermute | solution.py:207
  33.5 1.0 copy-start.14
  35.1 1.2 copy-start.8
  50.7 41.2 %all-to-all-start.2 = ((bf16[8,48,2048]{2,1,0:T(8,128)(2,1)}), bf16[8,48,2048]{2,1,0:T(8,128)(2,1)}, u32[]{:S(2)}, u32[]{:S(2)}) async-start(bf16[8,48,2048]{2,1,0:T(8,128)(2,1)} %bitcast.17), calls=%async_computation.2 | async-start | bytes 3145728 | tf_op jit(solution)/shard_map/all_to_all | solution.py:222
  55.0 17.5 %collective-permute-start.2 = (bf16[2048,384]{1,0:T(8,128)(2,1)S(1)}, bf16[2048,384]{1,0:T(8,128)(2,1)S(1)}, u32[]{:S(2)}, u32[]{:S(2)}) collective-permute-start(bf16[2048,384]{1,0:T(8,128)(2,1)S(1)} %collective-permute-done.refs_0_._.refs_6_), channel_id=1, source_target_pairs={{0,1},{1,0},{2,3},{3,2},{4,5},{5,4},{6,7},{7,6},{8,9},{9,8},{10,11... | collective-permute-start | bytes 4718600 | tf_op jit(solution)/shard_map/ppermute | solution.py:211
  55.6 29.5 %copy-start = (bf16[2048,384]{1,0:T(8,128)(2,1)}, bf16[2048,384]{1,0:T(8,128)(2,1)S(1)}, u32[]{:S(2)}) copy-start(bf16[2048,384]{1,0:T(8,128)(2,1)S(1)} %collective-permute-done.1.refs_1_.refs_8_) | copy-start | bytes 4718596
  55.6 16.9 %collective-permute-start.3 = (bf16[2048,384]{1,0:T(8,128)(2,1)S(1)}, bf16[2048,384]{1,0:T(8,128)(2,1)S(1)}, u32[]{:S(2)}, u32[]{:S(2)}) collective-permute-start(bf16[2048,384]{1,0:T(8,128)(2,1)S(1)} %collective-permute-done.1.refs_1_.refs_8_), channel_id=1, source_target_pairs={{0,1},{1,0},{2,3},{3,2},{4,5},{5,4},{6,7},{7,6},{8,9},{9,8},{10,11... | collective-permute-start | bytes 4718600 | tf_op jit(solution)/shard_map/ppermute | solution.py:211
  72.4 3.6 %collective-permute-start.5 = (bf16[384,2048]{1,0:T(8,128)(2,1)}, bf16[384,2048]{1,0:T(8,128)(2,1)S(1)}, u32[]{:S(2)}, u32[]{:S(2)}) collective-permute-start(bf16[384,2048]{1,0:T(8,128)(2,1)} %collective-permute-done.4.refs_4_.refs_2_), channel_id=1, source_target_pairs={{0,1},{1,0},{2,3},{3,2},{4,5},{5,4},{6,7},{7,6},{8,9},{9,8},{10,11... | collective-permute-start | bytes 4718600 | tf_op jit(solution)/shard_map/ppermute | solution.py:211
  85.1 1.1 copy-start.2
  86.2 1.2 copy-start.4
  87.4 1.2 copy-start.6
  88.7 1.1 copy-start.9
  89.8 1.0 copy-start.10
  90.8 1.0 copy-start.12
  91.8 57.2 %all-to-all-start.1 = ((bf16[16,24,2048]{2,1,0:T(8,128)(2,1)}), bf16[16,24,2048]{2,1,0:T(8,128)(2,1)S(1)}, u32[]{:S(2)}, u32[]{:S(2)}) async-start(bf16[16,24,2048]{2,1,0:T(8,128)(2,1)} %bitcast.18), calls=%async_computation.1 | async-start | bytes 3145728 | tf_op jit(solution)/shard_map/all_to_all | solution.py:216
  99.7 36.3 %copy-start.1 = (bf16[2048,384]{1,0:T(8,128)(2,1)S(1)}, bf16[2048,384]{1,0:T(8,128)(2,1)}, u32[]{:S(2)}) copy-start(bf16[2048,384]{1,0:T(8,128)(2,1)} %copy-done) | copy-start | bytes 4718596
  99.7 36.3 %copy-start.3 = (bf16[2048,384]{1,0:T(8,128)(2,1)S(1)}, bf16[2048,384]{1,0:T(8,128)(2,1)}, u32[]{:S(2)}) copy-start(bf16[2048,384]{1,0:T(8,128)(2,1)} %copy-done.2) | copy-start | bytes 4718596
  101.4 34.5 %collective-permute-start.6 = (bf16[192,2048]{1,0:T(8,128)(2,1)S(1)}, bf16[192,2048]{1,0:T(8,128)(2,1)S(1)}, u32[]{:S(2)}, u32[]{:S(2)}) collective-permute-start(bf16[192,2048]{1,0:T(8,128)(2,1)S(1)} %bitcast.19), channel_id=1, source_target_pairs={{0,16},{16,0},{1,17},{17,1},{2,18},{18,2},{3,19},{19,3},{4,20},{20... | collective-permute-start | bytes 2359304 | tf_op jit(solution)/shard_map/ppermute | solution.py:228
  135.9 1.4 copy-start.5
  137.3 1.4 copy-start.7
  138.8 1.3 copy-start.11
  140.0 1.3 copy-start.13
  149.0 5.6 %copy-start.17 = (f32[128,2]{0,1:T(2,128)S(1)}, f32[128,2]{0,1:T(2,128)}, u32[]{:S(2)}) copy-start(f32[128,2]{0,1:T(2,128)} %param.10) | copy-start | bytes 3076
  149.0 43.0 %all-to-all-start.3 = ((bf16[16,24,2048]{2,1,0:T(8,128)(2,1)}), bf16[16,24,2048]{2,1,0:T(8,128)(2,1)S(1)}, u32[]{:S(2)}, u32[]{:S(2)}) async-start(bf16[16,24,2048]{2,1,0:T(8,128)(2,1)} %bitcast.12), calls=%async_computation.3 | async-start | bytes 3145728 | tf_op jit(solution)/shard_map/all_to_all | solution.py:216
  154.7 1.0 copy-start.15

commit v8 on v7

--- a/solution.py
+++ b/solution.py
@@ -9,7 +9,7 @@
 
 BF16 = jnp.bfloat16
 F32 = jnp.float32
-VMEM_BYTES = 28 << 20
+SMALL_VMEM, LARGE_VMEM = 12 << 20, 60 << 20
 
 
 def dot(a, b, dims):
@@ -32,6 +32,14 @@
     copy = pltpu.make_async_copy(stage_ref, out_ref, sem)
     copy.start()
     return copy
+
+
+def shares(unit_ref, parts, joined, axis=1):
+    if not joined:
+        return [unit_ref.at[i] for i in range(parts)]
+    size = unit_ref.shape[1 + axis] // parts
+    cuts = [pl.ds(i * size, size) for i in range(parts)]
+    return [unit_ref.at[0, cut] if axis == 0 else unit_ref.at[0, :, cut] for cut in cuts]
 
 
 def place_kernel(experts, parts, plane_ref, routes_ref, tokens_ref, slots_ref, place_ref, near_ref):
@@ -72,65 +80,91 @@
         slots_ref[:, columns] = dot(near_ref[...], rows_ref[:, columns], (0, 0)).astype(BF16)
 
 
-def forward_kernel(parts, rows_ref, *refs):
-    sources, refs = refs[: 3 * parts], refs[3 * parts :]
-    out_ref, by_gate_ref, by_up_ref, sems, out_sems = refs[:5]
-    stage_ref, by_gate_stage, by_up_stage, hidden_ref, *weights = refs[5:]
-    copies = fetch(sources, weights, sems)
-    sent = []
-    for i in range(parts):
-        copies[2 * i].wait()
-        pre_gate = dot(rows_ref[...], weights[2 * i][...], (1, 0))
-        copies[1 + 2 * i].wait()
-        pre_up = dot(rows_ref[...], weights[2 * i + 1][...], (1, 0))
+def hidden_kernel(parts, joined, rows_ref, *refs):
+    sources, refs = [rows_ref, *refs[: 2 * parts]], refs[2 * parts :]
+    outs, (sems, out_sems), refs = refs[:3], refs[3:5], refs[5:]
+    hidden_ref, by_gate_ref, by_up_ref, rows_ref, gate_ref, up_ref = refs
+    gate, up = shares(gate_ref, parts, joined), shares(up_ref, parts, joined)
+    copies = fetch(sources, [rows_ref, *gate, *up], sems)
+    for copy in copies[: 1 + parts]:
+        copy.wait()
+    for i in range(gate_ref.shape[0]):
+        pre_gate = dot(rows_ref[...], gate_ref[i], (1, 0))
+        if i == 0:
+            for copy in copies[1 + parts :]:
+                copy.wait()
+        pre_up = dot(rows_ref[...], up_ref[i], (1, 0))
         sig = jax.nn.sigmoid(pre_gate)
         act = pre_gate * sig
         hidden_ref[i] = (act * pre_up).astype(BF16)
-        by_gate_stage[i] = pre_up * sig * (1.0 + pre_gate * (1.0 - sig))
-        by_up_stage[i] = act
-    sent.append(store(by_gate_stage, by_gate_ref, out_sems.at[0]))
-    sent.append(store(by_up_stage, by_up_ref, out_sems.at[1]))
-    for copy in copies[2 * parts :]:
-        copy.wait()
-    down = weights[2 * parts :]
-    for columns in tiles(out_ref.shape[1]):
+        by_gate_ref[i] = pre_up * sig * (1.0 + pre_gate * (1.0 - sig))
+        by_up_ref[i] = act
+    for copy in fetch([hidden_ref, by_gate_ref, by_up_ref], outs, out_sems):
+        copy.wait()
+
+
+def in_place_kernel(_, after_ref, out_ref):
+    pass
+
+
+def out_kernel(parts, joined, hidden_ref, *refs):
+    sources, refs = refs[:parts], refs[parts:]
+    out_ref, sems, out_sems, stage_ref, hidden_stage, down_ref = refs
+    down = shares(down_ref, parts, joined, 0)
+    pieces = tiles(out_ref.shape[1])
+    (first,) = fetch([hidden_ref], [hidden_stage], sems)
+    copies = [
+        fetch(
+            [source.at[:, columns] for source in sources],
+            [share.at[:, columns] for share in down],
+            sems.at[pl.ds(1 + d * parts, parts)],
+        )
+        for d, columns in enumerate(pieces)
+    ]
+    first.wait()
+    sent = []
+    for d, columns in enumerate(pieces):
+        for copy in copies[d]:
+            copy.wait()
         stage_ref[:, columns] = sum(
-            dot(hidden_ref[i], down[i][:, columns], (1, 0)) for i in range(parts)
+            dot(hidden_stage[i], down_ref[i, :, columns], (1, 0)) for i in range(down_ref.shape[0])
         ).astype(BF16)
-        sem = out_sems.at[len(sent)]
-        sent.append(store(stage_ref.at[:, columns], out_ref.at[:, columns], sem))
+        sent.append(store(stage_ref.at[:, columns], out_ref.at[:, columns], out_sems.at[d]))
     for copy in sent:
         copy.wait()
 
 
-def backward_kernel(parts, plane_ref, *refs):
+def backward_kernel(parts, joined, plane_ref, _, *refs):
     sources, refs = refs[: 2 + 4 * parts], refs[2 + 4 * parts :]
-    out_ref, sems, out_sems, back_gate_ref, back_up_ref, stage_ref, rows_ref, *targets = refs
+    out_ref, sems, out_sems, back_gate_ref, back_up_ref, stage_ref, rows_ref = refs[:7]
+    down_ref, by_gate_ref, by_up_ref, gate_ref, up_ref = refs[7:]
     share = rows_ref.shape[0] // parts
     places = [
         rows_ref.at[pl.ds(pl.multiple_of((plane_ref[0] + parts - i) % parts * share, share), share)]
         for i in range(parts)
     ]
-    copies = fetch(sources, [*places, *targets], sems)
-    down, (by_gate_ref, by_up_ref) = targets[:parts], targets[parts : parts + 2]
-    gate, up = targets[parts + 2 : 2 * parts + 2], targets[2 * parts + 2 :]
+    down, gate, up = (
+        shares(down_ref, parts, joined, 0),
+        shares(gate_ref, parts, joined),
+        shares(up_ref, parts, joined),
+    )
+    copies = fetch(sources, [*places, *down, by_gate_ref, by_up_ref, *gate, *up], sems)
     for copy in copies[: 2 + 2 * parts]:
         copy.wait()
-    for i in range(parts):
-        back_hidden = dot(rows_ref[...], down[i][...], (1, 1))
+    for i in range(down_ref.shape[0]):
+        back_hidden = dot(rows_ref[...], down_ref[i], (1, 1))
         back_gate_ref[i] = (back_hidden * by_gate_ref[i]).astype(BF16)
         back_up_ref[i] = (back_hidden * by_up_ref[i]).astype(BF16)
     for copy in copies[2 + 2 * parts :]:
         copy.wait()
     sent = []
-    for columns in tiles(out_ref.shape[1]):
+    for d, columns in enumerate(tiles(out_ref.shape[1])):
         stage_ref[:, columns] = sum(
-            dot(back_gate_ref[i], gate[i][columns, :], (1, 1))
-            + dot(back_up_ref[i], up[i][columns, :], (1, 1))
-            for i in range(parts)
+            dot(back_gate_ref[i], gate_ref[i, columns, :], (1, 1))
+            + dot(back_up_ref[i], up_ref[i, columns, :], (1, 1))
+            for i in range(down_ref.shape[0])
         ).astype(BF16)
-        sem = out_sems.at[len(sent)]
-        sent.append(store(stage_ref.at[:, columns], out_ref.at[:, columns], sem))
+        sent.append(store(stage_ref.at[:, columns], out_ref.at[:, columns], out_sems.at[d]))
     for copy in sent:
         copy.wait()
 
@@ -157,7 +191,7 @@
     out_ref[...] = total.astype(BF16)
 
 
-def call(kernel, outs, flops, scratch=(), far=(), far_out=False):
+def call(kernel, outs, flops, scratch=(), far=(), far_out=False, vmem=SMALL_VMEM, aliases=None):
     def run(*args):
         moved = sum(a.size * a.dtype.itemsize for a in (*args, *outs))
         spaces = [
@@ -166,13 +200,14 @@
         ]
         return pl.pallas_call(
             kernel,
-            out_shape=tuple(outs),
+            out_shape=tuple(jax.ShapeDtypeStruct(o.shape, o.dtype) for o in outs),
             in_specs=[pl.BlockSpec(memory_space=space) for space in spaces],
             out_specs=tuple(
                 pl.BlockSpec(memory_space=pl.ANY if far_out else pltpu.VMEM) for _ in outs
             ),
             scratch_shapes=scratch,
-            compiler_params=pltpu.CompilerParams(vmem_limit_bytes=VMEM_BYTES),
+            input_output_aliases=aliases or {},
+            compiler_params=pltpu.CompilerParams(vmem_limit_bytes=vmem),
             cost_estimate=pl.CostEstimate(flops=flops, bytes_accessed=moved, transcendentals=0),
         )(*args)
 
@@ -203,13 +238,15 @@
     everywhere = [[d for plane in planes[c] for d in plane] for c in range(parts)]
     in_plane = [plane for c in range(parts) for plane in planes[c]]
 
-    def whole_expert(weight):
-        own = lax.ppermute(weight[0], axes, swap)
-        shares = [own]
+    def swapped(weight):
+        return lax.ppermute(weight[0], axes, swap)
+
+    def whole_expert(own):
+        held = [own]
         for step in range(1, parts):
             turn = [(j, j // parts * parts + (j + step) % parts) for j in range(experts)]
-            shares.append(lax.ppermute(own, "expert", turn))
-        return shares
+            held.append(lax.ppermute(own, "expert", turn))
+        return held
 
     def exchange(rows):
         rows = rows.reshape(experts, capacity, width)
@@ -221,30 +258,35 @@
         rows = rows.reshape(sets, parts * capacity, width)
         rows = lax.all_to_all(rows, axes, 0, 0, axis_index_groups=in_plane, tiled=True)
         rows = rows.reshape(sets, parts, capacity, width)
-        shares = []
+        crossed = []
         for i in range(parts):
             share = rows[:, i].reshape(sets * capacity, width)
             if i > 0:
                 share = lax.ppermute(share, "dp", [(g, (g + i) % parts) for g in range(parts)])
-            shares.append(share)
-        return shares
+            crossed.append(share)
+        return crossed
 
     spread_flops = 2 * slots * tok_rows * width
     dot_flops = 2 * slots * width * hidden * parts
     slot_shape = jax.ShapeDtypeStruct((slots, width), BF16)
     place_shape = jax.ShapeDtypeStruct((top_count * tok_rows, slots), BF16)
-    unit_shape = jax.ShapeDtypeStruct((parts, slots, hidden), F32)
+    joined = hidden % 128 == 0
+    units, span = (1, parts * hidden) if joined else (parts, hidden)
+    unit_shape = jax.ShapeDtypeStruct((units, slots, span), F32)
+    hidden_shape = jax.ShapeDtypeStruct((units, slots, span), BF16)
     token_shape = jax.ShapeDtypeStruct((tok_rows, width), BF16)
-    hidden_scratch = pltpu.VMEM((parts, slots, hidden), BF16)
+    hidden_scratch = pltpu.VMEM((units, slots, span), BF16)
+    unit_scratch = pltpu.VMEM((units, slots, span), F32)
     row_scratch = pltpu.VMEM((slots, width), BF16)
-    in_scratch = pltpu.VMEM((width, hidden), BF16)
-    down_scratch = pltpu.VMEM((hidden, width), BF16)
-    unit_stage = pltpu.VMEM((parts, slots, hidden), F32)
+    in_scratch = pltpu.VMEM((units, width, span), BF16)
+    down_scratch = pltpu.VMEM((units, span, width), BF16)
+    pieces = len(tiles(width))
 
     def sems(number):
         return pltpu.SemaphoreType.DMA((number,))
 
-    gate_w, up_w, down_w = whole_expert(w_gate), whole_expert(w_up), whole_expert(w_down)
+    gate_own, up_own, down_own = swapped(w_gate), swapped(w_up), swapped(w_down)
+    gate_w, up_w = whole_expert(gate_own), whole_expert(up_own)
     plane = lax.axis_index("dp").astype(jnp.int32).reshape(1)
     x_slots, place, near = call(
         functools.partial(place_kernel, experts, parts),
@@ -253,33 +295,43 @@
     )(plane, routes, tokens)
     x_rows = exchange(x_slots)
     (dy_slots,) = call(spread_kernel, [slot_shape], 256 * spread_flops, far=(2,))(
-        near, cotangent, gate_w[0]
+        near, cotangent, gate_own
     )
     dy_shares = exchange_late(dy_slots)
-    out_rows, by_gate, by_up = call(
-        functools.partial(forward_kernel, parts),
-        [slot_shape, unit_shape, unit_shape],
-        3 * dot_flops,
-        [sems(3 * parts), sems(2 + len(tiles(width))), row_scratch, unit_stage, unit_stage]
-        + [hidden_scratch]
-        + [in_scratch] * (2 * parts)
-        + [down_scratch] * parts,
-        far=range(1, 1 + 3 * parts),
+    hidden_rows, by_gate, by_up = call(
+        functools.partial(hidden_kernel, parts, joined),
+        [hidden_shape, unit_shape, unit_shape],
+        2 * dot_flops,
+        [sems(1 + 2 * parts), sems(3), hidden_scratch, unit_scratch, unit_scratch, row_scratch]
+        + [in_scratch] * 2,
+        far=range(1 + 2 * parts),
         far_out=True,
-    )(x_rows, *(w for pair in zip(gate_w, up_w) for w in pair), *down_w)
+        vmem=LARGE_VMEM,
+    )(x_rows, *gate_w, *up_w)
+    (down_own,) = call(
+        in_place_kernel, [down_own], 0, far=range(2), far_out=True, vmem=LARGE_VMEM, aliases={0: 0}
+    )(down_own, hidden_rows)
+    down_w = whole_expert(down_own)
+    (out_rows,) = call(
+        functools.partial(out_kernel, parts, joined),
+        [slot_shape],
+        dot_flops,
+        [sems(1 + pieces * parts), sems(pieces), row_scratch, hidden_scratch, down_scratch],
+        far=range(1 + parts),
+        far_out=True,
+    )(hidden_rows, *down_w)
     out_slots = exchange(out_rows)
     (grad_rows,) = call(
-        functools.partial(backward_kernel, parts),
+        functools.partial(backward_kernel, parts, joined),
         [slot_shape],
-        3 * dot_flops,
-        [sems(2 + 4 * parts), sems(len(tiles(width))), hidden_scratch, hidden_scratch]
-        + [row_scratch] * 2
-        + [down_scratch] * parts
-        + [unit_stage] * 2
-        + [in_scratch] * (2 * parts),
-        far=range(1, 3 + 4 * parts),
+        64 * dot_flops,
+        [sems(2 + 4 * parts), sems(pieces), hidden_scratch, hidden_scratch]
+        + [row_scratch, row_scratch, down_scratch, unit_scratch, unit_scratch]
+        + [in_scratch] * 2,
+        far=range(1, 4 + 4 * parts),
         far_out=True,
-    )(plane, *dy_shares, *down_w, by_gate, by_up, *gate_w, *up_w)
+        vmem=LARGE_VMEM,
+    )(plane, out_rows, *dy_shares, *down_w, by_gate, by_up, *gate_w, *up_w)
     grad_slots = exchange(grad_rows)
     mixed, gate_grad = call(
         mix_kernel, [token_shape, jax.ShapeDtypeStruct(gates.shape, F32)], 2 * spread_flops

time: 194 us -> 190 us (0.979)
  local copies, waits for them, and re-layouts: 19.6 us -> 10.7 us
  waiting for transfers between devices: 120 us -> 124 us
  Pallas kernels: 22.8 us -> 26.6 us
  starting transfers between devices: 30.6 us -> 27.3 us
    all_to_all x1, waiting for transfers between devices: 0.01 us -> 14.4 us  [exchange_late(): lax.all_to_all(rows, axes, 0, 0, axis_index_groups=in_plane, tiled=True)]
    all_to_all x3, waiting for transfers between devices: 48.4 us -> 60.4 us  [exchange(): lax.all_to_all(rows, axes, 0, 0, axis_index_groups=everywhere, tiled=True)]
    ppermute x1, waiting for transfers between devices: 32.6 us -> 21 us  [exchange_late(): lax.ppermute(share, 'dp', [(g, (g + i) % parts) for g in range(parts)])]
    ppermute x6, waiting for transfers between devices: 38.9 us -> 27.9 us  [the longest x3 26.2 us: swapped(): return lax.ppermute(weight[0], axes, swap)]
    unnamed x39 -> x27, local copies, waits for them, and re-layouts: 17.9 us -> 8.08 us
    all_to_all x3, starting transfers between devices: 19.3 us -> 15.3 us  [exchange(): lax.all_to_all(rows, axes, 0, 0, axis_index_groups=everywhere, tiled=True)]
    pallas_call x6 -> x8, Pallas kernels: 22.8 us -> 26.6 us  [run(): pl.pallas_call(kernel, out_shape=tuple((jax.ShapeDtypeStruct(o.shape, o.d...]
  transfers between devices with their start and end apart: 11 -> 11, of which waited for: 7 -> 8; matrix products, arithmetic and copies ran while one was open for 2% -> 2% of each run, Pallas kernels for 11% -> 13%
where the time goes in v8:
time: 190 us; the launch traced here: 189 us
  waiting for transfers between devices  124 us (65%)
  starting transfers between devices  27.3 us (14%)
  Pallas kernels  26.6 us (14%)
  local copies, waits for them, and re-layouts  10.7 us (6%)
    all_to_all x3, waiting for transfers between devices, exchange(): lax.all_to_all(rows, axes, 0, 0, axis_index_groups=everywhere, tiled=True)  60.4 us
    pallas_call x8, Pallas kernels, run(): pl.pallas_call(kernel, out_shape=tuple((jax.ShapeDtypeStruct(o.shape, o.d...  26.6 us
    ppermute x3, waiting for transfers between devices, swapped(): return lax.ppermute(weight[0], axes, swap)  26.2 us
    ppermute x1, waiting for transfers between devices, exchange_late(): lax.ppermute(share, 'dp', [(g, (g + i) % parts) for g in range(parts)])  21 us
    all_to_all x3, starting transfers between devices, exchange(): lax.all_to_all(rows, axes, 0, 0, axis_index_groups=everywhere, tiled=True)  15.3 us
    all_to_all x1, waiting for transfers between devices, exchange_late(): lax.all_to_all(rows, axes, 0, 0, axis_index_groups=in_plane, tiled=True)  14.4 us
    unnamed x27, local copies, waits for them, and re-layouts  8.08 us
    all_to_all x1, starting transfers between devices, exchange_late(): lax.all_to_all(rows, axes, 0, 0, axis_index_groups=in_plane, tiled=True)  5.81 us
  transfers between devices with their start and end apart: 11, of which 8 were waited for; matrix products, arithmetic and copies ran while one was open for 2% of the time, Pallas kernels for 13%

profile of v8, /device:TPU:0, one launch (start us, length us, event | category | flops | bytes accessed | tf_op | source)
XLA Modules:
  0.0 189.0 jit_solution(3772439813593448588)
XLA Ops:
  0.6 3.0 %collective-permute-start = (bf16[2048,384]{1,0:T(8,128)(2,1)}, bf16[2048,384]{1,0:T(8,128)(2,1)S(1)}, u32[]{:S(2)}, u32[]{:S(2)}) collective-permute-start(bf16[2048,384]{1,0:T(8,128)(2,1)} %bitcast.19), channel_id=1, source_target_pairs={{0,16},{1,0},{2,18},{3,2},{4,20},{5,4},{6,22},{7,6},{8,24},{9,8},{... | collective-permute-start | bytes 4718600 | tf_op jit(solution)/shard_map/ppermute | solution.py:242
  3.6 0.0 collective-permute-start.2
  3.7 0.8 copy.15.routes_ref
  4.4 0.0 copy-start.7
  4.4 1.0 copy-done.7
  5.5 2.2 %shard_map.94 = (bf16[384,2048]{1,0:T(8,128)(2,1)}, bf16[256,384]{1,0:T(8,128)(2,1)S(1)}, bf16[128,384]{1,0:T(8,128)(2,1)S(1)}) custom-call(s32[1]{0:T(128)} %bitcast.plane_ref, s32[128,2]{1,0:T(8,128)S(1)} %copy.15.routes_ref, bf16[128,2048]{1,0:T(8,128)(2,1)S(1)} %copy-done.7), custom_call_target="tpu_custom_call" | custom-call | flops 201326592 | bytes 2393092 | tf_op jit(solution)/shard_map/pallas_call | solution.py:201
  7.7 0.0 copy-start.4
  7.7 6.1 %all-to-all-start = ((bf16[16,24,2048]{2,1,0:T(8,128)(2,1)}), bf16[16,24,2048]{2,1,0:T(8,128)(2,1)}, u32[]{:S(2)}, u32[]{:S(2)}) async-start(bf16[16,24,2048]{2,1,0:T(8,128)(2,1)} %bitcast.1), calls=%async_computation | async-start | bytes 3145728 | tf_op jit(solution)/shard_map/all_to_all | solution.py:253
  13.8 19.7 %collective-permute-done.refs_0_._.refs_6_ = bf16[2048,384]{1,0:T(8,128)(2,1)S(1)} collective-permute-done((bf16[2048,384]{1,0:T(8,128)(2,1)}, bf16[2048,384]{1,0:T(8,128)(2,1)S(1)}, u32[]{:S(2)}, u32[]{:S(2)}) %collective-permute-start) | collective-permute-done | bytes 1572896 | tf_op jit(solution)/shard_map/ppermute | solution.py:242
  33.5 0.0 copy-start.6
  33.5 0.0 copy-done.4
  33.5 1.8 shard_map.99
  35.3 20.3 %all-to-all-done = bf16[16,24,2048]{2,1,0:T(8,128)(2,1)} async-done(((bf16[16,24,2048]{2,1,0:T(8,128)(2,1)}), bf16[16,24,2048]{2,1,0:T(8,128)(2,1)}, u32[]{:S(2)}, u32[]{:S(2)}) %all-to-all-start) | async-done | bytes 1572896 | tf_op jit(solution)/shard_map/all_to_all | solution.py:253
  55.6 5.8 %all-to-all-start.2 = ((bf16[8,48,2048]{2,1,0:T(8,128)(2,1)}), bf16[8,48,2048]{2,1,0:T(8,128)(2,1)}, u32[]{:S(2)}, u32[]{:S(2)}) async-start(bf16[8,48,2048]{2,1,0:T(8,128)(2,1)} %bitcast.8), calls=%async_computation.2 | async-start | bytes 3145728 | tf_op jit(solution)/shard_map/all_to_all | solution.py:259
  61.4 0.0 copy-done.6
  61.4 0.1 collective-permute-start.1
  61.5 0.0 collective-permute-done.2.refs_2_.refs_8_
  61.5 0.5 collective-permute-start.3
  62.0 2.5 %collective-permute-start.4 = (bf16[384,2048]{1,0:T(8,128)(2,1)}, bf16[384,2048]{1,0:T(8,128)(2,1)S(1)}, u32[]{:S(2)}, u32[]{:S(2)}) collective-permute-start(bf16[384,2048]{1,0:T(8,128)(2,1)} %bitcast.21), channel_id=1, source_target_pairs={{0,16},{1,0},{2,18},{3,2},{4,20},{5,4},{6,22},{7,6},{8,24},{9,8},{... | collective-permute-start | bytes 4718600 | tf_op jit(solution)/shard_map/ppermute | solution.py:242
  64.4 1.8 collective-permute-done.1.refs_1_.refs_7_
  66.2 0.0 copy-start.9
  66.2 1.2 copy-done.9
  67.4 0.0 collective-permute-done.3.refs_3_.refs_9_
  67.4 0.0 copy-start.10
  67.4 1.2 copy-done.10
  68.6 7.6 %shard_map.95 = (bf16[1,384,768]{2,1,0:T(8,128)(2,1)}, f32[1,384,768]{2,1,0:T(8,128)}, f32[1,384,768]{2,1,0:T(8,128)}) custom-call(bf16[384,2048]{1,0:T(8,128)(2,1)} %bitcast.2.rows_ref, bf16[2048,384]{1,0:T(8,128)(2,1)} %copy-done.6, bf16[2048,384]{1,0:T(8,128)(2,1)} %copy-done.9, bf16[2048,384]{1,0:T(8,128)(2,1)} %collective-permute-done.2.refs_2_.refs_8_, ...), custom_call_target="tpu_custom_call" | custom-call | flops 2415919104 | bytes 10813440 | tf_op jit(solution)/shard_map/pallas_call | solution.py:201
  76.2 6.5 %collective-permute-done.4._ = bf16[384,2048]{1,0:T(8,128)(2,1)S(1)} collective-permute-done((bf16[384,2048]{1,0:T(8,128)(2,1)}, bf16[384,2048]{1,0:T(8,128)(2,1)S(1)}, u32[]{:S(2)}, u32[]{:S(2)}) %collective-permute-start.4) | collective-permute-done | bytes 1572896 | tf_op jit(solution)/shard_map/ppermute | solution.py:242
  82.7 0.0 copy-start
  82.7 1.2 copy-done
  83.9 0.0 collective-permute-start.5
  83.9 14.4 %all-to-all-done.2 = bf16[8,48,2048]{2,1,0:T(8,128)(2,1)} async-done(((bf16[8,48,2048]{2,1,0:T(8,128)(2,1)}), bf16[8,48,2048]{2,1,0:T(8,128)(2,1)}, u32[]{:S(2)}, u32[]{:S(2)}) %all-to-all-start.2) | async-done | bytes 1572896 | tf_op jit(solution)/shard_map/all_to_all | solution.py:259
  98.3 0.0 copy-start.1
  98.3 0.0 copy-start.2
  98.3 2.6 %fusion = (bf16[8,1,24,2048]{3,2,1,0:T(8,128)(2,1)S(1)}, bf16[8,1,24,2048]{3,2,1,0:T(8,128)(2,1)}) fusion(bf16[8,2,24,2048]{3,2,1,0:T(8,128)(2,1)} %bitcast.9), kind=kLoop, calls=%fused_computation | loop fusion | bytes 3145728 | tf_op jit(solution)/shard_map/slice | solution.py:263
  100.9 0.1 collective-permute-start.6
  100.9 0.0 collective-permute-done.5.refs_1_.refs_3_
  100.9 0.0 copy-done.1
  101.0 0.0 copy-done.2
  101.0 0.0 copy-start.3
  101.0 3.2 %shard_map.97._ = bf16[384,2048]{1,0:T(8,128)(2,1)} custom-call(bf16[1,384,768]{2,1,0:T(8,128)(2,1)S(1)} %copy-done.2, bf16[384,2048]{1,0:T(8,128)(2,1)S(1)} %copy-done.1, bf16[384,2048]{1,0:T(8,128)(2,1)S(1)} %collective-permute-done.5.refs_1_.refs_3_), custom_call_target="tpu_custom_call" | custom-call | flops 1207959552 | bytes 5308416 | tf_op jit(solution)/shard_map/pallas_call | solution.py:201
  104.2 0.0 copy-done.3
  104.2 5.1 %all-to-all-start.1 = ((bf16[16,24,2048]{2,1,0:T(8,128)(2,1)}), bf16[16,24,2048]{2,1,0:T(8,128)(2,1)S(1)}, u32[]{:S(2)}, u32[]{:S(2)}) async-start(bf16[16,24,2048]{2,1,0:T(8,128)(2,1)} %bitcast.6), calls=%async_computation.1 | async-start | bytes 3145728 | tf_op jit(solution)/shard_map/all_to_all | solution.py:253
  109.4 21.0 %collective-permute-done.6.refs_1_ = bf16[192,2048]{1,0:T(8,128)(2,1)S(1)} collective-permute-done((bf16[192,2048]{1,0:T(8,128)(2,1)S(1)}, bf16[192,2048]{1,0:T(8,128)(2,1)S(1)}, u32[]{:S(2)}, u32[]{:S(2)}) %collective-permute-start.6) | collective-permute-done | bytes 786464 | tf_op jit(solution)/shard_map/ppermute | solution.py:265
  130.4 0.0 copy-start.11
  130.4 0.9 copy-done.11
  131.3 8.6 %shard_map.100 = bf16[384,2048]{1,0:T(8,128)(2,1)} custom-call(s32[1]{0:T(128)} %bitcast.plane_ref, bf16[384,2048]{1,0:T(8,128)(2,1)} %shard_map.97._, bf16[192,2048]{1,0:T(8,128)(2,1)} %bitcast.17, bf16[192,2048]{1,0:T(8,128)(2,1)} %copy-done.11, bf16[384,2048]{1,0:T(8,128)(2,1)} %shard_map.96.refs_0_.refs_2_, bf16[384,2048]{1,0:T(8,128)(2,1)} %copy-done.3, ...), custom_call_target="tpu_custom_call" | custom-call | flops 77309411328 | bytes 16515076 | tf_op jit(solution)/shard_map/pallas_call | solution.py:201
  139.9 6.7 %all-to-all-done.1 = bf16[16,24,2048]{2,1,0:T(8,128)(2,1)S(1)} async-done(((bf16[16,24,2048]{2,1,0:T(8,128)(2,1)}), bf16[16,24,2048]{2,1,0:T(8,128)(2,1)S(1)}, u32[]{:S(2)}, u32[]{:S(2)}) %all-to-all-start.1) | async-done | bytes 1572896 | tf_op jit(solution)/shard_map/all_to_all | solution.py:253
  146.6 0.0 copy-start.8
  146.6 4.1 %all-to-all-start.3 = ((bf16[16,24,2048]{2,1,0:T(8,128)(2,1)}), bf16[16,24,2048]{2,1,0:T(8,128)(2,1)S(1)}, u32[]{:S(2)}, u32[]{:S(2)}) async-start(bf16[16,24,2048]{2,1,0:T(8,128)(2,1)} %bitcast.16), calls=%async_computation.3 | async-start | bytes 3145728 | tf_op jit(solution)/shard_map/all_to_all | solution.py:253
  150.6 0.0 copy-done.8
  150.7 0.1 copy.16.gates_ref
  150.8 0.0 copy-start.5
  150.8 1.0 copy-done.5
  151.8 1.7 shard_map.98
  153.5 0.6 copy.18
  154.1 33.4 %all-to-all-done.3 = bf16[16,24,2048]{2,1,0:T(8,128)(2,1)S(1)} async-done(((bf16[16,24,2048]{2,1,0:T(8,128)(2,1)}), bf16[16,24,2048]{2,1,0:T(8,128)(2,1)S(1)}, u32[]{:S(2)}, u32[]{:S(2)}) %all-to-all-start.3) | async-done | bytes 1572896 | tf_op jit(solution)/shard_map/all_to_all | solution.py:253
  187.5 1.5 shard_map.101
  (1 shorter events, 0.0 us)
Async XLA Ops:
  0.6 32.8 %collective-permute-start = (bf16[2048,384]{1,0:T(8,128)(2,1)}, bf16[2048,384]{1,0:T(8,128)(2,1)S(1)}, u32[]{:S(2)}, u32[]{:S(2)}) collective-permute-start(bf16[2048,384]{1,0:T(8,128)(2,1)} %bitcast.19), channel_id=1, source_target_pairs={{0,16},{1,0},{2,18},{3,2},{4,20},{5,4},{6,22},{7,6},{8,24},{9,8},{... | collective-permute-start | bytes 4718600 | tf_op jit(solution)/shard_map/ppermute | solution.py:242
  3.6 57.9 %collective-permute-start.2 = (bf16[2048,384]{1,0:T(8,128)(2,1)}, bf16[2048,384]{1,0:T(8,128)(2,1)}, u32[]{:S(2)}, u32[]{:S(2)}) collective-permute-start(bf16[2048,384]{1,0:T(8,128)(2,1)} %bitcast.20), channel_id=1, source_target_pairs={{0,16},{1,0},{2,18},{3,2},{4,20},{5,4},{6,22},{7,6},{8,24},{9,8},{... | collective-permute-start | bytes 4718600 | tf_op jit(solution)/shard_map/ppermute | solution.py:242
  4.4 1.0 copy-start.7
  7.7 25.8 %copy-start.4 = (bf16[128,2048]{1,0:T(8,128)(2,1)S(1)}, bf16[128,2048]{1,0:T(8,128)(2,1)}, u32[]{:S(2)}) copy-start(bf16[128,2048]{1,0:T(8,128)(2,1)} %rows_ref.1) | copy-start | bytes 1572868
  7.7 47.9 %all-to-all-start = ((bf16[16,24,2048]{2,1,0:T(8,128)(2,1)}), bf16[16,24,2048]{2,1,0:T(8,128)(2,1)}, u32[]{:S(2)}, u32[]{:S(2)}) async-start(bf16[16,24,2048]{2,1,0:T(8,128)(2,1)} %bitcast.1), calls=%async_computation | async-start | bytes 3145728 | tf_op jit(solution)/shard_map/all_to_all | solution.py:253
  33.5 27.9 %copy-start.6 = (bf16[2048,384]{1,0:T(8,128)(2,1)}, bf16[2048,384]{1,0:T(8,128)(2,1)S(1)}, u32[]{:S(2)}) copy-start(bf16[2048,384]{1,0:T(8,128)(2,1)S(1)} %collective-permute-done.refs_0_._.refs_6_) | copy-start | bytes 4718596
  55.6 42.7 %all-to-all-start.2 = ((bf16[8,48,2048]{2,1,0:T(8,128)(2,1)}), bf16[8,48,2048]{2,1,0:T(8,128)(2,1)}, u32[]{:S(2)}, u32[]{:S(2)}) async-start(bf16[8,48,2048]{2,1,0:T(8,128)(2,1)} %bitcast.8), calls=%async_computation.2 | async-start | bytes 3145728 | tf_op jit(solution)/shard_map/all_to_all | solution.py:259
  61.4 4.8 %collective-permute-start.1 = (bf16[2048,384]{1,0:T(8,128)(2,1)S(1)}, bf16[2048,384]{1,0:T(8,128)(2,1)S(1)}, u32[]{:S(2)}, u32[]{:S(2)}) collective-permute-start(bf16[2048,384]{1,0:T(8,128)(2,1)S(1)} %collective-permute-done.refs_0_._.refs_6_), channel_id=1, source_target_pairs={{0,1},{1,0},{2,3},{3,2},{4,5},{5,4},{6,7},{7,6},{8,9},{9,8},{10,11... | collective-permute-start | bytes 4718600 | tf_op jit(solution)/shard_map/ppermute | solution.py:248
  61.5 5.9 %collective-permute-start.3 = (bf16[2048,384]{1,0:T(8,128)(2,1)}, bf16[2048,384]{1,0:T(8,128)(2,1)S(1)}, u32[]{:S(2)}, u32[]{:S(2)}) collective-permute-start(bf16[2048,384]{1,0:T(8,128)(2,1)} %collective-permute-done.2.refs_2_.refs_8_), channel_id=1, source_target_pairs={{0,1},{1,0},{2,3},{3,2},{4,5},{5,4},{6,7},{7,6},{8,9},{9,8},{10,11... | collective-permute-start | bytes 4718600 | tf_op jit(solution)/shard_map/ppermute | solution.py:248
  62.0 20.7 %collective-permute-start.4 = (bf16[384,2048]{1,0:T(8,128)(2,1)}, bf16[384,2048]{1,0:T(8,128)(2,1)S(1)}, u32[]{:S(2)}, u32[]{:S(2)}) collective-permute-start(bf16[384,2048]{1,0:T(8,128)(2,1)} %bitcast.21), channel_id=1, source_target_pairs={{0,16},{1,0},{2,18},{3,2},{4,20},{5,4},{6,22},{7,6},{8,24},{9,8},{... | collective-permute-start | bytes 4718600 | tf_op jit(solution)/shard_map/ppermute | solution.py:242
  66.2 1.2 copy-start.9
  67.4 1.2 copy-start.10
  82.7 1.2 copy-start
  83.9 17.1 %collective-permute-start.5 = (bf16[384,2048]{1,0:T(8,128)(2,1)}, bf16[384,2048]{1,0:T(8,128)(2,1)S(1)}, u32[]{:S(2)}, u32[]{:S(2)}) collective-permute-start(bf16[384,2048]{1,0:T(8,128)(2,1)} %shard_map.96.refs_0_.refs_2_), channel_id=1, source_target_pairs={{0,1},{1,0},{2,3},{3,2},{4,5},{5,4},{6,7},{7,6},{8,9},{9,8},{10,11... | collective-permute-start | bytes 4718600 | tf_op jit(solution)/shard_map/ppermute | solution.py:248
  98.3 2.7 %copy-start.1 = (bf16[384,2048]{1,0:T(8,128)(2,1)S(1)}, bf16[384,2048]{1,0:T(8,128)(2,1)}, u32[]{:S(2)}) copy-start(bf16[384,2048]{1,0:T(8,128)(2,1)} %shard_map.96.refs_0_.refs_2_) | copy-start | bytes 4718596
  98.3 2.7 %copy-start.2 = (bf16[1,384,768]{2,1,0:T(8,128)(2,1)S(1)}, bf16[1,384,768]{2,1,0:T(8,128)(2,1)}, u32[]{:S(2)}) copy-start(bf16[1,384,768]{2,1,0:T(8,128)(2,1)} %get-tuple-element.13.after_ref.hidden_ref) | copy-start | bytes 1769476
  100.9 29.5 %collective-permute-start.6 = (bf16[192,2048]{1,0:T(8,128)(2,1)S(1)}, bf16[192,2048]{1,0:T(8,128)(2,1)S(1)}, u32[]{:S(2)}, u32[]{:S(2)}) collective-permute-start(bf16[192,2048]{1,0:T(8,128)(2,1)S(1)} %bitcast.18), channel_id=1, source_target_pairs={{0,16},{16,0},{1,17},{17,1},{2,18},{18,2},{3,19},{19,3},{4,20},{20... | collective-permute-start | bytes 2359304 | tf_op jit(solution)/shard_map/ppermute | solution.py:265
  101.0 3.3 %copy-start.3 = (bf16[384,2048]{1,0:T(8,128)(2,1)}, bf16[384,2048]{1,0:T(8,128)(2,1)S(1)}, u32[]{:S(2)}) copy-start(bf16[384,2048]{1,0:T(8,128)(2,1)S(1)} %collective-permute-done.5.refs_1_.refs_3_) | copy-start | bytes 4718596
  104.2 42.3 %all-to-all-start.1 = ((bf16[16,24,2048]{2,1,0:T(8,128)(2,1)}), bf16[16,24,2048]{2,1,0:T(8,128)(2,1)S(1)}, u32[]{:S(2)}, u32[]{:S(2)}) async-start(bf16[16,24,2048]{2,1,0:T(8,128)(2,1)} %bitcast.6), calls=%async_computation.1 | async-start | bytes 3145728 | tf_op jit(solution)/shard_map/all_to_all | solution.py:253
  130.4 0.9 copy-start.11
  146.6 4.1 %copy-start.8 = (f32[128,2]{0,1:T(2,128)S(1)}, f32[128,2]{0,1:T(2,128)}, u32[]{:S(2)}) copy-start(f32[128,2]{0,1:T(2,128)} %param.10) | copy-start | bytes 3076
  146.6 41.0 %all-to-all-start.3 = ((bf16[16,24,2048]{2,1,0:T(8,128)(2,1)}), bf16[16,24,2048]{2,1,0:T(8,128)(2,1)S(1)}, u32[]{:S(2)}, u32[]{:S(2)}) async-start(bf16[16,24,2048]{2,1,0:T(8,128)(2,1)} %bitcast.16), calls=%async_computation.3 | async-start | bytes 3145728 | tf_op jit(solution)/shard_map/all_to_all | solution.py:253
  150.8 1.0 copy-start.5

commit v9 on v8

--- a/solution.py
+++ b/solution.py
@@ -59,7 +59,7 @@
     ).astype(F32)
     rank = dot(earlier.astype(BF16), chosen.astype(BF16), (1, 0))
     slot_numbers = lax.broadcasted_iota(jnp.int32, (tok_rows, slots), 1)
-    total, near = None, None
+    near = None
     for k in range(top_count):
         own = jnp.sum(jnp.where(named[k], rank, 0.0), axis=1, keepdims=True).astype(jnp.int32)
         mark, near_mark = (
@@ -67,12 +67,11 @@
             for order in (lanes, near_lanes)
         )
         place_ref[k * tok_rows : (k + 1) * tok_rows, :] = mark.astype(BF16)
-        total = mark if total is None else total + mark
         near = near_mark if near is None else near + near_mark
-    near_ref[...] = near.astype(BF16)
-    total = total.astype(BF16)
+    near = near.astype(BF16)
+    near_ref[...] = near
     for columns in tiles(width):
-        slots_ref[:, columns] = dot(total, tokens_ref[:, columns], (0, 0)).astype(BF16)
+        slots_ref[:, columns] = dot(near, tokens_ref[:, columns], (0, 0)).astype(BF16)
 
 
 def spread_kernel(near_ref, rows_ref, _, slots_ref):
@@ -80,18 +79,35 @@
         slots_ref[:, columns] = dot(near_ref[...], rows_ref[:, columns], (0, 0)).astype(BF16)
 
 
-def hidden_kernel(parts, joined, rows_ref, *refs):
-    sources, refs = [rows_ref, *refs[: 2 * parts]], refs[2 * parts :]
+def cut_kernel(parts, rows_ref, *refs):
+    out_refs, sems = refs[-1 - parts : -1], refs[-1]
+    sets = rows_ref.shape[0]
+    for copy in fetch(
+        [rows_ref.at[q, i] for i in range(parts) for q in range(sets)],
+        [out_refs[i].at[q] for i in range(parts) for q in range(sets)],
+        sems,
+    ):
+        copy.wait()
+
+
+def by_plane(rows_ref, plane_ref, parts):
+    size = rows_ref.shape[0] // parts
+    starts = [lax.rem(plane_ref[0] + (parts - i), parts) * size for i in range(parts)]
+    return [rows_ref.at[pl.ds(pl.multiple_of(start, size), size)] for start in starts]
+
+
+def hidden_kernel(parts, joined, plane_ref, *refs):
+    sources, refs = refs[: 3 * parts], refs[3 * parts :]
     outs, (sems, out_sems), refs = refs[:3], refs[3:5], refs[5:]
     hidden_ref, by_gate_ref, by_up_ref, rows_ref, gate_ref, up_ref = refs
     gate, up = shares(gate_ref, parts, joined), shares(up_ref, parts, joined)
-    copies = fetch(sources, [rows_ref, *gate, *up], sems)
-    for copy in copies[: 1 + parts]:
+    copies = fetch(sources, [*by_plane(rows_ref, plane_ref, parts), *gate, *up], sems)
+    for copy in copies[: 2 * parts]:
         copy.wait()
     for i in range(gate_ref.shape[0]):
         pre_gate = dot(rows_ref[...], gate_ref[i], (1, 0))
         if i == 0:
-            for copy in copies[1 + parts :]:
+            for copy in copies[2 * parts :]:
                 copy.wait()
         pre_up = dot(rows_ref[...], up_ref[i], (1, 0))
         sig = jax.nn.sigmoid(pre_gate)
@@ -134,21 +150,16 @@
         copy.wait()
 
 
-def backward_kernel(parts, joined, plane_ref, _, *refs):
+def backward_kernel(parts, joined, plane_ref, *refs):
     sources, refs = refs[: 2 + 4 * parts], refs[2 + 4 * parts :]
     out_ref, sems, out_sems, back_gate_ref, back_up_ref, stage_ref, rows_ref = refs[:7]
     down_ref, by_gate_ref, by_up_ref, gate_ref, up_ref = refs[7:]
-    share = rows_ref.shape[0] // parts
-    places = [
-        rows_ref.at[pl.ds(pl.multiple_of((plane_ref[0] + parts - i) % parts * share, share), share)]
-        for i in range(parts)
-    ]
     down, gate, up = (
         shares(down_ref, parts, joined, 0),
         shares(gate_ref, parts, joined),
         shares(up_ref, parts, joined),
     )
-    copies = fetch(sources, [*places, *down, by_gate_ref, by_up_ref, *gate, *up], sems)
+    copies = fetch(sources, [*by_plane(rows_ref, plane_ref, parts), *down, by_gate_ref, by_up_ref, *gate, *up], sems)
     for copy in copies[: 2 + 2 * parts]:
         copy.wait()
     for i in range(down_ref.shape[0]):
@@ -248,23 +259,30 @@
             held.append(lax.ppermute(own, "expert", turn))
         return held
 
-    def exchange(rows):
+    def dispatch(rows, after=()):
+        rows = rows.reshape(sets, parts * capacity, width)
+        rows = lax.all_to_all(rows, axes, 0, 0, axis_index_groups=in_plane, tiled=True)
+        cut = call(
+            functools.partial(cut_kernel, parts),
+            [jax.ShapeDtypeStruct((sets, capacity, width), BF16)] * parts,
+            0,
+            [sems(parts * sets)],
+            far=range(1 + len(after)),
+            far_out=True,
+        )(rows.reshape(sets, parts, capacity, width), *after)
+        crossed = []
+        for i, rows in enumerate(cut):
+            rows = rows.reshape(sets * capacity, width)
+            if i > 0:
+                rows = lax.ppermute(rows, "dp", [(g, (g + i) % parts) for g in range(parts)])
+            crossed.append(rows)
+        return crossed
+
+    def send_back(rows):
         rows = rows.reshape(experts, capacity, width)
         return lax.all_to_all(
             rows, axes, 0, 0, axis_index_groups=everywhere, tiled=True
         ).reshape(slots, width)
-
-    def exchange_late(rows):
-        rows = rows.reshape(sets, parts * capacity, width)
-        rows = lax.all_to_all(rows, axes, 0, 0, axis_index_groups=in_plane, tiled=True)
-        rows = rows.reshape(sets, parts, capacity, width)
-        crossed = []
-        for i in range(parts):
-            share = rows[:, i].reshape(sets * capacity, width)
-            if i > 0:
-                share = lax.ppermute(share, "dp", [(g, (g + i) % parts) for g in range(parts)])
-            crossed.append(share)
-        return crossed
 
     spread_flops = 2 * slots * tok_rows * width
     dot_flops = 2 * slots * width * hidden * parts
@@ -293,21 +311,20 @@
         [slot_shape, place_shape, jax.ShapeDtypeStruct((tok_rows, slots), BF16)],
         spread_flops,
     )(plane, routes, tokens)
-    x_rows = exchange(x_slots)
+    x_shares = dispatch(x_slots)
     (dy_slots,) = call(spread_kernel, [slot_shape], 256 * spread_flops, far=(2,))(
         near, cotangent, gate_own
     )
-    dy_shares = exchange_late(dy_slots)
     hidden_rows, by_gate, by_up = call(
         functools.partial(hidden_kernel, parts, joined),
         [hidden_shape, unit_shape, unit_shape],
         2 * dot_flops,
-        [sems(1 + 2 * parts), sems(3), hidden_scratch, unit_scratch, unit_scratch, row_scratch]
+        [sems(3 * parts), sems(3), hidden_scratch, unit_scratch, unit_scratch, row_scratch]
         + [in_scratch] * 2,
-        far=range(1 + 2 * parts),
+        far=range(1, 1 + 3 * parts),
         far_out=True,
         vmem=LARGE_VMEM,
-    )(x_rows, *gate_w, *up_w)
+    )(plane, *x_shares, *gate_w, *up_w)
     (down_own,) = call(
         in_place_kernel, [down_own], 0, far=range(2), far_out=True, vmem=LARGE_VMEM, aliases={0: 0}
     )(down_own, hidden_rows)
@@ -320,7 +337,8 @@
         far=range(1 + parts),
         far_out=True,
     )(hidden_rows, *down_w)
-    out_slots = exchange(out_rows)
+    dy_shares = dispatch(dy_slots, (out_rows,))
+    out_slots = send_back(out_rows)
     (grad_rows,) = call(
         functools.partial(backward_kernel, parts, joined),
         [slot_shape],
@@ -328,11 +346,11 @@
         [sems(2 + 4 * parts), sems(pieces), hidden_scratch, hidden_scratch]
         + [row_scratch, row_scratch, down_scratch, unit_scratch, unit_scratch]
         + [in_scratch] * 2,
-        far=range(1, 4 + 4 * parts),
+        far=range(1, 3 + 4 * parts),
         far_out=True,
         vmem=LARGE_VMEM,
-    )(plane, out_rows, *dy_shares, *down_w, by_gate, by_up, *gate_w, *up_w)
-    grad_slots = exchange(grad_rows)
+    )(plane, *dy_shares, *down_w, by_gate, by_up, *gate_w, *up_w)
+    grad_slots = send_back(grad_rows)
     mixed, gate_grad = call(
         mix_kernel, [token_shape, jax.ShapeDtypeStruct(gates.shape, F32)], 2 * spread_flops
     )(place, gates, cotangent, out_slots)

time: 190 us -> 185 us (0.974)
  waiting for transfers between devices: 124 us -> 119 us
  Pallas kernels: 26.6 us -> 30.5 us
  starting transfers between devices: 27.3 us -> 24.3 us
    all_to_all x4, waiting for transfers between devices: 74.8 us -> 48.2 us  [the longest x2 37.5 us: send_back(): lax.all_to_all(rows, axes, 0, 0, axis_index_groups=everywhere, tiled=True)]
    ppermute x1 -> x2, waiting for transfers between devices: 21 us -> 42.6 us  [dispatch(): lax.ppermute(rows, 'dp', [(g, (g + i) % parts) for g in range(parts)])]
    pallas_call x8 -> x10, Pallas kernels: 26.6 us -> 30.5 us  [run(): pl.pallas_call(kernel, out_shape=tuple((jax.ShapeDtypeStruct(o.shape, o.d...]
    slice x1 -> x0, local copies, waits for them, and re-layouts: 2.57 us -> none  [exchange_late(): share = rows[:, i].reshape(sets * capacity, width)]
    ppermute x3, starting transfers between devices: 5.51 us -> 3.05 us  [swapped(): return lax.ppermute(weight[0], axes, swap)]
    unnamed x27 -> x25, local copies, waits for them, and re-layouts: 8.08 us -> 9.59 us
  transfers between devices with their start and end apart: 11 -> 12, of which waited for: 8 -> 8; matrix products, arithmetic and copies ran while one was open for 2% -> 1% of each run, Pallas kernels for 13% -> 15%
where the time goes in v9:
time: 185 us
  waiting for transfers between devices  119 us (64%)
  Pallas kernels  30.5 us (16%)
  starting transfers between devices  24.3 us (13%)
  local copies, waits for them, and re-layouts  9.59 us (5%)
    ppermute x2, waiting for transfers between devices, dispatch(): lax.ppermute(rows, 'dp', [(g, (g + i) % parts) for g in range(parts)])  42.6 us
    all_to_all x2, waiting for transfers between devices, send_back(): lax.all_to_all(rows, axes, 0, 0, axis_index_groups=everywhere, tiled=True)  37.5 us
    pallas_call x10, Pallas kernels, run(): pl.pallas_call(kernel, out_shape=tuple((jax.ShapeDtypeStruct(o.shape, o.d...  30.5 us
    ppermute x3, waiting for transfers between devices, swapped(): return lax.ppermute(weight[0], axes, swap)  25.1 us
    all_to_all x2, starting transfers between devices, send_back(): lax.all_to_all(rows, axes, 0, 0, axis_index_groups=everywhere, tiled=True)  11.1 us
    all_to_all x2, waiting for transfers between devices, dispatch(): lax.all_to_all(rows, axes, 0, 0, axis_index_groups=in_plane, tiled=True)  10.7 us
    unnamed x25, local copies, waits for them, and re-layouts  9.59 us
    all_to_all x2, starting transfers between devices, dispatch(): lax.all_to_all(rows, axes, 0, 0, axis_index_groups=in_plane, tiled=True)  9.57 us
  transfers between devices with their start and end apart: 12, of which 8 were waited for; matrix products, arithmetic and copies ran while one was open for 1% of the time, Pallas kernels for 15%

profile of v9, /device:TPU:0, one launch (start us, length us, event | category | flops | bytes accessed | tf_op | source)
XLA Modules:
  0.0 184.6 jit_solution(13607542602745790636)
XLA Ops:
  0.6 3.0 %collective-permute-start.1 = (bf16[2048,384]{1,0:T(8,128)(2,1)}, bf16[2048,384]{1,0:T(8,128)(2,1)}, u32[]{:S(2)}, u32[]{:S(2)}) collective-permute-start(bf16[2048,384]{1,0:T(8,128)(2,1)} %bitcast.26), channel_id=1, source_target_pairs={{0,16},{1,0},{2,18},{3,2},{4,20},{5,4},{6,22},{7,6},{8,24},{9,8},{... | collective-permute-start | bytes 4718600 | tf_op jit(solution)/shard_map/ppermute | solution.py:253
  3.6 0.0 collective-permute-start.3
  3.7 0.8 copy.11.routes_ref
  4.4 0.0 copy-start.7
  4.4 1.0 copy-done.7
  5.5 2.2 %shard_map.94 = (bf16[384,2048]{1,0:T(8,128)(2,1)}, bf16[256,384]{1,0:T(8,128)(2,1)S(1)}, bf16[128,384]{1,0:T(8,128)(2,1)S(1)}) custom-call(s32[1]{0:T(128)} %bitcast.plane_ref, s32[128,2]{1,0:T(8,128)S(1)} %copy.11.routes_ref, bf16[128,2048]{1,0:T(8,128)(2,1)S(1)} %copy-done.7), custom_call_target="tpu_custom_call" | custom-call | flops 201326592 | bytes 2393092 | tf_op jit(solution)/shard_map/pallas_call | solution.py:212
  7.7 0.0 copy-start.3
  7.7 5.9 %all-to-all-start = ((bf16[8,48,2048]{2,1,0:T(8,128)(2,1)}), bf16[8,48,2048]{2,1,0:T(8,128)(2,1)S(1)}, u32[]{:S(2)}, u32[]{:S(2)}) async-start(bf16[8,48,2048]{2,1,0:T(8,128)(2,1)} %bitcast.1), calls=%async_computation | async-start | bytes 3145728 | tf_op jit(solution)/shard_map/all_to_all | solution.py:264
  13.6 0.0 collective-permute-start.5
  13.6 8.2 %collective-permute-done.1.refs_2_._.refs_6_ = bf16[2048,384]{1,0:T(8,128)(2,1)} collective-permute-done((bf16[2048,384]{1,0:T(8,128)(2,1)}, bf16[2048,384]{1,0:T(8,128)(2,1)}, u32[]{:S(2)}, u32[]{:S(2)}) %collective-permute-start.1) | collective-permute-done | bytes 1572896 | tf_op jit(solution)/shard_map/ppermute | solution.py:253
  21.9 0.0 collective-permute-start.2
  21.9 16.8 %collective-permute-done.3.refs_4_.refs_8_ = bf16[2048,384]{1,0:T(8,128)(2,1)} collective-permute-done((bf16[2048,384]{1,0:T(8,128)(2,1)}, bf16[2048,384]{1,0:T(8,128)(2,1)}, u32[]{:S(2)}, u32[]{:S(2)}) %collective-permute-start.3) | collective-permute-done | bytes 1572896 | tf_op jit(solution)/shard_map/ppermute | solution.py:253
  38.7 0.0 collective-permute-start.4
  38.7 0.0 copy-done.3
  38.7 0.6 shard_map.100
  39.3 0.0 copy-start.1
  39.3 1.2 copy-done.1
  40.6 10.7 %all-to-all-done = bf16[8,48,2048]{2,1,0:T(8,128)(2,1)S(1)} async-done(((bf16[8,48,2048]{2,1,0:T(8,128)(2,1)}), bf16[8,48,2048]{2,1,0:T(8,128)(2,1)S(1)}, u32[]{:S(2)}, u32[]{:S(2)}) %all-to-all-start) | async-done | bytes 1572896 | tf_op jit(solution)/shard_map/all_to_all | solution.py:264
  51.2 3.6 %all-to-all-start.2 = ((bf16[8,48,2048]{2,1,0:T(8,128)(2,1)}), bf16[8,48,2048]{2,1,0:T(8,128)(2,1)S(1)}, u32[]{:S(2)}, u32[]{:S(2)}) async-start(bf16[8,48,2048]{2,1,0:T(8,128)(2,1)} %bitcast.20), calls=%async_computation.2 | async-start | bytes 3145728 | tf_op jit(solution)/shard_map/all_to_all | solution.py:264
  54.9 2.2 %shard_map.95 = (bf16[8,24,2048]{2,1,0:T(8,128)(2,1)S(1)}, bf16[8,24,2048]{2,1,0:T(8,128)(2,1)S(1)}) custom-call(bf16[8,2,24,2048]{3,2,1,0:T(8,128)(2,1)S(1)} %bitcast.17), custom_call_target="tpu_custom_call" | custom-call | bytes 3145728 | tf_op jit(solution)/shard_map/pallas_call | solution.py:212
  57.1 0.0 copy-start.6
  57.1 0.9 copy-done.6
  58.0 0.3 collective-permute-start
  58.2 0.0 collective-permute-done.2.refs_3_.refs_7_
  58.2 0.0 collective-permute-done.4.refs_5_.refs_9_
  58.2 18.9 %collective-permute-done.refs_1_ = bf16[192,2048]{1,0:T(8,128)(2,1)S(1)} collective-permute-done((bf16[192,2048]{1,0:T(8,128)(2,1)S(1)}, bf16[192,2048]{1,0:T(8,128)(2,1)S(1)}, u32[]{:S(2)}, u32[]{:S(2)}) %collective-permute-start) | collective-permute-done | bytes 786464 | tf_op jit(solution)/shard_map/ppermute | solution.py:277
  77.2 0.0 copy-start.10
  77.2 0.9 copy-done.10
  78.1 7.6 %shard_map.96 = (bf16[1,384,768]{2,1,0:T(8,128)(2,1)}, f32[1,384,768]{2,1,0:T(8,128)}, f32[1,384,768]{2,1,0:T(8,128)}) custom-call(s32[1]{0:T(128)} %bitcast.plane_ref, bf16[192,2048]{1,0:T(8,128)(2,1)} %bitcast.22, bf16[192,2048]{1,0:T(8,128)(2,1)} %copy-done.10, bf16[2048,384]{1,0:T(8,128)(2,1)} %collective-permute-done.1.refs_2_._.refs_6_, ...), custom_call_target="tpu_custom_call" | custom-call | flops 2415919104 | bytes 10813444 | tf_op jit(solution)/shard_map/pallas_call | solution.py:212
  85.7 0.0 collective-permute-done.5._
  85.7 0.0 copy-start
  85.7 0.1 collective-permute-start.6
  85.8 3.6 %collective-permute-done.6.refs_1_.refs_3_ = bf16[384,2048]{1,0:T(8,128)(2,1)S(1)} collective-permute-done((bf16[384,2048]{1,0:T(8,128)(2,1)}, bf16[384,2048]{1,0:T(8,128)(2,1)S(1)}, u32[]{:S(2)}, u32[]{:S(2)}) %collective-permute-start.6) | collective-permute-done | bytes 1572896 | tf_op jit(solution)/shard_map/ppermute | solution.py:259
  89.4 0.0 copy-done
  89.4 3.9 %shard_map.98.refs_0_ = bf16[384,2048]{1,0:T(8,128)(2,1)} custom-call(bf16[1,384,768]{2,1,0:T(8,128)(2,1)S(1)} %copy-done, bf16[384,2048]{1,0:T(8,128)(2,1)} %shard_map.97.refs_0_.refs_2_, bf16[384,2048]{1,0:T(8,128)(2,1)S(1)} %collective-permute-done.6.refs_1_.refs_3_), custom_call_target="tpu_custom_call" | custom-call | flops 1207959552 | bytes 5308416 | tf_op jit(solution)/shard_map/pallas_call | solution.py:212
  93.4 0.0 copy-start.2
  93.4 1.2 copy-done.2
  94.5 0.0 all-to-all-done.2
  94.5 2.2 %shard_map.101 = (bf16[8,24,2048]{2,1,0:T(8,128)(2,1)S(1)}, bf16[8,24,2048]{2,1,0:T(8,128)(2,1)S(1)}) custom-call(bf16[8,2,24,2048]{3,2,1,0:T(8,128)(2,1)S(1)} %bitcast.16, bf16[384,2048]{1,0:T(8,128)(2,1)} %shard_map.98.refs_0_), custom_call_target="tpu_custom_call" | custom-call | bytes 4718592 | tf_op jit(solution)/shard_map/pallas_call | solution.py:212
  96.7 0.0 copy-start.5
  96.7 0.9 copy-done.5
  97.6 0.3 collective-permute-start.7
  97.9 7.0 %all-to-all-start.1 = ((bf16[16,24,2048]{2,1,0:T(8,128)(2,1)}), bf16[16,24,2048]{2,1,0:T(8,128)(2,1)S(1)}, u32[]{:S(2)}, u32[]{:S(2)}) async-start(bf16[16,24,2048]{2,1,0:T(8,128)(2,1)} %bitcast.8), calls=%async_computation.1 | async-start | bytes 3145728 | tf_op jit(solution)/shard_map/all_to_all | solution.py:283
  104.9 23.6 %collective-permute-done.7.refs_1_ = bf16[192,2048]{1,0:T(8,128)(2,1)S(1)} collective-permute-done((bf16[192,2048]{1,0:T(8,128)(2,1)S(1)}, bf16[192,2048]{1,0:T(8,128)(2,1)S(1)}, u32[]{:S(2)}, u32[]{:S(2)}) %collective-permute-start.7) | collective-permute-done | bytes 786464 | tf_op jit(solution)/shard_map/ppermute | solution.py:277
  128.5 0.0 copy-start.9
  128.5 0.9 copy-done.9
  129.4 8.6 %shard_map.102 = bf16[384,2048]{1,0:T(8,128)(2,1)} custom-call(s32[1]{0:T(128)} %bitcast.plane_ref, bf16[192,2048]{1,0:T(8,128)(2,1)} %bitcast.21, bf16[192,2048]{1,0:T(8,128)(2,1)} %copy-done.9, bf16[384,2048]{1,0:T(8,128)(2,1)} %shard_map.97.refs_0_.refs_2_, bf16[384,2048]{1,0:T(8,128)(2,1)} %copy-done.2, f32[1,384,768]{2,1,0:T(8,128)} %get-tuple-element.24.refs_4_, ...), custom_call_target="tpu_custom_call" | custom-call | flops 77309411328 | bytes 14942212 | tf_op jit(solution)/shard_map/pallas_call | solution.py:212
  138.1 4.1 %all-to-all-done.1 = bf16[16,24,2048]{2,1,0:T(8,128)(2,1)S(1)} async-done(((bf16[16,24,2048]{2,1,0:T(8,128)(2,1)}), bf16[16,24,2048]{2,1,0:T(8,128)(2,1)S(1)}, u32[]{:S(2)}, u32[]{:S(2)}) %all-to-all-start.1) | async-done | bytes 1572896 | tf_op jit(solution)/shard_map/all_to_all | solution.py:283
  142.2 0.0 copy-start.8
  142.2 4.1 %all-to-all-start.3 = ((bf16[16,24,2048]{2,1,0:T(8,128)(2,1)}), bf16[16,24,2048]{2,1,0:T(8,128)(2,1)S(1)}, u32[]{:S(2)}, u32[]{:S(2)}) async-start(bf16[16,24,2048]{2,1,0:T(8,128)(2,1)} %bitcast.25), calls=%async_computation.3 | async-start | bytes 3145728 | tf_op jit(solution)/shard_map/all_to_all | solution.py:283
  146.3 0.0 copy-done.8
  146.3 0.1 copy.12.gates_ref
  146.4 0.0 copy-start.4
  146.4 1.0 copy-done.4
  147.5 1.7 shard_map.99
  149.1 0.6 copy.14
  149.8 33.4 %all-to-all-done.3 = bf16[16,24,2048]{2,1,0:T(8,128)(2,1)S(1)} async-done(((bf16[16,24,2048]{2,1,0:T(8,128)(2,1)}), bf16[16,24,2048]{2,1,0:T(8,128)(2,1)S(1)}, u32[]{:S(2)}, u32[]{:S(2)}) %all-to-all-start.3) | async-done | bytes 1572896 | tf_op jit(solution)/shard_map/all_to_all | solution.py:283
  183.1 1.5 shard_map.103
  (1 shorter events, 0.0 us)
Async XLA Ops:
  0.6 21.2 %collective-permute-start.1 = (bf16[2048,384]{1,0:T(8,128)(2,1)}, bf16[2048,384]{1,0:T(8,128)(2,1)}, u32[]{:S(2)}, u32[]{:S(2)}) collective-permute-start(bf16[2048,384]{1,0:T(8,128)(2,1)} %bitcast.26), channel_id=1, source_target_pairs={{0,16},{1,0},{2,18},{3,2},{4,20},{5,4},{6,22},{7,6},{8,24},{9,8},{... | collective-permute-start | bytes 4718600 | tf_op jit(solution)/shard_map/ppermute | solution.py:253
  3.6 35.1 %collective-permute-start.3 = (bf16[2048,384]{1,0:T(8,128)(2,1)}, bf16[2048,384]{1,0:T(8,128)(2,1)}, u32[]{:S(2)}, u32[]{:S(2)}) collective-permute-start(bf16[2048,384]{1,0:T(8,128)(2,1)} %bitcast.27), channel_id=1, source_target_pairs={{0,16},{1,0},{2,18},{3,2},{4,20},{5,4},{6,22},{7,6},{8,24},{9,8},{... | collective-permute-start | bytes 4718600 | tf_op jit(solution)/shard_map/ppermute | solution.py:253
  4.4 1.0 copy-start.7
  7.7 31.1 %copy-start.3 = (bf16[128,2048]{1,0:T(8,128)(2,1)S(1)}, bf16[128,2048]{1,0:T(8,128)(2,1)}, u32[]{:S(2)}) copy-start(bf16[128,2048]{1,0:T(8,128)(2,1)} %rows_ref.1) | copy-start | bytes 1572868
  7.7 43.6 %all-to-all-start = ((bf16[8,48,2048]{2,1,0:T(8,128)(2,1)}), bf16[8,48,2048]{2,1,0:T(8,128)(2,1)S(1)}, u32[]{:S(2)}, u32[]{:S(2)}) async-start(bf16[8,48,2048]{2,1,0:T(8,128)(2,1)} %bitcast.1), calls=%async_computation | async-start | bytes 3145728 | tf_op jit(solution)/shard_map/all_to_all | solution.py:264
  13.6 72.1 %collective-permute-start.5 = (bf16[384,2048]{1,0:T(8,128)(2,1)}, bf16[384,2048]{1,0:T(8,128)(2,1)}, u32[]{:S(2)}, u32[]{:S(2)}) collective-permute-start(bf16[384,2048]{1,0:T(8,128)(2,1)} %bitcast.28), channel_id=1, source_target_pairs={{0,16},{1,0},{2,18},{3,2},{4,20},{5,4},{6,22},{7,6},{8,24},{9,8},{... | collective-permute-start | bytes 4718600 | tf_op jit(solution)/shard_map/ppermute | solution.py:253
  21.9 36.4 %collective-permute-start.2 = (bf16[2048,384]{1,0:T(8,128)(2,1)}, bf16[2048,384]{1,0:T(8,128)(2,1)}, u32[]{:S(2)}, u32[]{:S(2)}) collective-permute-start(bf16[2048,384]{1,0:T(8,128)(2,1)} %collective-permute-done.1.refs_2_._.refs_6_), channel_id=1, source_target_pairs={{0,1},{1,0},{2,3},{3,2},{4,5},{5,4},{6,7},{7,6},{8,9},{9,8},{10,11... | collective-permute-start | bytes 4718600 | tf_op jit(solution)/shard_map/ppermute | solution.py:259
  38.7 19.5 %collective-permute-start.4 = (bf16[2048,384]{1,0:T(8,128)(2,1)}, bf16[2048,384]{1,0:T(8,128)(2,1)}, u32[]{:S(2)}, u32[]{:S(2)}) collective-permute-start(bf16[2048,384]{1,0:T(8,128)(2,1)} %collective-permute-done.3.refs_4_.refs_8_), channel_id=1, source_target_pairs={{0,1},{1,0},{2,3},{3,2},{4,5},{5,4},{6,7},{7,6},{8,9},{9,8},{10,11... | collective-permute-start | bytes 4718600 | tf_op jit(solution)/shard_map/ppermute | solution.py:259
  39.3 1.2 copy-start.1
  51.2 43.3 %all-to-all-start.2 = ((bf16[8,48,2048]{2,1,0:T(8,128)(2,1)}), bf16[8,48,2048]{2,1,0:T(8,128)(2,1)S(1)}, u32[]{:S(2)}, u32[]{:S(2)}) async-start(bf16[8,48,2048]{2,1,0:T(8,128)(2,1)} %bitcast.20), calls=%async_computation.2 | async-start | bytes 3145728 | tf_op jit(solution)/shard_map/all_to_all | solution.py:264
  57.1 0.9 copy-start.6
  58.0 19.2 %collective-permute-start = (bf16[192,2048]{1,0:T(8,128)(2,1)S(1)}, bf16[192,2048]{1,0:T(8,128)(2,1)S(1)}, u32[]{:S(2)}, u32[]{:S(2)}) collective-permute-start(bf16[192,2048]{1,0:T(8,128)(2,1)S(1)} %bitcast.23), channel_id=1, source_target_pairs={{0,16},{16,0},{1,17},{17,1},{2,18},{18,2},{3,19},{19,3},{4,20},{20... | collective-permute-start | bytes 2359304 | tf_op jit(solution)/shard_map/ppermute | solution.py:277
  77.2 0.9 copy-start.10
  85.7 3.7 %copy-start = (bf16[1,384,768]{2,1,0:T(8,128)(2,1)S(1)}, bf16[1,384,768]{2,1,0:T(8,128)(2,1)}, u32[]{:S(2)}) copy-start(bf16[1,384,768]{2,1,0:T(8,128)(2,1)} %get-tuple-element.19.after_ref.hidden_ref) | copy-start | bytes 1769476
  85.7 3.7 %collective-permute-start.6 = (bf16[384,2048]{1,0:T(8,128)(2,1)}, bf16[384,2048]{1,0:T(8,128)(2,1)S(1)}, u32[]{:S(2)}, u32[]{:S(2)}) collective-permute-start(bf16[384,2048]{1,0:T(8,128)(2,1)} %shard_map.97.refs_0_.refs_2_), channel_id=1, source_target_pairs={{0,1},{1,0},{2,3},{3,2},{4,5},{5,4},{6,7},{7,6},{8,9},{9,8},{10,11... | collective-permute-start | bytes 4718600 | tf_op jit(solution)/shard_map/ppermute | solution.py:259
  93.4 1.2 copy-start.2
  96.7 0.9 copy-start.5
  97.6 30.9 %collective-permute-start.7 = (bf16[192,2048]{1,0:T(8,128)(2,1)S(1)}, bf16[192,2048]{1,0:T(8,128)(2,1)S(1)}, u32[]{:S(2)}, u32[]{:S(2)}) collective-permute-start(bf16[192,2048]{1,0:T(8,128)(2,1)S(1)} %bitcast.24), channel_id=1, source_target_pairs={{0,16},{16,0},{1,17},{17,1},{2,18},{18,2},{3,19},{19,3},{4,20},{20... | collective-permute-start | bytes 2359304 | tf_op jit(solution)/shard_map/ppermute | solution.py:277
  97.9 44.3 %all-to-all-start.1 = ((bf16[16,24,2048]{2,1,0:T(8,128)(2,1)}), bf16[16,24,2048]{2,1,0:T(8,128)(2,1)S(1)}, u32[]{:S(2)}, u32[]{:S(2)}) async-start(bf16[16,24,2048]{2,1,0:T(8,128)(2,1)} %bitcast.8), calls=%async_computation.1 | async-start | bytes 3145728 | tf_op jit(solution)/shard_map/all_to_all | solution.py:283
  128.5 0.9 copy-start.9
  142.2 4.1 %copy-start.8 = (f32[128,2]{0,1:T(2,128)S(1)}, f32[128,2]{0,1:T(2,128)}, u32[]{:S(2)}) copy-start(f32[128,2]{0,1:T(2,128)} %param.10) | copy-start | bytes 3076
  142.2 40.9 %all-to-all-start.3 = ((bf16[16,24,2048]{2,1,0:T(8,128)(2,1)}), bf16[16,24,2048]{2,1,0:T(8,128)(2,1)S(1)}, u32[]{:S(2)}, u32[]{:S(2)}) async-start(bf16[16,24,2048]{2,1,0:T(8,128)(2,1)} %bitcast.25), calls=%async_computation.3 | async-start | bytes 3145728 | tf_op jit(solution)/shard_map/all_to_all | solution.py:283
  146.4 1.0 copy-start.4

commit v10 on v9

--- a/solution.py
+++ b/solution.py
@@ -42,41 +42,54 @@
     return [unit_ref.at[0, cut] if axis == 0 else unit_ref.at[0, :, cut] for cut in cuts]
 
 
-def place_kernel(experts, parts, plane_ref, routes_ref, tokens_ref, slots_ref, place_ref, near_ref):
+def place_kernel(sets, parts, here_ref, *refs):
+    route_refs, token_refs, (slots_ref, place_ref, near_ref) = refs[:2], refs[2:4], refs[4:]
     slots, width = slots_ref.shape
-    capacity = slots // experts
-    tok_rows, top_count = routes_ref.shape
-    routes = routes_ref[...]
-    home_plane, home_set = lax.rem(routes + 1, parts), lax.div(routes, parts)
-    lanes = home_plane * (experts // parts) + home_set
-    near_lanes = home_set * parts + lax.rem(home_plane + (parts - plane_ref[0]), parts)
-    numbers = lax.broadcasted_iota(jnp.int32, (tok_rows, experts), 1)
-    named = [numbers == routes[:, k : k + 1] for k in range(top_count)]
-    chosen = sum(n.astype(F32) for n in named)
+    capacity = slots // (2 * sets * parts)
+    tok_rows, top_count = route_refs[0].shape
     earlier = (
         lax.broadcasted_iota(jnp.int32, (tok_rows, tok_rows), 1)
         < lax.broadcasted_iota(jnp.int32, (tok_rows, tok_rows), 0)
-    ).astype(F32)
-    rank = dot(earlier.astype(BF16), chosen.astype(BF16), (1, 0))
+    ).astype(BF16)
     slot_numbers = lax.broadcasted_iota(jnp.int32, (tok_rows, slots), 1)
-    near = None
-    for k in range(top_count):
-        own = jnp.sum(jnp.where(named[k], rank, 0.0), axis=1, keepdims=True).astype(jnp.int32)
-        mark, near_mark = (
-            (slot_numbers == order[:, k : k + 1] * capacity + own).astype(F32)
-            for order in (lanes, near_lanes)
-        )
-        place_ref[k * tok_rows : (k + 1) * tok_rows, :] = mark.astype(BF16)
-        near = near_mark if near is None else near + near_mark
-    near = near.astype(BF16)
-    near_ref[...] = near
+    for block, route_ref in enumerate(route_refs):
+        routes = route_ref[...]
+        home_plane, home_set = lax.rem(routes + 1, parts), lax.div(routes, parts) - here_ref[1]
+        inside = (home_set >= 0) & (home_set < sets)
+        back = home_plane * sets + home_set
+        out = home_set * parts + lax.rem(home_plane + (parts - here_ref[0]), parts)
+        numbers = lax.broadcasted_iota(jnp.int32, (tok_rows, 2 * sets * parts), 1)
+        named = [numbers == routes[:, k : k + 1] for k in range(top_count)]
+        chosen = sum(n.astype(F32) for n in named)
+        rank = dot(earlier, chosen.astype(BF16), (1, 0))
+        near = None
+        for k in range(top_count):
+            own = jnp.sum(jnp.where(named[k], rank, 0.0), axis=1, keepdims=True).astype(jnp.int32)
+            own = own + block * capacity
+            mark, near_mark = (
+                (
+                    slot_numbers
+                    == jnp.where(
+                        inside[:, k : k + 1], lane[:, k : k + 1] * (2 * capacity) + own, slots
+                    )
+                ).astype(F32)
+                for lane in (back, out)
+            )
+            place_ref[block, k] = mark.astype(BF16)
+            near = near_mark if near is None else near + near_mark
+        near_ref[block] = near.astype(BF16)
     for columns in tiles(width):
-        slots_ref[:, columns] = dot(near, tokens_ref[:, columns], (0, 0)).astype(BF16)
-
-
-def spread_kernel(near_ref, rows_ref, _, slots_ref):
-    for columns in tiles(rows_ref.shape[1]):
-        slots_ref[:, columns] = dot(near_ref[...], rows_ref[:, columns], (0, 0)).astype(BF16)
+        slots_ref[:, columns] = sum(
+            dot(near_ref[block], token_refs[block][:, columns], (0, 0)) for block in range(2)
+        ).astype(BF16)
+
+
+def spread_kernel(near_ref, *refs):
+    row_refs, slots_ref = refs[:2], refs[-1]
+    for columns in tiles(slots_ref.shape[1]):
+        slots_ref[:, columns] = sum(
+            dot(near_ref[block], row_refs[block][:, columns], (0, 0)) for block in range(2)
+        ).astype(BF16)
 
 
 def cut_kernel(parts, rows_ref, *refs):
@@ -117,10 +130,6 @@
         by_up_ref[i] = act
     for copy in fetch([hidden_ref, by_gate_ref, by_up_ref], outs, out_sems):
         copy.wait()
-
-
-def in_place_kernel(_, after_ref, out_ref):
-    pass
 
 
 def out_kernel(parts, joined, hidden_ref, *refs):
@@ -180,33 +189,25 @@
         copy.wait()
 
 
-def mix_kernel(place_ref, gates_ref, cotangent_ref, slots_ref, mixed_ref, gate_grad_ref):
-    tok_rows, top_count = gates_ref.shape
+def combine_kernel(block, place_ref, gates_ref, slots_ref, *refs):
+    cotangent_ref, refs = (refs[0], refs[1:]) if len(refs) == 3 else (None, refs)
     total, grads = None, []
-    for k in range(top_count):
-        raw = dot(place_ref[k * tok_rows : (k + 1) * tok_rows, :], slots_ref[...], (1, 0))
-        grads.append(jnp.sum(raw * cotangent_ref[...].astype(F32), axis=1, keepdims=True))
+    for k in range(gates_ref.shape[1]):
+        raw = dot(place_ref[block, k], slots_ref[...], (1, 0))
+        if cotangent_ref is not None:
+            grads.append(jnp.sum(raw * cotangent_ref[...].astype(F32), axis=1, keepdims=True))
         term = raw * gates_ref[:, k : k + 1]
         total = term if total is None else total + term
-    mixed_ref[...] = total.astype(BF16)
-    gate_grad_ref[...] = jnp.concatenate(grads, axis=1)
-
-
-def sum_kernel(place_ref, gates_ref, slots_ref, out_ref):
-    tok_rows, top_count = gates_ref.shape
-    total = None
-    for k in range(top_count):
-        raw = dot(place_ref[k * tok_rows : (k + 1) * tok_rows, :], slots_ref[...], (1, 0))
-        term = raw * gates_ref[:, k : k + 1]
-        total = term if total is None else total + term
-    out_ref[...] = total.astype(BF16)
+    refs[0][...] = total.astype(refs[0].dtype)
+    if grads:
+        refs[1][...] = jnp.concatenate(grads, axis=1)
 
 
 def call(kernel, outs, flops, scratch=(), far=(), far_out=False, vmem=SMALL_VMEM, aliases=None):
     def run(*args):
         moved = sum(a.size * a.dtype.itemsize for a in (*args, *outs))
         spaces = [
-            pltpu.SMEM if a.shape == (1,) else pl.ANY if i in far else pltpu.VMEM
+            pltpu.SMEM if a.ndim == 1 else pl.ANY if i in far else pltpu.VMEM
             for i, a in enumerate(args)
         ]
         return pl.pallas_call(
@@ -231,23 +232,29 @@
     parts, experts = lax.axis_size("dp"), lax.axis_size("expert")
     hidden = w_gate.shape[2]
     capacity = max(2, 3 * tok_rows * top_count // (2 * experts))
-    slots = experts * capacity
+    rows_per_lane = 2 * capacity
+    slots = experts // 2 * rows_per_lane
     axes = ("dp", "expert")
 
     def device(g, j):
         return g * experts + j
 
-    sets = experts // parts
+    sets = experts // parts // 2
 
     def home(e, c):
         return device((e + 1) % parts, e // parts * parts + c)
 
     swap = [(device(g, e), home(e, g)) for g in range(parts) for e in range(experts)]
+    across = [(j, (j + experts // 2) % experts) for j in range(experts)]
     planes = [
-        [[device(g, parts * q + c) for q in range(sets)] for g in range(parts)] for c in range(parts)
+        [
+            [[device(g, parts * (half * sets + q) + c) for q in range(sets)] for g in range(parts)]
+            for half in range(2)
+        ]
+        for c in range(parts)
     ]
-    everywhere = [[d for plane in planes[c] for d in plane] for c in range(parts)]
-    in_plane = [plane for c in range(parts) for plane in planes[c]]
+    everywhere = [[d for plane in half for d in plane] for c in planes for half in c]
+    in_plane = [plane for c in planes for half in c for plane in half]
 
     def swapped(weight):
         return lax.ppermute(weight[0], axes, swap)
@@ -260,26 +267,26 @@
         return held
 
     def dispatch(rows, after=()):
-        rows = rows.reshape(sets, parts * capacity, width)
+        rows = rows.reshape(sets, parts * rows_per_lane, width)
         rows = lax.all_to_all(rows, axes, 0, 0, axis_index_groups=in_plane, tiled=True)
         cut = call(
             functools.partial(cut_kernel, parts),
-            [jax.ShapeDtypeStruct((sets, capacity, width), BF16)] * parts,
+            [jax.ShapeDtypeStruct((sets, rows_per_lane, width), BF16)] * parts,
             0,
             [sems(parts * sets)],
             far=range(1 + len(after)),
             far_out=True,
-        )(rows.reshape(sets, parts, capacity, width), *after)
+        )(rows.reshape(sets, parts, rows_per_lane, width), *after)
         crossed = []
         for i, rows in enumerate(cut):
-            rows = rows.reshape(sets * capacity, width)
+            rows = rows.reshape(sets * rows_per_lane, width)
             if i > 0:
                 rows = lax.ppermute(rows, "dp", [(g, (g + i) % parts) for g in range(parts)])
             crossed.append(rows)
         return crossed
 
     def send_back(rows):
-        rows = rows.reshape(experts, capacity, width)
+        rows = rows.reshape(sets * parts, rows_per_lane, width)
         return lax.all_to_all(
             rows, axes, 0, 0, axis_index_groups=everywhere, tiled=True
         ).reshape(slots, width)
@@ -287,12 +294,15 @@
     spread_flops = 2 * slots * tok_rows * width
     dot_flops = 2 * slots * width * hidden * parts
     slot_shape = jax.ShapeDtypeStruct((slots, width), BF16)
-    place_shape = jax.ShapeDtypeStruct((top_count * tok_rows, slots), BF16)
+    place_shape = jax.ShapeDtypeStruct((2, top_count, tok_rows, slots), BF16)
+    near_shape = jax.ShapeDtypeStruct((2, tok_rows, slots), BF16)
     joined = hidden % 128 == 0
     units, span = (1, parts * hidden) if joined else (parts, hidden)
     unit_shape = jax.ShapeDtypeStruct((units, slots, span), F32)
     hidden_shape = jax.ShapeDtypeStruct((units, slots, span), BF16)
+    sum_shape = jax.ShapeDtypeStruct((tok_rows, width), F32)
     token_shape = jax.ShapeDtypeStruct((tok_rows, width), BF16)
+    gate_shape = jax.ShapeDtypeStruct(gates.shape, F32)
     hidden_scratch = pltpu.VMEM((units, slots, span), BF16)
     unit_scratch = pltpu.VMEM((units, slots, span), F32)
     row_scratch = pltpu.VMEM((slots, width), BF16)
@@ -303,17 +313,23 @@
     def sems(number):
         return pltpu.SemaphoreType.DMA((number,))
 
+    def far_side(array):
+        return lax.ppermute(array, "expert", across)
+
+    far_routes, far_tokens = far_side(routes), far_side(tokens)
     gate_own, up_own, down_own = swapped(w_gate), swapped(w_up), swapped(w_down)
-    gate_w, up_w = whole_expert(gate_own), whole_expert(up_own)
+    far_cotangent, far_gates = far_side(cotangent), far_side(gates)
+    gate_w, up_w, down_w = whole_expert(gate_own), whole_expert(up_own), whole_expert(down_own)
     plane = lax.axis_index("dp").astype(jnp.int32).reshape(1)
+    first_set = (lax.axis_index("expert") // (experts // 2) * sets).astype(jnp.int32).reshape(1)
     x_slots, place, near = call(
-        functools.partial(place_kernel, experts, parts),
-        [slot_shape, place_shape, jax.ShapeDtypeStruct((tok_rows, slots), BF16)],
-        spread_flops,
-    )(plane, routes, tokens)
+        functools.partial(place_kernel, sets, parts),
+        [slot_shape, place_shape, near_shape],
+        2 * spread_flops,
+    )(jnp.concatenate([plane, first_set]), routes, far_routes, tokens, far_tokens)
     x_shares = dispatch(x_slots)
-    (dy_slots,) = call(spread_kernel, [slot_shape], 256 * spread_flops, far=(2,))(
-        near, cotangent, gate_own
+    (dy_slots,) = call(spread_kernel, [slot_shape], 2 * spread_flops)(
+        near, cotangent, far_cotangent
     )
     hidden_rows, by_gate, by_up = call(
         functools.partial(hidden_kernel, parts, joined),
@@ -325,10 +341,6 @@
         far_out=True,
         vmem=LARGE_VMEM,
     )(plane, *x_shares, *gate_w, *up_w)
-    (down_own,) = call(
-        in_place_kernel, [down_own], 0, far=range(2), far_out=True, vmem=LARGE_VMEM, aliases={0: 0}
-    )(down_own, hidden_rows)
-    down_w = whole_expert(down_own)
     (out_rows,) = call(
         functools.partial(out_kernel, parts, joined),
         [slot_shape],
@@ -351,10 +363,20 @@
         vmem=LARGE_VMEM,
     )(plane, *dy_shares, *down_w, by_gate, by_up, *gate_w, *up_w)
     grad_slots = send_back(grad_rows)
-    mixed, gate_grad = call(
-        mix_kernel, [token_shape, jax.ShapeDtypeStruct(gates.shape, F32)], 2 * spread_flops
-    )(place, gates, cotangent, out_slots)
-    (token_grad,) = call(sum_kernel, [token_shape], 2 * spread_flops)(place, gates, grad_slots)
+    def combine(block, slot_rows, gates, outs, *cotangent):
+        return call(functools.partial(combine_kernel, block), outs, 2 * spread_flops)(
+            place, gates, slot_rows, *cotangent
+        )
+
+    far_sum, far_grad = combine(1, out_slots, far_gates, [token_shape, gate_shape], far_cotangent)
+    far_sum, far_grad = far_side(far_sum), far_side(far_grad)
+    own_sum, own_grad = combine(0, out_slots, gates, [sum_shape, gate_shape], cotangent)
+    mixed = (own_sum + far_sum.astype(F32)).astype(BF16)
+    gate_grad = own_grad + far_grad
+    (far_sum,) = combine(1, grad_slots, far_gates, [token_shape])
+    far_sum = far_side(far_sum)
+    (own_sum,) = combine(0, grad_slots, gates, [sum_shape])
+    token_grad = (own_sum + far_sum.astype(F32)).astype(BF16)
     return (mixed, token_grad, gate_grad)
 
 

time: 185 us -> 255 us (1.38)
  waiting for transfers between devices: 119 us -> 165 us
  starting transfers between devices: 24.3 us -> 40.1 us
  local copies, waits for them, and re-layouts: 9.59 us -> 14 us
  other arithmetic: 0 us -> 2.93 us
    ppermute x0 -> x7, waiting for transfers between devices: none -> 105 us  [far_side(): return lax.ppermute(array, 'expert', across)]
    all_to_all x2, waiting for transfers between devices: 37.5 us -> 0.01 us  [send_back(): lax.all_to_all(rows, axes, 0, 0, axis_index_groups=everywhere, tiled=True)]
    ppermute x0 -> x7, starting transfers between devices: none -> 12.9 us  [far_side(): return lax.ppermute(array, 'expert', across)]
    all_to_all x2, waiting for transfers between devices: 10.7 us -> 0.01 us  [dispatch(): lax.all_to_all(rows, axes, 0, 0, axis_index_groups=in_plane, tiled=True)]
    ppermute x3, waiting for transfers between devices: 25.1 us -> 14.4 us  [swapped(): return lax.ppermute(weight[0], axes, swap)]
    unnamed x25 -> x45, local copies, waits for them, and re-layouts: 9.59 us -> 14 us
    ppermute x2, starting transfers between devices: 0.55 us -> 4.23 us  [dispatch(): lax.ppermute(rows, 'dp', [(g, (g + i) % parts) for g in range(parts)])]
    ppermute x3, waiting for transfers between devices: 3.61 us -> 0.01 us  [whole_expert(): held.append(lax.ppermute(own, 'expert', turn))]
  transfers between devices with their start and end apart: 12 -> 19, of which waited for: 8 -> 8; matrix products, arithmetic and copies ran while one was open for 1% -> 2% of each run, Pallas kernels for 15% -> 11%
where the time goes in v10:
time: 255 us
  waiting for transfers between devices  165 us (65%)
  starting transfers between devices  40.1 us (16%)
  Pallas kernels  31.5 us (12%)
  local copies, waits for them, and re-layouts  14 us (5%)
  other arithmetic  2.93 us (1%)
    ppermute x7, waiting for transfers between devices, far_side(): return lax.ppermute(array, 'expert', across)  105 us
    ppermute x2, waiting for transfers between devices, dispatch(): lax.ppermute(rows, 'dp', [(g, (g + i) % parts) for g in range(parts)])  45.5 us
    pallas_call x11, Pallas kernels, run(): pl.pallas_call(kernel, out_shape=tuple((jax.ShapeDtypeStruct(o.shape, o.d...  31.5 us
    ppermute x3, waiting for transfers between devices, swapped(): return lax.ppermute(weight[0], axes, swap)  14.4 us
    unnamed x45, local copies, waits for them, and re-layouts  14 us
    ppermute x7, starting transfers between devices, far_side(): return lax.ppermute(array, 'expert', across)  12.9 us
    all_to_all x2, starting transfers between devices, dispatch(): lax.all_to_all(rows, axes, 0, 0, axis_index_groups=in_plane, tiled=True)  11.3 us
    all_to_all x2, starting transfers between devices, send_back(): lax.all_to_all(rows, axes, 0, 0, axis_index_groups=everywhere, tiled=True)  9.52 us
  transfers between devices with their start and end apart: 19, of which 8 were waited for; matrix products, arithmetic and copies ran while one was open for 2% of the time, Pallas kernels for 11%

profile of v10, /device:TPU:0, one launch (start us, length us, event | category | flops | bytes accessed | tf_op | source)
XLA Modules:
  0.0 254.8 jit_solution(9463985812523231067)
XLA Ops:
  0.6 4.1 %collective-permute-start.1 = (bf16[128,2048]{1,0:T(8,128)(2,1)}, bf16[128,2048]{1,0:T(8,128)(2,1)S(1)}, u32[]{:S(2)}, u32[]{:S(2)}) collective-permute-start(bf16[128,2048]{1,0:T(8,128)(2,1)} %refs_2_.1), channel_id=1, source_target_pairs={{0,8},{1,9},{2,10},{3,11},{4,12},{5,13},{6,14},{7,15},{8,0},{9,1},... | collective-permute-start | bytes 1572872 | tf_op jit(solution)/shard_map/ppermute | solution.py:317
  4.7 0.8 copy.11.refs_0_
  5.5 0.1 collective-permute-start
  5.6 0.1 pad_add_fusion.here_ref
  5.7 25.2 %collective-permute-done.refs_1_ = s32[128,2]{1,0:T(8,128)S(1)} collective-permute-done((s32[128,2]{1,0:T(8,128)S(1)}, s32[128,2]{1,0:T(8,128)S(1)}, u32[]{:S(2)}, u32[]{:S(2)}) %collective-permute-start) | collective-permute-done | bytes 1056 | tf_op jit(solution)/shard_map/ppermute | solution.py:317
  30.9 0.0 collective-permute-done.1.refs_3_
  30.9 1.0 copy-done.15
  32.0 2.2 shard_map.94
  34.2 1.2 copy-done.5
  35.3 3.7 %all-to-all-start = ((bf16[4,96,2048]{2,1,0:T(8,128)(2,1)}), bf16[4,96,2048]{2,1,0:T(8,128)(2,1)S(1)}, u32[]{:S(2)}, u32[]{:S(2)}) async-start(bf16[4,96,2048]{2,1,0:T(8,128)(2,1)} %bitcast.24), calls=%async_computation | async-start | bytes 3145728 | tf_op jit(solution)/shard_map/all_to_all | solution.py:271
  39.0 1.6 collective-permute-start.3
  40.6 0.0 collective-permute-start.5
  40.7 0.0 collective-permute-start.7
  40.7 2.7 %collective-permute-start.10 = (bf16[128,2048]{1,0:T(8,128)(2,1)S(1)}, bf16[128,2048]{1,0:T(8,128)(2,1)S(1)}, u32[]{:S(2)}, u32[]{:S(2)}) collective-permute-start(bf16[128,2048]{1,0:T(8,128)(2,1)S(1)} %copy-done.1), channel_id=1, source_target_pairs={{0,8},{1,9},{2,10},{3,11},{4,12},{5,13},{6,14},{7,15},{8,0},{9,1},... | collective-permute-start | bytes 1572872 | tf_op jit(solution)/shard_map/ppermute | solution.py:317
  43.4 23.7 %collective-permute-done.10.refs_0_.refs_1_ = bf16[128,2048]{1,0:T(8,128)(2,1)S(1)} collective-permute-done((bf16[128,2048]{1,0:T(8,128)(2,1)S(1)}, bf16[128,2048]{1,0:T(8,128)(2,1)S(1)}, u32[]{:S(2)}, u32[]{:S(2)}) %collective-permute-start.10) | collective-permute-done | bytes 524320 | tf_op jit(solution)/shard_map/ppermute | solution.py:317
  67.0 1.0 shard_map.100
  68.1 1.2 copy-done
  69.3 0.8 copy-done.3
  70.1 7.6 %all-to-all-start.2 = ((bf16[4,96,2048]{2,1,0:T(8,128)(2,1)}), bf16[4,96,2048]{2,1,0:T(8,128)(2,1)S(1)}, u32[]{:S(2)}, u32[]{:S(2)}) async-start(bf16[4,96,2048]{2,1,0:T(8,128)(2,1)} %bitcast.23), calls=%async_computation.2 | async-start | bytes 3145728 | tf_op jit(solution)/shard_map/all_to_all | solution.py:271
  77.7 0.0 collective-permute-done.3.refs_2_.refs_6_
  77.7 0.0 collective-permute-start.4
  77.7 0.5 collective-permute-start.6
  78.2 14.4 %collective-permute-done.7.refs_0_.refs_2_ = bf16[384,2048]{1,0:T(8,128)(2,1)} collective-permute-done((bf16[384,2048]{1,0:T(8,128)(2,1)}, bf16[384,2048]{1,0:T(8,128)(2,1)}, u32[]{:S(2)}, u32[]{:S(2)}) %collective-permute-start.7) | collective-permute-done | bytes 1572896 | tf_op jit(solution)/shard_map/ppermute | solution.py:260
  92.6 0.0 collective-permute-start.8
  92.6 2.1 shard_map.95
  94.7 0.9 copy-done.14
  95.6 2.5 collective-permute-start.2
  98.1 0.0 collective-permute-done.4.refs_3_.refs_7_
  98.1 0.0 collective-permute-done.6.refs_5_.refs_9_
  98.1 18.2 %collective-permute-done.2.refs_1_ = bf16[192,2048]{1,0:T(8,128)(2,1)S(1)} collective-permute-done((bf16[192,2048]{1,0:T(8,128)(2,1)S(1)}, bf16[192,2048]{1,0:T(8,128)(2,1)S(1)}, u32[]{:S(2)}, u32[]{:S(2)}) %collective-permute-start.2) | collective-permute-done | bytes 786464 | tf_op jit(solution)/shard_map/ppermute | solution.py:284
  116.3 0.9 copy-done.20
  117.2 7.6 %shard_map.96 = (bf16[1,384,768]{2,1,0:T(8,128)(2,1)}, f32[1,384,768]{2,1,0:T(8,128)}, f32[1,384,768]{2,1,0:T(8,128)}) custom-call(s32[1]{0:T(128)} %bitcast.plane_ref, bf16[192,2048]{1,0:T(8,128)(2,1)} %bitcast.26, bf16[192,2048]{1,0:T(8,128)(2,1)} %copy-done.20, bf16[2048,384]{1,0:T(8,128)(2,1)} %collective-permute-done.3.refs_2_.refs_6_, ...), custom_call_target="tpu_custom_call" | custom-call | flops 2415919104 | bytes 10813444 | tf_op jit(solution)/shard_map/pallas_call | solution.py:213
  124.8 0.0 collective-permute-done.8.refs_1_.refs_3_
  124.8 1.1 copy-done.10
  125.9 4.0 %shard_map.97.refs_0_ = bf16[384,2048]{1,0:T(8,128)(2,1)} custom-call(bf16[1,384,768]{2,1,0:T(8,128)(2,1)S(1)} %copy-done.10, bf16[384,2048]{1,0:T(8,128)(2,1)} %collective-permute-done.7.refs_0_.refs_2_, bf16[384,2048]{1,0:T(8,128)(2,1)} %collective-permute-done.8.refs_1_.refs_3_), custom_call_target="tpu_custom_call" | custom-call | flops 1207959552 | bytes 5308416 | tf_op jit(solution)/shard_map/pallas_call | solution.py:213
  129.9 0.0 all-to-all-done.2
  129.9 2.0 shard_map.101
  131.9 0.9 copy-done.13
  132.8 1.7 collective-permute-start.12
  134.5 4.1 %all-to-all-start.1 = ((bf16[8,48,2048]{2,1,0:T(8,128)(2,1)}), bf16[8,48,2048]{2,1,0:T(8,128)(2,1)S(1)}, u32[]{:S(2)}, u32[]{:S(2)}) async-start(bf16[8,48,2048]{2,1,0:T(8,128)(2,1)} %bitcast.9), calls=%async_computation.1 | async-start | bytes 3145728 | tf_op jit(solution)/shard_map/all_to_all | solution.py:290
  138.7 27.4 %collective-permute-done.12.refs_1_ = bf16[192,2048]{1,0:T(8,128)(2,1)S(1)} collective-permute-done((bf16[192,2048]{1,0:T(8,128)(2,1)}, bf16[192,2048]{1,0:T(8,128)(2,1)S(1)}, u32[]{:S(2)}, u32[]{:S(2)}) %collective-permute-start.12) | collective-permute-done | bytes 786464 | tf_op jit(solution)/shard_map/ppermute | solution.py:284
  166.1 0.9 copy-done.19
  167.0 8.6 %shard_map.102 = bf16[384,2048]{1,0:T(8,128)(2,1)} custom-call(s32[1]{0:T(128)} %bitcast.plane_ref, bf16[192,2048]{1,0:T(8,128)(2,1)} %bitcast.25, bf16[192,2048]{1,0:T(8,128)(2,1)} %copy-done.19, bf16[384,2048]{1,0:T(8,128)(2,1)} %collective-permute-done.7.refs_0_.refs_2_, bf16[384,2048]{1,0:T(8,128)(2,1)} %collective-permute-done.8.refs_1_.refs_3_, ...), custom_call_target="tpu_custom_call" | custom-call | flops 77309411328 | bytes 14942212 | tf_op jit(solution)/shard_map/pallas_call | solution.py:213
  175.6 0.0 all-to-all-done.1
  175.6 0.0 copy-start.16
  175.6 5.4 %all-to-all-start.3 = ((bf16[8,48,2048]{2,1,0:T(8,128)(2,1)}), bf16[8,48,2048]{2,1,0:T(8,128)(2,1)S(1)}, u32[]{:S(2)}, u32[]{:S(2)}) async-start(bf16[8,48,2048]{2,1,0:T(8,128)(2,1)} %bitcast.28), calls=%async_computation.3 | async-start | bytes 3145728 | tf_op jit(solution)/shard_map/all_to_all | solution.py:290
  181.0 0.7 copy.12.gates_ref
  181.7 2.7 %collective-permute-start.9 = (f32[128,2]{1,0:T(8,128)}, f32[128,2]{1,0:T(8,128)S(1)}, u32[]{:S(2)}, u32[]{:S(2)}) collective-permute-start(f32[128,2]{1,0:T(8,128)} %copy.12.gates_ref), channel_id=1, source_target_pairs={{0,8},{1,9},{2,10},{3,11},{4,12},{5,13},{6,14},{7,15},{8,0},{9,1},... | collective-permute-start | bytes 3080 | tf_op jit(solution)/shard_map/ppermute | solution.py:317
  184.4 13.8 %collective-permute-done.9.gates_ref = f32[128,2]{1,0:T(8,128)S(1)} collective-permute-done((f32[128,2]{1,0:T(8,128)}, f32[128,2]{1,0:T(8,128)S(1)}, u32[]{:S(2)}, u32[]{:S(2)}) %collective-permute-start.9) | collective-permute-done | bytes 1056 | tf_op jit(solution)/shard_map/ppermute | solution.py:317
  198.2 1.1 copy-done.4
  199.3 1.7 shard_map.99
  200.9 3.3 %collective-permute-start.11 = (bf16[128,2048]{1,0:T(8,128)(2,1)}, bf16[128,2048]{1,0:T(8,128)(2,1)}, u32[]{:S(2)}, u32[]{:S(2)}) collective-permute-start(bf16[128,2048]{1,0:T(8,128)(2,1)} %get-tuple-element.23), channel_id=1, source_target_pairs={{0,8},{1,9},{2,10},{3,11},{4,12},{5,13},{6,14},{7,15},{8,0},{9,1},... | collective-permute-start | bytes 1572872 | tf_op jit(solution)/shard_map/ppermute | solution.py:317
  204.2 0.0 collective-permute-start.14
  204.3 0.9 shard_map.98
  205.1 1.0 copy-done.6
  206.1 21.8 %collective-permute-done.14 = f32[128,2]{1,0:T(8,128)S(1)} collective-permute-done((f32[128,2]{1,0:T(8,128)S(1)}, f32[128,2]{1,0:T(8,128)S(1)}, u32[]{:S(2)}, u32[]{:S(2)}) %collective-permute-start.14) | collective-permute-done | bytes 1056 | tf_op jit(solution)/shard_map/ppermute | solution.py:317
  227.9 0.6 copy.15
  228.6 0.8 copy-done.12
  229.4 0.7 shard_map.104
  230.2 0.1 collective-permute-start.13
  230.3 1.9 add_convert_fusion.1
  232.2 0.7 shard_map.103
  233.0 20.9 %collective-permute-done.13 = bf16[128,2048]{1,0:T(8,128)(2,1)S(1)} collective-permute-done((bf16[128,2048]{1,0:T(8,128)(2,1)S(1)}, bf16[128,2048]{1,0:T(8,128)(2,1)S(1)}, u32[]{:S(2)}, u32[]{:S(2)}) %collective-permute-start.13) | collective-permute-done | bytes 524320 | tf_op jit(solution)/shard_map/ppermute | solution.py:317
  253.9 0.9 add_convert_fusion
  (34 shorter events, 0.1 us)
Async XLA Ops:
  0.6 30.3 %collective-permute-start.1 = (bf16[128,2048]{1,0:T(8,128)(2,1)}, bf16[128,2048]{1,0:T(8,128)(2,1)S(1)}, u32[]{:S(2)}, u32[]{:S(2)}) collective-permute-start(bf16[128,2048]{1,0:T(8,128)(2,1)} %refs_2_.1), channel_id=1, source_target_pairs={{0,8},{1,9},{2,10},{3,11},{4,12},{5,13},{6,14},{7,15},{8,0},{9,1},... | collective-permute-start | bytes 1572872 | tf_op jit(solution)/shard_map/ppermute | solution.py:317
  5.5 25.4 %collective-permute-start = (s32[128,2]{1,0:T(8,128)S(1)}, s32[128,2]{1,0:T(8,128)S(1)}, u32[]{:S(2)}, u32[]{:S(2)}) collective-permute-start(s32[128,2]{1,0:T(8,128)S(1)} %copy.11.refs_0_), channel_id=1, source_target_pairs={{0,8},{1,9},{2,10},{3,11},{4,12},{5,13},{6,14},{7,15},{8,0},{9,1},... | collective-permute-start | bytes 3080 | tf_op jit(solution)/shard_map/ppermute | solution.py:317
  30.9 1.0 copy-start.15
  34.2 1.2 copy-start.5
  35.3 5.4 %copy-start.1 = (bf16[128,2048]{1,0:T(8,128)(2,1)S(1)}, bf16[128,2048]{1,0:T(8,128)(2,1)}, u32[]{:S(2)}) copy-start(bf16[128,2048]{1,0:T(8,128)(2,1)} %refs_0_.4) | copy-start | bytes 1572868
  35.3 34.7 %all-to-all-start = ((bf16[4,96,2048]{2,1,0:T(8,128)(2,1)}), bf16[4,96,2048]{2,1,0:T(8,128)(2,1)S(1)}, u32[]{:S(2)}, u32[]{:S(2)}) async-start(bf16[4,96,2048]{2,1,0:T(8,128)(2,1)} %bitcast.24), calls=%async_computation | async-start | bytes 3145728 | tf_op jit(solution)/shard_map/all_to_all | solution.py:271
  39.0 38.6 %collective-permute-start.3 = (bf16[2048,384]{1,0:T(8,128)(2,1)}, bf16[2048,384]{1,0:T(8,128)(2,1)}, u32[]{:S(2)}, u32[]{:S(2)}) collective-permute-start(bf16[2048,384]{1,0:T(8,128)(2,1)} %bitcast.29), channel_id=1, source_target_pairs={{0,16},{1,0},{2,18},{3,2},{4,20},{5,4},{6,22},{7,6},{8,24},{9,8},{... | collective-permute-start | bytes 4718600 | tf_op jit(solution)/shard_map/ppermute | solution.py:260
  40.6 37.0 %collective-permute-start.5 = (bf16[2048,384]{1,0:T(8,128)(2,1)}, bf16[2048,384]{1,0:T(8,128)(2,1)}, u32[]{:S(2)}, u32[]{:S(2)}) collective-permute-start(bf16[2048,384]{1,0:T(8,128)(2,1)} %bitcast.30), channel_id=1, source_target_pairs={{0,16},{1,0},{2,18},{3,2},{4,20},{5,4},{6,22},{7,6},{8,24},{9,8},{... | collective-permute-start | bytes 4718600 | tf_op jit(solution)/shard_map/ppermute | solution.py:260
  40.7 51.9 %collective-permute-start.7 = (bf16[384,2048]{1,0:T(8,128)(2,1)}, bf16[384,2048]{1,0:T(8,128)(2,1)}, u32[]{:S(2)}, u32[]{:S(2)}) collective-permute-start(bf16[384,2048]{1,0:T(8,128)(2,1)} %bitcast.31), channel_id=1, source_target_pairs={{0,16},{1,0},{2,18},{3,2},{4,20},{5,4},{6,22},{7,6},{8,24},{9,8},{... | collective-permute-start | bytes 4718600 | tf_op jit(solution)/shard_map/ppermute | solution.py:260
  40.7 26.3 %collective-permute-start.10 = (bf16[128,2048]{1,0:T(8,128)(2,1)S(1)}, bf16[128,2048]{1,0:T(8,128)(2,1)S(1)}, u32[]{:S(2)}, u32[]{:S(2)}) collective-permute-start(bf16[128,2048]{1,0:T(8,128)(2,1)S(1)} %copy-done.1), channel_id=1, source_target_pairs={{0,8},{1,9},{2,10},{3,11},{4,12},{5,13},{6,14},{7,15},{8,0},{9,1},... | collective-permute-start | bytes 1572872 | tf_op jit(solution)/shard_map/ppermute | solution.py:317
  68.0 1.2 copy-start
  69.3 0.8 copy-start.3
  70.1 59.8 %all-to-all-start.2 = ((bf16[4,96,2048]{2,1,0:T(8,128)(2,1)}), bf16[4,96,2048]{2,1,0:T(8,128)(2,1)S(1)}, u32[]{:S(2)}, u32[]{:S(2)}) async-start(bf16[4,96,2048]{2,1,0:T(8,128)(2,1)} %bitcast.23), calls=%async_computation.2 | async-start | bytes 3145728 | tf_op jit(solution)/shard_map/all_to_all | solution.py:271
  77.7 20.4 %collective-permute-start.4 = (bf16[2048,384]{1,0:T(8,128)(2,1)}, bf16[2048,384]{1,0:T(8,128)(2,1)S(1)}, u32[]{:S(2)}, u32[]{:S(2)}) collective-permute-start(bf16[2048,384]{1,0:T(8,128)(2,1)} %collective-permute-done.3.refs_2_.refs_6_), channel_id=1, source_target_pairs={{0,1},{1,0},{2,3},{3,2},{4,5},{5,4},{6,7},{7,6},{8,9},{9,8},{10,11... | collective-permute-start | bytes 4718600 | tf_op jit(solution)/shard_map/ppermute | solution.py:266
  77.7 20.4 %collective-permute-start.6 = (bf16[2048,384]{1,0:T(8,128)(2,1)}, bf16[2048,384]{1,0:T(8,128)(2,1)S(1)}, u32[]{:S(2)}, u32[]{:S(2)}) collective-permute-start(bf16[2048,384]{1,0:T(8,128)(2,1)} %collective-permute-done.5.refs_4_.refs_8_), channel_id=1, source_target_pairs={{0,1},{1,0},{2,3},{3,2},{4,5},{5,4},{6,7},{7,6},{8,9},{9,8},{10,11... | collective-permute-start | bytes 4718600 | tf_op jit(solution)/shard_map/ppermute | solution.py:266
  92.6 32.2 %collective-permute-start.8 = (bf16[384,2048]{1,0:T(8,128)(2,1)}, bf16[384,2048]{1,0:T(8,128)(2,1)}, u32[]{:S(2)}, u32[]{:S(2)}) collective-permute-start(bf16[384,2048]{1,0:T(8,128)(2,1)} %collective-permute-done.7.refs_0_.refs_2_), channel_id=1, source_target_pairs={{0,1},{1,0},{2,3},{3,2},{4,5},{5,4},{6,7},{7,6},{8,9},{9,8},{10,11... | collective-permute-start | bytes 4718600 | tf_op jit(solution)/shard_map/ppermute | solution.py:266
  94.7 0.9 copy-start.14
  95.6 20.7 %collective-permute-start.2 = (bf16[192,2048]{1,0:T(8,128)(2,1)S(1)}, bf16[192,2048]{1,0:T(8,128)(2,1)S(1)}, u32[]{:S(2)}, u32[]{:S(2)}) collective-permute-start(bf16[192,2048]{1,0:T(8,128)(2,1)S(1)} %bitcast.27), channel_id=1, source_target_pairs={{0,16},{16,0},{1,17},{17,1},{2,18},{18,2},{3,19},{19,3},{4,20},{20... | collective-permute-start | bytes 2359304 | tf_op jit(solution)/shard_map/ppermute | solution.py:284
  98.1 18.2 %copy-start.17 = (bf16[2048,384]{1,0:T(8,128)(2,1)}, bf16[2048,384]{1,0:T(8,128)(2,1)S(1)}, u32[]{:S(2)}) copy-start(bf16[2048,384]{1,0:T(8,128)(2,1)S(1)} %collective-permute-done.4.refs_3_.refs_7_) | copy-start | bytes 4718596
  98.1 18.2 %copy-start.18 = (bf16[2048,384]{1,0:T(8,128)(2,1)}, bf16[2048,384]{1,0:T(8,128)(2,1)S(1)}, u32[]{:S(2)}) copy-start(bf16[2048,384]{1,0:T(8,128)(2,1)S(1)} %collective-permute-done.6.refs_5_.refs_9_) | copy-start | bytes 4718596
  116.3 0.9 copy-start.20
  124.8 1.1 copy-start.10
  131.9 0.9 copy-start.13
  132.8 33.3 %collective-permute-start.12 = (bf16[192,2048]{1,0:T(8,128)(2,1)}, bf16[192,2048]{1,0:T(8,128)(2,1)S(1)}, u32[]{:S(2)}, u32[]{:S(2)}) collective-permute-start(bf16[192,2048]{1,0:T(8,128)(2,1)} %bitcast.14), channel_id=1, source_target_pairs={{0,16},{16,0},{1,17},{17,1},{2,18},{18,2},{3,19},{19,3},{4,20},{20... | collective-permute-start | bytes 2359304 | tf_op jit(solution)/shard_map/ppermute | solution.py:284
  134.5 41.0 %all-to-all-start.1 = ((bf16[8,48,2048]{2,1,0:T(8,128)(2,1)}), bf16[8,48,2048]{2,1,0:T(8,128)(2,1)S(1)}, u32[]{:S(2)}, u32[]{:S(2)}) async-start(bf16[8,48,2048]{2,1,0:T(8,128)(2,1)} %bitcast.9), calls=%async_computation.1 | async-start | bytes 3145728 | tf_op jit(solution)/shard_map/all_to_all | solution.py:290
  166.1 0.9 copy-start.19
  175.6 5.4 %copy-start.16 = (f32[128,2]{0,1:T(2,128)S(1)}, f32[128,2]{0,1:T(2,128)}, u32[]{:S(2)}) copy-start(f32[128,2]{0,1:T(2,128)} %param.10) | copy-start | bytes 3076
  175.6 53.0 %all-to-all-start.3 = ((bf16[8,48,2048]{2,1,0:T(8,128)(2,1)}), bf16[8,48,2048]{2,1,0:T(8,128)(2,1)S(1)}, u32[]{:S(2)}, u32[]{:S(2)}) async-start(bf16[8,48,2048]{2,1,0:T(8,128)(2,1)} %bitcast.28), calls=%async_computation.3 | async-start | bytes 3145728 | tf_op jit(solution)/shard_map/all_to_all | solution.py:290
  181.7 22.5 %copy-start.2 = (bf16[128,2048]{1,0:T(8,128)(2,1)S(1)}, bf16[128,2048]{1,0:T(8,128)(2,1)}, u32[]{:S(2)}) copy-start(bf16[128,2048]{1,0:T(8,128)(2,1)} %refs_0_.4) | copy-start | bytes 1572868
  181.7 16.5 %collective-permute-start.9 = (f32[128,2]{1,0:T(8,128)}, f32[128,2]{1,0:T(8,128)S(1)}, u32[]{:S(2)}, u32[]{:S(2)}) collective-permute-start(f32[128,2]{1,0:T(8,128)} %copy.12.gates_ref), channel_id=1, source_target_pairs={{0,8},{1,9},{2,10},{3,11},{4,12},{5,13},{6,14},{7,15},{8,0},{9,1},... | collective-permute-start | bytes 3080 | tf_op jit(solution)/shard_map/ppermute | solution.py:317
  198.2 6.9 %copy-start.11 = (f32[128,2]{1,0:T(8,128)}, f32[128,2]{1,0:T(8,128)S(1)}, u32[]{:S(2)}) copy-start(f32[128,2]{1,0:T(8,128)S(1)} %collective-permute-done.9.gates_ref) | copy-start | bytes 3076
  198.2 1.1 copy-start.4
  199.3 5.0 %copy-start.8 = (f32[128,2]{1,0:T(8,128)S(1)}, f32[128,2]{1,0:T(8,128)}, u32[]{:S(2)}) copy-start(f32[128,2]{1,0:T(8,128)} %copy.12.gates_ref) | copy-start | bytes 3076
  200.9 29.3 %collective-permute-start.11 = (bf16[128,2048]{1,0:T(8,128)(2,1)}, bf16[128,2048]{1,0:T(8,128)(2,1)}, u32[]{:S(2)}, u32[]{:S(2)}) collective-permute-start(bf16[128,2048]{1,0:T(8,128)(2,1)} %get-tuple-element.23), channel_id=1, source_target_pairs={{0,8},{1,9},{2,10},{3,11},{4,12},{5,13},{6,14},{7,15},{8,0},{9,1},... | collective-permute-start | bytes 1572872 | tf_op jit(solution)/shard_map/ppermute | solution.py:317
  204.2 23.7 %collective-permute-start.14 = (f32[128,2]{1,0:T(8,128)S(1)}, f32[128,2]{1,0:T(8,128)S(1)}, u32[]{:S(2)}, u32[]{:S(2)}) collective-permute-start(f32[128,2]{1,0:T(8,128)S(1)} %get-tuple-element.30), channel_id=1, source_target_pairs={{0,8},{1,9},{2,10},{3,11},{4,12},{5,13},{6,14},{7,15},{8,0},{9,1},... | collective-permute-start | bytes 3080 | tf_op jit(solution)/shard_map/ppermute | solution.py:317
  205.1 1.0 copy-start.6
  227.9 2.3 copy-start.7
  228.6 0.8 copy-start.12
  230.2 2.1 copy-start.9
  230.2 23.7 %collective-permute-start.13 = (bf16[128,2048]{1,0:T(8,128)(2,1)S(1)}, bf16[128,2048]{1,0:T(8,128)(2,1)S(1)}, u32[]{:S(2)}, u32[]{:S(2)}) collective-permute-start(bf16[128,2048]{1,0:T(8,128)(2,1)S(1)} %shard_map.104), channel_id=1, source_target_pairs={{0,8},{1,9},{2,10},{3,11},{4,12},{5,13},{6,14},{7,15},{8,0},{9,1},... | collective-permute-start | bytes 1572872 | tf_op jit(solution)/shard_map/ppermute | solution.py:317

commit v11 on v9

--- a/solution.py
+++ b/solution.py
@@ -96,84 +96,75 @@
     return [rows_ref.at[pl.ds(pl.multiple_of(start, size), size)] for start in starts]
 
 
-def hidden_kernel(parts, joined, plane_ref, *refs):
-    sources, refs = refs[: 3 * parts], refs[3 * parts :]
-    outs, (sems, out_sems), refs = refs[:3], refs[3:5], refs[5:]
-    hidden_ref, by_gate_ref, by_up_ref, rows_ref, gate_ref, up_ref = refs
-    gate, up = shares(gate_ref, parts, joined), shares(up_ref, parts, joined)
-    copies = fetch(sources, [*by_plane(rows_ref, plane_ref, parts), *gate, *up], sems)
-    for copy in copies[: 2 * parts]:
-        copy.wait()
-    for i in range(gate_ref.shape[0]):
-        pre_gate = dot(rows_ref[...], gate_ref[i], (1, 0))
-        if i == 0:
-            for copy in copies[2 * parts :]:
-                copy.wait()
-        pre_up = dot(rows_ref[...], up_ref[i], (1, 0))
-        sig = jax.nn.sigmoid(pre_gate)
-        act = pre_gate * sig
-        hidden_ref[i] = (act * pre_up).astype(BF16)
-        by_gate_ref[i] = pre_up * sig * (1.0 + pre_gate * (1.0 - sig))
-        by_up_ref[i] = act
-    for copy in fetch([hidden_ref, by_gate_ref, by_up_ref], outs, out_sems):
-        copy.wait()
-
-
-def in_place_kernel(_, after_ref, out_ref):
-    pass
-
-
-def out_kernel(parts, joined, hidden_ref, *refs):
-    sources, refs = refs[:parts], refs[parts:]
-    out_ref, sems, out_sems, stage_ref, hidden_stage, down_ref = refs
-    down = shares(down_ref, parts, joined, 0)
-    pieces = tiles(out_ref.shape[1])
-    (first,) = fetch([hidden_ref], [hidden_stage], sems)
-    copies = [
-        fetch(
-            [source.at[:, columns] for source in sources],
-            [share.at[:, columns] for share in down],
-            sems.at[pl.ds(1 + d * parts, parts)],
-        )
-        for d, columns in enumerate(pieces)
+def chunks(span):
+    size = 256 if span % 256 == 0 else span
+    return [pl.ds(start, size) for start in range(0, span, size)]
+
+
+def forward_kernel(parts, joined, plane_ref, *refs):
+    sources, outs, refs = refs[: 4 * parts], refs[4 * parts : 4 * parts + 3], refs[4 * parts + 3 :]
+    sems, out_sems, rows_ref, gate_ref, up_ref, down_ref = refs[:6]
+    stage_ref, hidden_ref, by_gate_ref, by_up_ref = refs[6:]
+    units, span = gate_ref.shape[0], gate_ref.shape[2]
+    targets = [
+        *by_plane(rows_ref, plane_ref, parts),
+        *shares(gate_ref, parts, joined),
+        *shares(up_ref, parts, joined),
+        *shares(down_ref, parts, joined, 0),
     ]
-    first.wait()
-    sent = []
-    for d, columns in enumerate(pieces):
-        for copy in copies[d]:
-            copy.wait()
+    copies = fetch(sources, targets, sems)
+    for copy in copies[: 3 * parts]:
+        copy.wait()
+    for i in range(units):
+        for cut in chunks(span):
+            pre_gate = dot(rows_ref[...], gate_ref[i, :, cut], (1, 0))
+            pre_up = dot(rows_ref[...], up_ref[i, :, cut], (1, 0))
+            sig = 0.5 + 0.5 * jnp.tanh(0.5 * pre_gate)
+            act = pre_gate * sig
+            hidden_ref[i, :, cut] = (act * pre_up).astype(BF16)
+            by_gate_ref[i, :, cut] = pre_up * (sig + act * (1.0 - sig))
+            by_up_ref[i, :, cut] = act
+    sent = fetch([by_gate_ref, by_up_ref], outs[1:], out_sems)
+    for copy in copies[3 * parts :]:
+        copy.wait()
+    for d, columns in enumerate(tiles(stage_ref.shape[1])):
         stage_ref[:, columns] = sum(
-            dot(hidden_stage[i], down_ref[i, :, columns], (1, 0)) for i in range(down_ref.shape[0])
+            dot(hidden_ref[i], down_ref[i, :, columns], (1, 0)) for i in range(units)
         ).astype(BF16)
-        sent.append(store(stage_ref.at[:, columns], out_ref.at[:, columns], out_sems.at[d]))
+        sent.append(store(stage_ref.at[:, columns], outs[0].at[:, columns], out_sems.at[2 + d]))
     for copy in sent:
         copy.wait()
 
 
 def backward_kernel(parts, joined, plane_ref, *refs):
     sources, refs = refs[: 2 + 4 * parts], refs[2 + 4 * parts :]
-    out_ref, sems, out_sems, back_gate_ref, back_up_ref, stage_ref, rows_ref = refs[:7]
-    down_ref, by_gate_ref, by_up_ref, gate_ref, up_ref = refs[7:]
-    down, gate, up = (
-        shares(down_ref, parts, joined, 0),
-        shares(gate_ref, parts, joined),
-        shares(up_ref, parts, joined),
-    )
-    copies = fetch(sources, [*by_plane(rows_ref, plane_ref, parts), *down, by_gate_ref, by_up_ref, *gate, *up], sems)
+    out_ref, sems, out_sems, rows_ref, down_ref, by_gate_ref, by_up_ref, gate_ref, up_ref = refs[:9]
+    stage_ref, back_gate_ref, back_up_ref = refs[9:]
+    units, span = down_ref.shape[:2]
+    targets = [
+        *by_plane(rows_ref, plane_ref, parts),
+        *shares(down_ref, parts, joined, 0),
+        by_gate_ref,
+        by_up_ref,
+        *shares(gate_ref, parts, joined),
+        *shares(up_ref, parts, joined),
+    ]
+    copies = fetch(sources, targets, sems)
     for copy in copies[: 2 + 2 * parts]:
         copy.wait()
-    for i in range(down_ref.shape[0]):
-        back_hidden = dot(rows_ref[...], down_ref[i], (1, 1))
-        back_gate_ref[i] = (back_hidden * by_gate_ref[i]).astype(BF16)
-        back_up_ref[i] = (back_hidden * by_up_ref[i]).astype(BF16)
+    for i in range(units):
+        for cut in chunks(span):
+            back_hidden = dot(rows_ref[...], down_ref[i, cut, :], (1, 1))
+            back_gate_ref[i, :, cut] = (back_hidden * by_gate_ref[i, :, cut]).astype(BF16)
+            back_up_ref[i, :, cut] = (back_hidden * by_up_ref[i, :, cut]).astype(BF16)
     for copy in copies[2 + 2 * parts :]:
         copy.wait()
     sent = []
-    for d, columns in enumerate(tiles(out_ref.shape[1])):
+    for d, columns in enumerate(tiles(stage_ref.shape[1])):
         stage_ref[:, columns] = sum(
             dot(back_gate_ref[i], gate_ref[i, columns, :], (1, 1))
             + dot(back_up_ref[i], up_ref[i, columns, :], (1, 1))
-            for i in range(down_ref.shape[0])
+            for i in range(units)
         ).astype(BF16)
         sent.append(store(stage_ref.at[:, columns], out_ref.at[:, columns], out_sems.at[d]))
     for copy in sent:
@@ -202,7 +193,7 @@
     out_ref[...] = total.astype(BF16)
 
 
-def call(kernel, outs, flops, scratch=(), far=(), far_out=False, vmem=SMALL_VMEM, aliases=None):
+def call(kernel, outs, flops, scratch=(), far=(), far_out=False, vmem=SMALL_VMEM):
     def run(*args):
         moved = sum(a.size * a.dtype.itemsize for a in (*args, *outs))
         spaces = [
@@ -217,7 +208,6 @@
                 pl.BlockSpec(memory_space=pl.ANY if far_out else pltpu.VMEM) for _ in outs
             ),
             scratch_shapes=scratch,
-            input_output_aliases=aliases or {},
             compiler_params=pltpu.CompilerParams(vmem_limit_bytes=vmem),
             cost_estimate=pl.CostEstimate(flops=flops, bytes_accessed=moved, transcendentals=0),
         )(*args)
@@ -291,7 +281,6 @@
     joined = hidden % 128 == 0
     units, span = (1, parts * hidden) if joined else (parts, hidden)
     unit_shape = jax.ShapeDtypeStruct((units, slots, span), F32)
-    hidden_shape = jax.ShapeDtypeStruct((units, slots, span), BF16)
     token_shape = jax.ShapeDtypeStruct((tok_rows, width), BF16)
     hidden_scratch = pltpu.VMEM((units, slots, span), BF16)
     unit_scratch = pltpu.VMEM((units, slots, span), F32)
@@ -304,7 +293,7 @@
         return pltpu.SemaphoreType.DMA((number,))
 
     gate_own, up_own, down_own = swapped(w_gate), swapped(w_up), swapped(w_down)
-    gate_w, up_w = whole_expert(gate_own), whole_expert(up_own)
+    gate_w, up_w, down_w = whole_expert(gate_own), whole_expert(up_own), whole_expert(down_own)
     plane = lax.axis_index("dp").astype(jnp.int32).reshape(1)
     x_slots, place, near = call(
         functools.partial(place_kernel, experts, parts),
@@ -315,37 +304,24 @@
     (dy_slots,) = call(spread_kernel, [slot_shape], 256 * spread_flops, far=(2,))(
         near, cotangent, gate_own
     )
-    hidden_rows, by_gate, by_up = call(
-        functools.partial(hidden_kernel, parts, joined),
-        [hidden_shape, unit_shape, unit_shape],
-        2 * dot_flops,
-        [sems(3 * parts), sems(3), hidden_scratch, unit_scratch, unit_scratch, row_scratch]
-        + [in_scratch] * 2,
-        far=range(1, 1 + 3 * parts),
+    out_rows, by_gate, by_up = call(
+        functools.partial(forward_kernel, parts, joined),
+        [slot_shape, unit_shape, unit_shape],
+        3 * dot_flops,
+        [sems(4 * parts), sems(2 + pieces), row_scratch, in_scratch, in_scratch, down_scratch]
+        + [row_scratch, hidden_scratch, unit_scratch, unit_scratch],
+        far=range(1, 1 + 4 * parts),
         far_out=True,
         vmem=LARGE_VMEM,
-    )(plane, *x_shares, *gate_w, *up_w)
-    (down_own,) = call(
-        in_place_kernel, [down_own], 0, far=range(2), far_out=True, vmem=LARGE_VMEM, aliases={0: 0}
-    )(down_own, hidden_rows)
-    down_w = whole_expert(down_own)
-    (out_rows,) = call(
-        functools.partial(out_kernel, parts, joined),
-        [slot_shape],
-        dot_flops,
-        [sems(1 + pieces * parts), sems(pieces), row_scratch, hidden_scratch, down_scratch],
-        far=range(1 + parts),
-        far_out=True,
-    )(hidden_rows, *down_w)
+    )(plane, *x_shares, *gate_w, *up_w, *down_w)
     dy_shares = dispatch(dy_slots, (out_rows,))
     out_slots = send_back(out_rows)
     (grad_rows,) = call(
         functools.partial(backward_kernel, parts, joined),
         [slot_shape],
-        64 * dot_flops,
-        [sems(2 + 4 * parts), sems(pieces), hidden_scratch, hidden_scratch]
-        + [row_scratch, row_scratch, down_scratch, unit_scratch, unit_scratch]
-        + [in_scratch] * 2,
+        3 * dot_flops,
+        [sems(2 + 4 * parts), sems(pieces), row_scratch, down_scratch, unit_scratch, unit_scratch]
+        + [in_scratch, in_scratch, row_scratch, hidden_scratch, hidden_scratch],
         far=range(1, 3 + 4 * parts),
         far_out=True,
         vmem=LARGE_VMEM,

time: 185 us -> 186 us (level)
  Pallas kernels: 30.5 us -> 26.1 us
  starting transfers between devices: 24.3 us -> 28.2 us
  local copies, waits for them, and re-layouts: 9.59 us -> 12.4 us
    all_to_all x2, waiting for transfers between devices: 10.7 us -> 26.5 us  [dispatch(): lax.all_to_all(rows, axes, 0, 0, axis_index_groups=in_plane, tiled=True)]
    ppermute x3, waiting for transfers between devices: 25.1 us -> 10 us  [swapped(): return lax.ppermute(weight[0], axes, swap)]
    ppermute x2, waiting for transfers between devices: 42.6 us -> 47.2 us  [dispatch(): lax.ppermute(rows, 'dp', [(g, (g + i) % parts) for g in range(parts)])]
    pallas_call x10 -> x8, Pallas kernels: 30.5 us -> 26.1 us  [run(): pl.pallas_call(kernel, out_shape=tuple((jax.ShapeDtypeStruct(o.shape, o.d...]
    ppermute x2, starting transfers between devices: 0.55 us -> 4.42 us  [dispatch(): lax.ppermute(rows, 'dp', [(g, (g + i) % parts) for g in range(parts)])]
    all_to_all x2, waiting for transfers between devices: 37.5 us -> 33.8 us  [send_back(): lax.all_to_all(rows, axes, 0, 0, axis_index_groups=everywhere, tiled=True)]
    ppermute x3, waiting for transfers between devices: 3.61 us -> 0.33 us  [whole_expert(): held.append(lax.ppermute(own, 'expert', turn))]
    unnamed x25 -> x33, local copies, waits for them, and re-layouts: 9.59 us -> 12.4 us
  transfers between devices with their start and end apart: 12 -> 12, of which waited for: 8 -> 8; matrix products, arithmetic and copies ran while one was open for 1% -> 1% of each run, Pallas kernels for 15% -> 13%
where the time goes in v11:
time: 186 us; the launch traced here: 185 us
  waiting for transfers between devices  118 us (63%)
  starting transfers between devices  28.2 us (15%)
  Pallas kernels  26.1 us (14%)
  local copies, waits for them, and re-layouts  12.4 us (7%)
    ppermute x2, waiting for transfers between devices, dispatch(): lax.ppermute(rows, 'dp', [(g, (g + i) % parts) for g in range(parts)])  47.2 us
    all_to_all x2, waiting for transfers between devices, send_back(): lax.all_to_all(rows, axes, 0, 0, axis_index_groups=everywhere, tiled=True)  33.8 us
    all_to_all x2, waiting for transfers between devices, dispatch(): lax.all_to_all(rows, axes, 0, 0, axis_index_groups=in_plane, tiled=True)  26.5 us
    pallas_call x8, Pallas kernels, run(): pl.pallas_call(kernel, out_shape=tuple((jax.ShapeDtypeStruct(o.shape, o.d...  26.1 us
    unnamed x33, local copies, waits for them, and re-layouts  12.4 us
    all_to_all x2, starting transfers between devices, send_back(): lax.all_to_all(rows, axes, 0, 0, axis_index_groups=everywhere, tiled=True)  10.8 us
    ppermute x3, waiting for transfers between devices, swapped(): return lax.ppermute(weight[0], axes, swap)  10 us
    all_to_all x2, starting transfers between devices, dispatch(): lax.all_to_all(rows, axes, 0, 0, axis_index_groups=in_plane, tiled=True)  9.39 us
  transfers between devices with their start and end apart: 12, of which 8 were waited for; matrix products, arithmetic and copies ran while one was open for 1% of the time, Pallas kernels for 13%

profile of v11, /device:TPU:0, one launch (start us, length us, event | category | flops | bytes accessed | tf_op | source)
XLA Modules:
  0.0 185.3 jit_solution(13808606355239498747)
XLA Ops:
  0.6 3.0 %collective-permute-start.1 = (bf16[2048,384]{1,0:T(8,128)(2,1)}, bf16[2048,384]{1,0:T(8,128)(2,1)S(1)}, u32[]{:S(2)}, u32[]{:S(2)}) collective-permute-start(bf16[2048,384]{1,0:T(8,128)(2,1)} %bitcast.28), channel_id=1, source_target_pairs={{0,16},{1,0},{2,18},{3,2},{4,20},{5,4},{6,22},{7,6},{8,24},{9,8},{... | collective-permute-start | bytes 4718600 | tf_op jit(solution)/shard_map/ppermute | solution.py:243
  3.6 0.8 copy.10.routes_ref
  4.4 0.0 copy-start.8
  4.4 1.0 copy-done.8
  5.4 1.0 shard_map.94
  6.5 0.0 copy-start.3
  6.5 1.2 copy-done.3
  7.7 5.8 %all-to-all-start = ((bf16[8,48,2048]{2,1,0:T(8,128)(2,1)}), bf16[8,48,2048]{2,1,0:T(8,128)(2,1)S(1)}, u32[]{:S(2)}, u32[]{:S(2)}) async-start(bf16[8,48,2048]{2,1,0:T(8,128)(2,1)} %bitcast.22), calls=%async_computation | async-start | bytes 3145728 | tf_op jit(solution)/shard_map/all_to_all | solution.py:254
  13.5 0.0 collective-permute-start.3
  13.5 0.0 collective-permute-start.5
  13.5 8.3 %collective-permute-done.1.refs_2_._.refs_6_ = bf16[2048,384]{1,0:T(8,128)(2,1)S(1)} collective-permute-done((bf16[2048,384]{1,0:T(8,128)(2,1)}, bf16[2048,384]{1,0:T(8,128)(2,1)S(1)}, u32[]{:S(2)}, u32[]{:S(2)}) %collective-permute-start.1) | collective-permute-done | bytes 1572896 | tf_op jit(solution)/shard_map/ppermute | solution.py:243
  21.9 0.0 copy-start.1
  21.9 0.0 copy-start.5
  21.9 1.4 copy-done.5
  23.3 0.6 shard_map.98
  23.9 0.0 copy-done.1
  23.9 0.0 copy-start.2
  23.9 1.2 copy-done.2
  25.1 24.6 %all-to-all-done = bf16[8,48,2048]{2,1,0:T(8,128)(2,1)S(1)} async-done(((bf16[8,48,2048]{2,1,0:T(8,128)(2,1)}), bf16[8,48,2048]{2,1,0:T(8,128)(2,1)S(1)}, u32[]{:S(2)}, u32[]{:S(2)}) %all-to-all-start) | async-done | bytes 1572896 | tf_op jit(solution)/shard_map/all_to_all | solution.py:254
  49.7 3.6 %all-to-all-start.2 = ((bf16[8,48,2048]{2,1,0:T(8,128)(2,1)}), bf16[8,48,2048]{2,1,0:T(8,128)(2,1)S(1)}, u32[]{:S(2)}, u32[]{:S(2)}) async-start(bf16[8,48,2048]{2,1,0:T(8,128)(2,1)} %bitcast.21), calls=%async_computation.2 | async-start | bytes 3145728 | tf_op jit(solution)/shard_map/all_to_all | solution.py:254
  53.3 0.1 collective-permute-start.2
  53.4 0.0 collective-permute-done.3.refs_4_.refs_8_
  53.4 0.5 collective-permute-start.4
  53.9 1.7 collective-permute-done.5.refs_6_.refs_2_
  55.6 0.0 collective-permute-start.6
  55.6 2.2 %shard_map.95 = (bf16[8,24,2048]{2,1,0:T(8,128)(2,1)S(1)}, bf16[8,24,2048]{2,1,0:T(8,128)(2,1)S(1)}) custom-call(bf16[8,2,24,2048]{3,2,1,0:T(8,128)(2,1)S(1)} %bitcast.17), custom_call_target="tpu_custom_call" | custom-call | bytes 3145728 | tf_op jit(solution)/shard_map/pallas_call | solution.py:203
  57.8 0.0 copy-start.7
  57.8 0.9 copy-done.7
  58.6 2.5 %collective-permute-start = (bf16[192,2048]{1,0:T(8,128)(2,1)S(1)}, bf16[192,2048]{1,0:T(8,128)(2,1)S(1)}, u32[]{:S(2)}, u32[]{:S(2)}) collective-permute-start(bf16[192,2048]{1,0:T(8,128)(2,1)S(1)} %bitcast.25), channel_id=1, source_target_pairs={{0,16},{16,0},{1,17},{17,1},{2,18},{18,2},{3,19},{19,3},{4,20},{20... | collective-permute-start | bytes 2359304 | tf_op jit(solution)/shard_map/ppermute | solution.py:267
  61.1 0.0 collective-permute-done.2.refs_3_.refs_7_
  61.1 0.0 copy-start.9
  61.1 0.0 collective-permute-done.4.refs_5_.refs_9_
  61.1 0.0 copy-start.10
  61.2 0.3 collective-permute-done.6.refs_7_.refs_3_
  61.5 0.0 copy-start.11
  61.5 17.8 %collective-permute-done.refs_1_ = bf16[192,2048]{1,0:T(8,128)(2,1)S(1)} collective-permute-done((bf16[192,2048]{1,0:T(8,128)(2,1)S(1)}, bf16[192,2048]{1,0:T(8,128)(2,1)S(1)}, u32[]{:S(2)}, u32[]{:S(2)}) %collective-permute-start) | collective-permute-done | bytes 786464 | tf_op jit(solution)/shard_map/ppermute | solution.py:267
  79.3 0.0 copy-done.9
  79.3 0.0 copy-done.10
  79.3 0.0 copy-done.11
  79.3 0.9 copy-done.14
  80.2 8.3 %shard_map.96 = (bf16[384,2048]{1,0:T(8,128)(2,1)}, f32[1,384,768]{2,1,0:T(8,128)}, f32[1,384,768]{2,1,0:T(8,128)}) custom-call(s32[1]{0:T(128)} %bitcast.plane_ref, bf16[192,2048]{1,0:T(8,128)(2,1)} %bitcast.24, bf16[192,2048]{1,0:T(8,128)(2,1)} %copy-done.14, bf16[2048,384]{1,0:T(8,128)(2,1)} %copy-done.1, bf16[2048,384]{1,0:T(8,128)(2,1)} %copy-done.9, ...), custom_call_target="tpu_custom_call" | custom-call | flops 3623878656 | bytes 14942212 | tf_op jit(solution)/shard_map/pallas_call | solution.py:203
  88.5 1.9 %all-to-all-done.2 = bf16[8,48,2048]{2,1,0:T(8,128)(2,1)S(1)} async-done(((bf16[8,48,2048]{2,1,0:T(8,128)(2,1)}), bf16[8,48,2048]{2,1,0:T(8,128)(2,1)S(1)}, u32[]{:S(2)}, u32[]{:S(2)}) %all-to-all-start.2) | async-done | bytes 1572896 | tf_op jit(solution)/shard_map/all_to_all | solution.py:254
  90.4 5.2 %all-to-all-start.1 = ((bf16[16,24,2048]{2,1,0:T(8,128)(2,1)}), bf16[16,24,2048]{2,1,0:T(8,128)(2,1)S(1)}, u32[]{:S(2)}, u32[]{:S(2)}) async-start(bf16[16,24,2048]{2,1,0:T(8,128)(2,1)} %bitcast.19), calls=%async_computation.1 | async-start | bytes 3145728 | tf_op jit(solution)/shard_map/all_to_all | solution.py:273
  95.7 0.0 copy-start
  95.7 1.4 copy-done
  97.1 2.2 %shard_map.99 = (bf16[8,24,2048]{2,1,0:T(8,128)(2,1)S(1)}, bf16[8,24,2048]{2,1,0:T(8,128)(2,1)S(1)}) custom-call(bf16[8,2,24,2048]{3,2,1,0:T(8,128)(2,1)S(1)} %bitcast.16, bf16[384,2048]{1,0:T(8,128)(2,1)S(1)} %copy-done), custom_call_target="tpu_custom_call" | custom-call | bytes 4718592 | tf_op jit(solution)/shard_map/pallas_call | solution.py:203
  99.3 0.0 copy-start.4
  99.3 0.9 copy-done.4
  100.2 1.9 %collective-permute-start.7 = (bf16[192,2048]{1,0:T(8,128)(2,1)S(1)}, bf16[192,2048]{1,0:T(8,128)(2,1)S(1)}, u32[]{:S(2)}, u32[]{:S(2)}) collective-permute-start(bf16[192,2048]{1,0:T(8,128)(2,1)S(1)} %bitcast.26), channel_id=1, source_target_pairs={{0,16},{16,0},{1,17},{17,1},{2,18},{18,2},{3,19},{19,3},{4,20},{20... | collective-permute-start | bytes 2359304 | tf_op jit(solution)/shard_map/ppermute | solution.py:267
  102.1 29.4 %collective-permute-done.7.refs_1_ = bf16[192,2048]{1,0:T(8,128)(2,1)S(1)} collective-permute-done((bf16[192,2048]{1,0:T(8,128)(2,1)S(1)}, bf16[192,2048]{1,0:T(8,128)(2,1)S(1)}, u32[]{:S(2)}, u32[]{:S(2)}) %collective-permute-start.7) | collective-permute-done | bytes 786464 | tf_op jit(solution)/shard_map/ppermute | solution.py:267
  131.5 0.0 copy-start.12
  131.5 0.9 copy-done.12
  132.4 8.6 %shard_map.100 = bf16[384,2048]{1,0:T(8,128)(2,1)} custom-call(s32[1]{0:T(128)} %bitcast.plane_ref, bf16[192,2048]{1,0:T(8,128)(2,1)} %bitcast.23, bf16[192,2048]{1,0:T(8,128)(2,1)} %copy-done.12, bf16[384,2048]{1,0:T(8,128)(2,1)} %collective-permute-done.5.refs_6_.refs_2_, bf16[384,2048]{1,0:T(8,128)(2,1)} %copy-done.11, ...), custom_call_target="tpu_custom_call" | custom-call | flops 3623878656 | bytes 14942212 | tf_op jit(solution)/shard_map/pallas_call | solution.py:203
  141.0 0.0 all-to-all-done.1
  141.0 0.0 copy-start.13
  141.0 5.6 %all-to-all-start.3 = ((bf16[16,24,2048]{2,1,0:T(8,128)(2,1)}), bf16[16,24,2048]{2,1,0:T(8,128)(2,1)S(1)}, u32[]{:S(2)}, u32[]{:S(2)}) async-start(bf16[16,24,2048]{2,1,0:T(8,128)(2,1)} %bitcast.27), calls=%async_computation.3 | async-start | bytes 3145728 | tf_op jit(solution)/shard_map/all_to_all | solution.py:273
  146.6 0.0 copy-done.13
  146.6 0.1 copy.11.gates_ref
  146.7 0.0 copy-start.6
  146.7 1.0 copy-done.6
  147.7 1.7 shard_map.97
  149.4 0.6 copy.13
  150.0 33.8 %all-to-all-done.3 = bf16[16,24,2048]{2,1,0:T(8,128)(2,1)S(1)} async-done(((bf16[16,24,2048]{2,1,0:T(8,128)(2,1)}), bf16[16,24,2048]{2,1,0:T(8,128)(2,1)S(1)}, u32[]{:S(2)}, u32[]{:S(2)}) %all-to-all-start.3) | async-done | bytes 1572896 | tf_op jit(solution)/shard_map/all_to_all | solution.py:273
  183.8 1.5 shard_map.101
  (1 shorter events, 0.0 us)
Async XLA Ops:
  0.6 21.2 %collective-permute-start.1 = (bf16[2048,384]{1,0:T(8,128)(2,1)}, bf16[2048,384]{1,0:T(8,128)(2,1)S(1)}, u32[]{:S(2)}, u32[]{:S(2)}) collective-permute-start(bf16[2048,384]{1,0:T(8,128)(2,1)} %bitcast.28), channel_id=1, source_target_pairs={{0,16},{1,0},{2,18},{3,2},{4,20},{5,4},{6,22},{7,6},{8,24},{9,8},{... | collective-permute-start | bytes 4718600 | tf_op jit(solution)/shard_map/ppermute | solution.py:243
  4.4 1.0 copy-start.8
  6.5 1.2 copy-start.3
  7.7 42.0 %all-to-all-start = ((bf16[8,48,2048]{2,1,0:T(8,128)(2,1)}), bf16[8,48,2048]{2,1,0:T(8,128)(2,1)S(1)}, u32[]{:S(2)}, u32[]{:S(2)}) async-start(bf16[8,48,2048]{2,1,0:T(8,128)(2,1)} %bitcast.22), calls=%async_computation | async-start | bytes 3145728 | tf_op jit(solution)/shard_map/all_to_all | solution.py:254
  13.5 39.9 %collective-permute-start.3 = (bf16[2048,384]{1,0:T(8,128)(2,1)}, bf16[2048,384]{1,0:T(8,128)(2,1)}, u32[]{:S(2)}, u32[]{:S(2)}) collective-permute-start(bf16[2048,384]{1,0:T(8,128)(2,1)} %bitcast.29), channel_id=1, source_target_pairs={{0,16},{1,0},{2,18},{3,2},{4,20},{5,4},{6,22},{7,6},{8,24},{9,8},{... | collective-permute-start | bytes 4718600 | tf_op jit(solution)/shard_map/ppermute | solution.py:243
  13.5 42.1 %collective-permute-start.5 = (bf16[384,2048]{1,0:T(8,128)(2,1)}, bf16[384,2048]{1,0:T(8,128)(2,1)}, u32[]{:S(2)}, u32[]{:S(2)}) collective-permute-start(bf16[384,2048]{1,0:T(8,128)(2,1)} %bitcast.30), channel_id=1, source_target_pairs={{0,16},{1,0},{2,18},{3,2},{4,20},{5,4},{6,22},{7,6},{8,24},{9,8},{... | collective-permute-start | bytes 4718600 | tf_op jit(solution)/shard_map/ppermute | solution.py:243
  21.9 2.0 %copy-start.1 = (bf16[2048,384]{1,0:T(8,128)(2,1)}, bf16[2048,384]{1,0:T(8,128)(2,1)S(1)}, u32[]{:S(2)}) copy-start(bf16[2048,384]{1,0:T(8,128)(2,1)S(1)} %collective-permute-done.1.refs_2_._.refs_6_) | copy-start | bytes 4718596
  21.9 1.4 copy-start.5
  23.9 1.2 copy-start.2
  49.7 40.7 %all-to-all-start.2 = ((bf16[8,48,2048]{2,1,0:T(8,128)(2,1)}), bf16[8,48,2048]{2,1,0:T(8,128)(2,1)S(1)}, u32[]{:S(2)}, u32[]{:S(2)}) async-start(bf16[8,48,2048]{2,1,0:T(8,128)(2,1)} %bitcast.21), calls=%async_computation.2 | async-start | bytes 3145728 | tf_op jit(solution)/shard_map/all_to_all | solution.py:254
  53.3 7.8 %collective-permute-start.2 = (bf16[2048,384]{1,0:T(8,128)(2,1)}, bf16[2048,384]{1,0:T(8,128)(2,1)S(1)}, u32[]{:S(2)}, u32[]{:S(2)}) collective-permute-start(bf16[2048,384]{1,0:T(8,128)(2,1)} %copy-done.1), channel_id=1, source_target_pairs={{0,1},{1,0},{2,3},{3,2},{4,5},{5,4},{6,7},{7,6},{8,9},{9,8},{10,11... | collective-permute-start | bytes 4718600 | tf_op jit(solution)/shard_map/ppermute | solution.py:249
  53.4 7.8 %collective-permute-start.4 = (bf16[2048,384]{1,0:T(8,128)(2,1)}, bf16[2048,384]{1,0:T(8,128)(2,1)S(1)}, u32[]{:S(2)}, u32[]{:S(2)}) collective-permute-start(bf16[2048,384]{1,0:T(8,128)(2,1)} %collective-permute-done.3.refs_4_.refs_8_), channel_id=1, source_target_pairs={{0,1},{1,0},{2,3},{3,2},{4,5},{5,4},{6,7},{7,6},{8,9},{9,8},{10,11... | collective-permute-start | bytes 4718600 | tf_op jit(solution)/shard_map/ppermute | solution.py:249
  55.6 5.9 %collective-permute-start.6 = (bf16[384,2048]{1,0:T(8,128)(2,1)}, bf16[384,2048]{1,0:T(8,128)(2,1)S(1)}, u32[]{:S(2)}, u32[]{:S(2)}) collective-permute-start(bf16[384,2048]{1,0:T(8,128)(2,1)} %collective-permute-done.5.refs_6_.refs_2_), channel_id=1, source_target_pairs={{0,1},{1,0},{2,3},{3,2},{4,5},{5,4},{6,7},{7,6},{8,9},{9,8},{10,11... | collective-permute-start | bytes 4718600 | tf_op jit(solution)/shard_map/ppermute | solution.py:249
  57.8 0.9 copy-start.7
  58.6 20.7 %collective-permute-start = (bf16[192,2048]{1,0:T(8,128)(2,1)S(1)}, bf16[192,2048]{1,0:T(8,128)(2,1)S(1)}, u32[]{:S(2)}, u32[]{:S(2)}) collective-permute-start(bf16[192,2048]{1,0:T(8,128)(2,1)S(1)} %bitcast.25), channel_id=1, source_target_pairs={{0,16},{16,0},{1,17},{17,1},{2,18},{18,2},{3,19},{19,3},{4,20},{20... | collective-permute-start | bytes 2359304 | tf_op jit(solution)/shard_map/ppermute | solution.py:267
  61.1 18.2 %copy-start.9 = (bf16[2048,384]{1,0:T(8,128)(2,1)}, bf16[2048,384]{1,0:T(8,128)(2,1)S(1)}, u32[]{:S(2)}) copy-start(bf16[2048,384]{1,0:T(8,128)(2,1)S(1)} %collective-permute-done.2.refs_3_.refs_7_) | copy-start | bytes 4718596
  61.1 18.2 %copy-start.10 = (bf16[2048,384]{1,0:T(8,128)(2,1)}, bf16[2048,384]{1,0:T(8,128)(2,1)S(1)}, u32[]{:S(2)}) copy-start(bf16[2048,384]{1,0:T(8,128)(2,1)S(1)} %collective-permute-done.4.refs_5_.refs_9_) | copy-start | bytes 4718596
  61.5 17.9 %copy-start.11 = (bf16[384,2048]{1,0:T(8,128)(2,1)}, bf16[384,2048]{1,0:T(8,128)(2,1)S(1)}, u32[]{:S(2)}) copy-start(bf16[384,2048]{1,0:T(8,128)(2,1)S(1)} %collective-permute-done.6.refs_7_.refs_3_) | copy-start | bytes 4718596
  79.3 0.9 copy-start.14
  90.4 50.6 %all-to-all-start.1 = ((bf16[16,24,2048]{2,1,0:T(8,128)(2,1)}), bf16[16,24,2048]{2,1,0:T(8,128)(2,1)S(1)}, u32[]{:S(2)}, u32[]{:S(2)}) async-start(bf16[16,24,2048]{2,1,0:T(8,128)(2,1)} %bitcast.19), calls=%async_computation.1 | async-start | bytes 3145728 | tf_op jit(solution)/shard_map/all_to_all | solution.py:273
  95.7 1.4 copy-start
  99.3 0.9 copy-start.4
  100.2 31.3 %collective-permute-start.7 = (bf16[192,2048]{1,0:T(8,128)(2,1)S(1)}, bf16[192,2048]{1,0:T(8,128)(2,1)S(1)}, u32[]{:S(2)}, u32[]{:S(2)}) collective-permute-start(bf16[192,2048]{1,0:T(8,128)(2,1)S(1)} %bitcast.26), channel_id=1, source_target_pairs={{0,16},{16,0},{1,17},{17,1},{2,18},{18,2},{3,19},{19,3},{4,20},{20... | collective-permute-start | bytes 2359304 | tf_op jit(solution)/shard_map/ppermute | solution.py:267
  131.5 0.9 copy-start.12
  141.0 5.6 %copy-start.13 = (f32[128,2]{0,1:T(2,128)S(1)}, f32[128,2]{0,1:T(2,128)}, u32[]{:S(2)}) copy-start(f32[128,2]{0,1:T(2,128)} %param.10) | copy-start | bytes 3076
  141.0 42.8 %all-to-all-start.3 = ((bf16[16,24,2048]{2,1,0:T(8,128)(2,1)}), bf16[16,24,2048]{2,1,0:T(8,128)(2,1)S(1)}, u32[]{:S(2)}, u32[]{:S(2)}) async-start(bf16[16,24,2048]{2,1,0:T(8,128)(2,1)} %bitcast.27), calls=%async_computation.3 | async-start | bytes 3145728 | tf_op jit(solution)/shard_map/all_to_all | solution.py:273
  146.7 1.0 copy-start.6

commit v12 on v11

--- a/solution.py
+++ b/solution.py
@@ -9,7 +9,7 @@
 
 BF16 = jnp.bfloat16
 F32 = jnp.float32
-SMALL_VMEM, LARGE_VMEM = 12 << 20, 60 << 20
+SMALL_VMEM, LARGE_VMEM = 12 << 20, 62_300_000
 
 
 def dot(a, b, dims):
@@ -42,10 +42,12 @@
     return [unit_ref.at[0, cut] if axis == 0 else unit_ref.at[0, :, cut] for cut in cuts]
 
 
-def place_kernel(experts, parts, plane_ref, routes_ref, tokens_ref, slots_ref, place_ref, near_ref):
+def place_kernel(experts, parts, plane_ref, routes_ref, tokens_ref, slots_ref, near_ref, *refs):
+    place_ref, sems, out_sems, rows_ref, stage_ref = refs
     slots, width = slots_ref.shape
     capacity = slots // experts
     tok_rows, top_count = routes_ref.shape
+    (copy,) = fetch([tokens_ref], [rows_ref], sems)
     routes = routes_ref[...]
     home_plane, home_set = lax.rem(routes + 1, parts), lax.div(routes, parts)
     lanes = home_plane * (experts // parts) + home_set
@@ -68,23 +70,30 @@
         )
         place_ref[k * tok_rows : (k + 1) * tok_rows, :] = mark.astype(BF16)
         near = near_mark if near is None else near + near_mark
-    near = near.astype(BF16)
-    near_ref[...] = near
-    for columns in tiles(width):
-        slots_ref[:, columns] = dot(near, tokens_ref[:, columns], (0, 0)).astype(BF16)
-
-
-def spread_kernel(near_ref, rows_ref, _, slots_ref):
-    for columns in tiles(rows_ref.shape[1]):
-        slots_ref[:, columns] = dot(near_ref[...], rows_ref[:, columns], (0, 0)).astype(BF16)
-
-
-def cut_kernel(parts, rows_ref, *refs):
-    out_refs, sems = refs[-1 - parts : -1], refs[-1]
+    near_ref[...] = near.astype(BF16)
+    copy.wait()
+    spread(near_ref, rows_ref, stage_ref, slots_ref, out_sems)
+
+
+def spread(near_ref, rows_ref, stage_ref, slots_ref, sems):
+    sent = []
+    for d, columns in enumerate(tiles(rows_ref.shape[1])):
+        stage_ref[:, columns] = dot(near_ref[...], rows_ref[:, columns], (0, 0)).astype(BF16)
+        sent.append(store(stage_ref.at[:, columns], slots_ref.at[:, columns], sems.at[d]))
+    for copy in sent:
+        copy.wait()
+
+
+def spread_kernel(near_ref, rows_ref, _, slots_ref, out_sems, stage_ref):
+    spread(near_ref, rows_ref, stage_ref, slots_ref, out_sems)
+
+
+def cut_kernel(numbers, rows_ref, *refs):
+    out_refs, sems = refs[-1 - len(numbers) : -1], refs[-1]
     sets = rows_ref.shape[0]
     for copy in fetch(
-        [rows_ref.at[q, i] for i in range(parts) for q in range(sets)],
-        [out_refs[i].at[q] for i in range(parts) for q in range(sets)],
+        [rows_ref.at[q, i] for i in numbers for q in range(sets)],
+        [out_ref.at[q] for out_ref in out_refs for q in range(sets)],
         sems,
     ):
         copy.wait()
@@ -193,19 +202,26 @@
     out_ref[...] = total.astype(BF16)
 
 
-def call(kernel, outs, flops, scratch=(), far=(), far_out=False, vmem=SMALL_VMEM):
+def call(kernel, outs, flops, scratch=(), far=(), pinned=(), out_spaces=None, vmem=SMALL_VMEM):
     def run(*args):
         moved = sum(a.size * a.dtype.itemsize for a in (*args, *outs))
         spaces = [
-            pltpu.SMEM if a.shape == (1,) else pl.ANY if i in far else pltpu.VMEM
+            pltpu.SMEM
+            if a.shape == (1,)
+            else pl.ANY
+            if i in far
+            else pltpu.HBM
+            if i in pinned
+            else pltpu.VMEM
             for i, a in enumerate(args)
         ]
         return pl.pallas_call(
             kernel,
-            out_shape=tuple(jax.ShapeDtypeStruct(o.shape, o.dtype) for o in outs),
+            out_shape=tuple(outs),
             in_specs=[pl.BlockSpec(memory_space=space) for space in spaces],
             out_specs=tuple(
-                pl.BlockSpec(memory_space=pl.ANY if far_out else pltpu.VMEM) for _ in outs
+                pl.BlockSpec(memory_space=space)
+                for space in out_spaces or [pltpu.VMEM] * len(outs)
             ),
             scratch_shapes=scratch,
             compiler_params=pltpu.CompilerParams(vmem_limit_bytes=vmem),
@@ -252,16 +268,23 @@
     def dispatch(rows, after=()):
         rows = rows.reshape(sets, parts * capacity, width)
         rows = lax.all_to_all(rows, axes, 0, 0, axis_index_groups=in_plane, tiled=True)
-        cut = call(
-            functools.partial(cut_kernel, parts),
-            [jax.ShapeDtypeStruct((sets, capacity, width), BF16)] * parts,
-            0,
-            [sems(parts * sets)],
-            far=range(1 + len(after)),
-            far_out=True,
-        )(rows.reshape(sets, parts, capacity, width), *after)
+        rows = rows.reshape(sets, parts, capacity, width)
+
+        def cut(numbers, space):
+            return call(
+                functools.partial(cut_kernel, numbers),
+                [jax.ShapeDtypeStruct((sets, capacity, width), BF16)] * len(numbers),
+                0,
+                [sems(len(numbers) * sets)],
+                far=(0,),
+                pinned=range(1, 1 + len(after)),
+                out_spaces=[space] * len(numbers),
+            )(rows, *after)
+
+        leaving = cut(range(1, parts), pl.ANY)
+        cuts = [*cut(range(1), pltpu.HBM), *leaving]
         crossed = []
-        for i, rows in enumerate(cut):
+        for i, rows in enumerate(cuts):
             rows = rows.reshape(sets * capacity, width)
             if i > 0:
                 rows = lax.ppermute(rows, "dp", [(g, (g + i) % parts) for g in range(parts)])
@@ -295,15 +318,23 @@
     gate_own, up_own, down_own = swapped(w_gate), swapped(w_up), swapped(w_down)
     gate_w, up_w, down_w = whole_expert(gate_own), whole_expert(up_own), whole_expert(down_own)
     plane = lax.axis_index("dp").astype(jnp.int32).reshape(1)
-    x_slots, place, near = call(
+    x_slots, near, place = call(
         functools.partial(place_kernel, experts, parts),
-        [slot_shape, place_shape, jax.ShapeDtypeStruct((tok_rows, slots), BF16)],
+        [slot_shape, jax.ShapeDtypeStruct((tok_rows, slots), BF16), place_shape],
         spread_flops,
+        [sems(1), sems(pieces), pltpu.VMEM((tok_rows, width), BF16), row_scratch],
+        pinned=(2,),
+        out_spaces=[pltpu.HBM, pltpu.VMEM, pltpu.VMEM],
     )(plane, routes, tokens)
     x_shares = dispatch(x_slots)
-    (dy_slots,) = call(spread_kernel, [slot_shape], 256 * spread_flops, far=(2,))(
-        near, cotangent, gate_own
-    )
+    (dy_slots,) = call(
+        spread_kernel,
+        [slot_shape],
+        256 * spread_flops,
+        [sems(pieces), row_scratch],
+        pinned=(2,),
+        out_spaces=[pltpu.HBM],
+    )(near, cotangent, gate_own)
     out_rows, by_gate, by_up = call(
         functools.partial(forward_kernel, parts, joined),
         [slot_shape, unit_shape, unit_shape],
@@ -311,7 +342,7 @@
         [sems(4 * parts), sems(2 + pieces), row_scratch, in_scratch, in_scratch, down_scratch]
         + [row_scratch, hidden_scratch, unit_scratch, unit_scratch],
         far=range(1, 1 + 4 * parts),
-        far_out=True,
+        out_spaces=[pltpu.HBM] * 3,
         vmem=LARGE_VMEM,
     )(plane, *x_shares, *gate_w, *up_w, *down_w)
     dy_shares = dispatch(dy_slots, (out_rows,))
@@ -319,11 +350,11 @@
     (grad_rows,) = call(
         functools.partial(backward_kernel, parts, joined),
         [slot_shape],
-        3 * dot_flops,
+        64 * dot_flops,
         [sems(2 + 4 * parts), sems(pieces), row_scratch, down_scratch, unit_scratch, unit_scratch]
         + [in_scratch, in_scratch, row_scratch, hidden_scratch, hidden_scratch],
         far=range(1, 3 + 4 * parts),
-        far_out=True,
+        out_spaces=[pltpu.HBM],
         vmem=LARGE_VMEM,
     )(plane, *dy_shares, *down_w, by_gate, by_up, *gate_w, *up_w)
     grad_slots = send_back(grad_rows)

time: 186 us -> 177 us (0.952)
  local copies, waits for them, and re-layouts: 12.4 us -> 7.45 us
  starting transfers between devices: 28.2 us -> 25 us
  waiting for transfers between devices: 118 us -> 115 us
    ppermute x2, waiting for transfers between devices: 47.2 us -> 38.9 us  [dispatch(): lax.ppermute(rows, 'dp', [(g, (g + i) % parts) for g in range(parts)])]
    unnamed x33 -> x25, local copies, waits for them, and re-layouts: 12.4 us -> 7.45 us
    all_to_all x2, waiting for transfers between devices: 33.8 us -> 37 us  [send_back(): lax.all_to_all(rows, axes, 0, 0, axis_index_groups=everywhere, tiled=True)]
    all_to_all x2, starting transfers between devices: 10.8 us -> 8.16 us  [send_back(): lax.all_to_all(rows, axes, 0, 0, axis_index_groups=everywhere, tiled=True)]
    all_to_all x2, waiting for transfers between devices: 26.5 us -> 29.1 us  [dispatch(): lax.all_to_all(rows, axes, 0, 0, axis_index_groups=in_plane, tiled=True)]
    pallas_call x8 -> x10, Pallas kernels: 26.1 us -> 27.7 us  [run(): pl.pallas_call(kernel, out_shape=tuple(outs), in_specs=[pl.BlockSpec(memo...]
  transfers between devices with their start and end apart: 12 -> 12, of which waited for: 8 -> 9; matrix products, arithmetic and copies ran while one was open for 1% -> 1% of each run, Pallas kernels for 13% -> 14%
where the time goes in v12:
time: 177 us; the launch traced here: 176 us
  waiting for transfers between devices  115 us (65%)
  Pallas kernels  27.7 us (16%)
  starting transfers between devices  25 us (14%)
  local copies, waits for them, and re-layouts  7.45 us (4%)
    ppermute x2, waiting for transfers between devices, dispatch(): lax.ppermute(rows, 'dp', [(g, (g + i) % parts) for g in range(parts)])  38.9 us
    all_to_all x2, waiting for transfers between devices, send_back(): lax.all_to_all(rows, axes, 0, 0, axis_index_groups=everywhere, tiled=True)  37 us
    all_to_all x2, waiting for transfers between devices, dispatch(): lax.all_to_all(rows, axes, 0, 0, axis_index_groups=in_plane, tiled=True)  29.1 us
    pallas_call x10, Pallas kernels, run(): pl.pallas_call(kernel, out_shape=tuple(outs), in_specs=[pl.BlockSpec(memo...  27.7 us
    ppermute x3, waiting for transfers between devices, swapped(): return lax.ppermute(weight[0], axes, swap)  10 us
    all_to_all x2, starting transfers between devices, dispatch(): lax.all_to_all(rows, axes, 0, 0, axis_index_groups=in_plane, tiled=True)  9.53 us
    all_to_all x2, starting transfers between devices, send_back(): lax.all_to_all(rows, axes, 0, 0, axis_index_groups=everywhere, tiled=True)  8.16 us
    unnamed x25, local copies, waits for them, and re-layouts  7.45 us
  transfers between devices with their start and end apart: 12, of which 9 were waited for; matrix products, arithmetic and copies ran while one was open for 1% of the time, Pallas kernels for 14%

profile of v12, /device:TPU:0, one launch (start us, length us, event | category | flops | bytes accessed | tf_op | source)
XLA Modules:
  0.0 176.3 jit_solution(2858041809961546344)
XLA Ops:
  0.6 3.0 %collective-permute-start.1 = (bf16[2048,384]{1,0:T(8,128)(2,1)}, bf16[2048,384]{1,0:T(8,128)(2,1)}, u32[]{:S(2)}, u32[]{:S(2)}) collective-permute-start(bf16[2048,384]{1,0:T(8,128)(2,1)} %bitcast.27), channel_id=1, source_target_pairs={{0,16},{1,0},{2,18},{3,2},{4,20},{5,4},{6,22},{7,6},{8,24},{9,8},{... | collective-permute-start | bytes 4718600 | tf_op jit(solution)/shard_map/ppermute | solution.py:259
  3.6 0.8 copy.10.routes_ref
  4.4 0.0 copy-start.5
  4.4 1.0 copy-done.5
  5.4 2.1 %shard_map.94 = (bf16[384,2048]{1,0:T(8,128)(2,1)}, bf16[128,384]{1,0:T(8,128)(2,1)S(1)}, bf16[256,384]{1,0:T(8,128)(2,1)S(1)}) custom-call(s32[1]{0:T(128)} %bitcast.plane_ref, s32[128,2]{1,0:T(8,128)S(1)} %copy.10.routes_ref, bf16[128,2048]{1,0:T(8,128)(2,1)S(1)} %copy-done.5), custom_call_target="tpu_custom_call" | custom-call | flops 201326592 | bytes 2393092 | tf_op jit(solution)/shard_map/pallas_call | solution.py:218
  7.5 0.0 copy-start.3
  7.5 6.0 %all-to-all-start = ((bf16[8,48,2048]{2,1,0:T(8,128)(2,1)}), bf16[8,48,2048]{2,1,0:T(8,128)(2,1)S(1)}, u32[]{:S(2)}, u32[]{:S(2)}) async-start(bf16[8,48,2048]{2,1,0:T(8,128)(2,1)} %bitcast.1), calls=%async_computation | async-start | bytes 3145728 | tf_op jit(solution)/shard_map/all_to_all | solution.py:270
  13.5 0.0 collective-permute-start.3
  13.5 0.0 collective-permute-start.5
  13.5 8.3 %collective-permute-done.1.refs_2_._.refs_6_ = bf16[2048,384]{1,0:T(8,128)(2,1)} collective-permute-done((bf16[2048,384]{1,0:T(8,128)(2,1)}, bf16[2048,384]{1,0:T(8,128)(2,1)}, u32[]{:S(2)}, u32[]{:S(2)}) %collective-permute-start.1) | collective-permute-done | bytes 1572896 | tf_op jit(solution)/shard_map/ppermute | solution.py:259
  21.9 0.0 copy-done.3
  21.9 1.4 shard_map.99
  23.2 0.0 copy-start
  23.2 1.2 copy-done
  24.4 25.3 %all-to-all-done = bf16[8,48,2048]{2,1,0:T(8,128)(2,1)S(1)} async-done(((bf16[8,48,2048]{2,1,0:T(8,128)(2,1)}), bf16[8,48,2048]{2,1,0:T(8,128)(2,1)S(1)}, u32[]{:S(2)}, u32[]{:S(2)}) %all-to-all-start) | async-done | bytes 1572896 | tf_op jit(solution)/shard_map/all_to_all | solution.py:270
  49.7 3.6 %all-to-all-start.2 = ((bf16[8,48,2048]{2,1,0:T(8,128)(2,1)}), bf16[8,48,2048]{2,1,0:T(8,128)(2,1)S(1)}, u32[]{:S(2)}, u32[]{:S(2)}) async-start(bf16[8,48,2048]{2,1,0:T(8,128)(2,1)} %bitcast.22), calls=%async_computation.2 | async-start | bytes 3145728 | tf_op jit(solution)/shard_map/all_to_all | solution.py:270
  53.3 0.1 collective-permute-start.2
  53.4 0.0 collective-permute-done.3.refs_4_.refs_8_
  53.4 0.5 collective-permute-start.4
  53.9 1.7 collective-permute-done.5.refs_6_.refs_2_
  55.6 0.0 collective-permute-start.6
  55.6 1.1 shard_map.96
  56.7 2.6 %collective-permute-start = (bf16[192,2048]{1,0:T(8,128)(2,1)S(1)}, bf16[192,2048]{1,0:T(8,128)(2,1)S(1)}, u32[]{:S(2)}, u32[]{:S(2)}) collective-permute-start(bf16[192,2048]{1,0:T(8,128)(2,1)S(1)} %bitcast.24), channel_id=1, source_target_pairs={{0,16},{16,0},{1,17},{17,1},{2,18},{18,2},{3,19},{19,3},{4,20},{20... | collective-permute-start | bytes 2359304 | tf_op jit(solution)/shard_map/ppermute | solution.py:290
  59.2 1.1 shard_map.95
  60.3 0.0 copy-start.1
  60.3 0.9 copy-done.1
  61.2 0.0 collective-permute-done.2.refs_3_.refs_7_
  61.2 0.0 copy-start.7
  61.2 0.0 collective-permute-done.4.refs_5_.refs_9_
  61.2 0.0 copy-start.8
  61.2 0.3 collective-permute-done.6.refs_7_.refs_3_
  61.5 0.0 copy-start.9
  61.5 15.9 %collective-permute-done.refs_1_ = bf16[192,2048]{1,0:T(8,128)(2,1)S(1)} collective-permute-done((bf16[192,2048]{1,0:T(8,128)(2,1)S(1)}, bf16[192,2048]{1,0:T(8,128)(2,1)S(1)}, u32[]{:S(2)}, u32[]{:S(2)}) %collective-permute-start) | collective-permute-done | bytes 786464 | tf_op jit(solution)/shard_map/ppermute | solution.py:290
  77.4 0.0 copy-done.7
  77.4 0.0 copy-done.8
  77.4 0.0 copy-done.9
  77.4 0.0 copy-start.10
  77.4 0.9 copy-done.10
  78.3 8.3 %shard_map.97 = (bf16[384,2048]{1,0:T(8,128)(2,1)}, f32[1,384,768]{2,1,0:T(8,128)}, f32[1,384,768]{2,1,0:T(8,128)}) custom-call(s32[1]{0:T(128)} %bitcast.plane_ref, bf16[192,2048]{1,0:T(8,128)(2,1)} %bitcast.23, bf16[192,2048]{1,0:T(8,128)(2,1)} %copy-done.10, bf16[2048,384]{1,0:T(8,128)(2,1)} %collective-permute-done.1.refs_2_._.refs_6_, ...), custom_call_target="tpu_custom_call" | custom-call | flops 3623878656 | bytes 14942212 | tf_op jit(solution)/shard_map/pallas_call | solution.py:218
  86.6 3.8 %all-to-all-done.2 = bf16[8,48,2048]{2,1,0:T(8,128)(2,1)S(1)} async-done(((bf16[8,48,2048]{2,1,0:T(8,128)(2,1)}), bf16[8,48,2048]{2,1,0:T(8,128)(2,1)S(1)}, u32[]{:S(2)}, u32[]{:S(2)}) %all-to-all-start.2) | async-done | bytes 1572896 | tf_op jit(solution)/shard_map/all_to_all | solution.py:270
  90.4 1.0 shard_map.101
  91.4 1.2 collective-permute-start.7
  92.6 4.1 %all-to-all-start.1 = ((bf16[16,24,2048]{2,1,0:T(8,128)(2,1)}), bf16[16,24,2048]{2,1,0:T(8,128)(2,1)S(1)}, u32[]{:S(2)}, u32[]{:S(2)}) async-start(bf16[16,24,2048]{2,1,0:T(8,128)(2,1)} %bitcast.8), calls=%async_computation.1 | async-start | bytes 3145728 | tf_op jit(solution)/shard_map/all_to_all | solution.py:296
  96.7 1.1 shard_map.100
  97.8 0.0 copy-start.2
  97.8 0.9 copy-done.2
  98.7 23.0 %collective-permute-done.7.refs_1_ = bf16[192,2048]{1,0:T(8,128)(2,1)} collective-permute-done((bf16[192,2048]{1,0:T(8,128)(2,1)}, bf16[192,2048]{1,0:T(8,128)(2,1)}, u32[]{:S(2)}, u32[]{:S(2)}) %collective-permute-start.7) | collective-permute-done | bytes 786464 | tf_op jit(solution)/shard_map/ppermute | solution.py:290
  121.7 8.6 %shard_map.102 = bf16[384,2048]{1,0:T(8,128)(2,1)} custom-call(s32[1]{0:T(128)} %bitcast.plane_ref, bf16[192,2048]{1,0:T(8,128)(2,1)} %bitcast.25, bf16[192,2048]{1,0:T(8,128)(2,1)} %collective-permute-done.7.refs_1_, bf16[384,2048]{1,0:T(8,128)(2,1)} %collective-permute-done.5.refs_6_.refs_2_, bf16[384,2048]{1,0:T(8,128)(2,1)} %copy-done.9, ...), custom_call_target="tpu_custom_call" | custom-call | flops 77309411328 | bytes 14942212 | tf_op jit(solution)/shard_map/pallas_call | solution.py:218
  130.3 3.6 %all-to-all-done.1 = bf16[16,24,2048]{2,1,0:T(8,128)(2,1)S(1)} async-done(((bf16[16,24,2048]{2,1,0:T(8,128)(2,1)}), bf16[16,24,2048]{2,1,0:T(8,128)(2,1)S(1)}, u32[]{:S(2)}, u32[]{:S(2)}) %all-to-all-start.1) | async-done | bytes 1572896 | tf_op jit(solution)/shard_map/all_to_all | solution.py:296
  133.8 0.0 copy-start.6
  133.8 4.1 %all-to-all-start.3 = ((bf16[16,24,2048]{2,1,0:T(8,128)(2,1)}), bf16[16,24,2048]{2,1,0:T(8,128)(2,1)S(1)}, u32[]{:S(2)}, u32[]{:S(2)}) async-start(bf16[16,24,2048]{2,1,0:T(8,128)(2,1)} %bitcast.26), calls=%async_computation.3 | async-start | bytes 3145728 | tf_op jit(solution)/shard_map/all_to_all | solution.py:296
  137.9 0.0 copy-done.6
  137.9 0.1 copy.11.gates_ref
  138.1 0.0 copy-start.4
  138.1 1.0 copy-done.4
  139.1 1.7 shard_map.98
  140.8 0.6 copy.13
  141.4 33.4 %all-to-all-done.3 = bf16[16,24,2048]{2,1,0:T(8,128)(2,1)S(1)} async-done(((bf16[16,24,2048]{2,1,0:T(8,128)(2,1)}), bf16[16,24,2048]{2,1,0:T(8,128)(2,1)S(1)}, u32[]{:S(2)}, u32[]{:S(2)}) %all-to-all-start.3) | async-done | bytes 1572896 | tf_op jit(solution)/shard_map/all_to_all | solution.py:296
  174.8 1.5 shard_map.103
Async XLA Ops:
  0.6 21.2 %collective-permute-start.1 = (bf16[2048,384]{1,0:T(8,128)(2,1)}, bf16[2048,384]{1,0:T(8,128)(2,1)}, u32[]{:S(2)}, u32[]{:S(2)}) collective-permute-start(bf16[2048,384]{1,0:T(8,128)(2,1)} %bitcast.27), channel_id=1, source_target_pairs={{0,16},{1,0},{2,18},{3,2},{4,20},{5,4},{6,22},{7,6},{8,24},{9,8},{... | collective-permute-start | bytes 4718600 | tf_op jit(solution)/shard_map/ppermute | solution.py:259
  4.4 1.0 copy-start.5
  7.5 14.3 %copy-start.3 = (bf16[128,2048]{1,0:T(8,128)(2,1)S(1)}, bf16[128,2048]{1,0:T(8,128)(2,1)}, u32[]{:S(2)}) copy-start(bf16[128,2048]{1,0:T(8,128)(2,1)} %rows_ref.1) | copy-start | bytes 1572868
  7.5 42.2 %all-to-all-start = ((bf16[8,48,2048]{2,1,0:T(8,128)(2,1)}), bf16[8,48,2048]{2,1,0:T(8,128)(2,1)S(1)}, u32[]{:S(2)}, u32[]{:S(2)}) async-start(bf16[8,48,2048]{2,1,0:T(8,128)(2,1)} %bitcast.1), calls=%async_computation | async-start | bytes 3145728 | tf_op jit(solution)/shard_map/all_to_all | solution.py:270
  13.5 39.9 %collective-permute-start.3 = (bf16[2048,384]{1,0:T(8,128)(2,1)}, bf16[2048,384]{1,0:T(8,128)(2,1)}, u32[]{:S(2)}, u32[]{:S(2)}) collective-permute-start(bf16[2048,384]{1,0:T(8,128)(2,1)} %bitcast.28), channel_id=1, source_target_pairs={{0,16},{1,0},{2,18},{3,2},{4,20},{5,4},{6,22},{7,6},{8,24},{9,8},{... | collective-permute-start | bytes 4718600 | tf_op jit(solution)/shard_map/ppermute | solution.py:259
  13.5 42.1 %collective-permute-start.5 = (bf16[384,2048]{1,0:T(8,128)(2,1)}, bf16[384,2048]{1,0:T(8,128)(2,1)}, u32[]{:S(2)}, u32[]{:S(2)}) collective-permute-start(bf16[384,2048]{1,0:T(8,128)(2,1)} %bitcast.29), channel_id=1, source_target_pairs={{0,16},{1,0},{2,18},{3,2},{4,20},{5,4},{6,22},{7,6},{8,24},{9,8},{... | collective-permute-start | bytes 4718600 | tf_op jit(solution)/shard_map/ppermute | solution.py:259
  23.2 1.2 copy-start
  49.7 40.7 %all-to-all-start.2 = ((bf16[8,48,2048]{2,1,0:T(8,128)(2,1)}), bf16[8,48,2048]{2,1,0:T(8,128)(2,1)S(1)}, u32[]{:S(2)}, u32[]{:S(2)}) async-start(bf16[8,48,2048]{2,1,0:T(8,128)(2,1)} %bitcast.22), calls=%async_computation.2 | async-start | bytes 3145728 | tf_op jit(solution)/shard_map/all_to_all | solution.py:270
  53.3 7.9 %collective-permute-start.2 = (bf16[2048,384]{1,0:T(8,128)(2,1)}, bf16[2048,384]{1,0:T(8,128)(2,1)S(1)}, u32[]{:S(2)}, u32[]{:S(2)}) collective-permute-start(bf16[2048,384]{1,0:T(8,128)(2,1)} %collective-permute-done.1.refs_2_._.refs_6_), channel_id=1, source_target_pairs={{0,1},{1,0},{2,3},{3,2},{4,5},{5,4},{6,7},{7,6},{8,9},{9,8},{10,11... | collective-permute-start | bytes 4718600 | tf_op jit(solution)/shard_map/ppermute | solution.py:265
  53.4 7.8 %collective-permute-start.4 = (bf16[2048,384]{1,0:T(8,128)(2,1)}, bf16[2048,384]{1,0:T(8,128)(2,1)S(1)}, u32[]{:S(2)}, u32[]{:S(2)}) collective-permute-start(bf16[2048,384]{1,0:T(8,128)(2,1)} %collective-permute-done.3.refs_4_.refs_8_), channel_id=1, source_target_pairs={{0,1},{1,0},{2,3},{3,2},{4,5},{5,4},{6,7},{7,6},{8,9},{9,8},{10,11... | collective-permute-start | bytes 4718600 | tf_op jit(solution)/shard_map/ppermute | solution.py:265
  55.6 5.9 %collective-permute-start.6 = (bf16[384,2048]{1,0:T(8,128)(2,1)}, bf16[384,2048]{1,0:T(8,128)(2,1)S(1)}, u32[]{:S(2)}, u32[]{:S(2)}) collective-permute-start(bf16[384,2048]{1,0:T(8,128)(2,1)} %collective-permute-done.5.refs_6_.refs_2_), channel_id=1, source_target_pairs={{0,1},{1,0},{2,3},{3,2},{4,5},{5,4},{6,7},{7,6},{8,9},{9,8},{10,11... | collective-permute-start | bytes 4718600 | tf_op jit(solution)/shard_map/ppermute | solution.py:265
  56.7 20.7 %collective-permute-start = (bf16[192,2048]{1,0:T(8,128)(2,1)S(1)}, bf16[192,2048]{1,0:T(8,128)(2,1)S(1)}, u32[]{:S(2)}, u32[]{:S(2)}) collective-permute-start(bf16[192,2048]{1,0:T(8,128)(2,1)S(1)} %bitcast.24), channel_id=1, source_target_pairs={{0,16},{16,0},{1,17},{17,1},{2,18},{18,2},{3,19},{19,3},{4,20},{20... | collective-permute-start | bytes 2359304 | tf_op jit(solution)/shard_map/ppermute | solution.py:290
  60.3 0.9 copy-start.1
  61.2 16.2 %copy-start.7 = (bf16[2048,384]{1,0:T(8,128)(2,1)}, bf16[2048,384]{1,0:T(8,128)(2,1)S(1)}, u32[]{:S(2)}) copy-start(bf16[2048,384]{1,0:T(8,128)(2,1)S(1)} %collective-permute-done.2.refs_3_.refs_7_) | copy-start | bytes 4718596
  61.2 16.2 %copy-start.8 = (bf16[2048,384]{1,0:T(8,128)(2,1)}, bf16[2048,384]{1,0:T(8,128)(2,1)S(1)}, u32[]{:S(2)}) copy-start(bf16[2048,384]{1,0:T(8,128)(2,1)S(1)} %collective-permute-done.4.refs_5_.refs_9_) | copy-start | bytes 4718596
  61.5 15.9 %copy-start.9 = (bf16[384,2048]{1,0:T(8,128)(2,1)}, bf16[384,2048]{1,0:T(8,128)(2,1)S(1)}, u32[]{:S(2)}) copy-start(bf16[384,2048]{1,0:T(8,128)(2,1)S(1)} %collective-permute-done.6.refs_7_.refs_3_) | copy-start | bytes 4718596
  77.4 0.9 copy-start.10
  91.4 30.3 %collective-permute-start.7 = (bf16[192,2048]{1,0:T(8,128)(2,1)}, bf16[192,2048]{1,0:T(8,128)(2,1)}, u32[]{:S(2)}, u32[]{:S(2)}) collective-permute-start(bf16[192,2048]{1,0:T(8,128)(2,1)} %bitcast.13), channel_id=1, source_target_pairs={{0,16},{16,0},{1,17},{17,1},{2,18},{18,2},{3,19},{19,3},{4,20},{20... | collective-permute-start | bytes 2359304 | tf_op jit(solution)/shard_map/ppermute | solution.py:290
  92.6 41.3 %all-to-all-start.1 = ((bf16[16,24,2048]{2,1,0:T(8,128)(2,1)}), bf16[16,24,2048]{2,1,0:T(8,128)(2,1)S(1)}, u32[]{:S(2)}, u32[]{:S(2)}) async-start(bf16[16,24,2048]{2,1,0:T(8,128)(2,1)} %bitcast.8), calls=%async_computation.1 | async-start | bytes 3145728 | tf_op jit(solution)/shard_map/all_to_all | solution.py:296
  97.8 0.9 copy-start.2
  133.8 4.1 %copy-start.6 = (f32[128,2]{0,1:T(2,128)S(1)}, f32[128,2]{0,1:T(2,128)}, u32[]{:S(2)}) copy-start(f32[128,2]{0,1:T(2,128)} %param.10) | copy-start | bytes 3076
  133.8 41.0 %all-to-all-start.3 = ((bf16[16,24,2048]{2,1,0:T(8,128)(2,1)}), bf16[16,24,2048]{2,1,0:T(8,128)(2,1)S(1)}, u32[]{:S(2)}, u32[]{:S(2)}) async-start(bf16[16,24,2048]{2,1,0:T(8,128)(2,1)} %bitcast.26), calls=%async_computation.3 | async-start | bytes 3145728 | tf_op jit(solution)/shard_map/all_to_all | solution.py:296
  138.1 1.0 copy-start.4

commit v13 on v12

--- a/solution.py
+++ b/solution.py
@@ -1,4 +1,5 @@
 import functools
+import itertools
 
 import jax
 import jax.numpy as jnp
@@ -42,8 +43,8 @@
     return [unit_ref.at[0, cut] if axis == 0 else unit_ref.at[0, :, cut] for cut in cuts]
 
 
-def place_kernel(experts, parts, plane_ref, routes_ref, tokens_ref, slots_ref, near_ref, *refs):
-    place_ref, sems, out_sems, rows_ref, stage_ref = refs
+def place_kernel(experts, parts, plane_ref, spot_ref, routes_ref, tokens_ref, slots_ref, near_ref, *refs):
+    place_ref, turned_ref, sems, out_sems, rows_ref, stage_ref = refs
     slots, width = slots_ref.shape
     capacity = slots // experts
     tok_rows, top_count = routes_ref.shape
@@ -64,10 +65,11 @@
     near = None
     for k in range(top_count):
         own = jnp.sum(jnp.where(named[k], rank, 0.0), axis=1, keepdims=True).astype(jnp.int32)
-        mark, near_mark = (
+        mark, turned_mark, near_mark = (
             (slot_numbers == order[:, k : k + 1] * capacity + own).astype(F32)
-            for order in (lanes, near_lanes)
+            for order in (lanes, lanes ^ spot_ref[0], near_lanes)
         )
+        turned_ref[k * tok_rows : (k + 1) * tok_rows, :] = turned_mark.astype(BF16)
         place_ref[k * tok_rows : (k + 1) * tok_rows, :] = mark.astype(BF16)
         near = near_mark if near is None else near + near_mark
     near_ref[...] = near.astype(BF16)
@@ -145,10 +147,11 @@
         copy.wait()
 
 
-def backward_kernel(parts, joined, plane_ref, *refs):
+def backward_kernel(parts, joined, lanes, plane_ref, spot_ref, *refs):
     sources, refs = refs[: 2 + 4 * parts], refs[2 + 4 * parts :]
-    out_ref, sems, out_sems, rows_ref, down_ref, by_gate_ref, by_up_ref, gate_ref, up_ref = refs[:9]
-    stage_ref, back_gate_ref, back_up_ref = refs[9:]
+    out_refs, refs = refs[: max(lanes, 1)], refs[max(lanes, 1) :]
+    sems, out_sems, rows_ref, down_ref, by_gate_ref, by_up_ref, gate_ref, up_ref = refs[:8]
+    stage_ref, back_gate_ref, back_up_ref = refs[8:]
     units, span = down_ref.shape[:2]
     targets = [
         *by_plane(rows_ref, plane_ref, parts),
@@ -169,13 +172,20 @@
     for copy in copies[2 + 2 * parts :]:
         copy.wait()
     sent = []
-    for d, columns in enumerate(tiles(stage_ref.shape[1])):
-        stage_ref[:, columns] = sum(
+    for d, columns in enumerate(tiles(stage_ref.shape[-1])):
+        rows = sum(
             dot(back_gate_ref[i], gate_ref[i, columns, :], (1, 1))
             + dot(back_up_ref[i], up_ref[i, columns, :], (1, 1))
             for i in range(units)
-        ).astype(BF16)
-        sent.append(store(stage_ref.at[:, columns], out_ref.at[:, columns], out_sems.at[d]))
+        )
+        if lanes:
+            rows = rows.reshape(lanes, rows.shape[0] // lanes, rows.shape[1])
+            stage_ref[:, :, columns] = rows.astype(BF16)
+        else:
+            stage_ref[:, columns] = rows.astype(BF16)
+            sent.append(store(stage_ref.at[:, columns], out_refs[0].at[:, columns], out_sems.at[d]))
+    if lanes:
+        sent = fetch([stage_ref.at[spot_ref[0] ^ b] for b in range(lanes)], out_refs, out_sems)
     for copy in sent:
         copy.wait()
 
@@ -192,11 +202,19 @@
     gate_grad_ref[...] = jnp.concatenate(grads, axis=1)
 
 
-def sum_kernel(place_ref, gates_ref, slots_ref, out_ref):
+def sum_kernel(place_ref, gates_ref, *refs):
+    lane_refs, out_ref, rows_ref = refs[:-2], refs[-2], refs[-1]
+    if len(lane_refs) > 1:
+        for b in range(0, len(lane_refs), 2):
+            pair = jnp.concatenate([ref[...].astype(F32) for ref in lane_refs[b : b + 2]], axis=0)
+            size = pair.shape[0]
+            rows_ref[b // 2 * size : (b // 2 + 1) * size, :] = pair.astype(BF16)
+    else:
+        rows_ref = lane_refs[0]
     tok_rows, top_count = gates_ref.shape
     total = None
     for k in range(top_count):
-        raw = dot(place_ref[k * tok_rows : (k + 1) * tok_rows, :], slots_ref[...], (1, 0))
+        raw = dot(place_ref[k * tok_rows : (k + 1) * tok_rows, :], rows_ref[...], (1, 0))
         term = raw * gates_ref[:, k : k + 1]
         total = term if total is None else total + term
     out_ref[...] = total.astype(BF16)
@@ -297,6 +315,17 @@
             rows, axes, 0, 0, axis_index_groups=everywhere, tiled=True
         ).reshape(slots, width)
 
+    def send_lanes_back(lane_rows):
+        passing = [b for b in range(1, experts) if b & (sets // 2)]
+        others = [b for b in range(1, experts) if not b & (sets // 2)]
+        received = {0: lane_rows[0]}
+        for pair in itertools.zip_longest(passing, others):
+            for b in pair:
+                if b is not None:
+                    pairs = [(group[k], group[k ^ b]) for group in everywhere for k in range(experts)]
+                    received[b] = lax.ppermute(lane_rows[b], axes, pairs)
+        return [received[b] for b in range(experts)]
+
     spread_flops = 2 * slots * tok_rows * width
     dot_flops = 2 * slots * width * hidden * parts
     slot_shape = jax.ShapeDtypeStruct((slots, width), BF16)
@@ -318,14 +347,16 @@
     gate_own, up_own, down_own = swapped(w_gate), swapped(w_up), swapped(w_down)
     gate_w, up_w, down_w = whole_expert(gate_own), whole_expert(up_own), whole_expert(down_own)
     plane = lax.axis_index("dp").astype(jnp.int32).reshape(1)
-    x_slots, near, place = call(
+    spot = plane * sets + (lax.axis_index("expert") // parts).astype(jnp.int32)
+    by_lane = capacity % 8 == 0 and experts & (experts - 1) == 0
+    x_slots, near, place, turned = call(
         functools.partial(place_kernel, experts, parts),
-        [slot_shape, jax.ShapeDtypeStruct((tok_rows, slots), BF16), place_shape],
+        [slot_shape, jax.ShapeDtypeStruct((tok_rows, slots), BF16), place_shape, place_shape],
         spread_flops,
         [sems(1), sems(pieces), pltpu.VMEM((tok_rows, width), BF16), row_scratch],
-        pinned=(2,),
-        out_spaces=[pltpu.HBM, pltpu.VMEM, pltpu.VMEM],
-    )(plane, routes, tokens)
+        pinned=(3,),
+        out_spaces=[pltpu.HBM, pltpu.VMEM, pltpu.VMEM, pltpu.VMEM],
+    )(plane, spot, routes, tokens)
     x_shares = dispatch(x_slots)
     (dy_slots,) = call(
         spread_kernel,
@@ -347,21 +378,26 @@
     )(plane, *x_shares, *gate_w, *up_w, *down_w)
     dy_shares = dispatch(dy_slots, (out_rows,))
     out_slots = send_back(out_rows)
-    (grad_rows,) = call(
-        functools.partial(backward_kernel, parts, joined),
-        [slot_shape],
+    lane_shape = jax.ShapeDtypeStruct((capacity, width), BF16)
+    grad_stage = pltpu.VMEM((experts, capacity, width), BF16) if by_lane else row_scratch
+    grad_rows = call(
+        functools.partial(backward_kernel, parts, joined, experts if by_lane else 0),
+        [lane_shape] * experts if by_lane else [slot_shape],
         64 * dot_flops,
-        [sems(2 + 4 * parts), sems(pieces), row_scratch, down_scratch, unit_scratch, unit_scratch]
-        + [in_scratch, in_scratch, row_scratch, hidden_scratch, hidden_scratch],
-        far=range(1, 3 + 4 * parts),
-        out_spaces=[pltpu.HBM],
+        [sems(2 + 4 * parts), sems(experts if by_lane else pieces), row_scratch, down_scratch]
+        + [unit_scratch, unit_scratch, in_scratch, in_scratch]
+        + [grad_stage, hidden_scratch, hidden_scratch],
+        far=range(2, 4 + 4 * parts),
+        out_spaces=[pltpu.HBM] * (experts if by_lane else 1),
         vmem=LARGE_VMEM,
-    )(plane, *dy_shares, *down_w, by_gate, by_up, *gate_w, *up_w)
-    grad_slots = send_back(grad_rows)
+    )(plane, spot, *dy_shares, *down_w, by_gate, by_up, *gate_w, *up_w)
+    grad_slots = send_lanes_back(grad_rows) if by_lane else [send_back(grad_rows[0])]
     mixed, gate_grad = call(
         mix_kernel, [token_shape, jax.ShapeDtypeStruct(gates.shape, F32)], 2 * spread_flops
     )(place, gates, cotangent, out_slots)
-    (token_grad,) = call(sum_kernel, [token_shape], 2 * spread_flops)(place, gates, grad_slots)
+    (token_grad,) = call(sum_kernel, [token_shape], 2 * spread_flops, [row_scratch])(
+        turned if by_lane else place, gates, *grad_slots
+    )
     return (mixed, token_grad, gate_grad)
 
 

time: 177 us -> 177 us (level)
  waiting for transfers between devices: 115 us -> 89.9 us
  starting transfers between devices: 25 us -> 49.1 us
    all_to_all x2 -> x1, waiting for transfers between devices: 37 us -> 0.01 us  [send_back(): lax.all_to_all(rows, axes, 0, 0, axis_index_groups=everywhere, tiled=True)]
    ppermute x0 -> x15, starting transfers between devices: none -> 28.1 us  [send_lanes_back(): received[b] = lax.ppermute(lane_rows[b], axes, pairs)]
    ppermute x0 -> x15, waiting for transfers between devices: none -> 11.6 us  [send_lanes_back(): received[b] = lax.ppermute(lane_rows[b], axes, pairs)]
    all_to_all x2 -> x1, starting transfers between devices: 8.16 us -> 4.09 us  [send_back(): lax.all_to_all(rows, axes, 0, 0, axis_index_groups=everywhere, tiled=True)]
    unnamed x25 -> x27, local copies, waits for them, and re-layouts: 7.45 us -> 7.38 us
  transfers between devices with their start and end apart: 12 -> 26, of which waited for: 9 -> 12; matrix products, arithmetic and copies ran while one was open for 1% -> 1% of each run, Pallas kernels for 14% -> 15%
where the time goes in v13:
time: 177 us; the launch traced here: 176 us
  waiting for transfers between devices  89.9 us (51%)
  starting transfers between devices  49.1 us (28%)
  Pallas kernels  29 us (16%)
  local copies, waits for them, and re-layouts  7.38 us (4%)
    ppermute x2, waiting for transfers between devices, dispatch(): lax.ppermute(rows, 'dp', [(g, (g + i) % parts) for g in range(parts)])  39 us
    all_to_all x2, waiting for transfers between devices, dispatch(): lax.all_to_all(rows, axes, 0, 0, axis_index_groups=in_plane, tiled=True)  29.1 us
    pallas_call x10, Pallas kernels, run(): pl.pallas_call(kernel, out_shape=tuple(outs), in_specs=[pl.BlockSpec(memo...  29 us
    ppermute x15, starting transfers between devices, send_lanes_back(): received[b] = lax.ppermute(lane_rows[b], axes, pairs)  28.1 us
    ppermute x15, waiting for transfers between devices, send_lanes_back(): received[b] = lax.ppermute(lane_rows[b], axes, pairs)  11.6 us
    ppermute x3, waiting for transfers between devices, swapped(): return lax.ppermute(weight[0], axes, swap)  10 us
    all_to_all x2, starting transfers between devices, dispatch(): lax.all_to_all(rows, axes, 0, 0, axis_index_groups=in_plane, tiled=True)  9.53 us
    unnamed x27, local copies, waits for them, and re-layouts  7.38 us
  transfers between devices with their start and end apart: 26, of which 12 were waited for; matrix products, arithmetic and copies ran while one was open for 1% of the time, Pallas kernels for 15%

profile of v13, /device:TPU:0, one launch (start us, length us, event | category | flops | bytes accessed | tf_op | source)
XLA Modules:
  0.0 176.3 jit_solution(17149192174171224237)
XLA Ops:
  0.6 3.0 %collective-permute-start.1 = (bf16[2048,384]{1,0:T(8,128)(2,1)}, bf16[2048,384]{1,0:T(8,128)(2,1)}, u32[]{:S(2)}, u32[]{:S(2)}) collective-permute-start(bf16[2048,384]{1,0:T(8,128)(2,1)} %bitcast.24), channel_id=1, source_target_pairs={{0,16},{1,0},{2,18},{3,2},{4,20},{5,4},{6,22},{7,6},{8,24},{9,8},{... | collective-permute-start | bytes 4718600 | tf_op jit(solution)/shard_map/ppermute | solution.py:277
  3.6 0.8 copy.10.routes_ref
  4.4 0.0 copy-start.6
  4.4 1.0 copy-done.6
  5.5 2.1 %shard_map.94 = (bf16[384,2048]{1,0:T(8,128)(2,1)}, bf16[128,384]{1,0:T(8,128)(2,1)S(1)}, bf16[256,384]{1,0:T(8,128)(2,1)S(1)}, bf16[256,384]{1,0:T(8,128)(2,1)S(1)}) custom-call(s32[1]{0:T(128)} %bitcast.plane_ref, s32[1]{0:T(128)S(6)} %add.8.spot_ref, s32[128,2]{1,0:T(8,128)S(1)} %copy.10.routes_ref, bf16[128,2048]{1,0:T(8,128)(2,1)S(1)} %copy-done.6), custom_call_target="tpu_custom_call" | custom-call | flops 201326592 | bytes 2589704 | tf_op jit(solution)/shard_map/pallas_call | solution.py:236
  7.5 0.0 copy-start.3
  7.5 6.0 %all-to-all-start = ((bf16[8,48,2048]{2,1,0:T(8,128)(2,1)}), bf16[8,48,2048]{2,1,0:T(8,128)(2,1)S(1)}, u32[]{:S(2)}, u32[]{:S(2)}) async-start(bf16[8,48,2048]{2,1,0:T(8,128)(2,1)} %bitcast.2), calls=%async_computation | async-start | bytes 3145728 | tf_op jit(solution)/shard_map/all_to_all | solution.py:288
  13.5 0.0 collective-permute-start.3
  13.5 0.0 collective-permute-start.5
  13.5 8.3 %collective-permute-done.1.refs_2_._.refs_6_ = bf16[2048,384]{1,0:T(8,128)(2,1)} collective-permute-done((bf16[2048,384]{1,0:T(8,128)(2,1)}, bf16[2048,384]{1,0:T(8,128)(2,1)}, u32[]{:S(2)}, u32[]{:S(2)}) %collective-permute-start.1) | collective-permute-done | bytes 1572896 | tf_op jit(solution)/shard_map/ppermute | solution.py:277
  21.9 1.4 shard_map.99
  23.2 1.2 copy-done
  24.4 25.3 %all-to-all-done = bf16[8,48,2048]{2,1,0:T(8,128)(2,1)S(1)} async-done(((bf16[8,48,2048]{2,1,0:T(8,128)(2,1)}), bf16[8,48,2048]{2,1,0:T(8,128)(2,1)S(1)}, u32[]{:S(2)}, u32[]{:S(2)}) %all-to-all-start) | async-done | bytes 1572896 | tf_op jit(solution)/shard_map/all_to_all | solution.py:288
  49.7 3.6 %all-to-all-start.2 = ((bf16[8,48,2048]{2,1,0:T(8,128)(2,1)}), bf16[8,48,2048]{2,1,0:T(8,128)(2,1)S(1)}, u32[]{:S(2)}, u32[]{:S(2)}) async-start(bf16[8,48,2048]{2,1,0:T(8,128)(2,1)} %bitcast.20), calls=%async_computation.2 | async-start | bytes 3145728 | tf_op jit(solution)/shard_map/all_to_all | solution.py:288
  53.3 0.1 collective-permute-start.2
  53.4 0.0 collective-permute-done.3.refs_4_.refs_8_
  53.4 0.5 collective-permute-start.4
  53.9 1.7 collective-permute-done.5.refs_6_.refs_2_
  55.6 0.0 collective-permute-start.6
  55.6 1.1 shard_map.96
  56.7 2.6 %collective-permute-start = (bf16[192,2048]{1,0:T(8,128)(2,1)S(1)}, bf16[192,2048]{1,0:T(8,128)(2,1)S(1)}, u32[]{:S(2)}, u32[]{:S(2)}) collective-permute-start(bf16[192,2048]{1,0:T(8,128)(2,1)S(1)} %bitcast.22), channel_id=1, source_target_pairs={{0,16},{16,0},{1,17},{17,1},{2,18},{18,2},{3,19},{19,3},{4,20},{20... | collective-permute-start | bytes 2359304 | tf_op jit(solution)/shard_map/ppermute | solution.py:308
  59.2 1.1 shard_map.95
  60.3 0.9 copy-done.1
  61.2 0.2 collective-permute-done.6.refs_7_.refs_3_
  61.5 15.9 %collective-permute-done.refs_1_ = bf16[192,2048]{1,0:T(8,128)(2,1)S(1)} collective-permute-done((bf16[192,2048]{1,0:T(8,128)(2,1)S(1)}, bf16[192,2048]{1,0:T(8,128)(2,1)S(1)}, u32[]{:S(2)}, u32[]{:S(2)}) %collective-permute-start) | collective-permute-done | bytes 786464 | tf_op jit(solution)/shard_map/ppermute | solution.py:308
  77.4 0.9 copy-done.11
  78.3 8.3 %shard_map.97 = (bf16[384,2048]{1,0:T(8,128)(2,1)}, f32[1,384,768]{2,1,0:T(8,128)}, f32[1,384,768]{2,1,0:T(8,128)}) custom-call(s32[1]{0:T(128)} %bitcast.plane_ref, bf16[192,2048]{1,0:T(8,128)(2,1)} %bitcast.21, bf16[192,2048]{1,0:T(8,128)(2,1)} %copy-done.11, bf16[2048,384]{1,0:T(8,128)(2,1)} %collective-permute-done.1.refs_2_._.refs_6_, ...), custom_call_target="tpu_custom_call" | custom-call | flops 3623878656 | bytes 14942212 | tf_op jit(solution)/shard_map/pallas_call | solution.py:236
  86.6 3.8 %all-to-all-done.2 = bf16[8,48,2048]{2,1,0:T(8,128)(2,1)S(1)} async-done(((bf16[8,48,2048]{2,1,0:T(8,128)(2,1)}), bf16[8,48,2048]{2,1,0:T(8,128)(2,1)S(1)}, u32[]{:S(2)}, u32[]{:S(2)}) %all-to-all-start.2) | async-done | bytes 1572896 | tf_op jit(solution)/shard_map/all_to_all | solution.py:288
  90.4 1.0 shard_map.101
  91.4 1.2 collective-permute-start.7
  92.6 4.1 %all-to-all-start.1 = ((bf16[16,24,2048]{2,1,0:T(8,128)(2,1)}), bf16[16,24,2048]{2,1,0:T(8,128)(2,1)S(1)}, u32[]{:S(2)}, u32[]{:S(2)}) async-start(bf16[16,24,2048]{2,1,0:T(8,128)(2,1)} %bitcast.9), calls=%async_computation.1 | async-start | bytes 3145728 | tf_op jit(solution)/shard_map/all_to_all | solution.py:314
  96.7 1.1 shard_map.100
  97.8 0.9 copy-done.2
  98.7 23.0 %collective-permute-done.7.refs_1_ = bf16[192,2048]{1,0:T(8,128)(2,1)} collective-permute-done((bf16[192,2048]{1,0:T(8,128)(2,1)}, bf16[192,2048]{1,0:T(8,128)(2,1)}, u32[]{:S(2)}, u32[]{:S(2)}) %collective-permute-start.7) | collective-permute-done | bytes 786464 | tf_op jit(solution)/shard_map/ppermute | solution.py:308
  121.7 8.9 %shard_map.102 = (bf16[24,2048]{1,0:T(8,128)(2,1)}, bf16[24,2048]{1,0:T(8,128)(2,1)}, bf16[24,2048]{1,0:T(8,128)(2,1)}, bf16[24,2048]{1,0:T(8,128)(2,1)}, bf16[2...) custom-call(s32[1]{0:T(128)} %bitcast.plane_ref, ...), custom_call_target="tpu_custom_call" | custom-call | flops 77309411328 | bytes 14942216 | tf_op jit(solution)/shard_map/pallas_call | solution.py:236
  130.6 0.0 copy-start.4
  130.6 2.8 %collective-permute-start.10 = (bf16[24,2048]{1,0:T(8,128)(2,1)}, bf16[24,2048]{1,0:T(8,128)(2,1)S(1)}, u32[]{:S(2)}, u32[]{:S(2)}) collective-permute-start(bf16[24,2048]{1,0:T(8,128)(2,1)} %get-tuple-element.39), channel_id=1, source_target_pairs={{0,6},{2,4},{4,2},{6,0},{8,14},{10,12},{12,10},{14,8},{16,22},{18,... | collective-permute-start | bytes 294920 | tf_op jit(solution)/shard_map/ppermute | solution.py:326
  133.4 2.6 %collective-permute-start.11 = (bf16[24,2048]{1,0:T(8,128)(2,1)}, bf16[24,2048]{1,0:T(8,128)(2,1)S(1)}, u32[]{:S(2)}, u32[]{:S(2)}) collective-permute-start(bf16[24,2048]{1,0:T(8,128)(2,1)} %get-tuple-element.40), channel_id=1, source_target_pairs={{0,8},{2,10},{4,12},{6,14},{8,0},{10,2},{12,4},{14,6},{16,24},{18,... | collective-permute-start | bytes 294920 | tf_op jit(solution)/shard_map/ppermute | solution.py:326
  136.0 1.2 collective-permute-start.12
  137.2 1.3 collective-permute-start.13
  138.4 2.6 %collective-permute-start.14 = (bf16[24,2048]{1,0:T(8,128)(2,1)}, bf16[24,2048]{1,0:T(8,128)(2,1)S(1)}, u32[]{:S(2)}, u32[]{:S(2)}) collective-permute-start(bf16[24,2048]{1,0:T(8,128)(2,1)} %get-tuple-element.43), channel_id=1, source_target_pairs={{0,14},{2,12},{4,10},{6,8},{8,6},{10,4},{12,2},{14,0},{16,30},{18,... | collective-permute-start | bytes 294920 | tf_op jit(solution)/shard_map/ppermute | solution.py:326
  141.1 0.0 collective-permute-done.10.refs_3_
  141.1 1.5 collective-permute-start.15
  142.6 4.0 %collective-permute-done.11.refs_4_ = bf16[24,2048]{1,0:T(8,128)(2,1)S(1)} collective-permute-done((bf16[24,2048]{1,0:T(8,128)(2,1)}, bf16[24,2048]{1,0:T(8,128)(2,1)S(1)}, u32[]{:S(2)}, u32[]{:S(2)}) %collective-permute-start.11) | collective-permute-done | bytes 98336 | tf_op jit(solution)/shard_map/ppermute | solution.py:326
  146.6 2.3 %collective-permute-start.16 = (bf16[24,2048]{1,0:T(8,128)(2,1)}, bf16[24,2048]{1,0:T(8,128)(2,1)S(1)}, u32[]{:S(2)}, u32[]{:S(2)}) collective-permute-start(bf16[24,2048]{1,0:T(8,128)(2,1)} %get-tuple-element.45), channel_id=1, source_target_pairs={{0,18},{2,16},{4,22},{6,20},{8,26},{10,24},{12,30},{14,28},{16,2},... | collective-permute-start | bytes 294920 | tf_op jit(solution)/shard_map/ppermute | solution.py:326
  148.9 0.6 collective-permute-done.12.refs_5_
  149.5 0.0 collective-permute-start.17
  149.5 0.0 collective-permute-done.13.refs_6_
  149.5 3.0 %collective-permute-start.18 = (bf16[24,2048]{1,0:T(8,128)(2,1)}, bf16[24,2048]{1,0:T(8,128)(2,1)S(1)}, u32[]{:S(2)}, u32[]{:S(2)}) collective-permute-start(bf16[24,2048]{1,0:T(8,128)(2,1)} %get-tuple-element.47), channel_id=1, source_target_pairs={{0,22},{2,20},{4,18},{6,16},{8,30},{10,28},{12,26},{14,24},{16,6},... | collective-permute-start | bytes 294920 | tf_op jit(solution)/shard_map/ppermute | solution.py:326
  152.5 0.0 collective-permute-done.14.refs_7_
  152.5 2.2 %collective-permute-start.19 = (bf16[24,2048]{1,0:T(8,128)(2,1)}, bf16[24,2048]{1,0:T(8,128)(2,1)S(1)}, u32[]{:S(2)}, u32[]{:S(2)}) collective-permute-start(bf16[24,2048]{1,0:T(8,128)(2,1)} %get-tuple-element.48), channel_id=1, source_target_pairs={{0,24},{2,26},{4,28},{6,30},{8,16},{10,18},{12,20},{14,22},{16,8},... | collective-permute-start | bytes 294920 | tf_op jit(solution)/shard_map/ppermute | solution.py:326
  154.8 0.0 collective-permute-done.15.refs_8_
  154.8 2.4 %collective-permute-start.20 = (bf16[24,2048]{1,0:T(8,128)(2,1)}, bf16[24,2048]{1,0:T(8,128)(2,1)}, u32[]{:S(2)}, u32[]{:S(2)}) collective-permute-start(bf16[24,2048]{1,0:T(8,128)(2,1)} %get-tuple-element.49), channel_id=1, source_target_pairs={{0,26},{2,24},{4,30},{6,28},{8,18},{10,16},{12,22},{14,20},{16,10}... | collective-permute-start | bytes 294920 | tf_op jit(solution)/shard_map/ppermute | solution.py:326
  157.2 3.2 %collective-permute-start.21 = (bf16[24,2048]{1,0:T(8,128)(2,1)}, bf16[24,2048]{1,0:T(8,128)(2,1)}, u32[]{:S(2)}, u32[]{:S(2)}) collective-permute-start(bf16[24,2048]{1,0:T(8,128)(2,1)} %get-tuple-element.50), channel_id=1, source_target_pairs={{0,28},{2,30},{4,24},{6,26},{8,20},{10,22},{12,16},{14,18},{16,12}... | collective-permute-start | bytes 294920 | tf_op jit(solution)/shard_map/ppermute | solution.py:326
  160.4 1.6 collective-permute-start.22
  162.0 1.4 collective-permute-start.8
  163.4 2.2 %collective-permute-done.19.refs_12_ = bf16[24,2048]{1,0:T(8,128)(2,1)S(1)} collective-permute-done((bf16[24,2048]{1,0:T(8,128)(2,1)}, bf16[24,2048]{1,0:T(8,128)(2,1)S(1)}, u32[]{:S(2)}, u32[]{:S(2)}) %collective-permute-start.19) | collective-permute-done | bytes 98336 | tf_op jit(solution)/shard_map/ppermute | solution.py:326
  165.5 0.1 copy.11.gates_ref
  165.7 4.0 %collective-permute-done.20.refs_13_ = bf16[24,2048]{1,0:T(8,128)(2,1)} collective-permute-done((bf16[24,2048]{1,0:T(8,128)(2,1)}, bf16[24,2048]{1,0:T(8,128)(2,1)}, u32[]{:S(2)}, u32[]{:S(2)}) %collective-permute-start.20) | collective-permute-done | bytes 98336 | tf_op jit(solution)/shard_map/ppermute | solution.py:326
  169.6 0.8 collective-permute-done.9.refs_2_
  170.5 0.9 copy-done.5
  171.4 2.6 %shard_map.103 = bf16[128,2048]{1,0:T(8,128)(2,1)} custom-call(bf16[256,384]{1,0:T(8,128)(2,1)S(1)} %get-tuple-element.32.place_ref, f32[128,2]{1,0:T(8,128)S(1)} %copy.11.gates_ref, bf16[24,2048]{1,0:T(8,128)(2,1)S(1)} %copy-done.5, bf16[24,2048]{1,0:T(8,128)(2,1)} %collective-permute-done.8.refs_1_, bf16[24,2048]{1,0:T(8,128)(2,1)} %collective-permute-done.9.refs_2_, ...), custom_call_target="tpu_custom_call" | custom-call | flops 402653184 | bytes 2294784 | tf_op jit(solution)/shard_map/pallas_call | solution.py:236
  174.0 1.7 shard_map.98
  175.6 0.6 copy.13
  (25 shorter events, 0.1 us)
Async XLA Ops:
  0.6 21.2 %collective-permute-start.1 = (bf16[2048,384]{1,0:T(8,128)(2,1)}, bf16[2048,384]{1,0:T(8,128)(2,1)}, u32[]{:S(2)}, u32[]{:S(2)}) collective-permute-start(bf16[2048,384]{1,0:T(8,128)(2,1)} %bitcast.24), channel_id=1, source_target_pairs={{0,16},{1,0},{2,18},{3,2},{4,20},{5,4},{6,22},{7,6},{8,24},{9,8},{... | collective-permute-start | bytes 4718600 | tf_op jit(solution)/shard_map/ppermute | solution.py:277
  4.4 1.0 copy-start.6
  7.5 14.4 %copy-start.3 = (bf16[128,2048]{1,0:T(8,128)(2,1)S(1)}, bf16[128,2048]{1,0:T(8,128)(2,1)}, u32[]{:S(2)}) copy-start(bf16[128,2048]{1,0:T(8,128)(2,1)} %rows_ref.1) | copy-start | bytes 1572868
  7.5 42.2 %all-to-all-start = ((bf16[8,48,2048]{2,1,0:T(8,128)(2,1)}), bf16[8,48,2048]{2,1,0:T(8,128)(2,1)S(1)}, u32[]{:S(2)}, u32[]{:S(2)}) async-start(bf16[8,48,2048]{2,1,0:T(8,128)(2,1)} %bitcast.2), calls=%async_computation | async-start | bytes 3145728 | tf_op jit(solution)/shard_map/all_to_all | solution.py:288
  13.5 39.9 %collective-permute-start.3 = (bf16[2048,384]{1,0:T(8,128)(2,1)}, bf16[2048,384]{1,0:T(8,128)(2,1)}, u32[]{:S(2)}, u32[]{:S(2)}) collective-permute-start(bf16[2048,384]{1,0:T(8,128)(2,1)} %bitcast.25), channel_id=1, source_target_pairs={{0,16},{1,0},{2,18},{3,2},{4,20},{5,4},{6,22},{7,6},{8,24},{9,8},{... | collective-permute-start | bytes 4718600 | tf_op jit(solution)/shard_map/ppermute | solution.py:277
  13.5 42.1 %collective-permute-start.5 = (bf16[384,2048]{1,0:T(8,128)(2,1)}, bf16[384,2048]{1,0:T(8,128)(2,1)}, u32[]{:S(2)}, u32[]{:S(2)}) collective-permute-start(bf16[384,2048]{1,0:T(8,128)(2,1)} %bitcast.26), channel_id=1, source_target_pairs={{0,16},{1,0},{2,18},{3,2},{4,20},{5,4},{6,22},{7,6},{8,24},{9,8},{... | collective-permute-start | bytes 4718600 | tf_op jit(solution)/shard_map/ppermute | solution.py:277
  23.2 1.2 copy-start
  49.7 40.7 %all-to-all-start.2 = ((bf16[8,48,2048]{2,1,0:T(8,128)(2,1)}), bf16[8,48,2048]{2,1,0:T(8,128)(2,1)S(1)}, u32[]{:S(2)}, u32[]{:S(2)}) async-start(bf16[8,48,2048]{2,1,0:T(8,128)(2,1)} %bitcast.20), calls=%async_computation.2 | async-start | bytes 3145728 | tf_op jit(solution)/shard_map/all_to_all | solution.py:288
  53.3 7.9 %collective-permute-start.2 = (bf16[2048,384]{1,0:T(8,128)(2,1)}, bf16[2048,384]{1,0:T(8,128)(2,1)S(1)}, u32[]{:S(2)}, u32[]{:S(2)}) collective-permute-start(bf16[2048,384]{1,0:T(8,128)(2,1)} %collective-permute-done.1.refs_2_._.refs_6_), channel_id=1, source_target_pairs={{0,1},{1,0},{2,3},{3,2},{4,5},{5,4},{6,7},{7,6},{8,9},{9,8},{10,11... | collective-permute-start | bytes 4718600 | tf_op jit(solution)/shard_map/ppermute | solution.py:283
  53.4 7.8 %collective-permute-start.4 = (bf16[2048,384]{1,0:T(8,128)(2,1)}, bf16[2048,384]{1,0:T(8,128)(2,1)S(1)}, u32[]{:S(2)}, u32[]{:S(2)}) collective-permute-start(bf16[2048,384]{1,0:T(8,128)(2,1)} %collective-permute-done.3.refs_4_.refs_8_), channel_id=1, source_target_pairs={{0,1},{1,0},{2,3},{3,2},{4,5},{5,4},{6,7},{7,6},{8,9},{9,8},{10,11... | collective-permute-start | bytes 4718600 | tf_op jit(solution)/shard_map/ppermute | solution.py:283
  55.6 5.9 %collective-permute-start.6 = (bf16[384,2048]{1,0:T(8,128)(2,1)}, bf16[384,2048]{1,0:T(8,128)(2,1)S(1)}, u32[]{:S(2)}, u32[]{:S(2)}) collective-permute-start(bf16[384,2048]{1,0:T(8,128)(2,1)} %collective-permute-done.5.refs_6_.refs_2_), channel_id=1, source_target_pairs={{0,1},{1,0},{2,3},{3,2},{4,5},{5,4},{6,7},{7,6},{8,9},{9,8},{10,11... | collective-permute-start | bytes 4718600 | tf_op jit(solution)/shard_map/ppermute | solution.py:283
  56.7 20.7 %collective-permute-start = (bf16[192,2048]{1,0:T(8,128)(2,1)S(1)}, bf16[192,2048]{1,0:T(8,128)(2,1)S(1)}, u32[]{:S(2)}, u32[]{:S(2)}) collective-permute-start(bf16[192,2048]{1,0:T(8,128)(2,1)S(1)} %bitcast.22), channel_id=1, source_target_pairs={{0,16},{16,0},{1,17},{17,1},{2,18},{18,2},{3,19},{19,3},{4,20},{20... | collective-permute-start | bytes 2359304 | tf_op jit(solution)/shard_map/ppermute | solution.py:308
  60.3 0.9 copy-start.1
  61.2 16.2 %copy-start.8 = (bf16[2048,384]{1,0:T(8,128)(2,1)}, bf16[2048,384]{1,0:T(8,128)(2,1)S(1)}, u32[]{:S(2)}) copy-start(bf16[2048,384]{1,0:T(8,128)(2,1)S(1)} %collective-permute-done.2.refs_3_.refs_7_) | copy-start | bytes 4718596
  61.2 16.2 %copy-start.9 = (bf16[2048,384]{1,0:T(8,128)(2,1)}, bf16[2048,384]{1,0:T(8,128)(2,1)S(1)}, u32[]{:S(2)}) copy-start(bf16[2048,384]{1,0:T(8,128)(2,1)S(1)} %collective-permute-done.4.refs_5_.refs_9_) | copy-start | bytes 4718596
  61.5 15.9 %copy-start.10 = (bf16[384,2048]{1,0:T(8,128)(2,1)}, bf16[384,2048]{1,0:T(8,128)(2,1)S(1)}, u32[]{:S(2)}) copy-start(bf16[384,2048]{1,0:T(8,128)(2,1)S(1)} %collective-permute-done.6.refs_7_.refs_3_) | copy-start | bytes 4718596
  77.4 0.9 copy-start.11
  91.4 30.3 %collective-permute-start.7 = (bf16[192,2048]{1,0:T(8,128)(2,1)}, bf16[192,2048]{1,0:T(8,128)(2,1)}, u32[]{:S(2)}, u32[]{:S(2)}) collective-permute-start(bf16[192,2048]{1,0:T(8,128)(2,1)} %bitcast.14), channel_id=1, source_target_pairs={{0,16},{16,0},{1,17},{17,1},{2,18},{18,2},{3,19},{19,3},{4,20},{20... | collective-permute-start | bytes 2359304 | tf_op jit(solution)/shard_map/ppermute | solution.py:308
  92.6 81.4 %all-to-all-start.1 = ((bf16[16,24,2048]{2,1,0:T(8,128)(2,1)}), bf16[16,24,2048]{2,1,0:T(8,128)(2,1)S(1)}, u32[]{:S(2)}, u32[]{:S(2)}) async-start(bf16[16,24,2048]{2,1,0:T(8,128)(2,1)} %bitcast.9), calls=%async_computation.1 | async-start | bytes 3145728 | tf_op jit(solution)/shard_map/all_to_all | solution.py:314
  97.8 0.9 copy-start.2
  121.7 43.8 %copy-start.7 = (f32[128,2]{0,1:T(2,128)S(1)}, f32[128,2]{0,1:T(2,128)}, u32[]{:S(2)}) copy-start(f32[128,2]{0,1:T(2,128)} %param.10) | copy-start | bytes 3076
  130.6 43.4 %copy-start.4 = (bf16[128,2048]{1,0:T(8,128)(2,1)S(1)}, bf16[128,2048]{1,0:T(8,128)(2,1)}, u32[]{:S(2)}) copy-start(bf16[128,2048]{1,0:T(8,128)(2,1)} %rows_ref.1) | copy-start | bytes 1572868
  130.6 10.5 %collective-permute-start.10 = (bf16[24,2048]{1,0:T(8,128)(2,1)}, bf16[24,2048]{1,0:T(8,128)(2,1)S(1)}, u32[]{:S(2)}, u32[]{:S(2)}) collective-permute-start(bf16[24,2048]{1,0:T(8,128)(2,1)} %get-tuple-element.39), channel_id=1, source_target_pairs={{0,6},{2,4},{4,2},{6,0},{8,14},{10,12},{12,10},{14,8},{16,22},{18,... | collective-permute-start | bytes 294920 | tf_op jit(solution)/shard_map/ppermute | solution.py:326
  133.4 13.1 %collective-permute-start.11 = (bf16[24,2048]{1,0:T(8,128)(2,1)}, bf16[24,2048]{1,0:T(8,128)(2,1)S(1)}, u32[]{:S(2)}, u32[]{:S(2)}) collective-permute-start(bf16[24,2048]{1,0:T(8,128)(2,1)} %get-tuple-element.40), channel_id=1, source_target_pairs={{0,8},{2,10},{4,12},{6,14},{8,0},{10,2},{12,4},{14,6},{16,24},{18,... | collective-permute-start | bytes 294920 | tf_op jit(solution)/shard_map/ppermute | solution.py:326
  136.0 13.5 %collective-permute-start.12 = (bf16[24,2048]{1,0:T(8,128)(2,1)}, bf16[24,2048]{1,0:T(8,128)(2,1)S(1)}, u32[]{:S(2)}, u32[]{:S(2)}) collective-permute-start(bf16[24,2048]{1,0:T(8,128)(2,1)} %get-tuple-element.41), channel_id=1, source_target_pairs={{0,10},{2,8},{4,14},{6,12},{8,2},{10,0},{12,6},{14,4},{16,26},{18,... | collective-permute-start | bytes 294920 | tf_op jit(solution)/shard_map/ppermute | solution.py:326
  137.2 12.4 %collective-permute-start.13 = (bf16[24,2048]{1,0:T(8,128)(2,1)}, bf16[24,2048]{1,0:T(8,128)(2,1)S(1)}, u32[]{:S(2)}, u32[]{:S(2)}) collective-permute-start(bf16[24,2048]{1,0:T(8,128)(2,1)} %get-tuple-element.42), channel_id=1, source_target_pairs={{0,12},{2,14},{4,8},{6,10},{8,4},{10,6},{12,0},{14,2},{16,28},{18,... | collective-permute-start | bytes 294920 | tf_op jit(solution)/shard_map/ppermute | solution.py:326
  138.4 14.1 %collective-permute-start.14 = (bf16[24,2048]{1,0:T(8,128)(2,1)}, bf16[24,2048]{1,0:T(8,128)(2,1)S(1)}, u32[]{:S(2)}, u32[]{:S(2)}) collective-permute-start(bf16[24,2048]{1,0:T(8,128)(2,1)} %get-tuple-element.43), channel_id=1, source_target_pairs={{0,14},{2,12},{4,10},{6,8},{8,6},{10,4},{12,2},{14,0},{16,30},{18,... | collective-permute-start | bytes 294920 | tf_op jit(solution)/shard_map/ppermute | solution.py:326
  141.1 13.7 %collective-permute-start.15 = (bf16[24,2048]{1,0:T(8,128)(2,1)}, bf16[24,2048]{1,0:T(8,128)(2,1)S(1)}, u32[]{:S(2)}, u32[]{:S(2)}) collective-permute-start(bf16[24,2048]{1,0:T(8,128)(2,1)} %get-tuple-element.44), channel_id=1, source_target_pairs={{0,16},{2,18},{4,20},{6,22},{8,24},{10,26},{12,28},{14,30},{16,0},... | collective-permute-start | bytes 294920 | tf_op jit(solution)/shard_map/ppermute | solution.py:326
  146.6 10.6 %collective-permute-start.16 = (bf16[24,2048]{1,0:T(8,128)(2,1)}, bf16[24,2048]{1,0:T(8,128)(2,1)S(1)}, u32[]{:S(2)}, u32[]{:S(2)}) collective-permute-start(bf16[24,2048]{1,0:T(8,128)(2,1)} %get-tuple-element.45), channel_id=1, source_target_pairs={{0,18},{2,16},{4,22},{6,20},{8,26},{10,24},{12,30},{14,28},{16,2},... | collective-permute-start | bytes 294920 | tf_op jit(solution)/shard_map/ppermute | solution.py:326
  149.5 10.8 %collective-permute-start.17 = (bf16[24,2048]{1,0:T(8,128)(2,1)}, bf16[24,2048]{1,0:T(8,128)(2,1)S(1)}, u32[]{:S(2)}, u32[]{:S(2)}) collective-permute-start(bf16[24,2048]{1,0:T(8,128)(2,1)} %get-tuple-element.46), channel_id=1, source_target_pairs={{0,20},{2,22},{4,16},{6,18},{8,28},{10,30},{12,24},{14,26},{16,4},... | collective-permute-start | bytes 294920 | tf_op jit(solution)/shard_map/ppermute | solution.py:326
  149.5 12.5 %collective-permute-start.18 = (bf16[24,2048]{1,0:T(8,128)(2,1)}, bf16[24,2048]{1,0:T(8,128)(2,1)S(1)}, u32[]{:S(2)}, u32[]{:S(2)}) collective-permute-start(bf16[24,2048]{1,0:T(8,128)(2,1)} %get-tuple-element.47), channel_id=1, source_target_pairs={{0,22},{2,20},{4,18},{6,16},{8,30},{10,28},{12,26},{14,24},{16,6},... | collective-permute-start | bytes 294920 | tf_op jit(solution)/shard_map/ppermute | solution.py:326
  152.5 13.0 %collective-permute-start.19 = (bf16[24,2048]{1,0:T(8,128)(2,1)}, bf16[24,2048]{1,0:T(8,128)(2,1)S(1)}, u32[]{:S(2)}, u32[]{:S(2)}) collective-permute-start(bf16[24,2048]{1,0:T(8,128)(2,1)} %get-tuple-element.48), channel_id=1, source_target_pairs={{0,24},{2,26},{4,28},{6,30},{8,16},{10,18},{12,20},{14,22},{16,8},... | collective-permute-start | bytes 294920 | tf_op jit(solution)/shard_map/ppermute | solution.py:326
  154.8 14.9 %collective-permute-start.20 = (bf16[24,2048]{1,0:T(8,128)(2,1)}, bf16[24,2048]{1,0:T(8,128)(2,1)}, u32[]{:S(2)}, u32[]{:S(2)}) collective-permute-start(bf16[24,2048]{1,0:T(8,128)(2,1)} %get-tuple-element.49), channel_id=1, source_target_pairs={{0,26},{2,24},{4,30},{6,28},{8,18},{10,16},{12,22},{14,20},{16,10}... | collective-permute-start | bytes 294920 | tf_op jit(solution)/shard_map/ppermute | solution.py:326
  157.2 12.4 %collective-permute-start.21 = (bf16[24,2048]{1,0:T(8,128)(2,1)}, bf16[24,2048]{1,0:T(8,128)(2,1)}, u32[]{:S(2)}, u32[]{:S(2)}) collective-permute-start(bf16[24,2048]{1,0:T(8,128)(2,1)} %get-tuple-element.50), channel_id=1, source_target_pairs={{0,28},{2,30},{4,24},{6,26},{8,20},{10,22},{12,16},{14,18},{16,12}... | collective-permute-start | bytes 294920 | tf_op jit(solution)/shard_map/ppermute | solution.py:326
  160.4 9.3 %collective-permute-start.22 = (bf16[24,2048]{1,0:T(8,128)(2,1)}, bf16[24,2048]{1,0:T(8,128)(2,1)}, u32[]{:S(2)}, u32[]{:S(2)}) collective-permute-start(bf16[24,2048]{1,0:T(8,128)(2,1)} %get-tuple-element.51), channel_id=1, source_target_pairs={{0,30},{2,28},{4,26},{6,24},{8,22},{10,20},{12,18},{14,16},{16,14}... | collective-permute-start | bytes 294920 | tf_op jit(solution)/shard_map/ppermute | solution.py:326
  162.0 7.7 %collective-permute-start.8 = (bf16[24,2048]{1,0:T(8,128)(2,1)}, bf16[24,2048]{1,0:T(8,128)(2,1)}, u32[]{:S(2)}, u32[]{:S(2)}) collective-permute-start(bf16[24,2048]{1,0:T(8,128)(2,1)} %get-tuple-element.37), channel_id=1, source_target_pairs={{0,2},{2,0},{4,6},{6,4},{8,10},{10,8},{12,14},{14,12},{16,18},{18,... | collective-permute-start | bytes 294920 | tf_op jit(solution)/shard_map/ppermute | solution.py:326
  165.5 4.9 %collective-permute-start.9 = (bf16[24,2048]{1,0:T(8,128)(2,1)}, bf16[24,2048]{1,0:T(8,128)(2,1)}, u32[]{:S(2)}, u32[]{:S(2)}) collective-permute-start(bf16[24,2048]{1,0:T(8,128)(2,1)} %get-tuple-element.38), channel_id=1, source_target_pairs={{0,4},{2,6},{4,0},{6,2},{8,12},{10,14},{12,8},{14,10},{16,20},{18,... | collective-permute-start | bytes 294920 | tf_op jit(solution)/shard_map/ppermute | solution.py:326
  170.5 0.9 copy-start.5

commit v14 on v12

--- a/solution.py
+++ b/solution.py
@@ -42,16 +42,8 @@
     return [unit_ref.at[0, cut] if axis == 0 else unit_ref.at[0, :, cut] for cut in cuts]
 
 
-def place_kernel(experts, parts, plane_ref, routes_ref, tokens_ref, slots_ref, near_ref, *refs):
-    place_ref, sems, out_sems, rows_ref, stage_ref = refs
-    slots, width = slots_ref.shape
-    capacity = slots // experts
-    tok_rows, top_count = routes_ref.shape
-    (copy,) = fetch([tokens_ref], [rows_ref], sems)
-    routes = routes_ref[...]
-    home_plane, home_set = lax.rem(routes + 1, parts), lax.div(routes, parts)
-    lanes = home_plane * (experts // parts) + home_set
-    near_lanes = home_set * parts + lax.rem(home_plane + (parts - plane_ref[0]), parts)
+def ranks(routes, experts):
+    tok_rows, top_count = routes.shape
     numbers = lax.broadcasted_iota(jnp.int32, (tok_rows, experts), 1)
     named = [numbers == routes[:, k : k + 1] for k in range(top_count)]
     chosen = sum(n.astype(F32) for n in named)
@@ -60,18 +52,56 @@
         < lax.broadcasted_iota(jnp.int32, (tok_rows, tok_rows), 0)
     ).astype(F32)
     rank = dot(earlier.astype(BF16), chosen.astype(BF16), (1, 0))
-    slot_numbers = lax.broadcasted_iota(jnp.int32, (tok_rows, slots), 1)
-    near = None
-    for k in range(top_count):
-        own = jnp.sum(jnp.where(named[k], rank, 0.0), axis=1, keepdims=True).astype(jnp.int32)
-        mark, near_mark = (
-            (slot_numbers == order[:, k : k + 1] * capacity + own).astype(F32)
-            for order in (lanes, near_lanes)
-        )
+    return jnp.concatenate(
+        [jnp.sum(jnp.where(n, rank, 0.0), axis=1, keepdims=True) for n in named], axis=1
+    ).astype(jnp.int32)
+
+
+def lanes_of(routes, experts, parts, plane, half):
+    sets = experts // parts
+    home_plane, home_set = lax.rem(routes + 1, parts), lax.div(routes, parts)
+    local = home_set - half * (sets // 2)
+    inside = (local >= 0) & (local < sets // 2)
+    return home_plane * sets + home_set, local, lax.rem(home_plane + (parts - plane), parts), inside
+
+
+def marks(slot, count):
+    tok_rows, top_count = slot.shape
+    numbers = lax.broadcasted_iota(jnp.int32, (tok_rows, count), 1)
+    return [(numbers == slot[:, k : k + 1]).astype(F32) for k in range(top_count)]
+
+
+def place_kernel(experts, parts, plane_ref, half_ref, routes_ref, tokens_ref, cotangent_ref, *refs):
+    slots_ref, place_ref, sems, out_sems, rows_ref, near_ref, stage_ref = refs
+    slots = slots_ref.shape[0]
+    capacity = slots // experts
+    tok_rows = routes_ref.shape[0]
+    copies = fetch(
+        [tokens_ref, cotangent_ref],
+        [rows_ref.at[pl.ds(0, tok_rows)], rows_ref.at[pl.ds(tok_rows, tok_rows)]],
+        sems,
+    )
+    routes = routes_ref[...]
+    rank = ranks(routes, experts)
+    back, local, ahead, inside = lanes_of(routes, experts, parts, plane_ref[0], half_ref[0])
+    for k, mark in enumerate(marks(back * capacity + rank, slots)):
         place_ref[k * tok_rows : (k + 1) * tok_rows, :] = mark.astype(BF16)
-        near = near_mark if near is None else near + near_mark
-    near_ref[...] = near.astype(BF16)
-    copy.wait()
+    for i in range(2):
+        slot = ((local * 2 + i) * parts + ahead) * capacity + rank
+        near = sum(marks(jnp.where(inside, slot, -1), slots))
+        near_ref[i * tok_rows : (i + 1) * tok_rows, :] = near.astype(BF16)
+    for copy in copies:
+        copy.wait()
+    spread(near_ref, rows_ref, stage_ref, slots_ref, out_sems)
+
+
+def far_kernel(experts, parts, plane_ref, half_ref, routes_ref, rows_ref, _, *refs):
+    slots_ref, near_ref, out_sems, stage_ref = refs
+    slots = slots_ref.shape[0]
+    routes = routes_ref[...]
+    _, local, ahead, inside = lanes_of(routes, experts, parts, plane_ref[0], half_ref[0])
+    slot = (local * parts + ahead) * (2 * slots // experts) + ranks(routes, experts)
+    near_ref[...] = sum(marks(jnp.where(inside, slot, -1), slots)).astype(BF16)
     spread(near_ref, rows_ref, stage_ref, slots_ref, out_sems)
 
 
@@ -84,18 +114,19 @@
         copy.wait()
 
 
-def spread_kernel(near_ref, rows_ref, _, slots_ref, out_sems, stage_ref):
+def spread_kernel(near_ref, rows_ref, *refs):
+    slots_ref, out_sems, stage_ref = refs[-3:]
     spread(near_ref, rows_ref, stage_ref, slots_ref, out_sems)
 
 
-def cut_kernel(numbers, rows_ref, *refs):
+def cut_kernel(array, numbers, half_ref, own_ref, far_ref, *refs):
     out_refs, sems = refs[-1 - len(numbers) : -1], refs[-1]
-    sets = rows_ref.shape[0]
-    for copy in fetch(
-        [rows_ref.at[q, i] for i in numbers for q in range(sets)],
-        [out_ref.at[q] for out_ref in out_refs for q in range(sets)],
-        sems,
-    ):
+    sets = range(own_ref.shape[0])
+    sources = [own_ref.at[q, array, i] for i in numbers for q in sets]
+    targets = [out_ref.at[half_ref[0], q] for out_ref in out_refs for q in sets]
+    sources += [far_ref.at[q, i] for i in numbers for q in sets]
+    targets += [out_ref.at[1 - half_ref[0], q] for out_ref in out_refs for q in sets]
+    for copy in fetch(sources, targets, sems):
         copy.wait()
 
 
@@ -253,7 +284,14 @@
         [[device(g, parts * q + c) for q in range(sets)] for g in range(parts)] for c in range(parts)
     ]
     everywhere = [[d for plane in planes[c] for d in plane] for c in range(parts)]
-    in_plane = [plane for c in range(parts) for plane in planes[c]]
+    near_sets = sets // 2
+    in_half = [
+        plane[start : start + near_sets]
+        for c in range(parts)
+        for plane in planes[c]
+        for start in (0, near_sets)
+    ]
+    across = [(j, (j + experts // 2) % experts) for j in range(experts)]
 
     def swapped(weight):
         return lax.ppermute(weight[0], axes, swap)
@@ -265,26 +303,31 @@
             held.append(lax.ppermute(own, "expert", turn))
         return held
 
-    def dispatch(rows, after=()):
-        rows = rows.reshape(sets, parts * capacity, width)
-        rows = lax.all_to_all(rows, axes, 0, 0, axis_index_groups=in_plane, tiled=True)
-        rows = rows.reshape(sets, parts, capacity, width)
+    def far_side(array):
+        return lax.ppermute(array, "expert", across)
+
+    def to_sets(rows):
+        rows = rows.reshape(near_sets, rows.shape[0] // near_sets, width)
+        return lax.all_to_all(rows, axes, 0, 0, axis_index_groups=in_half, tiled=True)
+
+    def to_planes(array, own, far, after=()):
+        own = own.reshape(near_sets, 2, parts, capacity, width)
+        far = far.reshape(near_sets, parts, capacity, width)
 
         def cut(numbers, space):
             return call(
-                functools.partial(cut_kernel, numbers),
-                [jax.ShapeDtypeStruct((sets, capacity, width), BF16)] * len(numbers),
+                functools.partial(cut_kernel, array, numbers),
+                [jax.ShapeDtypeStruct((2, near_sets, capacity, width), BF16)] * len(numbers),
                 0,
                 [sems(len(numbers) * sets)],
-                far=(0,),
-                pinned=range(1, 1 + len(after)),
+                far=(1, 2),
+                pinned=range(3, 3 + len(after)),
                 out_spaces=[space] * len(numbers),
-            )(rows, *after)
+            )(half, own, far, *after)
 
         leaving = cut(range(1, parts), pl.ANY)
-        cuts = [*cut(range(1), pltpu.HBM), *leaving]
         crossed = []
-        for i, rows in enumerate(cuts):
+        for i, rows in enumerate([*cut(range(1), pltpu.HBM), *leaving]):
             rows = rows.reshape(sets * capacity, width)
             if i > 0:
                 rows = lax.ppermute(rows, "dp", [(g, (g + i) % parts) for g in range(parts)])
@@ -315,26 +358,42 @@
     def sems(number):
         return pltpu.SemaphoreType.DMA((number,))
 
+    far_tokens, far_routes = far_side(tokens), far_side(routes)
     gate_own, up_own, down_own = swapped(w_gate), swapped(w_up), swapped(w_down)
+    far_cotangent = far_side(cotangent)
     gate_w, up_w, down_w = whole_expert(gate_own), whole_expert(up_own), whole_expert(down_own)
     plane = lax.axis_index("dp").astype(jnp.int32).reshape(1)
-    x_slots, near, place = call(
+    half = (lax.axis_index("expert") // (experts // 2)).astype(jnp.int32).reshape(1)
+    far_shape = jax.ShapeDtypeStruct((slots // 2, width), BF16)
+    far_scratch = pltpu.VMEM((slots // 2, width), BF16)
+    own_slots, place = call(
         functools.partial(place_kernel, experts, parts),
-        [slot_shape, jax.ShapeDtypeStruct((tok_rows, slots), BF16), place_shape],
+        [slot_shape, place_shape],
+        2 * spread_flops,
+        [sems(2), sems(pieces), pltpu.VMEM((2 * tok_rows, width), BF16)]
+        + [pltpu.VMEM((2 * tok_rows, slots), BF16), row_scratch],
+        pinned=(3, 4),
+        out_spaces=[pltpu.HBM, pltpu.VMEM],
+    )(plane, half, routes, tokens, cotangent)
+    own_rows = to_sets(own_slots)
+    far_x_slots, near = call(
+        functools.partial(far_kernel, experts, parts),
+        [far_shape, jax.ShapeDtypeStruct((tok_rows, slots // 2), BF16)],
         spread_flops,
-        [sems(1), sems(pieces), pltpu.VMEM((tok_rows, width), BF16), row_scratch],
-        pinned=(2,),
-        out_spaces=[pltpu.HBM, pltpu.VMEM, pltpu.VMEM],
-    )(plane, routes, tokens)
-    x_shares = dispatch(x_slots)
-    (dy_slots,) = call(
+        [sems(pieces), far_scratch],
+        far=(4,),
+        out_spaces=[pltpu.HBM, pltpu.VMEM],
+    )(plane, half, far_routes, far_tokens, own_rows)
+    x_shares = to_planes(0, own_rows, to_sets(far_x_slots))
+    (far_dy_slots,) = call(
         spread_kernel,
-        [slot_shape],
+        [far_shape],
         256 * spread_flops,
-        [sems(pieces), row_scratch],
-        pinned=(2,),
+        [sems(pieces), far_scratch],
+        pinned=(2, 3),
         out_spaces=[pltpu.HBM],
-    )(near, cotangent, gate_own)
+    )(near, far_cotangent, gate_own, up_own)
+    far_dy_rows = to_sets(far_dy_slots)
     out_rows, by_gate, by_up = call(
         functools.partial(forward_kernel, parts, joined),
         [slot_shape, unit_shape, unit_shape],
@@ -345,7 +404,7 @@
         out_spaces=[pltpu.HBM] * 3,
         vmem=LARGE_VMEM,
     )(plane, *x_shares, *gate_w, *up_w, *down_w)
-    dy_shares = dispatch(dy_slots, (out_rows,))
+    dy_shares = to_planes(1, own_rows, far_dy_rows, (out_rows,))
     out_slots = send_back(out_rows)
     (grad_rows,) = call(
         functools.partial(backward_kernel, parts, joined),

time: 177 us -> 203 us (1.15)
  waiting for transfers between devices: 115 us -> 128 us
  starting transfers between devices: 25 us -> 35.4 us
  Pallas kernels: 27.7 us -> 30.3 us
    ppermute x2 -> x5, waiting for transfers between devices: 38.9 us -> 60.6 us  [the longest x2 35.4 us: to_planes(): lax.ppermute(rows, 'dp', [(g, (g + i) % parts) for g in range(parts)])]
    all_to_all x2 -> x3, waiting for transfers between devices: 29.1 us -> 8.44 us  [to_sets(): lax.all_to_all(rows, axes, 0, 0, axis_index_groups=in_half, tiled=True)]
    ppermute x3, waiting for transfers between devices: 10 us -> 20.3 us  [swapped(): return lax.ppermute(weight[0], axes, swap)]
    ppermute x2 -> x5, starting transfers between devices: 3.73 us -> 10.7 us  [the longest x3 6.38 us: far_side(): return lax.ppermute(array, 'expert', across)]
    all_to_all x2 -> x3, starting transfers between devices: 9.53 us -> 13.1 us  [to_sets(): lax.all_to_all(rows, axes, 0, 0, axis_index_groups=in_half, tiled=True)]
    pallas_call x10 -> x11, Pallas kernels: 27.7 us -> 30.3 us  [run(): pl.pallas_call(kernel, out_shape=tuple(outs), in_specs=[pl.BlockSpec(memo...]
    unnamed x25 -> x23, local copies, waits for them, and re-layouts: 7.45 us -> 8.2 us
  transfers between devices with their start and end apart: 12 -> 16, of which waited for: 9 -> 8; matrix products, arithmetic and copies ran while one was open for 1% -> 0% of each run, Pallas kernels for 14% -> 13%
where the time goes in v14:
time: 203 us
  waiting for transfers between devices  128 us (63%)
  starting transfers between devices  35.4 us (17%)
  Pallas kernels  30.3 us (15%)
  local copies, waits for them, and re-layouts  8.2 us (4%)
    all_to_all x2, waiting for transfers between devices, send_back(): lax.all_to_all(rows, axes, 0, 0, axis_index_groups=everywhere, tiled=True)  38.6 us
    ppermute x2, waiting for transfers between devices, to_planes(): lax.ppermute(rows, 'dp', [(g, (g + i) % parts) for g in range(parts)])  35.4 us
    pallas_call x11, Pallas kernels, run(): pl.pallas_call(kernel, out_shape=tuple(outs), in_specs=[pl.BlockSpec(memo...  30.3 us
    ppermute x3, waiting for transfers between devices, far_side(): return lax.ppermute(array, 'expert', across)  25.2 us
    ppermute x3, waiting for transfers between devices, swapped(): return lax.ppermute(weight[0], axes, swap)  20.3 us
    all_to_all x3, starting transfers between devices, to_sets(): lax.all_to_all(rows, axes, 0, 0, axis_index_groups=in_half, tiled=True)  13.1 us
    all_to_all x2, starting transfers between devices, send_back(): lax.all_to_all(rows, axes, 0, 0, axis_index_groups=everywhere, tiled=True)  10 us
    all_to_all x3, waiting for transfers between devices, to_sets(): lax.all_to_all(rows, axes, 0, 0, axis_index_groups=in_half, tiled=True)  8.44 us
  transfers between devices with their start and end apart: 16, of which 8 were waited for; matrix products, arithmetic and copies ran while one was open for 0% of the time, Pallas kernels for 13%

profile of v14, /device:TPU:0, one launch (start us, length us, event | category | flops | bytes accessed | tf_op | source)
XLA Modules:
  0.0 202.6 jit_solution(11439216757108643132)
XLA Ops:
  0.6 0.8 copy.10.routes_ref
  1.4 0.0 copy-start.3
  1.5 1.0 copy-done.3
  2.5 0.0 copy-start.6
  2.5 1.0 copy-done.6
  3.5 2.1 %shard_map.94 = (bf16[384,2048]{1,0:T(8,128)(2,1)}, bf16[256,384]{1,0:T(8,128)(2,1)S(1)}) custom-call(s32[1]{0:T(128)} %bitcast.plane_ref, s32[1]{0:T(128)} %bitcast.1.half_ref, s32[128,2]{1,0:T(8,128)S(1)} %copy.10.routes_ref, bf16[128,2048]{1,0:T(8,128)(2,1)S(1)} %copy-done.6, bf16[128,2048]{1,0:T(8,128)(2,1)S(1)} %copy-done.3), custom_call_target="tpu_custom_call" | custom-call | flops 402653184 | bytes 2819080 | tf_op jit(solution)/shard_map/pallas_call | solution.py:249
  5.6 0.0 copy-start.7
  5.6 0.0 copy-start.4
  5.6 5.4 %all-to-all-start = ((bf16[4,96,2048]{2,1,0:T(8,128)(2,1)}), bf16[4,96,2048]{2,1,0:T(8,128)(2,1)S(1)}, u32[]{:S(2)}, u32[]{:S(2)}) async-start(bf16[4,96,2048]{2,1,0:T(8,128)(2,1)} %bitcast.2), calls=%async_computation | async-start | bytes 3145728 | tf_op jit(solution)/shard_map/all_to_all | solution.py:311
  11.0 1.5 collective-permute-start.3
  12.5 0.0 collective-permute-start.5
  12.6 0.0 collective-permute-start.7
  12.6 0.0 copy-done.7
  12.6 2.6 %collective-permute-start.1 = (bf16[128,2048]{1,0:T(8,128)(2,1)S(1)}, bf16[128,2048]{1,0:T(8,128)(2,1)S(1)}, u32[]{:S(2)}, u32[]{:S(2)}) collective-permute-start(bf16[128,2048]{1,0:T(8,128)(2,1)S(1)} %copy-done.7), channel_id=1, source_target_pairs={{0,8},{1,9},{2,10},{3,11},{4,12},{5,13},{6,14},{7,15},{8,0},{9,1},... | collective-permute-start | bytes 1572872 | tf_op jit(solution)/shard_map/ppermute | solution.py:307
  15.2 0.3 collective-permute-start
  15.5 25.2 %collective-permute-done.routes_ref = s32[128,2]{1,0:T(8,128)S(1)} collective-permute-done((s32[128,2]{1,0:T(8,128)S(1)}, s32[128,2]{1,0:T(8,128)S(1)}, u32[]{:S(2)}, u32[]{:S(2)}) %collective-permute-start) | collective-permute-done | bytes 1056 | tf_op jit(solution)/shard_map/ppermute | solution.py:307
  40.8 0.0 copy-done.4
  40.8 3.4 %collective-permute-start.9 = (bf16[128,2048]{1,0:T(8,128)(2,1)S(1)}, bf16[128,2048]{1,0:T(8,128)(2,1)}, u32[]{:S(2)}, u32[]{:S(2)}) collective-permute-start(bf16[128,2048]{1,0:T(8,128)(2,1)S(1)} %copy-done.4), channel_id=1, source_target_pairs={{0,8},{1,9},{2,10},{3,11},{4,12},{5,13},{6,14},{7,15},{8,0},{9,1},... | collective-permute-start | bytes 1572872 | tf_op jit(solution)/shard_map/ppermute | solution.py:307
  44.2 0.0 collective-permute-done.3.refs_2_.refs_0_.refs_6_
  44.2 0.0 collective-permute-start.4
  44.2 3.4 %collective-permute-done.5.refs_4_.refs_1_.refs_8_ = bf16[2048,384]{1,0:T(8,128)(2,1)} collective-permute-done((bf16[2048,384]{1,0:T(8,128)(2,1)}, bf16[2048,384]{1,0:T(8,128)(2,1)}, u32[]{:S(2)}, u32[]{:S(2)}) %collective-permute-start.5) | collective-permute-done | bytes 1572896 | tf_op jit(solution)/shard_map/ppermute | solution.py:297
  47.6 0.0 collective-permute-start.6
  47.6 16.8 %collective-permute-done.7.refs_6_.refs_2_ = bf16[384,2048]{1,0:T(8,128)(2,1)} collective-permute-done((bf16[384,2048]{1,0:T(8,128)(2,1)}, bf16[384,2048]{1,0:T(8,128)(2,1)}, u32[]{:S(2)}, u32[]{:S(2)}) %collective-permute-start.7) | collective-permute-done | bytes 1572896 | tf_op jit(solution)/shard_map/ppermute | solution.py:297
  64.5 0.0 collective-permute-start.8
  64.5 0.0 collective-permute-done.1.rows_ref
  64.5 0.0 all-to-all-done._
  64.5 1.6 shard_map.95
  66.1 4.2 %all-to-all-start.1 = ((bf16[4,48,2048]{2,1,0:T(8,128)(2,1)}), bf16[4,48,2048]{2,1,0:T(8,128)(2,1)S(1)}, u32[]{:S(2)}, u32[]{:S(2)}) async-start(bf16[4,48,2048]{2,1,0:T(8,128)(2,1)} %bitcast.4), calls=%async_computation.1 | async-start | bytes 1572864 | tf_op jit(solution)/shard_map/all_to_all | solution.py:311
  70.3 0.0 collective-permute-done.9.rows_ref
  70.3 2.2 %shard_map.100 = bf16[192,2048]{1,0:T(8,128)(2,1)S(1)} custom-call(bf16[128,192]{1,0:T(8,128)(2,1)S(1)} %get-tuple-element.17.near_ref, bf16[128,2048]{1,0:T(8,128)(2,1)} %collective-permute-done.9.rows_ref, bf16[2048,384]{1,0:T(8,128)(2,1)} %collective-permute-done.3.refs_2_.refs_0_.refs_6_, bf16[2048,384]{1,0:T(8,128)(2,1)} %collective-permute-done.5.refs_4_.refs_1_.refs_8_), custom_call_target="tpu_custom_call" | custom-call | flops 51539607552 | bytes 4505600 | tf_op jit(solution)/shard_map/pallas_call | solution.py:249
  72.5 0.0 copy-start.1
  72.5 0.9 copy-done.1
  73.4 8.4 %all-to-all-done.1 = bf16[4,48,2048]{2,1,0:T(8,128)(2,1)S(1)} async-done(((bf16[4,48,2048]{2,1,0:T(8,128)(2,1)}), bf16[4,48,2048]{2,1,0:T(8,128)(2,1)S(1)}, u32[]{:S(2)}, u32[]{:S(2)}) %all-to-all-start.1) | async-done | bytes 786464 | tf_op jit(solution)/shard_map/all_to_all | solution.py:311
  81.8 3.5 %all-to-all-start.3 = ((bf16[4,48,2048]{2,1,0:T(8,128)(2,1)}), bf16[4,48,2048]{2,1,0:T(8,128)(2,1)S(1)}, u32[]{:S(2)}, u32[]{:S(2)}) async-start(bf16[4,48,2048]{2,1,0:T(8,128)(2,1)} %bitcast.31), calls=%async_computation.3 | async-start | bytes 1572864 | tf_op jit(solution)/shard_map/all_to_all | solution.py:311
  85.3 1.1 shard_map.97
  86.4 2.5 %collective-permute-start.2 = (bf16[192,2048]{1,0:T(8,128)(2,1)S(1)}, bf16[192,2048]{1,0:T(8,128)(2,1)S(1)}, u32[]{:S(2)}, u32[]{:S(2)}) collective-permute-start(bf16[192,2048]{1,0:T(8,128)(2,1)S(1)} %bitcast.33), channel_id=1, source_target_pairs={{0,16},{16,0},{1,17},{17,1},{2,18},{18,2},{3,19},{19,3},{4,20},{20... | collective-permute-start | bytes 2359304 | tf_op jit(solution)/shard_map/ppermute | solution.py:333
  89.0 1.1 shard_map.96
  90.0 0.0 copy-start.2
  90.1 0.9 copy-done.2
  91.0 0.0 collective-permute-done.4.refs_3_.refs_7_
  91.0 0.0 collective-permute-done.6.refs_5_.refs_9_
  91.0 0.0 collective-permute-done.8.refs_7_.refs_3_
  91.0 15.1 %collective-permute-done.2.refs_1_ = bf16[192,2048]{1,0:T(8,128)(2,1)S(1)} collective-permute-done((bf16[192,2048]{1,0:T(8,128)(2,1)S(1)}, bf16[192,2048]{1,0:T(8,128)(2,1)S(1)}, u32[]{:S(2)}, u32[]{:S(2)}) %collective-permute-start.2) | collective-permute-done | bytes 786464 | tf_op jit(solution)/shard_map/ppermute | solution.py:333
  106.1 0.0 copy-start.9
  106.1 0.9 copy-done.9
  107.0 8.3 %shard_map.98 = (bf16[384,2048]{1,0:T(8,128)(2,1)}, f32[1,384,768]{2,1,0:T(8,128)}, f32[1,384,768]{2,1,0:T(8,128)}) custom-call(s32[1]{0:T(128)} %bitcast.plane_ref, bf16[192,2048]{1,0:T(8,128)(2,1)} %bitcast.32, bf16[192,2048]{1,0:T(8,128)(2,1)} %copy-done.9, bf16[2048,384]{1,0:T(8,128)(2,1)} %collective-permute-done.3.refs_2_.refs_0_.refs_6_, ...), custom_call_target="tpu_custom_call" | custom-call | flops 3623878656 | bytes 14942212 | tf_op jit(solution)/shard_map/pallas_call | solution.py:249
  115.3 0.0 all-to-all-done.3
  115.3 1.1 shard_map.102
  116.4 1.8 collective-permute-start.10
  118.2 1.1 shard_map.101
  119.3 0.0 copy-start
  119.3 0.9 copy-done
  120.2 6.0 %all-to-all-start.2 = ((bf16[16,24,2048]{2,1,0:T(8,128)(2,1)}), bf16[16,24,2048]{2,1,0:T(8,128)(2,1)S(1)}, u32[]{:S(2)}, u32[]{:S(2)}) async-start(bf16[16,24,2048]{2,1,0:T(8,128)(2,1)} %bitcast.11), calls=%async_computation.2 | async-start | bytes 3145728 | tf_op jit(solution)/shard_map/all_to_all | solution.py:339
  126.1 20.2 %collective-permute-done.10.refs_1_ = bf16[192,2048]{1,0:T(8,128)(2,1)} collective-permute-done((bf16[192,2048]{1,0:T(8,128)(2,1)S(1)}, bf16[192,2048]{1,0:T(8,128)(2,1)}, u32[]{:S(2)}, u32[]{:S(2)}) %collective-permute-start.10) | collective-permute-done | bytes 786464 | tf_op jit(solution)/shard_map/ppermute | solution.py:333
  146.4 8.6 %shard_map.103 = bf16[384,2048]{1,0:T(8,128)(2,1)} custom-call(s32[1]{0:T(128)} %bitcast.plane_ref, bf16[192,2048]{1,0:T(8,128)(2,1)} %bitcast.29, bf16[192,2048]{1,0:T(8,128)(2,1)} %collective-permute-done.10.refs_1_, bf16[384,2048]{1,0:T(8,128)(2,1)} %collective-permute-done.7.refs_6_.refs_2_, bf16[384,2048]{1,0:T(8,128)(2,1)} %collective-permute-done.8.refs_7_.refs_3_, ...), custom_call_target="tpu_custom_call" | custom-call | flops 77309411328 | bytes 14942212 | tf_op jit(solution)/shard_map/pallas_call | solution.py:249
  155.0 6.5 %all-to-all-done.2 = bf16[16,24,2048]{2,1,0:T(8,128)(2,1)S(1)} async-done(((bf16[16,24,2048]{2,1,0:T(8,128)(2,1)}), bf16[16,24,2048]{2,1,0:T(8,128)(2,1)S(1)}, u32[]{:S(2)}, u32[]{:S(2)}) %all-to-all-start.2) | async-done | bytes 1572896 | tf_op jit(solution)/shard_map/all_to_all | solution.py:339
  161.5 4.0 %all-to-all-start.4 = ((bf16[16,24,2048]{2,1,0:T(8,128)(2,1)}), bf16[16,24,2048]{2,1,0:T(8,128)(2,1)S(1)}, u32[]{:S(2)}, u32[]{:S(2)}) async-start(bf16[16,24,2048]{2,1,0:T(8,128)(2,1)} %bitcast.34), calls=%async_computation.4 | async-start | bytes 3145728 | tf_op jit(solution)/shard_map/all_to_all | solution.py:339
  165.5 0.0 copy-done.8
  165.6 0.1 copy.12.gates_ref
  165.7 1.0 copy-done.5
  166.7 1.7 shard_map.99
  168.4 0.6 copy.14
  169.0 32.1 %all-to-all-done.4 = bf16[16,24,2048]{2,1,0:T(8,128)(2,1)S(1)} async-done(((bf16[16,24,2048]{2,1,0:T(8,128)(2,1)}), bf16[16,24,2048]{2,1,0:T(8,128)(2,1)S(1)}, u32[]{:S(2)}, u32[]{:S(2)}) %all-to-all-start.4) | async-done | bytes 1572896 | tf_op jit(solution)/shard_map/all_to_all | solution.py:339
  201.1 1.5 shard_map.104
  (2 shorter events, 0.0 us)
Async XLA Ops:
  1.4 1.0 copy-start.3
  2.5 1.0 copy-start.6
  5.6 7.0 %copy-start.7 = (bf16[128,2048]{1,0:T(8,128)(2,1)S(1)}, bf16[128,2048]{1,0:T(8,128)(2,1)}, u32[]{:S(2)}) copy-start(bf16[128,2048]{1,0:T(8,128)(2,1)} %tokens_ref.1) | copy-start | bytes 1572868
  5.6 35.1 %copy-start.4 = (bf16[128,2048]{1,0:T(8,128)(2,1)S(1)}, bf16[128,2048]{1,0:T(8,128)(2,1)}, u32[]{:S(2)}) copy-start(bf16[128,2048]{1,0:T(8,128)(2,1)} %cotangent_ref.3) | copy-start | bytes 1572868
  5.6 58.9 %all-to-all-start = ((bf16[4,96,2048]{2,1,0:T(8,128)(2,1)}), bf16[4,96,2048]{2,1,0:T(8,128)(2,1)S(1)}, u32[]{:S(2)}, u32[]{:S(2)}) async-start(bf16[4,96,2048]{2,1,0:T(8,128)(2,1)} %bitcast.2), calls=%async_computation | async-start | bytes 3145728 | tf_op jit(solution)/shard_map/all_to_all | solution.py:311
  11.0 33.2 %collective-permute-start.3 = (bf16[2048,384]{1,0:T(8,128)(2,1)}, bf16[2048,384]{1,0:T(8,128)(2,1)}, u32[]{:S(2)}, u32[]{:S(2)}) collective-permute-start(bf16[2048,384]{1,0:T(8,128)(2,1)} %bitcast.35), channel_id=1, source_target_pairs={{0,16},{1,0},{2,18},{3,2},{4,20},{5,4},{6,22},{7,6},{8,24},{9,8},{... | collective-permute-start | bytes 4718600 | tf_op jit(solution)/shard_map/ppermute | solution.py:297
  12.5 35.1 %collective-permute-start.5 = (bf16[2048,384]{1,0:T(8,128)(2,1)}, bf16[2048,384]{1,0:T(8,128)(2,1)}, u32[]{:S(2)}, u32[]{:S(2)}) collective-permute-start(bf16[2048,384]{1,0:T(8,128)(2,1)} %bitcast.36), channel_id=1, source_target_pairs={{0,16},{1,0},{2,18},{3,2},{4,20},{5,4},{6,22},{7,6},{8,24},{9,8},{... | collective-permute-start | bytes 4718600 | tf_op jit(solution)/shard_map/ppermute | solution.py:297
  12.6 51.9 %collective-permute-start.7 = (bf16[384,2048]{1,0:T(8,128)(2,1)}, bf16[384,2048]{1,0:T(8,128)(2,1)}, u32[]{:S(2)}, u32[]{:S(2)}) collective-permute-start(bf16[384,2048]{1,0:T(8,128)(2,1)} %bitcast.37), channel_id=1, source_target_pairs={{0,16},{1,0},{2,18},{3,2},{4,20},{5,4},{6,22},{7,6},{8,24},{9,8},{... | collective-permute-start | bytes 4718600 | tf_op jit(solution)/shard_map/ppermute | solution.py:297
  12.6 51.9 %collective-permute-start.1 = (bf16[128,2048]{1,0:T(8,128)(2,1)S(1)}, bf16[128,2048]{1,0:T(8,128)(2,1)S(1)}, u32[]{:S(2)}, u32[]{:S(2)}) collective-permute-start(bf16[128,2048]{1,0:T(8,128)(2,1)S(1)} %copy-done.7), channel_id=1, source_target_pairs={{0,8},{1,9},{2,10},{3,11},{4,12},{5,13},{6,14},{7,15},{8,0},{9,1},... | collective-permute-start | bytes 1572872 | tf_op jit(solution)/shard_map/ppermute | solution.py:307
  15.2 25.6 %collective-permute-start = (s32[128,2]{1,0:T(8,128)S(1)}, s32[128,2]{1,0:T(8,128)S(1)}, u32[]{:S(2)}, u32[]{:S(2)}) collective-permute-start(s32[128,2]{1,0:T(8,128)S(1)} %copy.10.routes_ref), channel_id=1, source_target_pairs={{0,8},{1,9},{2,10},{3,11},{4,12},{5,13},{6,14},{7,15},{8,0},{9,1},... | collective-permute-start | bytes 3080 | tf_op jit(solution)/shard_map/ppermute | solution.py:307
  40.8 29.6 %collective-permute-start.9 = (bf16[128,2048]{1,0:T(8,128)(2,1)S(1)}, bf16[128,2048]{1,0:T(8,128)(2,1)}, u32[]{:S(2)}, u32[]{:S(2)}) collective-permute-start(bf16[128,2048]{1,0:T(8,128)(2,1)S(1)} %copy-done.4), channel_id=1, source_target_pairs={{0,8},{1,9},{2,10},{3,11},{4,12},{5,13},{6,14},{7,15},{8,0},{9,1},... | collective-permute-start | bytes 1572872 | tf_op jit(solution)/shard_map/ppermute | solution.py:307
  44.2 46.8 %collective-permute-start.4 = (bf16[2048,384]{1,0:T(8,128)(2,1)}, bf16[2048,384]{1,0:T(8,128)(2,1)}, u32[]{:S(2)}, u32[]{:S(2)}) collective-permute-start(bf16[2048,384]{1,0:T(8,128)(2,1)} %collective-permute-done.3.refs_2_.refs_0_.refs_6_), channel_id=1, source_target_pairs={{0,1},{1,0},{2,3},{3,2},{4,5},{5,4},{6,7},{7,6},{8,9},{9,8},{10,11... | collective-permute-start | bytes 4718600 | tf_op jit(solution)/shard_map/ppermute | solution.py:303
  47.6 43.3 %collective-permute-start.6 = (bf16[2048,384]{1,0:T(8,128)(2,1)}, bf16[2048,384]{1,0:T(8,128)(2,1)}, u32[]{:S(2)}, u32[]{:S(2)}) collective-permute-start(bf16[2048,384]{1,0:T(8,128)(2,1)} %collective-permute-done.5.refs_4_.refs_1_.refs_8_), channel_id=1, source_target_pairs={{0,1},{1,0},{2,3},{3,2},{4,5},{5,4},{6,7},{7,6},{8,9},{9,8},{10,11... | collective-permute-start | bytes 4718600 | tf_op jit(solution)/shard_map/ppermute | solution.py:303
  64.5 26.5 %collective-permute-start.8 = (bf16[384,2048]{1,0:T(8,128)(2,1)}, bf16[384,2048]{1,0:T(8,128)(2,1)}, u32[]{:S(2)}, u32[]{:S(2)}) collective-permute-start(bf16[384,2048]{1,0:T(8,128)(2,1)} %collective-permute-done.7.refs_6_.refs_2_), channel_id=1, source_target_pairs={{0,1},{1,0},{2,3},{3,2},{4,5},{5,4},{6,7},{7,6},{8,9},{9,8},{10,11... | collective-permute-start | bytes 4718600 | tf_op jit(solution)/shard_map/ppermute | solution.py:303
  66.1 15.7 %all-to-all-start.1 = ((bf16[4,48,2048]{2,1,0:T(8,128)(2,1)}), bf16[4,48,2048]{2,1,0:T(8,128)(2,1)S(1)}, u32[]{:S(2)}, u32[]{:S(2)}) async-start(bf16[4,48,2048]{2,1,0:T(8,128)(2,1)} %bitcast.4), calls=%async_computation.1 | async-start | bytes 1572864 | tf_op jit(solution)/shard_map/all_to_all | solution.py:311
  72.5 0.9 copy-start.1
  81.8 33.5 %all-to-all-start.3 = ((bf16[4,48,2048]{2,1,0:T(8,128)(2,1)}), bf16[4,48,2048]{2,1,0:T(8,128)(2,1)S(1)}, u32[]{:S(2)}, u32[]{:S(2)}) async-start(bf16[4,48,2048]{2,1,0:T(8,128)(2,1)} %bitcast.31), calls=%async_computation.3 | async-start | bytes 1572864 | tf_op jit(solution)/shard_map/all_to_all | solution.py:311
  86.4 19.7 %collective-permute-start.2 = (bf16[192,2048]{1,0:T(8,128)(2,1)S(1)}, bf16[192,2048]{1,0:T(8,128)(2,1)S(1)}, u32[]{:S(2)}, u32[]{:S(2)}) collective-permute-start(bf16[192,2048]{1,0:T(8,128)(2,1)S(1)} %bitcast.33), channel_id=1, source_target_pairs={{0,16},{16,0},{1,17},{17,1},{2,18},{18,2},{3,19},{19,3},{4,20},{20... | collective-permute-start | bytes 2359304 | tf_op jit(solution)/shard_map/ppermute | solution.py:333
  90.0 0.9 copy-start.2
  106.1 0.9 copy-start.9
  116.4 30.0 %collective-permute-start.10 = (bf16[192,2048]{1,0:T(8,128)(2,1)S(1)}, bf16[192,2048]{1,0:T(8,128)(2,1)}, u32[]{:S(2)}, u32[]{:S(2)}) collective-permute-start(bf16[192,2048]{1,0:T(8,128)(2,1)S(1)} %bitcast.30), channel_id=1, source_target_pairs={{0,16},{16,0},{1,17},{17,1},{2,18},{18,2},{3,19},{19,3},{4,20},{20... | collective-permute-start | bytes 2359304 | tf_op jit(solution)/shard_map/ppermute | solution.py:333
  119.3 0.9 copy-start
  120.2 41.3 %all-to-all-start.2 = ((bf16[16,24,2048]{2,1,0:T(8,128)(2,1)}), bf16[16,24,2048]{2,1,0:T(8,128)(2,1)S(1)}, u32[]{:S(2)}, u32[]{:S(2)}) async-start(bf16[16,24,2048]{2,1,0:T(8,128)(2,1)} %bitcast.11), calls=%async_computation.2 | async-start | bytes 3145728 | tf_op jit(solution)/shard_map/all_to_all | solution.py:339
  161.5 4.1 %copy-start.8 = (f32[128,2]{0,1:T(2,128)S(1)}, f32[128,2]{0,1:T(2,128)}, u32[]{:S(2)}) copy-start(f32[128,2]{0,1:T(2,128)} %param.10) | copy-start | bytes 3076
  161.5 39.6 %all-to-all-start.4 = ((bf16[16,24,2048]{2,1,0:T(8,128)(2,1)}), bf16[16,24,2048]{2,1,0:T(8,128)(2,1)S(1)}, u32[]{:S(2)}, u32[]{:S(2)}) async-start(bf16[16,24,2048]{2,1,0:T(8,128)(2,1)} %bitcast.34), calls=%async_computation.4 | async-start | bytes 3145728 | tf_op jit(solution)/shard_map/all_to_all | solution.py:339
  165.7 1.0 copy-start.5

commit v15 on v14

--- a/solution.py
+++ b/solution.py
@@ -95,7 +95,7 @@
     spread(near_ref, rows_ref, stage_ref, slots_ref, out_sems)
 
 
-def far_kernel(experts, parts, plane_ref, half_ref, routes_ref, rows_ref, _, *refs):
+def far_kernel(experts, parts, plane_ref, half_ref, routes_ref, rows_ref, *refs):
     slots_ref, near_ref, out_sems, stage_ref = refs
     slots = slots_ref.shape[0]
     routes = routes_ref[...]
@@ -117,6 +117,10 @@
 def spread_kernel(near_ref, rows_ref, *refs):
     slots_ref, out_sems, stage_ref = refs[-3:]
     spread(near_ref, rows_ref, stage_ref, slots_ref, out_sems)
+
+
+def in_place_kernel(*refs):
+    pass
 
 
 def cut_kernel(array, numbers, half_ref, own_ref, far_ref, *refs):
@@ -233,7 +237,7 @@
     out_ref[...] = total.astype(BF16)
 
 
-def call(kernel, outs, flops, scratch=(), far=(), pinned=(), out_spaces=None, vmem=SMALL_VMEM):
+def call(kernel, outs, flops, scratch=(), far=(), pinned=(), out_spaces=None, vmem=SMALL_VMEM, aliases=None):
     def run(*args):
         moved = sum(a.size * a.dtype.itemsize for a in (*args, *outs))
         spaces = [
@@ -255,6 +259,7 @@
                 for space in out_spaces or [pltpu.VMEM] * len(outs)
             ),
             scratch_shapes=scratch,
+            input_output_aliases=aliases or {},
             compiler_params=pltpu.CompilerParams(vmem_limit_bytes=vmem),
             cost_estimate=pl.CostEstimate(flops=flops, bytes_accessed=moved, transcendentals=0),
         )(*args)
@@ -358,10 +363,19 @@
     def sems(number):
         return pltpu.SemaphoreType.DMA((number,))
 
+    def behind(arrays, last):
+        return call(
+            in_place_kernel,
+            [jax.ShapeDtypeStruct(a.shape, a.dtype) for a in arrays],
+            0,
+            pinned=range(len(arrays) + 1),
+            out_spaces=[pltpu.HBM] * len(arrays),
+            aliases={i: i for i in range(len(arrays))},
+        )(*arrays, last)
+
     far_tokens, far_routes = far_side(tokens), far_side(routes)
     gate_own, up_own, down_own = swapped(w_gate), swapped(w_up), swapped(w_down)
     far_cotangent = far_side(cotangent)
-    gate_w, up_w, down_w = whole_expert(gate_own), whole_expert(up_own), whole_expert(down_own)
     plane = lax.axis_index("dp").astype(jnp.int32).reshape(1)
     half = (lax.axis_index("expert") // (experts // 2)).astype(jnp.int32).reshape(1)
     far_shape = jax.ShapeDtypeStruct((slots // 2, width), BF16)
@@ -379,11 +393,11 @@
     far_x_slots, near = call(
         functools.partial(far_kernel, experts, parts),
         [far_shape, jax.ShapeDtypeStruct((tok_rows, slots // 2), BF16)],
-        spread_flops,
+        256 * spread_flops,
         [sems(pieces), far_scratch],
-        far=(4,),
         out_spaces=[pltpu.HBM, pltpu.VMEM],
-    )(plane, half, far_routes, far_tokens, own_rows)
+    )(plane, half, far_routes, far_tokens)
+    (far_x_slots,) = behind([far_x_slots], own_rows)
     x_shares = to_planes(0, own_rows, to_sets(far_x_slots))
     (far_dy_slots,) = call(
         spread_kernel,
@@ -394,6 +408,7 @@
         out_spaces=[pltpu.HBM],
     )(near, far_cotangent, gate_own, up_own)
     far_dy_rows = to_sets(far_dy_slots)
+    gate_w, up_w, down_w = map(whole_expert, behind([gate_own, up_own, down_own], far_dy_slots))
     out_rows, by_gate, by_up = call(
         functools.partial(forward_kernel, parts, joined),
         [slot_shape, unit_shape, unit_shape],

time: 203 us -> 193 us (0.951)
  waiting for transfers between devices: 128 us -> 120 us
  starting transfers between devices: 35.4 us -> 32 us
    ppermute x3, waiting for transfers between devices: 20.3 us -> 0.01 us  [swapped(): return lax.ppermute(weight[0], axes, swap)]
    all_to_all x3, waiting for transfers between devices: 8.44 us -> 19.9 us  [to_sets(): lax.all_to_all(rows, axes, 0, 0, axis_index_groups=in_half, tiled=True)]
    ppermute x2, starting transfers between devices: 4.35 us -> 1.38 us  [to_planes(): lax.ppermute(rows, 'dp', [(g, (g + i) % parts) for g in range(parts)])]
    ppermute x2, waiting for transfers between devices: 35.4 us -> 37.9 us  [to_planes(): lax.ppermute(rows, 'dp', [(g, (g + i) % parts) for g in range(parts)])]
    all_to_all x3, starting transfers between devices: 13.1 us -> 10.8 us  [to_sets(): lax.all_to_all(rows, axes, 0, 0, axis_index_groups=in_half, tiled=True)]
    ppermute x3, starting transfers between devices: 1.57 us -> 3.73 us  [swapped(): return lax.ppermute(weight[0], axes, swap)]
    pallas_call x11 -> x13, Pallas kernels: 30.3 us -> 29.1 us  [run(): pl.pallas_call(kernel, out_shape=tuple(outs), in_specs=[pl.BlockSpec(memo...]
  transfers between devices with their start and end apart: 16 -> 16, of which waited for: 8 -> 7; matrix products, arithmetic and copies ran while one was open for 0% -> 1% of each run, Pallas kernels for 13% -> 14%
where the time goes in v15:
time: 193 us; the launch traced here: 192 us
  waiting for transfers between devices  120 us (62%)
  starting transfers between devices  32 us (17%)
  Pallas kernels  29.1 us (15%)
  local copies, waits for them, and re-layouts  10 us (5%)
    ppermute x2, waiting for transfers between devices, to_planes(): lax.ppermute(rows, 'dp', [(g, (g + i) % parts) for g in range(parts)])  37.9 us
    all_to_all x2, waiting for transfers between devices, send_back(): lax.all_to_all(rows, axes, 0, 0, axis_index_groups=everywhere, tiled=True)  37.1 us
    pallas_call x13, Pallas kernels, run(): pl.pallas_call(kernel, out_shape=tuple(outs), in_specs=[pl.BlockSpec(memo...  29.1 us
    ppermute x3, waiting for transfers between devices, far_side(): return lax.ppermute(array, 'expert', across)  25 us
    all_to_all x3, waiting for transfers between devices, to_sets(): lax.all_to_all(rows, axes, 0, 0, axis_index_groups=in_half, tiled=True)  19.9 us
    all_to_all x3, starting transfers between devices, to_sets(): lax.all_to_all(rows, axes, 0, 0, axis_index_groups=in_half, tiled=True)  10.8 us
    unnamed x23, local copies, waits for them, and re-layouts  10 us
    all_to_all x2, starting transfers between devices, send_back(): lax.all_to_all(rows, axes, 0, 0, axis_index_groups=everywhere, tiled=True)  8.85 us
  transfers between devices with their start and end apart: 16, of which 7 were waited for; matrix products, arithmetic and copies ran while one was open for 1% of the time, Pallas kernels for 14%

profile of v15, /device:TPU:0, one launch (start us, length us, event | category | flops | bytes accessed | tf_op | source)
XLA Modules:
  0.0 191.8 jit_solution(10974816826773027449)
XLA Ops:
  0.6 4.1 %collective-permute-start.1 = (bf16[128,2048]{1,0:T(8,128)(2,1)}, bf16[128,2048]{1,0:T(8,128)(2,1)S(1)}, u32[]{:S(2)}, u32[]{:S(2)}) collective-permute-start(bf16[128,2048]{1,0:T(8,128)(2,1)} %tokens_ref.1), channel_id=1, source_target_pairs={{0,8},{1,9},{2,10},{3,11},{4,12},{5,13},{6,14},{7,15},{8,0},{9,1},... | collective-permute-start | bytes 1572872 | tf_op jit(solution)/shard_map/ppermute | solution.py:312
  4.7 0.8 copy.14.routes_ref
  5.5 0.1 collective-permute-start
  5.6 1.8 collective-permute-start.3
  7.4 0.0 collective-permute-start.4
  7.5 2.6 %collective-permute-start.6 = (bf16[128,2048]{1,0:T(8,128)(2,1)}, bf16[128,2048]{1,0:T(8,128)(2,1)S(1)}, u32[]{:S(2)}, u32[]{:S(2)}) collective-permute-start(bf16[128,2048]{1,0:T(8,128)(2,1)} %cotangent_ref.3), channel_id=1, source_target_pairs={{0,8},{1,9},{2,10},{3,11},{4,12},{5,13},{6,14},{7,15},{8,0},{9,1},... | collective-permute-start | bytes 1572872 | tf_op jit(solution)/shard_map/ppermute | solution.py:312
  10.1 0.0 copy-start.3
  10.1 1.1 copy-done.3
  11.1 0.0 copy-start.5
  11.1 1.0 copy-done.5
  12.2 2.1 %shard_map.94 = (bf16[384,2048]{1,0:T(8,128)(2,1)}, bf16[256,384]{1,0:T(8,128)(2,1)S(1)}) custom-call(s32[1]{0:T(128)} %bitcast.plane_ref, s32[1]{0:T(128)} %bitcast.1.half_ref, s32[128,2]{1,0:T(8,128)S(1)} %copy.14.routes_ref, bf16[128,2048]{1,0:T(8,128)(2,1)S(1)} %copy-done.5, bf16[128,2048]{1,0:T(8,128)(2,1)S(1)} %copy-done.3), custom_call_target="tpu_custom_call" | custom-call | flops 402653184 | bytes 2819080 | tf_op jit(solution)/shard_map/pallas_call | solution.py:253
  14.3 3.8 %all-to-all-start = ((bf16[4,96,2048]{2,1,0:T(8,128)(2,1)}), bf16[4,96,2048]{2,1,0:T(8,128)(2,1)S(1)}, u32[]{:S(2)}, u32[]{:S(2)}) async-start(bf16[4,96,2048]{2,1,0:T(8,128)(2,1)} %bitcast.2), calls=%async_computation | async-start | bytes 3145728 | tf_op jit(solution)/shard_map/all_to_all | solution.py:316
  18.0 25.0 %collective-permute-done.routes_ref = s32[128,2]{1,0:T(8,128)S(1)} collective-permute-done((s32[128,2]{1,0:T(8,128)S(1)}, s32[128,2]{1,0:T(8,128)S(1)}, u32[]{:S(2)}, u32[]{:S(2)}) %collective-permute-start) | collective-permute-done | bytes 1056 | tf_op jit(solution)/shard_map/ppermute | solution.py:312
  43.1 1.9 collective-permute-start.5
  44.9 0.0 collective-permute-done.1.rows_ref
  44.9 1.6 shard_map.95
  46.6 13.8 %all-to-all-done.refs_1_ = bf16[4,96,2048]{2,1,0:T(8,128)(2,1)S(1)} async-done(((bf16[4,96,2048]{2,1,0:T(8,128)(2,1)}), bf16[4,96,2048]{2,1,0:T(8,128)(2,1)S(1)}, u32[]{:S(2)}, u32[]{:S(2)}) %all-to-all-start) | async-done | bytes 1572896 | tf_op jit(solution)/shard_map/all_to_all | solution.py:316
  60.4 3.5 %all-to-all-start.1 = ((bf16[4,48,2048]{2,1,0:T(8,128)(2,1)}), bf16[4,48,2048]{2,1,0:T(8,128)(2,1)S(1)}, u32[]{:S(2)}, u32[]{:S(2)}) async-start(bf16[4,48,2048]{2,1,0:T(8,128)(2,1)} %bitcast.4), calls=%async_computation.1 | async-start | bytes 1572864 | tf_op jit(solution)/shard_map/all_to_all | solution.py:316
  63.9 0.0 collective-permute-done.6.rows_ref
  63.9 0.0 copy-start.6
  63.9 0.8 copy-done.6
  64.7 0.0 collective-permute-done.3.refs_0_
  64.7 0.0 collective-permute-done.4.refs_1_
  64.7 0.0 copy-start.7
  64.7 1.0 copy-done.7
  65.8 1.1 shard_map.99.refs_3_
  66.9 0.0 copy-start
  66.9 0.0 collective-permute-done.5.refs_2_
  66.9 0.9 copy-done
  67.8 0.0 collective-permute-start.7
  67.8 0.5 collective-permute-start.8
  68.3 0.0 collective-permute-start.9
  68.3 6.0 %all-to-all-done.1 = bf16[4,48,2048]{2,1,0:T(8,128)(2,1)S(1)} async-done(((bf16[4,48,2048]{2,1,0:T(8,128)(2,1)}), bf16[4,48,2048]{2,1,0:T(8,128)(2,1)S(1)}, u32[]{:S(2)}, u32[]{:S(2)}) %all-to-all-start.1) | async-done | bytes 786464 | tf_op jit(solution)/shard_map/all_to_all | solution.py:316
  74.3 3.5 %all-to-all-start.3 = ((bf16[4,48,2048]{2,1,0:T(8,128)(2,1)}), bf16[4,48,2048]{2,1,0:T(8,128)(2,1)S(1)}, u32[]{:S(2)}, u32[]{:S(2)}) async-start(bf16[4,48,2048]{2,1,0:T(8,128)(2,1)} %bitcast.29), calls=%async_computation.3 | async-start | bytes 1572864 | tf_op jit(solution)/shard_map/all_to_all | solution.py:316
  77.8 1.1 shard_map.98
  78.9 0.7 collective-permute-start.2
  79.6 1.1 shard_map.97
  80.7 0.0 copy-start.2
  80.7 0.9 copy-done.2
  81.6 0.0 collective-permute-done.7.refs_3_.refs_7_
  81.6 0.0 collective-permute-done.8.refs_5_.refs_9_
  81.6 0.0 collective-permute-done.9.refs_7_.refs_3_
  81.6 15.8 %collective-permute-done.2.refs_1_ = bf16[192,2048]{1,0:T(8,128)(2,1)S(1)} collective-permute-done((bf16[192,2048]{1,0:T(8,128)(2,1)S(1)}, bf16[192,2048]{1,0:T(8,128)(2,1)S(1)}, u32[]{:S(2)}, u32[]{:S(2)}) %collective-permute-start.2) | collective-permute-done | bytes 786464 | tf_op jit(solution)/shard_map/ppermute | solution.py:338
  97.4 0.0 copy-start.9
  97.4 0.9 copy-done.9
  98.3 8.3 %shard_map.101 = (bf16[384,2048]{1,0:T(8,128)(2,1)}, f32[1,384,768]{2,1,0:T(8,128)}, f32[1,384,768]{2,1,0:T(8,128)}) custom-call(s32[1]{0:T(128)} %bitcast.plane_ref, bf16[192,2048]{1,0:T(8,128)(2,1)} %bitcast.31, bf16[192,2048]{1,0:T(8,128)(2,1)} %copy-done.9, bf16[2048,384]{1,0:T(8,128)(2,1)} %get-tuple-element.19.refs_2_.refs_6_, ...), custom_call_target="tpu_custom_call" | custom-call | flops 3623878656 | bytes 14942212 | tf_op jit(solution)/shard_map/pallas_call | solution.py:253
  106.6 0.0 all-to-all-done.3
  106.6 1.0 shard_map.104
  107.6 0.7 collective-permute-start.10
  108.3 1.1 shard_map.103
  109.4 0.0 copy-start.1
  109.4 0.9 copy-done.1
  110.3 4.8 %all-to-all-start.2 = ((bf16[16,24,2048]{2,1,0:T(8,128)(2,1)}), bf16[16,24,2048]{2,1,0:T(8,128)(2,1)S(1)}, u32[]{:S(2)}, u32[]{:S(2)}) async-start(bf16[16,24,2048]{2,1,0:T(8,128)(2,1)} %bitcast.11), calls=%async_computation.2 | async-start | bytes 3145728 | tf_op jit(solution)/shard_map/all_to_all | solution.py:344
  115.1 22.0 %collective-permute-done.10.refs_1_ = bf16[192,2048]{1,0:T(8,128)(2,1)} collective-permute-done((bf16[192,2048]{1,0:T(8,128)(2,1)}, bf16[192,2048]{1,0:T(8,128)(2,1)}, u32[]{:S(2)}, u32[]{:S(2)}) %collective-permute-start.10) | collective-permute-done | bytes 786464 | tf_op jit(solution)/shard_map/ppermute | solution.py:338
  137.1 8.6 %shard_map.105 = bf16[384,2048]{1,0:T(8,128)(2,1)} custom-call(s32[1]{0:T(128)} %bitcast.plane_ref, bf16[192,2048]{1,0:T(8,128)(2,1)} %bitcast.30, bf16[192,2048]{1,0:T(8,128)(2,1)} %collective-permute-done.10.refs_1_, bf16[384,2048]{1,0:T(8,128)(2,1)} %get-tuple-element.21.refs_6_.refs_2_, bf16[384,2048]{1,0:T(8,128)(2,1)} %collective-permute-done.9.refs_7_.refs_3_, ...), custom_call_target="tpu_custom_call" | custom-call | flops 77309411328 | bytes 14942212 | tf_op jit(solution)/shard_map/pallas_call | solution.py:253
  145.7 4.9 %all-to-all-done.2 = bf16[16,24,2048]{2,1,0:T(8,128)(2,1)S(1)} async-done(((bf16[16,24,2048]{2,1,0:T(8,128)(2,1)}), bf16[16,24,2048]{2,1,0:T(8,128)(2,1)S(1)}, u32[]{:S(2)}, u32[]{:S(2)}) %all-to-all-start.2) | async-done | bytes 1572896 | tf_op jit(solution)/shard_map/all_to_all | solution.py:344
  150.6 4.1 %all-to-all-start.4 = ((bf16[16,24,2048]{2,1,0:T(8,128)(2,1)}), bf16[16,24,2048]{2,1,0:T(8,128)(2,1)S(1)}, u32[]{:S(2)}, u32[]{:S(2)}) async-start(bf16[16,24,2048]{2,1,0:T(8,128)(2,1)} %bitcast.33), calls=%async_computation.4 | async-start | bytes 3145728 | tf_op jit(solution)/shard_map/all_to_all | solution.py:344
  154.7 0.0 copy-done.8
  154.7 0.1 copy.16.gates_ref
  154.8 1.0 copy-done.4
  155.8 1.7 shard_map.102
  157.5 0.6 copy.18
  158.1 32.2 %all-to-all-done.4 = bf16[16,24,2048]{2,1,0:T(8,128)(2,1)S(1)} async-done(((bf16[16,24,2048]{2,1,0:T(8,128)(2,1)}), bf16[16,24,2048]{2,1,0:T(8,128)(2,1)S(1)}, u32[]{:S(2)}, u32[]{:S(2)}) %all-to-all-start.4) | async-done | bytes 1572896 | tf_op jit(solution)/shard_map/all_to_all | solution.py:344
  190.3 1.5 shard_map.106
  (4 shorter events, 0.0 us)
Async XLA Ops:
  0.6 44.3 %collective-permute-start.1 = (bf16[128,2048]{1,0:T(8,128)(2,1)}, bf16[128,2048]{1,0:T(8,128)(2,1)S(1)}, u32[]{:S(2)}, u32[]{:S(2)}) collective-permute-start(bf16[128,2048]{1,0:T(8,128)(2,1)} %tokens_ref.1), channel_id=1, source_target_pairs={{0,8},{1,9},{2,10},{3,11},{4,12},{5,13},{6,14},{7,15},{8,0},{9,1},... | collective-permute-start | bytes 1572872 | tf_op jit(solution)/shard_map/ppermute | solution.py:312
  5.5 37.6 %collective-permute-start = (s32[128,2]{1,0:T(8,128)S(1)}, s32[128,2]{1,0:T(8,128)S(1)}, u32[]{:S(2)}, u32[]{:S(2)}) collective-permute-start(s32[128,2]{1,0:T(8,128)S(1)} %copy.14.routes_ref), channel_id=1, source_target_pairs={{0,8},{1,9},{2,10},{3,11},{4,12},{5,13},{6,14},{7,15},{8,0},{9,1},... | collective-permute-start | bytes 3080 | tf_op jit(solution)/shard_map/ppermute | solution.py:312
  5.6 59.1 %collective-permute-start.3 = (bf16[2048,384]{1,0:T(8,128)(2,1)}, bf16[2048,384]{1,0:T(8,128)(2,1)}, u32[]{:S(2)}, u32[]{:S(2)}) collective-permute-start(bf16[2048,384]{1,0:T(8,128)(2,1)} %bitcast.34), channel_id=1, source_target_pairs={{0,16},{1,0},{2,18},{3,2},{4,20},{5,4},{6,22},{7,6},{8,24},{9,8},{... | collective-permute-start | bytes 4718600 | tf_op jit(solution)/shard_map/ppermute | solution.py:302
  7.4 57.3 %collective-permute-start.4 = (bf16[2048,384]{1,0:T(8,128)(2,1)}, bf16[2048,384]{1,0:T(8,128)(2,1)}, u32[]{:S(2)}, u32[]{:S(2)}) collective-permute-start(bf16[2048,384]{1,0:T(8,128)(2,1)} %bitcast.35), channel_id=1, source_target_pairs={{0,16},{1,0},{2,18},{3,2},{4,20},{5,4},{6,22},{7,6},{8,24},{9,8},{... | collective-permute-start | bytes 4718600 | tf_op jit(solution)/shard_map/ppermute | solution.py:302
  7.5 56.5 %collective-permute-start.6 = (bf16[128,2048]{1,0:T(8,128)(2,1)}, bf16[128,2048]{1,0:T(8,128)(2,1)S(1)}, u32[]{:S(2)}, u32[]{:S(2)}) collective-permute-start(bf16[128,2048]{1,0:T(8,128)(2,1)} %cotangent_ref.3), channel_id=1, source_target_pairs={{0,8},{1,9},{2,10},{3,11},{4,12},{5,13},{6,14},{7,15},{8,0},{9,1},... | collective-permute-start | bytes 1572872 | tf_op jit(solution)/shard_map/ppermute | solution.py:312
  10.1 1.1 copy-start.3
  11.1 1.0 copy-start.5
  14.3 46.2 %all-to-all-start = ((bf16[4,96,2048]{2,1,0:T(8,128)(2,1)}), bf16[4,96,2048]{2,1,0:T(8,128)(2,1)S(1)}, u32[]{:S(2)}, u32[]{:S(2)}) async-start(bf16[4,96,2048]{2,1,0:T(8,128)(2,1)} %bitcast.2), calls=%async_computation | async-start | bytes 3145728 | tf_op jit(solution)/shard_map/all_to_all | solution.py:316
  43.1 23.8 %collective-permute-start.5 = (bf16[384,2048]{1,0:T(8,128)(2,1)}, bf16[384,2048]{1,0:T(8,128)(2,1)}, u32[]{:S(2)}, u32[]{:S(2)}) collective-permute-start(bf16[384,2048]{1,0:T(8,128)(2,1)} %bitcast.36), channel_id=1, source_target_pairs={{0,16},{1,0},{2,18},{3,2},{4,20},{5,4},{6,22},{7,6},{8,24},{9,8},{... | collective-permute-start | bytes 4718600 | tf_op jit(solution)/shard_map/ppermute | solution.py:302
  60.4 13.9 %all-to-all-start.1 = ((bf16[4,48,2048]{2,1,0:T(8,128)(2,1)}), bf16[4,48,2048]{2,1,0:T(8,128)(2,1)S(1)}, u32[]{:S(2)}, u32[]{:S(2)}) async-start(bf16[4,48,2048]{2,1,0:T(8,128)(2,1)} %bitcast.4), calls=%async_computation.1 | async-start | bytes 1572864 | tf_op jit(solution)/shard_map/all_to_all | solution.py:316
  63.9 0.8 copy-start.6
  64.7 1.0 copy-start.7
  66.9 0.9 copy-start
  67.8 13.8 %collective-permute-start.7 = (bf16[2048,384]{1,0:T(8,128)(2,1)}, bf16[2048,384]{1,0:T(8,128)(2,1)}, u32[]{:S(2)}, u32[]{:S(2)}) collective-permute-start(bf16[2048,384]{1,0:T(8,128)(2,1)} %get-tuple-element.19.refs_2_.refs_6_), channel_id=1, source_target_pairs={{0,1},{1,0},{2,3},{3,2},{4,5},{5,4},{6,7},{7,6},{8,9},{9,8},{10,11... | collective-permute-start | bytes 4718600 | tf_op jit(solution)/shard_map/ppermute | solution.py:308
  67.8 13.8 %collective-permute-start.8 = (bf16[2048,384]{1,0:T(8,128)(2,1)}, bf16[2048,384]{1,0:T(8,128)(2,1)}, u32[]{:S(2)}, u32[]{:S(2)}) collective-permute-start(bf16[2048,384]{1,0:T(8,128)(2,1)} %get-tuple-element.20.refs_4_.refs_8_), channel_id=1, source_target_pairs={{0,1},{1,0},{2,3},{3,2},{4,5},{5,4},{6,7},{7,6},{8,9},{9,8},{10,11... | collective-permute-start | bytes 4718600 | tf_op jit(solution)/shard_map/ppermute | solution.py:308
  68.3 13.3 %collective-permute-start.9 = (bf16[384,2048]{1,0:T(8,128)(2,1)}, bf16[384,2048]{1,0:T(8,128)(2,1)}, u32[]{:S(2)}, u32[]{:S(2)}) collective-permute-start(bf16[384,2048]{1,0:T(8,128)(2,1)} %get-tuple-element.21.refs_6_.refs_2_), channel_id=1, source_target_pairs={{0,1},{1,0},{2,3},{3,2},{4,5},{5,4},{6,7},{7,6},{8,9},{9,8},{10,11... | collective-permute-start | bytes 4718600 | tf_op jit(solution)/shard_map/ppermute | solution.py:308
  74.3 32.3 %all-to-all-start.3 = ((bf16[4,48,2048]{2,1,0:T(8,128)(2,1)}), bf16[4,48,2048]{2,1,0:T(8,128)(2,1)S(1)}, u32[]{:S(2)}, u32[]{:S(2)}) async-start(bf16[4,48,2048]{2,1,0:T(8,128)(2,1)} %bitcast.29), calls=%async_computation.3 | async-start | bytes 1572864 | tf_op jit(solution)/shard_map/all_to_all | solution.py:316
  78.9 18.5 %collective-permute-start.2 = (bf16[192,2048]{1,0:T(8,128)(2,1)S(1)}, bf16[192,2048]{1,0:T(8,128)(2,1)S(1)}, u32[]{:S(2)}, u32[]{:S(2)}) collective-permute-start(bf16[192,2048]{1,0:T(8,128)(2,1)S(1)} %bitcast.32), channel_id=1, source_target_pairs={{0,16},{16,0},{1,17},{17,1},{2,18},{18,2},{3,19},{19,3},{4,20},{20... | collective-permute-start | bytes 2359304 | tf_op jit(solution)/shard_map/ppermute | solution.py:338
  80.7 0.9 copy-start.2
  97.4 0.9 copy-start.9
  107.6 29.5 %collective-permute-start.10 = (bf16[192,2048]{1,0:T(8,128)(2,1)}, bf16[192,2048]{1,0:T(8,128)(2,1)}, u32[]{:S(2)}, u32[]{:S(2)}) collective-permute-start(bf16[192,2048]{1,0:T(8,128)(2,1)} %bitcast.16), channel_id=1, source_target_pairs={{0,16},{16,0},{1,17},{17,1},{2,18},{18,2},{3,19},{19,3},{4,20},{20... | collective-permute-start | bytes 2359304 | tf_op jit(solution)/shard_map/ppermute | solution.py:338
  109.4 0.9 copy-start.1
  110.3 40.3 %all-to-all-start.2 = ((bf16[16,24,2048]{2,1,0:T(8,128)(2,1)}), bf16[16,24,2048]{2,1,0:T(8,128)(2,1)S(1)}, u32[]{:S(2)}, u32[]{:S(2)}) async-start(bf16[16,24,2048]{2,1,0:T(8,128)(2,1)} %bitcast.11), calls=%async_computation.2 | async-start | bytes 3145728 | tf_op jit(solution)/shard_map/all_to_all | solution.py:344
  150.6 4.1 %copy-start.8 = (f32[128,2]{0,1:T(2,128)S(1)}, f32[128,2]{0,1:T(2,128)}, u32[]{:S(2)}) copy-start(f32[128,2]{0,1:T(2,128)} %param.10) | copy-start | bytes 3076
  150.6 39.7 %all-to-all-start.4 = ((bf16[16,24,2048]{2,1,0:T(8,128)(2,1)}), bf16[16,24,2048]{2,1,0:T(8,128)(2,1)S(1)}, u32[]{:S(2)}, u32[]{:S(2)}) async-start(bf16[16,24,2048]{2,1,0:T(8,128)(2,1)} %bitcast.33), calls=%async_computation.4 | async-start | bytes 3145728 | tf_op jit(solution)/shard_map/all_to_all | solution.py:344
  154.8 1.0 copy-start.4

commit v16 on v12

--- a/solution.py
+++ b/solution.py
@@ -46,9 +46,13 @@
     place_ref, sems, out_sems, rows_ref, stage_ref = refs
     slots, width = slots_ref.shape
     capacity = slots // experts
-    tok_rows, top_count = routes_ref.shape
+    top_count, tok_rows = routes_ref.shape
     (copy,) = fetch([tokens_ref], [rows_ref], sems)
-    routes = routes_ref[...]
+    same = lax.broadcasted_iota(jnp.int32, (tok_rows, tok_rows), 0) == lax.broadcasted_iota(
+        jnp.int32, (tok_rows, tok_rows), 1
+    )
+    routes = dot(same.astype(F32).astype(BF16), routes_ref[...].astype(F32).astype(BF16), (1, 1))
+    routes = routes.astype(jnp.int32)
     home_plane, home_set = lax.rem(routes + 1, parts), lax.div(routes, parts)
     lanes = home_plane * (experts // parts) + home_set
     near_lanes = home_set * parts + lax.rem(home_plane + (parts - plane_ref[0]), parts)
@@ -325,7 +329,8 @@
         [sems(1), sems(pieces), pltpu.VMEM((tok_rows, width), BF16), row_scratch],
         pinned=(2,),
         out_spaces=[pltpu.HBM, pltpu.VMEM, pltpu.VMEM],
-    )(plane, routes, tokens)
+        vmem=LARGE_VMEM,
+    )(plane, routes.T, tokens)
     x_shares = dispatch(x_slots)
     (dy_slots,) = call(
         spread_kernel,

time: 177 us -> 177 us (level)
  Pallas kernels: 27.7 us -> 29.6 us
    pallas_call x10, Pallas kernels: 27.7 us -> 29.6 us  [run(): pl.pallas_call(kernel, out_shape=tuple(outs), in_specs=[pl.BlockSpec(memo...]
    unnamed x25 -> x26, local copies, waits for them, and re-layouts: 7.45 us -> 5.69 us
  transfers between devices with their start and end apart: 12 -> 12, of which waited for: 9 -> 9; matrix products, arithmetic and copies ran while one was open for 1% -> 0% of each run, Pallas kernels for 14% -> 15%
where the time goes in v16:
time: 177 us; the launch traced here: 176 us
  waiting for transfers between devices  115 us (65%)
  Pallas kernels  29.6 us (17%)
  starting transfers between devices  25 us (14%)
  local copies, waits for them, and re-layouts  5.69 us (3%)
    ppermute x2, waiting for transfers between devices, dispatch(): lax.ppermute(rows, 'dp', [(g, (g + i) % parts) for g in range(parts)])  38.8 us
    all_to_all x2, waiting for transfers between devices, send_back(): lax.all_to_all(rows, axes, 0, 0, axis_index_groups=everywhere, tiled=True)  36.9 us
    pallas_call x10, Pallas kernels, run(): pl.pallas_call(kernel, out_shape=tuple(outs), in_specs=[pl.BlockSpec(memo...  29.6 us
    all_to_all x2, waiting for transfers between devices, dispatch(): lax.all_to_all(rows, axes, 0, 0, axis_index_groups=in_plane, tiled=True)  29.3 us
    ppermute x3, waiting for transfers between devices, swapped(): return lax.ppermute(weight[0], axes, swap)  9.85 us
    all_to_all x2, starting transfers between devices, dispatch(): lax.all_to_all(rows, axes, 0, 0, axis_index_groups=in_plane, tiled=True)  9.53 us
    all_to_all x2, starting transfers between devices, send_back(): lax.all_to_all(rows, axes, 0, 0, axis_index_groups=everywhere, tiled=True)  8.16 us
    unnamed x26, local copies, waits for them, and re-layouts  5.69 us
  transfers between devices with their start and end apart: 12, of which 9 were waited for; matrix products, arithmetic and copies ran while one was open for 0% of the time, Pallas kernels for 15%

profile of v16, /device:TPU:0, one launch (start us, length us, event | category | flops | bytes accessed | tf_op | source)
XLA Modules:
  0.0 176.4 jit_solution(13678020591622445921)
XLA Ops:
  0.6 3.0 %collective-permute-start.1 = (bf16[2048,384]{1,0:T(8,128)(2,1)}, bf16[2048,384]{1,0:T(8,128)(2,1)}, u32[]{:S(2)}, u32[]{:S(2)}) collective-permute-start(bf16[2048,384]{1,0:T(8,128)(2,1)} %bitcast.29), channel_id=1, source_target_pairs={{0,16},{1,0},{2,18},{3,2},{4,20},{5,4},{6,22},{7,6},{8,24},{9,8},{... | collective-permute-start | bytes 4718600 | tf_op jit(solution)/shard_map/ppermute | solution.py:263
  3.6 4.0 %shard_map.94 = (bf16[384,2048]{1,0:T(8,128)(2,1)}, bf16[128,384]{1,0:T(8,128)(2,1)}, bf16[256,384]{1,0:T(8,128)(2,1)}) custom-call(s32[1]{0:T(128)} %bitcast.plane_ref, s32[2,128]{1,0:T(2,128)} %bitcast.32, bf16[128,2048]{1,0:T(8,128)(2,1)} %tokens_ref.1), custom_call_target="tpu_custom_call" | custom-call | flops 201326592 | bytes 2393092 | tf_op jit(solution)/shard_map/pallas_call | solution.py:222
  7.6 0.0 copy-start.4
  7.6 0.0 copy-start.6
  7.6 5.9 %all-to-all-start = ((bf16[8,48,2048]{2,1,0:T(8,128)(2,1)}), bf16[8,48,2048]{2,1,0:T(8,128)(2,1)S(1)}, u32[]{:S(2)}, u32[]{:S(2)}) async-start(bf16[8,48,2048]{2,1,0:T(8,128)(2,1)} %bitcast.28), calls=%async_computation | async-start | bytes 3145728 | tf_op jit(solution)/shard_map/all_to_all | solution.py:274
  13.6 0.0 collective-permute-start.3
  13.6 0.0 collective-permute-start.5
  13.6 8.2 %collective-permute-done.1.refs_2_._.refs_6_ = bf16[2048,384]{1,0:T(8,128)(2,1)} collective-permute-done((bf16[2048,384]{1,0:T(8,128)(2,1)}, bf16[2048,384]{1,0:T(8,128)(2,1)}, u32[]{:S(2)}, u32[]{:S(2)}) %collective-permute-start.1) | collective-permute-done | bytes 1572896 | tf_op jit(solution)/shard_map/ppermute | solution.py:263
  21.9 0.0 copy-done.4
  21.9 0.0 copy-done.6
  21.9 1.4 shard_map.99
  23.2 0.0 copy-start
  23.2 1.2 copy-done
  24.4 25.4 %all-to-all-done = bf16[8,48,2048]{2,1,0:T(8,128)(2,1)S(1)} async-done(((bf16[8,48,2048]{2,1,0:T(8,128)(2,1)}), bf16[8,48,2048]{2,1,0:T(8,128)(2,1)S(1)}, u32[]{:S(2)}, u32[]{:S(2)}) %all-to-all-start) | async-done | bytes 1572896 | tf_op jit(solution)/shard_map/all_to_all | solution.py:274
  49.8 3.6 %all-to-all-start.2 = ((bf16[8,48,2048]{2,1,0:T(8,128)(2,1)}), bf16[8,48,2048]{2,1,0:T(8,128)(2,1)S(1)}, u32[]{:S(2)}, u32[]{:S(2)}) async-start(bf16[8,48,2048]{2,1,0:T(8,128)(2,1)} %bitcast.23), calls=%async_computation.2 | async-start | bytes 3145728 | tf_op jit(solution)/shard_map/all_to_all | solution.py:274
  53.4 0.1 collective-permute-start.2
  53.5 0.0 collective-permute-done.3.refs_4_.refs_8_
  53.5 0.5 collective-permute-start.4
  54.0 1.6 collective-permute-done.5.refs_6_.refs_2_
  55.6 0.0 collective-permute-start.6
  55.6 1.1 shard_map.96
  56.7 2.6 %collective-permute-start = (bf16[192,2048]{1,0:T(8,128)(2,1)S(1)}, bf16[192,2048]{1,0:T(8,128)(2,1)S(1)}, u32[]{:S(2)}, u32[]{:S(2)}) collective-permute-start(bf16[192,2048]{1,0:T(8,128)(2,1)S(1)} %bitcast.25), channel_id=1, source_target_pairs={{0,16},{16,0},{1,17},{17,1},{2,18},{18,2},{3,19},{19,3},{4,20},{20... | collective-permute-start | bytes 2359304 | tf_op jit(solution)/shard_map/ppermute | solution.py:294
  59.2 1.1 shard_map.95
  60.3 0.0 copy-start.2
  60.3 0.9 copy-done.2
  61.2 0.0 collective-permute-done.2.refs_3_.refs_7_
  61.2 0.0 copy-start.8
  61.2 0.0 collective-permute-done.4.refs_5_.refs_9_
  61.2 0.0 copy-start.9
  61.2 0.4 collective-permute-done.6.refs_7_.refs_3_
  61.6 0.0 copy-start.10
  61.6 15.8 %collective-permute-done.refs_1_ = bf16[192,2048]{1,0:T(8,128)(2,1)S(1)} collective-permute-done((bf16[192,2048]{1,0:T(8,128)(2,1)S(1)}, bf16[192,2048]{1,0:T(8,128)(2,1)S(1)}, u32[]{:S(2)}, u32[]{:S(2)}) %collective-permute-start) | collective-permute-done | bytes 786464 | tf_op jit(solution)/shard_map/ppermute | solution.py:294
  77.4 0.0 copy-done.8
  77.4 0.0 copy-done.9
  77.4 0.0 copy-done.10
  77.4 0.0 copy-start.11
  77.4 0.9 copy-done.11
  78.3 8.3 %shard_map.97 = (bf16[384,2048]{1,0:T(8,128)(2,1)}, f32[1,384,768]{2,1,0:T(8,128)}, f32[1,384,768]{2,1,0:T(8,128)}) custom-call(s32[1]{0:T(128)} %bitcast.plane_ref, bf16[192,2048]{1,0:T(8,128)(2,1)} %bitcast.24, bf16[192,2048]{1,0:T(8,128)(2,1)} %copy-done.11, bf16[2048,384]{1,0:T(8,128)(2,1)} %collective-permute-done.1.refs_2_._.refs_6_, ...), custom_call_target="tpu_custom_call" | custom-call | flops 3623878656 | bytes 14942212 | tf_op jit(solution)/shard_map/pallas_call | solution.py:222
  86.6 3.9 %all-to-all-done.2 = bf16[8,48,2048]{2,1,0:T(8,128)(2,1)S(1)} async-done(((bf16[8,48,2048]{2,1,0:T(8,128)(2,1)}), bf16[8,48,2048]{2,1,0:T(8,128)(2,1)S(1)}, u32[]{:S(2)}, u32[]{:S(2)}) %all-to-all-start.2) | async-done | bytes 1572896 | tf_op jit(solution)/shard_map/all_to_all | solution.py:274
  90.5 1.0 shard_map.101
  91.5 1.2 collective-permute-start.7
  92.6 4.1 %all-to-all-start.1 = ((bf16[16,24,2048]{2,1,0:T(8,128)(2,1)}), bf16[16,24,2048]{2,1,0:T(8,128)(2,1)S(1)}, u32[]{:S(2)}, u32[]{:S(2)}) async-start(bf16[16,24,2048]{2,1,0:T(8,128)(2,1)} %bitcast.9), calls=%async_computation.1 | async-start | bytes 3145728 | tf_op jit(solution)/shard_map/all_to_all | solution.py:300
  96.7 1.1 shard_map.100
  97.8 0.0 copy-start.3
  97.9 0.9 copy-done.3
  98.8 23.0 %collective-permute-done.7.refs_1_ = bf16[192,2048]{1,0:T(8,128)(2,1)} collective-permute-done((bf16[192,2048]{1,0:T(8,128)(2,1)}, bf16[192,2048]{1,0:T(8,128)(2,1)}, u32[]{:S(2)}, u32[]{:S(2)}) %collective-permute-start.7) | collective-permute-done | bytes 786464 | tf_op jit(solution)/shard_map/ppermute | solution.py:294
  121.8 8.6 %shard_map.102 = bf16[384,2048]{1,0:T(8,128)(2,1)} custom-call(s32[1]{0:T(128)} %bitcast.plane_ref, bf16[192,2048]{1,0:T(8,128)(2,1)} %bitcast.26, bf16[192,2048]{1,0:T(8,128)(2,1)} %collective-permute-done.7.refs_1_, bf16[384,2048]{1,0:T(8,128)(2,1)} %collective-permute-done.5.refs_6_.refs_2_, bf16[384,2048]{1,0:T(8,128)(2,1)} %copy-done.10, ...), custom_call_target="tpu_custom_call" | custom-call | flops 77309411328 | bytes 14942212 | tf_op jit(solution)/shard_map/pallas_call | solution.py:222
  130.4 3.5 %all-to-all-done.1 = bf16[16,24,2048]{2,1,0:T(8,128)(2,1)S(1)} async-done(((bf16[16,24,2048]{2,1,0:T(8,128)(2,1)}), bf16[16,24,2048]{2,1,0:T(8,128)(2,1)S(1)}, u32[]{:S(2)}, u32[]{:S(2)}) %all-to-all-start.1) | async-done | bytes 1572896 | tf_op jit(solution)/shard_map/all_to_all | solution.py:300
  133.9 0.0 copy-start.7
  133.9 0.0 copy-start.1
  133.9 4.1 %all-to-all-start.3 = ((bf16[16,24,2048]{2,1,0:T(8,128)(2,1)}), bf16[16,24,2048]{2,1,0:T(8,128)(2,1)S(1)}, u32[]{:S(2)}, u32[]{:S(2)}) async-start(bf16[16,24,2048]{2,1,0:T(8,128)(2,1)} %bitcast.27), calls=%async_computation.3 | async-start | bytes 3145728 | tf_op jit(solution)/shard_map/all_to_all | solution.py:300
  138.0 0.0 copy-done.7
  138.0 0.1 copy.10.gates_ref
  138.1 0.0 copy-done.1
  138.1 0.0 copy-start.5
  138.1 1.0 copy-done.5
  139.2 1.7 shard_map.98
  140.8 0.6 copy.12
  141.5 33.4 %all-to-all-done.3 = bf16[16,24,2048]{2,1,0:T(8,128)(2,1)S(1)} async-done(((bf16[16,24,2048]{2,1,0:T(8,128)(2,1)}), bf16[16,24,2048]{2,1,0:T(8,128)(2,1)S(1)}, u32[]{:S(2)}, u32[]{:S(2)}) %all-to-all-start.3) | async-done | bytes 1572896 | tf_op jit(solution)/shard_map/all_to_all | solution.py:300
  174.9 1.5 shard_map.103
Async XLA Ops:
  0.6 21.2 %collective-permute-start.1 = (bf16[2048,384]{1,0:T(8,128)(2,1)}, bf16[2048,384]{1,0:T(8,128)(2,1)}, u32[]{:S(2)}, u32[]{:S(2)}) collective-permute-start(bf16[2048,384]{1,0:T(8,128)(2,1)} %bitcast.29), channel_id=1, source_target_pairs={{0,16},{1,0},{2,18},{3,2},{4,20},{5,4},{6,22},{7,6},{8,24},{9,8},{... | collective-permute-start | bytes 4718600 | tf_op jit(solution)/shard_map/ppermute | solution.py:263
  7.6 14.3 %copy-start.4 = (bf16[128,2048]{1,0:T(8,128)(2,1)S(1)}, bf16[128,2048]{1,0:T(8,128)(2,1)}, u32[]{:S(2)}) copy-start(bf16[128,2048]{1,0:T(8,128)(2,1)} %rows_ref.1) | copy-start | bytes 1572868
  7.6 14.3 %copy-start.6 = (bf16[128,384]{1,0:T(8,128)(2,1)S(1)}, bf16[128,384]{1,0:T(8,128)(2,1)}, u32[]{:S(2)}) copy-start(bf16[128,384]{1,0:T(8,128)(2,1)} %get-tuple-element.15.near_ref) | copy-start | bytes 294916
  7.6 42.2 %all-to-all-start = ((bf16[8,48,2048]{2,1,0:T(8,128)(2,1)}), bf16[8,48,2048]{2,1,0:T(8,128)(2,1)S(1)}, u32[]{:S(2)}, u32[]{:S(2)}) async-start(bf16[8,48,2048]{2,1,0:T(8,128)(2,1)} %bitcast.28), calls=%async_computation | async-start | bytes 3145728 | tf_op jit(solution)/shard_map/all_to_all | solution.py:274
  13.6 39.9 %collective-permute-start.3 = (bf16[2048,384]{1,0:T(8,128)(2,1)}, bf16[2048,384]{1,0:T(8,128)(2,1)}, u32[]{:S(2)}, u32[]{:S(2)}) collective-permute-start(bf16[2048,384]{1,0:T(8,128)(2,1)} %bitcast.30), channel_id=1, source_target_pairs={{0,16},{1,0},{2,18},{3,2},{4,20},{5,4},{6,22},{7,6},{8,24},{9,8},{... | collective-permute-start | bytes 4718600 | tf_op jit(solution)/shard_map/ppermute | solution.py:263
  13.6 42.0 %collective-permute-start.5 = (bf16[384,2048]{1,0:T(8,128)(2,1)}, bf16[384,2048]{1,0:T(8,128)(2,1)}, u32[]{:S(2)}, u32[]{:S(2)}) collective-permute-start(bf16[384,2048]{1,0:T(8,128)(2,1)} %bitcast.31), channel_id=1, source_target_pairs={{0,16},{1,0},{2,18},{3,2},{4,20},{5,4},{6,22},{7,6},{8,24},{9,8},{... | collective-permute-start | bytes 4718600 | tf_op jit(solution)/shard_map/ppermute | solution.py:263
  23.2 1.2 copy-start
  49.8 40.7 %all-to-all-start.2 = ((bf16[8,48,2048]{2,1,0:T(8,128)(2,1)}), bf16[8,48,2048]{2,1,0:T(8,128)(2,1)S(1)}, u32[]{:S(2)}, u32[]{:S(2)}) async-start(bf16[8,48,2048]{2,1,0:T(8,128)(2,1)} %bitcast.23), calls=%async_computation.2 | async-start | bytes 3145728 | tf_op jit(solution)/shard_map/all_to_all | solution.py:274
  53.4 7.8 %collective-permute-start.2 = (bf16[2048,384]{1,0:T(8,128)(2,1)}, bf16[2048,384]{1,0:T(8,128)(2,1)S(1)}, u32[]{:S(2)}, u32[]{:S(2)}) collective-permute-start(bf16[2048,384]{1,0:T(8,128)(2,1)} %collective-permute-done.1.refs_2_._.refs_6_), channel_id=1, source_target_pairs={{0,1},{1,0},{2,3},{3,2},{4,5},{5,4},{6,7},{7,6},{8,9},{9,8},{10,11... | collective-permute-start | bytes 4718600 | tf_op jit(solution)/shard_map/ppermute | solution.py:269
  53.5 7.7 %collective-permute-start.4 = (bf16[2048,384]{1,0:T(8,128)(2,1)}, bf16[2048,384]{1,0:T(8,128)(2,1)S(1)}, u32[]{:S(2)}, u32[]{:S(2)}) collective-permute-start(bf16[2048,384]{1,0:T(8,128)(2,1)} %collective-permute-done.3.refs_4_.refs_8_), channel_id=1, source_target_pairs={{0,1},{1,0},{2,3},{3,2},{4,5},{5,4},{6,7},{7,6},{8,9},{9,8},{10,11... | collective-permute-start | bytes 4718600 | tf_op jit(solution)/shard_map/ppermute | solution.py:269
  55.6 6.0 %collective-permute-start.6 = (bf16[384,2048]{1,0:T(8,128)(2,1)}, bf16[384,2048]{1,0:T(8,128)(2,1)S(1)}, u32[]{:S(2)}, u32[]{:S(2)}) collective-permute-start(bf16[384,2048]{1,0:T(8,128)(2,1)} %collective-permute-done.5.refs_6_.refs_2_), channel_id=1, source_target_pairs={{0,1},{1,0},{2,3},{3,2},{4,5},{5,4},{6,7},{7,6},{8,9},{9,8},{10,11... | collective-permute-start | bytes 4718600 | tf_op jit(solution)/shard_map/ppermute | solution.py:269
  56.7 20.7 %collective-permute-start = (bf16[192,2048]{1,0:T(8,128)(2,1)S(1)}, bf16[192,2048]{1,0:T(8,128)(2,1)S(1)}, u32[]{:S(2)}, u32[]{:S(2)}) collective-permute-start(bf16[192,2048]{1,0:T(8,128)(2,1)S(1)} %bitcast.25), channel_id=1, source_target_pairs={{0,16},{16,0},{1,17},{17,1},{2,18},{18,2},{3,19},{19,3},{4,20},{20... | collective-permute-start | bytes 2359304 | tf_op jit(solution)/shard_map/ppermute | solution.py:294
  60.3 0.9 copy-start.2
  61.2 16.2 %copy-start.8 = (bf16[2048,384]{1,0:T(8,128)(2,1)}, bf16[2048,384]{1,0:T(8,128)(2,1)S(1)}, u32[]{:S(2)}) copy-start(bf16[2048,384]{1,0:T(8,128)(2,1)S(1)} %collective-permute-done.2.refs_3_.refs_7_) | copy-start | bytes 4718596
  61.2 16.2 %copy-start.9 = (bf16[2048,384]{1,0:T(8,128)(2,1)}, bf16[2048,384]{1,0:T(8,128)(2,1)S(1)}, u32[]{:S(2)}) copy-start(bf16[2048,384]{1,0:T(8,128)(2,1)S(1)} %collective-permute-done.4.refs_5_.refs_9_) | copy-start | bytes 4718596
  61.6 15.8 %copy-start.10 = (bf16[384,2048]{1,0:T(8,128)(2,1)}, bf16[384,2048]{1,0:T(8,128)(2,1)S(1)}, u32[]{:S(2)}) copy-start(bf16[384,2048]{1,0:T(8,128)(2,1)S(1)} %collective-permute-done.6.refs_7_.refs_3_) | copy-start | bytes 4718596
  77.4 0.9 copy-start.11
  91.5 30.3 %collective-permute-start.7 = (bf16[192,2048]{1,0:T(8,128)(2,1)}, bf16[192,2048]{1,0:T(8,128)(2,1)}, u32[]{:S(2)}, u32[]{:S(2)}) collective-permute-start(bf16[192,2048]{1,0:T(8,128)(2,1)} %bitcast.14), channel_id=1, source_target_pairs={{0,16},{16,0},{1,17},{17,1},{2,18},{18,2},{3,19},{19,3},{4,20},{20... | collective-permute-start | bytes 2359304 | tf_op jit(solution)/shard_map/ppermute | solution.py:294
  92.6 41.3 %all-to-all-start.1 = ((bf16[16,24,2048]{2,1,0:T(8,128)(2,1)}), bf16[16,24,2048]{2,1,0:T(8,128)(2,1)S(1)}, u32[]{:S(2)}, u32[]{:S(2)}) async-start(bf16[16,24,2048]{2,1,0:T(8,128)(2,1)} %bitcast.9), calls=%async_computation.1 | async-start | bytes 3145728 | tf_op jit(solution)/shard_map/all_to_all | solution.py:300
  97.8 0.9 copy-start.3
  133.9 4.1 %copy-start.7 = (f32[128,2]{0,1:T(2,128)S(1)}, f32[128,2]{0,1:T(2,128)}, u32[]{:S(2)}) copy-start(f32[128,2]{0,1:T(2,128)} %param.10) | copy-start | bytes 3076
  133.9 4.2 %copy-start.1 = (bf16[256,384]{1,0:T(8,128)(2,1)S(1)}, bf16[256,384]{1,0:T(8,128)(2,1)}, u32[]{:S(2)}) copy-start(bf16[256,384]{1,0:T(8,128)(2,1)} %get-tuple-element.11.place_ref) | copy-start | bytes 589828
  133.9 41.0 %all-to-all-start.3 = ((bf16[16,24,2048]{2,1,0:T(8,128)(2,1)}), bf16[16,24,2048]{2,1,0:T(8,128)(2,1)S(1)}, u32[]{:S(2)}, u32[]{:S(2)}) async-start(bf16[16,24,2048]{2,1,0:T(8,128)(2,1)} %bitcast.27), calls=%async_computation.3 | async-start | bytes 3145728 | tf_op jit(solution)/shard_map/all_to_all | solution.py:300
  138.1 1.0 copy-start.5

commit v17 on v12

--- a/solution.py
+++ b/solution.py
@@ -99,10 +99,14 @@
         copy.wait()
 
 
+def plane_rows(plane_ref, parts, size, i):
+    start = lax.rem(plane_ref[0] + (parts - i), parts) * size
+    return pl.ds(pl.multiple_of(start, size), size)
+
+
 def by_plane(rows_ref, plane_ref, parts):
     size = rows_ref.shape[0] // parts
-    starts = [lax.rem(plane_ref[0] + (parts - i), parts) * size for i in range(parts)]
-    return [rows_ref.at[pl.ds(pl.multiple_of(start, size), size)] for start in starts]
+    return [rows_ref.at[plane_rows(plane_ref, parts, size, i)] for i in range(parts)]
 
 
 def chunks(span):
@@ -145,28 +149,35 @@
         copy.wait()
 
 
-def backward_kernel(parts, joined, plane_ref, *refs):
-    sources, refs = refs[: 2 + 4 * parts], refs[2 + 4 * parts :]
-    out_ref, sems, out_sems, rows_ref, down_ref, by_gate_ref, by_up_ref, gate_ref, up_ref = refs[:9]
-    stage_ref, back_gate_ref, back_up_ref = refs[9:]
+def backward_kernel(parts, joined, numbers, plane_ref, *refs):
+    count = len(numbers)
+    sources, refs = refs[: count + 2 + 3 * parts], refs[count + 2 + 3 * parts :]
+    out_ref, sems, out_sems, rows_ref, down_ref, by_gate_ref, by_up_ref, gate_ref, up_ref = refs[-12:-3]
+    stage_ref, back_gate_ref, back_up_ref = refs[-3:]
     units, span = down_ref.shape[:2]
-    targets = [
-        *by_plane(rows_ref, plane_ref, parts),
-        *shares(down_ref, parts, joined, 0),
-        by_gate_ref,
-        by_up_ref,
-        *shares(gate_ref, parts, joined),
-        *shares(up_ref, parts, joined),
-    ]
-    copies = fetch(sources, targets, sems)
-    for copy in copies[: 2 + 2 * parts]:
+    size = out_ref.shape[0] // parts
+    there = [plane_rows(plane_ref, parts, size, i) for i in numbers]
+    here = [pl.ds(n * size, size) for n in range(count)]
+    first = fetch(
+        [*sources[:count], *sources[count : count + parts]]
+        + [ref.at[:, rows] for ref in sources[count + parts : count + parts + 2] for rows in there],
+        [*(rows_ref.at[rows] for rows in here), *shares(down_ref, parts, joined, 0)]
+        + [ref.at[:, rows] for ref in (by_gate_ref, by_up_ref) for rows in here],
+        sems.at[pl.ds(0, 3 * count + parts)],
+    )
+    second = fetch(
+        sources[count + parts + 2 :],
+        [*shares(gate_ref, parts, joined), *shares(up_ref, parts, joined)],
+        sems.at[pl.ds(3 * count + parts, 2 * parts)],
+    )
+    for copy in first:
         copy.wait()
     for i in range(units):
         for cut in chunks(span):
             back_hidden = dot(rows_ref[...], down_ref[i, cut, :], (1, 1))
             back_gate_ref[i, :, cut] = (back_hidden * by_gate_ref[i, :, cut]).astype(BF16)
             back_up_ref[i, :, cut] = (back_hidden * by_up_ref[i, :, cut]).astype(BF16)
-    for copy in copies[2 + 2 * parts :]:
+    for copy in second:
         copy.wait()
     sent = []
     for d, columns in enumerate(tiles(stage_ref.shape[1])):
@@ -175,7 +186,9 @@
             + dot(back_up_ref[i], up_ref[i, columns, :], (1, 1))
             for i in range(units)
         ).astype(BF16)
-        sent.append(store(stage_ref.at[:, columns], out_ref.at[:, columns], out_sems.at[d]))
+        for n in range(count):
+            target = out_ref.at[there[n], columns]
+            sent.append(store(stage_ref.at[here[n], columns], target, out_sems.at[d * count + n]))
     for copy in sent:
         copy.wait()
 
@@ -202,7 +215,7 @@
     out_ref[...] = total.astype(BF16)
 
 
-def call(kernel, outs, flops, scratch=(), far=(), pinned=(), out_spaces=None, vmem=SMALL_VMEM):
+def call(kernel, outs, flops, scratch=(), far=(), pinned=(), out_spaces=None, vmem=SMALL_VMEM, aliases=None):
     def run(*args):
         moved = sum(a.size * a.dtype.itemsize for a in (*args, *outs))
         spaces = [
@@ -224,6 +237,7 @@
                 for space in out_spaces or [pltpu.VMEM] * len(outs)
             ),
             scratch_shapes=scratch,
+            input_output_aliases=aliases or {},
             compiler_params=pltpu.CompilerParams(vmem_limit_bytes=vmem),
             cost_estimate=pl.CostEstimate(flops=flops, bytes_accessed=moved, transcendentals=0),
         )(*args)
@@ -347,16 +361,27 @@
     )(plane, *x_shares, *gate_w, *up_w, *down_w)
     dy_shares = dispatch(dy_slots, (out_rows,))
     out_slots = send_back(out_rows)
-    (grad_rows,) = call(
-        functools.partial(backward_kernel, parts, joined),
-        [slot_shape],
-        64 * dot_flops,
-        [sems(2 + 4 * parts), sems(pieces), row_scratch, down_scratch, unit_scratch, unit_scratch]
-        + [in_scratch, in_scratch, row_scratch, hidden_scratch, hidden_scratch],
-        far=range(1, 3 + 4 * parts),
-        out_spaces=[pltpu.HBM],
-        vmem=LARGE_VMEM,
-    )(plane, *dy_shares, *down_w, by_gate, by_up, *gate_w, *up_w)
+    def backward(numbers, *into):
+        count = len(numbers)
+        rows = count * slots // parts
+        unit = pltpu.VMEM((units, rows, span), F32)
+        hidden_unit = pltpu.VMEM((units, rows, span), BF16)
+        row_unit = pltpu.VMEM((rows, width), BF16)
+        last = 1 + count + 2 + 3 * parts
+        return call(
+            functools.partial(backward_kernel, parts, joined, numbers),
+            [slot_shape],
+            3 * dot_flops * count // parts,
+            [sems(3 * count + 3 * parts), sems(pieces * count), row_unit, down_scratch]
+            + [unit, unit, in_scratch, in_scratch, row_unit, hidden_unit, hidden_unit],
+            far=range(1, last),
+            pinned=(last,),
+            out_spaces=[pltpu.HBM],
+            vmem=LARGE_VMEM,
+            aliases={last: 0} if into else {},
+        )(plane, *(dy_shares[i] for i in numbers), *down_w, by_gate, by_up, *gate_w, *up_w, *into)
+
+    (grad_rows,) = backward(range(1, parts), *backward(range(1)))
     grad_slots = send_back(grad_rows)
     mixed, gate_grad = call(
         mix_kernel, [token_shape, jax.ShapeDtypeStruct(gates.shape, F32)], 2 * spread_flops

time: 177 us -> 187 us (1.056)
  Pallas kernels: 27.7 us -> 35.2 us
  starting transfers between devices: 25 us -> 27.6 us
    pallas_call x10 -> x11, Pallas kernels: 27.7 us -> 35.2 us  [run(): pl.pallas_call(kernel, out_shape=tuple(outs), in_specs=[pl.BlockSpec(memo...]
    all_to_all x2, waiting for transfers between devices: 29.1 us -> 32.5 us  [dispatch(): lax.all_to_all(rows, axes, 0, 0, axis_index_groups=in_plane, tiled=True)]
    all_to_all x2, waiting for transfers between devices: 37 us -> 33.6 us  [send_back(): lax.all_to_all(rows, axes, 0, 0, axis_index_groups=everywhere, tiled=True)]
    all_to_all x2, starting transfers between devices: 8.16 us -> 10.8 us  [send_back(): lax.all_to_all(rows, axes, 0, 0, axis_index_groups=everywhere, tiled=True)]
    ppermute x3, waiting for transfers between devices: 10 us -> 7.46 us  [swapped(): return lax.ppermute(weight[0], axes, swap)]
    ppermute x3, waiting for transfers between devices: 0.3 us -> 2.64 us  [whole_expert(): held.append(lax.ppermute(own, 'expert', turn))]
    unnamed x25 -> x31, local copies, waits for them, and re-layouts: 7.45 us -> 9.09 us
  transfers between devices with their start and end apart: 12 -> 12, of which waited for: 9 -> 8; matrix products, arithmetic and copies ran while one was open for 1% -> 1% of each run, Pallas kernels for 14% -> 18%
where the time goes in v17:
time: 187 us; the launch traced here: 186 us
  waiting for transfers between devices  114 us (61%)
  Pallas kernels  35.2 us (19%)
  starting transfers between devices  27.6 us (15%)
  local copies, waits for them, and re-layouts  9.09 us (5%)
    ppermute x2, waiting for transfers between devices, dispatch(): lax.ppermute(rows, 'dp', [(g, (g + i) % parts) for g in range(parts)])  37.3 us
    pallas_call x11, Pallas kernels, run(): pl.pallas_call(kernel, out_shape=tuple(outs), in_specs=[pl.BlockSpec(memo...  35.2 us
    all_to_all x2, waiting for transfers between devices, send_back(): lax.all_to_all(rows, axes, 0, 0, axis_index_groups=everywhere, tiled=True)  33.6 us
    all_to_all x2, waiting for transfers between devices, dispatch(): lax.all_to_all(rows, axes, 0, 0, axis_index_groups=in_plane, tiled=True)  32.5 us
    all_to_all x2, starting transfers between devices, send_back(): lax.all_to_all(rows, axes, 0, 0, axis_index_groups=everywhere, tiled=True)  10.8 us
    all_to_all x2, starting transfers between devices, dispatch(): lax.all_to_all(rows, axes, 0, 0, axis_index_groups=in_plane, tiled=True)  9.44 us
    unnamed x31, local copies, waits for them, and re-layouts  9.09 us
    ppermute x3, waiting for transfers between devices, swapped(): return lax.ppermute(weight[0], axes, swap)  7.46 us
  transfers between devices with their start and end apart: 12, of which 8 were waited for; matrix products, arithmetic and copies ran while one was open for 1% of the time, Pallas kernels for 18%

profile of v17, /device:TPU:0, one launch (start us, length us, event | category | flops | bytes accessed | tf_op | source)
XLA Modules:
  0.0 186.3 jit_solution(1074463625546992870)
XLA Ops:
  0.6 3.0 %collective-permute-start.1 = (bf16[2048,384]{1,0:T(8,128)(2,1)}, bf16[2048,384]{1,0:T(8,128)(2,1)S(1)}, u32[]{:S(2)}, u32[]{:S(2)}) collective-permute-start(bf16[2048,384]{1,0:T(8,128)(2,1)} %bitcast.29), channel_id=1, source_target_pairs={{0,16},{1,0},{2,18},{3,2},{4,20},{5,4},{6,22},{7,6},{8,24},{9,8},{... | collective-permute-start | bytes 4718600 | tf_op jit(solution)/shard_map/ppermute | solution.py:273
  3.6 0.0 collective-permute-start.3
  3.7 0.0 collective-permute-start.5
  3.7 0.8 copy.11.routes_ref
  4.5 0.0 copy-start.8
  4.5 1.0 copy-done.8
  5.5 1.9 %shard_map.94 = (bf16[384,2048]{1,0:T(8,128)(2,1)S(1)}, bf16[128,384]{1,0:T(8,128)(2,1)S(1)}, bf16[256,384]{1,0:T(8,128)(2,1)S(1)}) custom-call(s32[1]{0:T(128)} %bitcast.plane_ref, s32[128,2]{1,0:T(8,128)S(1)} %copy.11.routes_ref, bf16[128,2048]{1,0:T(8,128)(2,1)S(1)} %copy-done.8), custom_call_target="tpu_custom_call" | custom-call | flops 201326592 | bytes 2393092 | tf_op jit(solution)/shard_map/pallas_call | solution.py:231
  7.4 0.0 copy-start.4
  7.4 1.2 copy-done.4
  8.6 5.8 %all-to-all-start = ((bf16[8,48,2048]{2,1,0:T(8,128)(2,1)}), bf16[8,48,2048]{2,1,0:T(8,128)(2,1)S(1)}, u32[]{:S(2)}, u32[]{:S(2)}) async-start(bf16[8,48,2048]{2,1,0:T(8,128)(2,1)} %bitcast.24), calls=%async_computation | async-start | bytes 3145728 | tf_op jit(solution)/shard_map/all_to_all | solution.py:284
  14.4 7.5 %collective-permute-done.1.refs_2_._.refs_5_ = bf16[2048,384]{1,0:T(8,128)(2,1)S(1)} collective-permute-done((bf16[2048,384]{1,0:T(8,128)(2,1)}, bf16[2048,384]{1,0:T(8,128)(2,1)S(1)}, u32[]{:S(2)}, u32[]{:S(2)}) %collective-permute-start.1) | collective-permute-done | bytes 1572896 | tf_op jit(solution)/shard_map/ppermute | solution.py:273
  21.9 0.0 copy-start.1
  21.9 0.0 copy-start.6
  21.9 1.4 copy-done.6
  23.3 1.4 shard_map.99
  24.6 0.0 copy-done.1
  24.6 0.0 copy-start.3
  24.7 1.2 copy-done.3
  25.8 26.2 %all-to-all-done = bf16[8,48,2048]{2,1,0:T(8,128)(2,1)S(1)} async-done(((bf16[8,48,2048]{2,1,0:T(8,128)(2,1)}), bf16[8,48,2048]{2,1,0:T(8,128)(2,1)S(1)}, u32[]{:S(2)}, u32[]{:S(2)}) %all-to-all-start) | async-done | bytes 1572896 | tf_op jit(solution)/shard_map/all_to_all | solution.py:284
  52.1 3.6 %all-to-all-start.2 = ((bf16[8,48,2048]{2,1,0:T(8,128)(2,1)}), bf16[8,48,2048]{2,1,0:T(8,128)(2,1)S(1)}, u32[]{:S(2)}, u32[]{:S(2)}) async-start(bf16[8,48,2048]{2,1,0:T(8,128)(2,1)} %bitcast.23), calls=%async_computation.2 | async-start | bytes 3145728 | tf_op jit(solution)/shard_map/all_to_all | solution.py:284
  55.7 0.0 collective-permute-start.2
  55.7 0.0 collective-permute-done.3.refs_4_.refs_7_
  55.8 0.5 collective-permute-start.4
  56.2 0.0 collective-permute-done.5.refs_6_.refs_1_
  56.3 0.1 collective-permute-start.6
  56.3 1.1 shard_map.96
  57.4 1.8 collective-permute-start
  59.2 1.1 shard_map.95
  60.3 0.0 copy-start.5
  60.3 0.9 copy-done.5
  61.2 0.0 collective-permute-done.2.refs_3_.refs_6_
  61.2 0.0 copy-start.9
  61.2 0.4 collective-permute-done.4.refs_5_.refs_8_
  61.6 0.0 copy-start.10
  61.6 2.2 %collective-permute-done.6.refs_7_.refs_2_ = bf16[384,2048]{1,0:T(8,128)(2,1)S(1)} collective-permute-done((bf16[384,2048]{1,0:T(8,128)(2,1)}, bf16[384,2048]{1,0:T(8,128)(2,1)S(1)}, u32[]{:S(2)}, u32[]{:S(2)}) %collective-permute-start.6) | collective-permute-done | bytes 1572896 | tf_op jit(solution)/shard_map/ppermute | solution.py:279
  63.9 13.6 %collective-permute-done.refs_1_ = bf16[192,2048]{1,0:T(8,128)(2,1)S(1)} collective-permute-done((bf16[192,2048]{1,0:T(8,128)(2,1)S(1)}, bf16[192,2048]{1,0:T(8,128)(2,1)S(1)}, u32[]{:S(2)}, u32[]{:S(2)}) %collective-permute-start) | collective-permute-done | bytes 786464 | tf_op jit(solution)/shard_map/ppermute | solution.py:304
  77.4 0.0 copy-done.9
  77.4 0.0 copy-done.10
  77.4 0.0 copy-done.11
  77.4 0.0 copy-start.13
  77.4 0.9 copy-done.13
  78.3 8.3 %shard_map.97 = (bf16[384,2048]{1,0:T(8,128)(2,1)}, f32[1,384,768]{2,1,0:T(8,128)}, f32[1,384,768]{2,1,0:T(8,128)}) custom-call(s32[1]{0:T(128)} %bitcast.plane_ref, bf16[192,2048]{1,0:T(8,128)(2,1)} %bitcast.25, bf16[192,2048]{1,0:T(8,128)(2,1)} %copy-done.13, bf16[2048,384]{1,0:T(8,128)(2,1)} %copy-done.1, bf16[2048,384]{1,0:T(8,128)(2,1)} %copy-done.9, ...), custom_call_target="tpu_custom_call" | custom-call | flops 3623878656 | bytes 14942212 | tf_op jit(solution)/shard_map/pallas_call | solution.py:231
  86.6 6.3 %all-to-all-done.2 = bf16[8,48,2048]{2,1,0:T(8,128)(2,1)S(1)} async-done(((bf16[8,48,2048]{2,1,0:T(8,128)(2,1)}), bf16[8,48,2048]{2,1,0:T(8,128)(2,1)S(1)}, u32[]{:S(2)}, u32[]{:S(2)}) %all-to-all-start.2) | async-done | bytes 1572896 | tf_op jit(solution)/shard_map/all_to_all | solution.py:284
  92.9 5.1 %all-to-all-start.1 = ((bf16[16,24,2048]{2,1,0:T(8,128)(2,1)}), bf16[16,24,2048]{2,1,0:T(8,128)(2,1)}, u32[]{:S(2)}, u32[]{:S(2)}) async-start(bf16[16,24,2048]{2,1,0:T(8,128)(2,1)} %bitcast.20), calls=%async_computation.1 | async-start | bytes 3145728 | tf_op jit(solution)/shard_map/all_to_all | solution.py:310
  98.0 0.0 copy-done
  98.0 1.1 shard_map.100
  99.1 1.9 %collective-permute-start.7 = (bf16[192,2048]{1,0:T(8,128)(2,1)S(1)}, bf16[192,2048]{1,0:T(8,128)(2,1)}, u32[]{:S(2)}, u32[]{:S(2)}) collective-permute-start(bf16[192,2048]{1,0:T(8,128)(2,1)S(1)} %bitcast.27), channel_id=1, source_target_pairs={{0,16},{16,0},{1,17},{17,1},{2,18},{18,2},{3,19},{19,3},{4,20},{20... | collective-permute-start | bytes 2359304 | tf_op jit(solution)/shard_map/ppermute | solution.py:304
  101.1 1.1 shard_map.101
  102.1 0.0 copy-start.2
  102.1 0.9 copy-done.2
  103.1 7.4 %shard_map.102.refs_9_ = bf16[384,2048]{1,0:T(8,128)(2,1)} custom-call(s32[1]{0:T(128)} %bitcast.plane_ref, bf16[192,2048]{1,0:T(8,128)(2,1)} %bitcast.22, bf16[384,2048]{1,0:T(8,128)(2,1)} %collective-permute-done.5.refs_6_.refs_1_, bf16[384,2048]{1,0:T(8,128)(2,1)} %copy-done.11, f32[1,384,768]{2,1,0:T(8,128)} %get-tuple-element.16.refs_3_, ...), custom_call_target="tpu_custom_call" | custom-call | flops 1811939328 | bytes 14155780 | tf_op jit(solution)/shard_map/pallas_call | solution.py:231
  110.5 23.8 %collective-permute-done.7.refs_0_ = bf16[192,2048]{1,0:T(8,128)(2,1)} collective-permute-done((bf16[192,2048]{1,0:T(8,128)(2,1)S(1)}, bf16[192,2048]{1,0:T(8,128)(2,1)}, u32[]{:S(2)}, u32[]{:S(2)}) %collective-permute-start.7) | collective-permute-done | bytes 786464 | tf_op jit(solution)/shard_map/ppermute | solution.py:304
  134.2 7.4 %shard_map.103 = bf16[384,2048]{1,0:T(8,128)(2,1)} custom-call(s32[1]{0:T(128)} %bitcast.plane_ref, bf16[192,2048]{1,0:T(8,128)(2,1)} %collective-permute-done.7.refs_0_, bf16[384,2048]{1,0:T(8,128)(2,1)} %collective-permute-done.5.refs_6_.refs_1_, bf16[384,2048]{1,0:T(8,128)(2,1)} %copy-done.11, ...), custom_call_target="tpu_custom_call", output_to_operand_aliasing={{}: (10, {})} | custom-call | flops 1811939328 | bytes 15728644 | tf_op jit(solution)/shard_map/pallas_call | solution.py:231
  141.6 0.0 all-to-all-done.1
  141.6 0.0 copy-start.12
  141.6 0.0 copy-start.7
  141.6 5.7 %all-to-all-start.3 = ((bf16[16,24,2048]{2,1,0:T(8,128)(2,1)}), bf16[16,24,2048]{2,1,0:T(8,128)(2,1)S(1)}, u32[]{:S(2)}, u32[]{:S(2)}) async-start(bf16[16,24,2048]{2,1,0:T(8,128)(2,1)} %bitcast.28), calls=%async_computation.3 | async-start | bytes 3145728 | tf_op jit(solution)/shard_map/all_to_all | solution.py:310
  147.3 0.0 copy-done.12
  147.3 0.1 copy.12.gates_ref
  147.5 0.0 copy-done.7
  147.5 3.1 %shard_map.98 = (bf16[128,2048]{1,0:T(8,128)(2,1)}, f32[128,2]{1,0:T(8,128)S(1)}) custom-call(bf16[256,384]{1,0:T(8,128)(2,1)S(1)} %get-tuple-element.11.place_ref, f32[128,2]{1,0:T(8,128)S(1)} %copy.12.gates_ref, bf16[128,2048]{1,0:T(8,128)(2,1)S(1)} %copy-done.7, bf16[384,2048]{1,0:T(8,128)(2,1)} %bitcast.9.slots_ref), custom_call_target="tpu_custom_call" | custom-call | flops 402653184 | bytes 2820096 | tf_op jit(solution)/shard_map/pallas_call | solution.py:231
  150.5 0.6 copy.14
  151.2 33.6 %all-to-all-done.3 = bf16[16,24,2048]{2,1,0:T(8,128)(2,1)S(1)} async-done(((bf16[16,24,2048]{2,1,0:T(8,128)(2,1)}), bf16[16,24,2048]{2,1,0:T(8,128)(2,1)S(1)}, u32[]{:S(2)}, u32[]{:S(2)}) %all-to-all-start.3) | async-done | bytes 1572896 | tf_op jit(solution)/shard_map/all_to_all | solution.py:310
  184.8 1.5 shard_map.104
  (2 shorter events, 0.0 us)
Async XLA Ops:
  0.6 21.2 %collective-permute-start.1 = (bf16[2048,384]{1,0:T(8,128)(2,1)}, bf16[2048,384]{1,0:T(8,128)(2,1)S(1)}, u32[]{:S(2)}, u32[]{:S(2)}) collective-permute-start(bf16[2048,384]{1,0:T(8,128)(2,1)} %bitcast.29), channel_id=1, source_target_pairs={{0,16},{1,0},{2,18},{3,2},{4,20},{5,4},{6,22},{7,6},{8,24},{9,8},{... | collective-permute-start | bytes 4718600 | tf_op jit(solution)/shard_map/ppermute | solution.py:273
  3.6 52.1 %collective-permute-start.3 = (bf16[2048,384]{1,0:T(8,128)(2,1)}, bf16[2048,384]{1,0:T(8,128)(2,1)}, u32[]{:S(2)}, u32[]{:S(2)}) collective-permute-start(bf16[2048,384]{1,0:T(8,128)(2,1)} %bitcast.30), channel_id=1, source_target_pairs={{0,16},{1,0},{2,18},{3,2},{4,20},{5,4},{6,22},{7,6},{8,24},{9,8},{... | collective-permute-start | bytes 4718600 | tf_op jit(solution)/shard_map/ppermute | solution.py:273
  3.7 52.6 %collective-permute-start.5 = (bf16[384,2048]{1,0:T(8,128)(2,1)}, bf16[384,2048]{1,0:T(8,128)(2,1)}, u32[]{:S(2)}, u32[]{:S(2)}) collective-permute-start(bf16[384,2048]{1,0:T(8,128)(2,1)} %bitcast.31), channel_id=1, source_target_pairs={{0,16},{1,0},{2,18},{3,2},{4,20},{5,4},{6,22},{7,6},{8,24},{9,8},{... | collective-permute-start | bytes 4718600 | tf_op jit(solution)/shard_map/ppermute | solution.py:273
  4.5 1.0 copy-start.8
  7.4 1.2 copy-start.4
  8.6 43.5 %all-to-all-start = ((bf16[8,48,2048]{2,1,0:T(8,128)(2,1)}), bf16[8,48,2048]{2,1,0:T(8,128)(2,1)S(1)}, u32[]{:S(2)}, u32[]{:S(2)}) async-start(bf16[8,48,2048]{2,1,0:T(8,128)(2,1)} %bitcast.24), calls=%async_computation | async-start | bytes 3145728 | tf_op jit(solution)/shard_map/all_to_all | solution.py:284
  21.9 2.8 %copy-start.1 = (bf16[2048,384]{1,0:T(8,128)(2,1)}, bf16[2048,384]{1,0:T(8,128)(2,1)S(1)}, u32[]{:S(2)}) copy-start(bf16[2048,384]{1,0:T(8,128)(2,1)S(1)} %collective-permute-done.1.refs_2_._.refs_5_) | copy-start | bytes 4718596
  21.9 1.4 copy-start.6
  24.6 1.2 copy-start.3
  52.1 40.8 %all-to-all-start.2 = ((bf16[8,48,2048]{2,1,0:T(8,128)(2,1)}), bf16[8,48,2048]{2,1,0:T(8,128)(2,1)S(1)}, u32[]{:S(2)}, u32[]{:S(2)}) async-start(bf16[8,48,2048]{2,1,0:T(8,128)(2,1)} %bitcast.23), calls=%async_computation.2 | async-start | bytes 3145728 | tf_op jit(solution)/shard_map/all_to_all | solution.py:284
  55.7 5.5 %collective-permute-start.2 = (bf16[2048,384]{1,0:T(8,128)(2,1)}, bf16[2048,384]{1,0:T(8,128)(2,1)S(1)}, u32[]{:S(2)}, u32[]{:S(2)}) collective-permute-start(bf16[2048,384]{1,0:T(8,128)(2,1)} %copy-done.1), channel_id=1, source_target_pairs={{0,1},{1,0},{2,3},{3,2},{4,5},{5,4},{6,7},{7,6},{8,9},{9,8},{10,11... | collective-permute-start | bytes 4718600 | tf_op jit(solution)/shard_map/ppermute | solution.py:279
  55.8 5.8 %collective-permute-start.4 = (bf16[2048,384]{1,0:T(8,128)(2,1)}, bf16[2048,384]{1,0:T(8,128)(2,1)S(1)}, u32[]{:S(2)}, u32[]{:S(2)}) collective-permute-start(bf16[2048,384]{1,0:T(8,128)(2,1)} %collective-permute-done.3.refs_4_.refs_7_), channel_id=1, source_target_pairs={{0,1},{1,0},{2,3},{3,2},{4,5},{5,4},{6,7},{7,6},{8,9},{9,8},{10,11... | collective-permute-start | bytes 4718600 | tf_op jit(solution)/shard_map/ppermute | solution.py:279
  56.3 7.6 %collective-permute-start.6 = (bf16[384,2048]{1,0:T(8,128)(2,1)}, bf16[384,2048]{1,0:T(8,128)(2,1)S(1)}, u32[]{:S(2)}, u32[]{:S(2)}) collective-permute-start(bf16[384,2048]{1,0:T(8,128)(2,1)} %collective-permute-done.5.refs_6_.refs_1_), channel_id=1, source_target_pairs={{0,1},{1,0},{2,3},{3,2},{4,5},{5,4},{6,7},{7,6},{8,9},{9,8},{10,11... | collective-permute-start | bytes 4718600 | tf_op jit(solution)/shard_map/ppermute | solution.py:279
  57.4 20.0 %collective-permute-start = (bf16[192,2048]{1,0:T(8,128)(2,1)S(1)}, bf16[192,2048]{1,0:T(8,128)(2,1)S(1)}, u32[]{:S(2)}, u32[]{:S(2)}) collective-permute-start(bf16[192,2048]{1,0:T(8,128)(2,1)S(1)} %bitcast.26), channel_id=1, source_target_pairs={{0,16},{16,0},{1,17},{17,1},{2,18},{18,2},{3,19},{19,3},{4,20},{20... | collective-permute-start | bytes 2359304 | tf_op jit(solution)/shard_map/ppermute | solution.py:304
  60.3 0.9 copy-start.5
  61.2 16.2 %copy-start.9 = (bf16[2048,384]{1,0:T(8,128)(2,1)}, bf16[2048,384]{1,0:T(8,128)(2,1)S(1)}, u32[]{:S(2)}) copy-start(bf16[2048,384]{1,0:T(8,128)(2,1)S(1)} %collective-permute-done.2.refs_3_.refs_6_) | copy-start | bytes 4718596
  61.6 15.8 %copy-start.10 = (bf16[2048,384]{1,0:T(8,128)(2,1)}, bf16[2048,384]{1,0:T(8,128)(2,1)S(1)}, u32[]{:S(2)}) copy-start(bf16[2048,384]{1,0:T(8,128)(2,1)S(1)} %collective-permute-done.4.refs_5_.refs_8_) | copy-start | bytes 4718596
  63.9 13.6 %copy-start.11 = (bf16[384,2048]{1,0:T(8,128)(2,1)}, bf16[384,2048]{1,0:T(8,128)(2,1)S(1)}, u32[]{:S(2)}) copy-start(bf16[384,2048]{1,0:T(8,128)(2,1)S(1)} %collective-permute-done.6.refs_7_.refs_2_) | copy-start | bytes 4718596
  77.4 0.9 copy-start.13
  92.9 5.1 %copy-start = (bf16[384,2048]{1,0:T(8,128)(2,1)S(1)}, bf16[384,2048]{1,0:T(8,128)(2,1)}, u32[]{:S(2)}) copy-start(bf16[384,2048]{1,0:T(8,128)(2,1)} %get-tuple-element.13.refs_0_) | copy-start | bytes 4718596
  92.9 48.7 %all-to-all-start.1 = ((bf16[16,24,2048]{2,1,0:T(8,128)(2,1)}), bf16[16,24,2048]{2,1,0:T(8,128)(2,1)}, u32[]{:S(2)}, u32[]{:S(2)}) async-start(bf16[16,24,2048]{2,1,0:T(8,128)(2,1)} %bitcast.20), calls=%async_computation.1 | async-start | bytes 3145728 | tf_op jit(solution)/shard_map/all_to_all | solution.py:310
  99.1 35.1 %collective-permute-start.7 = (bf16[192,2048]{1,0:T(8,128)(2,1)S(1)}, bf16[192,2048]{1,0:T(8,128)(2,1)}, u32[]{:S(2)}, u32[]{:S(2)}) collective-permute-start(bf16[192,2048]{1,0:T(8,128)(2,1)S(1)} %bitcast.27), channel_id=1, source_target_pairs={{0,16},{16,0},{1,17},{17,1},{2,18},{18,2},{3,19},{19,3},{4,20},{20... | collective-permute-start | bytes 2359304 | tf_op jit(solution)/shard_map/ppermute | solution.py:304
  102.1 0.9 copy-start.2
  141.6 5.7 %copy-start.12 = (f32[128,2]{0,1:T(2,128)S(1)}, f32[128,2]{0,1:T(2,128)}, u32[]{:S(2)}) copy-start(f32[128,2]{0,1:T(2,128)} %param.10) | copy-start | bytes 3076
  141.6 5.8 %copy-start.7 = (bf16[128,2048]{1,0:T(8,128)(2,1)S(1)}, bf16[128,2048]{1,0:T(8,128)(2,1)}, u32[]{:S(2)}) copy-start(bf16[128,2048]{1,0:T(8,128)(2,1)} %rows_ref.1) | copy-start | bytes 1572868
  141.6 43.1 %all-to-all-start.3 = ((bf16[16,24,2048]{2,1,0:T(8,128)(2,1)}), bf16[16,24,2048]{2,1,0:T(8,128)(2,1)S(1)}, u32[]{:S(2)}, u32[]{:S(2)}) async-start(bf16[16,24,2048]{2,1,0:T(8,128)(2,1)} %bitcast.28), calls=%async_computation.3 | async-start | bytes 3145728 | tf_op jit(solution)/shard_map/all_to_all | solution.py:310

commit v18 on v16

--- a/solution.py
+++ b/solution.py
@@ -43,11 +43,10 @@
 
 
 def place_kernel(experts, parts, plane_ref, routes_ref, tokens_ref, slots_ref, near_ref, *refs):
-    place_ref, sems, out_sems, rows_ref, stage_ref = refs
+    place_ref, out_sems, stage_ref = refs
     slots, width = slots_ref.shape
     capacity = slots // experts
     top_count, tok_rows = routes_ref.shape
-    (copy,) = fetch([tokens_ref], [rows_ref], sems)
     same = lax.broadcasted_iota(jnp.int32, (tok_rows, tok_rows), 0) == lax.broadcasted_iota(
         jnp.int32, (tok_rows, tok_rows), 1
     )
@@ -75,8 +74,7 @@
         place_ref[k * tok_rows : (k + 1) * tok_rows, :] = mark.astype(BF16)
         near = near_mark if near is None else near + near_mark
     near_ref[...] = near.astype(BF16)
-    copy.wait()
-    spread(near_ref, rows_ref, stage_ref, slots_ref, out_sems)
+    spread(near_ref, tokens_ref, stage_ref, slots_ref, out_sems)
 
 
 def spread(near_ref, rows_ref, stage_ref, slots_ref, sems):
@@ -196,14 +194,19 @@
     gate_grad_ref[...] = jnp.concatenate(grads, axis=1)
 
 
-def sum_kernel(place_ref, gates_ref, slots_ref, out_ref):
+def sum_kernel(place_ref, gates_ref, slots_ref, out_ref, sems, stage_ref):
     tok_rows, top_count = gates_ref.shape
-    total = None
-    for k in range(top_count):
-        raw = dot(place_ref[k * tok_rows : (k + 1) * tok_rows, :], slots_ref[...], (1, 0))
-        term = raw * gates_ref[:, k : k + 1]
-        total = term if total is None else total + term
-    out_ref[...] = total.astype(BF16)
+    sent = []
+    for d, columns in enumerate(tiles(out_ref.shape[1])):
+        raw = dot(place_ref[...], slots_ref[:, columns], (1, 0))
+        total = None
+        for k in range(top_count):
+            term = raw[k * tok_rows : (k + 1) * tok_rows, :] * gates_ref[:, k : k + 1]
+            total = term if total is None else total + term
+        stage_ref[:, columns] = total.astype(BF16)
+        sent.append(store(stage_ref.at[:, columns], out_ref.at[:, columns], sems.at[d]))
+    for copy in sent:
+        copy.wait()
 
 
 def call(kernel, outs, flops, scratch=(), far=(), pinned=(), out_spaces=None, vmem=SMALL_VMEM):
@@ -326,10 +329,8 @@
         functools.partial(place_kernel, experts, parts),
         [slot_shape, jax.ShapeDtypeStruct((tok_rows, slots), BF16), place_shape],
         spread_flops,
-        [sems(1), sems(pieces), pltpu.VMEM((tok_rows, width), BF16), row_scratch],
-        pinned=(2,),
+        [sems(pieces), row_scratch],
         out_spaces=[pltpu.HBM, pltpu.VMEM, pltpu.VMEM],
-        vmem=LARGE_VMEM,
     )(plane, routes.T, tokens)
     x_shares = dispatch(x_slots)
     (dy_slots,) = call(
@@ -366,7 +367,13 @@
     mixed, gate_grad = call(
         mix_kernel, [token_shape, jax.ShapeDtypeStruct(gates.shape, F32)], 2 * spread_flops
     )(place, gates, cotangent, out_slots)
-    (token_grad,) = call(sum_kernel, [token_shape], 2 * spread_flops)(place, gates, grad_slots)
+    (token_grad,) = call(
+        sum_kernel,
+        [token_shape],
+        2 * spread_flops,
+        [sems(pieces), pltpu.VMEM((tok_rows, width), BF16)],
+        out_spaces=[pltpu.HBM],
+    )(place, gates, grad_slots)
     return (mixed, token_grad, gate_grad)
 
 

time: 177 us -> 177 us (level)
  Pallas kernels: 29.6 us -> 27.6 us
    pallas_call x10, Pallas kernels: 29.6 us -> 27.6 us  [run(): pl.pallas_call(kernel, out_shape=tuple(outs), in_specs=[pl.BlockSpec(memo...]
  transfers between devices with their start and end apart: 12 -> 12, of which waited for: 9 -> 9; matrix products, arithmetic and copies ran while one was open for 0% -> 0% of each run, Pallas kernels for 15% -> 14%
where the time goes in v18:
time: 177 us; the launch traced here: 176 us
  waiting for transfers between devices  115 us (65%)
  Pallas kernels  27.6 us (16%)
  starting transfers between devices  25 us (14%)
  local copies, waits for them, and re-layouts  7.4 us (4%)
    ppermute x2, waiting for transfers between devices, dispatch(): lax.ppermute(rows, 'dp', [(g, (g + i) % parts) for g in range(parts)])  39 us
    all_to_all x2, waiting for transfers between devices, send_back(): lax.all_to_all(rows, axes, 0, 0, axis_index_groups=everywhere, tiled=True)  37 us
    all_to_all x2, waiting for transfers between devices, dispatch(): lax.all_to_all(rows, axes, 0, 0, axis_index_groups=in_plane, tiled=True)  28.9 us
    pallas_call x10, Pallas kernels, run(): pl.pallas_call(kernel, out_shape=tuple(outs), in_specs=[pl.BlockSpec(memo...  27.6 us
    ppermute x3, waiting for transfers between devices, swapped(): return lax.ppermute(weight[0], axes, swap)  10.2 us
    all_to_all x2, starting transfers between devices, dispatch(): lax.all_to_all(rows, axes, 0, 0, axis_index_groups=in_plane, tiled=True)  9.53 us
    all_to_all x2, starting transfers between devices, send_back(): lax.all_to_all(rows, axes, 0, 0, axis_index_groups=everywhere, tiled=True)  8.16 us
    unnamed x26, local copies, waits for them, and re-layouts  7.4 us
  transfers between devices with their start and end apart: 12, of which 9 were waited for; matrix products, arithmetic and copies ran while one was open for 0% of the time, Pallas kernels for 14%

profile of v18, /device:TPU:0, one launch (start us, length us, event | category | flops | bytes accessed | tf_op | source)
XLA Modules:
  0.0 176.1 jit_solution(15793882346944416492)
XLA Ops:
  0.6 3.0 %collective-permute-start.1 = (bf16[2048,384]{1,0:T(8,128)(2,1)}, bf16[2048,384]{1,0:T(8,128)(2,1)}, u32[]{:S(2)}, u32[]{:S(2)}) collective-permute-start(bf16[2048,384]{1,0:T(8,128)(2,1)} %bitcast.29), channel_id=1, source_target_pairs={{0,16},{1,0},{2,18},{3,2},{4,20},{5,4},{6,22},{7,6},{8,24},{9,8},{... | collective-permute-start | bytes 4718600 | tf_op jit(solution)/shard_map/ppermute | solution.py:266
  3.6 0.0 copy-start.5
  3.6 1.0 copy-done.5
  4.7 0.0 copy-start.6
  4.7 0.7 copy-done.6
  5.3 2.1 %shard_map.94 = (bf16[384,2048]{1,0:T(8,128)(2,1)}, bf16[128,384]{1,0:T(8,128)(2,1)S(1)}, bf16[256,384]{1,0:T(8,128)(2,1)S(1)}) custom-call(s32[1]{0:T(128)} %bitcast.plane_ref, s32[2,128]{1,0:T(2,128)S(1)} %bitcast.27, bf16[128,2048]{1,0:T(8,128)(2,1)S(1)} %copy-done.5), custom_call_target="tpu_custom_call" | custom-call | flops 201326592 | bytes 2393092 | tf_op jit(solution)/shard_map/pallas_call | solution.py:225
  7.4 0.0 copy-start.3
  7.4 5.9 %all-to-all-start = ((bf16[8,48,2048]{2,1,0:T(8,128)(2,1)}), bf16[8,48,2048]{2,1,0:T(8,128)(2,1)S(1)}, u32[]{:S(2)}, u32[]{:S(2)}) async-start(bf16[8,48,2048]{2,1,0:T(8,128)(2,1)} %bitcast.2), calls=%async_computation | async-start | bytes 3145728 | tf_op jit(solution)/shard_map/all_to_all | solution.py:277
  13.4 0.0 collective-permute-start.3
  13.4 0.0 collective-permute-start.5
  13.5 8.4 %collective-permute-done.1.refs_2_._.refs_6_ = bf16[2048,384]{1,0:T(8,128)(2,1)} collective-permute-done((bf16[2048,384]{1,0:T(8,128)(2,1)}, bf16[2048,384]{1,0:T(8,128)(2,1)}, u32[]{:S(2)}, u32[]{:S(2)}) %collective-permute-start.1) | collective-permute-done | bytes 1572896 | tf_op jit(solution)/shard_map/ppermute | solution.py:266
  21.9 0.0 copy-done.3
  21.9 1.4 shard_map.99
  23.2 0.0 copy-start
  23.2 1.2 copy-done
  24.4 25.2 %all-to-all-done = bf16[8,48,2048]{2,1,0:T(8,128)(2,1)S(1)} async-done(((bf16[8,48,2048]{2,1,0:T(8,128)(2,1)}), bf16[8,48,2048]{2,1,0:T(8,128)(2,1)S(1)}, u32[]{:S(2)}, u32[]{:S(2)}) %all-to-all-start) | async-done | bytes 1572896 | tf_op jit(solution)/shard_map/all_to_all | solution.py:277
  49.6 3.6 %all-to-all-start.2 = ((bf16[8,48,2048]{2,1,0:T(8,128)(2,1)}), bf16[8,48,2048]{2,1,0:T(8,128)(2,1)S(1)}, u32[]{:S(2)}, u32[]{:S(2)}) async-start(bf16[8,48,2048]{2,1,0:T(8,128)(2,1)} %bitcast.23), calls=%async_computation.2 | async-start | bytes 3145728 | tf_op jit(solution)/shard_map/all_to_all | solution.py:277
  53.2 0.1 collective-permute-start.2
  53.3 0.0 collective-permute-done.3.refs_4_.refs_8_
  53.3 0.5 collective-permute-start.4
  53.8 1.8 %collective-permute-done.5.refs_6_.refs_2_ = bf16[384,2048]{1,0:T(8,128)(2,1)} collective-permute-done((bf16[384,2048]{1,0:T(8,128)(2,1)}, bf16[384,2048]{1,0:T(8,128)(2,1)}, u32[]{:S(2)}, u32[]{:S(2)}) %collective-permute-start.5) | collective-permute-done | bytes 1572896 | tf_op jit(solution)/shard_map/ppermute | solution.py:266
  55.6 0.0 collective-permute-start.6
  55.6 1.1 shard_map.96
  56.7 2.6 %collective-permute-start = (bf16[192,2048]{1,0:T(8,128)(2,1)S(1)}, bf16[192,2048]{1,0:T(8,128)(2,1)S(1)}, u32[]{:S(2)}, u32[]{:S(2)}) collective-permute-start(bf16[192,2048]{1,0:T(8,128)(2,1)S(1)} %bitcast.25), channel_id=1, source_target_pairs={{0,16},{16,0},{1,17},{17,1},{2,18},{18,2},{3,19},{19,3},{4,20},{20... | collective-permute-start | bytes 2359304 | tf_op jit(solution)/shard_map/ppermute | solution.py:297
  59.2 1.1 shard_map.95
  60.3 0.0 copy-start.1
  60.3 0.9 copy-done.1
  61.2 0.0 collective-permute-done.2.refs_3_.refs_7_
  61.2 0.0 copy-start.8
  61.2 0.0 collective-permute-done.4.refs_5_.refs_9_
  61.2 0.0 copy-start.9
  61.2 0.2 collective-permute-done.6.refs_7_.refs_3_
  61.4 0.0 copy-start.10
  61.4 16.0 %collective-permute-done.refs_1_ = bf16[192,2048]{1,0:T(8,128)(2,1)S(1)} collective-permute-done((bf16[192,2048]{1,0:T(8,128)(2,1)S(1)}, bf16[192,2048]{1,0:T(8,128)(2,1)S(1)}, u32[]{:S(2)}, u32[]{:S(2)}) %collective-permute-start) | collective-permute-done | bytes 786464 | tf_op jit(solution)/shard_map/ppermute | solution.py:297
  77.4 0.0 copy-done.8
  77.4 0.0 copy-done.9
  77.4 0.0 copy-done.10
  77.4 0.0 copy-start.11
  77.4 0.9 copy-done.11
  78.3 8.3 %shard_map.97 = (bf16[384,2048]{1,0:T(8,128)(2,1)}, f32[1,384,768]{2,1,0:T(8,128)}, f32[1,384,768]{2,1,0:T(8,128)}) custom-call(s32[1]{0:T(128)} %bitcast.plane_ref, bf16[192,2048]{1,0:T(8,128)(2,1)} %bitcast.24, bf16[192,2048]{1,0:T(8,128)(2,1)} %copy-done.11, bf16[2048,384]{1,0:T(8,128)(2,1)} %collective-permute-done.1.refs_2_._.refs_6_, ...), custom_call_target="tpu_custom_call" | custom-call | flops 3623878656 | bytes 14942212 | tf_op jit(solution)/shard_map/pallas_call | solution.py:225
  86.6 3.7 %all-to-all-done.2 = bf16[8,48,2048]{2,1,0:T(8,128)(2,1)S(1)} async-done(((bf16[8,48,2048]{2,1,0:T(8,128)(2,1)}), bf16[8,48,2048]{2,1,0:T(8,128)(2,1)S(1)}, u32[]{:S(2)}, u32[]{:S(2)}) %all-to-all-start.2) | async-done | bytes 1572896 | tf_op jit(solution)/shard_map/all_to_all | solution.py:277
  90.3 1.0 shard_map.101
  91.3 1.2 collective-permute-start.7
  92.5 4.1 %all-to-all-start.1 = ((bf16[16,24,2048]{2,1,0:T(8,128)(2,1)}), bf16[16,24,2048]{2,1,0:T(8,128)(2,1)S(1)}, u32[]{:S(2)}, u32[]{:S(2)}) async-start(bf16[16,24,2048]{2,1,0:T(8,128)(2,1)} %bitcast.9), calls=%async_computation.1 | async-start | bytes 3145728 | tf_op jit(solution)/shard_map/all_to_all | solution.py:303
  96.6 1.1 shard_map.100
  97.7 0.0 copy-start.2
  97.7 0.9 copy-done.2
  98.6 23.0 %collective-permute-done.7.refs_1_ = bf16[192,2048]{1,0:T(8,128)(2,1)} collective-permute-done((bf16[192,2048]{1,0:T(8,128)(2,1)}, bf16[192,2048]{1,0:T(8,128)(2,1)}, u32[]{:S(2)}, u32[]{:S(2)}) %collective-permute-start.7) | collective-permute-done | bytes 786464 | tf_op jit(solution)/shard_map/ppermute | solution.py:297
  121.6 8.6 %shard_map.102 = bf16[384,2048]{1,0:T(8,128)(2,1)} custom-call(s32[1]{0:T(128)} %bitcast.plane_ref, bf16[192,2048]{1,0:T(8,128)(2,1)} %bitcast.26, bf16[192,2048]{1,0:T(8,128)(2,1)} %collective-permute-done.7.refs_1_, bf16[384,2048]{1,0:T(8,128)(2,1)} %collective-permute-done.5.refs_6_.refs_2_, bf16[384,2048]{1,0:T(8,128)(2,1)} %copy-done.10, ...), custom_call_target="tpu_custom_call" | custom-call | flops 77309411328 | bytes 14942212 | tf_op jit(solution)/shard_map/pallas_call | solution.py:225
  130.2 3.5 %all-to-all-done.1 = bf16[16,24,2048]{2,1,0:T(8,128)(2,1)S(1)} async-done(((bf16[16,24,2048]{2,1,0:T(8,128)(2,1)}), bf16[16,24,2048]{2,1,0:T(8,128)(2,1)S(1)}, u32[]{:S(2)}, u32[]{:S(2)}) %all-to-all-start.1) | async-done | bytes 1572896 | tf_op jit(solution)/shard_map/all_to_all | solution.py:303
  133.8 0.0 copy-start.7
  133.8 4.1 %all-to-all-start.3 = ((bf16[16,24,2048]{2,1,0:T(8,128)(2,1)}), bf16[16,24,2048]{2,1,0:T(8,128)(2,1)S(1)}, u32[]{:S(2)}, u32[]{:S(2)}) async-start(bf16[16,24,2048]{2,1,0:T(8,128)(2,1)} %bitcast.28), calls=%async_computation.3 | async-start | bytes 3145728 | tf_op jit(solution)/shard_map/all_to_all | solution.py:303
  137.8 0.0 copy-done.7
  137.8 0.1 copy.10.gates_ref
  138.0 0.0 copy-start.4
  138.0 1.0 copy-done.4
  139.0 1.7 shard_map.98
  140.7 0.6 copy.12
  141.3 33.4 %all-to-all-done.3 = bf16[16,24,2048]{2,1,0:T(8,128)(2,1)S(1)} async-done(((bf16[16,24,2048]{2,1,0:T(8,128)(2,1)}), bf16[16,24,2048]{2,1,0:T(8,128)(2,1)S(1)}, u32[]{:S(2)}, u32[]{:S(2)}) %all-to-all-start.3) | async-done | bytes 1572896 | tf_op jit(solution)/shard_map/all_to_all | solution.py:303
  174.7 1.4 shard_map.103
Async XLA Ops:
  0.6 21.2 %collective-permute-start.1 = (bf16[2048,384]{1,0:T(8,128)(2,1)}, bf16[2048,384]{1,0:T(8,128)(2,1)}, u32[]{:S(2)}, u32[]{:S(2)}) collective-permute-start(bf16[2048,384]{1,0:T(8,128)(2,1)} %bitcast.29), channel_id=1, source_target_pairs={{0,16},{1,0},{2,18},{3,2},{4,20},{5,4},{6,22},{7,6},{8,24},{9,8},{... | collective-permute-start | bytes 4718600 | tf_op jit(solution)/shard_map/ppermute | solution.py:266
  3.6 1.0 copy-start.5
  4.7 0.7 copy-start.6
  7.4 14.4 %copy-start.3 = (bf16[128,2048]{1,0:T(8,128)(2,1)S(1)}, bf16[128,2048]{1,0:T(8,128)(2,1)}, u32[]{:S(2)}) copy-start(bf16[128,2048]{1,0:T(8,128)(2,1)} %rows_ref.1) | copy-start | bytes 1572868
  7.4 42.2 %all-to-all-start = ((bf16[8,48,2048]{2,1,0:T(8,128)(2,1)}), bf16[8,48,2048]{2,1,0:T(8,128)(2,1)S(1)}, u32[]{:S(2)}, u32[]{:S(2)}) async-start(bf16[8,48,2048]{2,1,0:T(8,128)(2,1)} %bitcast.2), calls=%async_computation | async-start | bytes 3145728 | tf_op jit(solution)/shard_map/all_to_all | solution.py:277
  13.4 39.9 %collective-permute-start.3 = (bf16[2048,384]{1,0:T(8,128)(2,1)}, bf16[2048,384]{1,0:T(8,128)(2,1)}, u32[]{:S(2)}, u32[]{:S(2)}) collective-permute-start(bf16[2048,384]{1,0:T(8,128)(2,1)} %bitcast.30), channel_id=1, source_target_pairs={{0,16},{1,0},{2,18},{3,2},{4,20},{5,4},{6,22},{7,6},{8,24},{9,8},{... | collective-permute-start | bytes 4718600 | tf_op jit(solution)/shard_map/ppermute | solution.py:266
  13.4 42.2 %collective-permute-start.5 = (bf16[384,2048]{1,0:T(8,128)(2,1)}, bf16[384,2048]{1,0:T(8,128)(2,1)}, u32[]{:S(2)}, u32[]{:S(2)}) collective-permute-start(bf16[384,2048]{1,0:T(8,128)(2,1)} %bitcast.31), channel_id=1, source_target_pairs={{0,16},{1,0},{2,18},{3,2},{4,20},{5,4},{6,22},{7,6},{8,24},{9,8},{... | collective-permute-start | bytes 4718600 | tf_op jit(solution)/shard_map/ppermute | solution.py:266
  23.2 1.2 copy-start
  49.6 40.7 %all-to-all-start.2 = ((bf16[8,48,2048]{2,1,0:T(8,128)(2,1)}), bf16[8,48,2048]{2,1,0:T(8,128)(2,1)S(1)}, u32[]{:S(2)}, u32[]{:S(2)}) async-start(bf16[8,48,2048]{2,1,0:T(8,128)(2,1)} %bitcast.23), calls=%async_computation.2 | async-start | bytes 3145728 | tf_op jit(solution)/shard_map/all_to_all | solution.py:277
  53.2 8.0 %collective-permute-start.2 = (bf16[2048,384]{1,0:T(8,128)(2,1)}, bf16[2048,384]{1,0:T(8,128)(2,1)S(1)}, u32[]{:S(2)}, u32[]{:S(2)}) collective-permute-start(bf16[2048,384]{1,0:T(8,128)(2,1)} %collective-permute-done.1.refs_2_._.refs_6_), channel_id=1, source_target_pairs={{0,1},{1,0},{2,3},{3,2},{4,5},{5,4},{6,7},{7,6},{8,9},{9,8},{10,11... | collective-permute-start | bytes 4718600 | tf_op jit(solution)/shard_map/ppermute | solution.py:272
  53.3 7.9 %collective-permute-start.4 = (bf16[2048,384]{1,0:T(8,128)(2,1)}, bf16[2048,384]{1,0:T(8,128)(2,1)S(1)}, u32[]{:S(2)}, u32[]{:S(2)}) collective-permute-start(bf16[2048,384]{1,0:T(8,128)(2,1)} %collective-permute-done.3.refs_4_.refs_8_), channel_id=1, source_target_pairs={{0,1},{1,0},{2,3},{3,2},{4,5},{5,4},{6,7},{7,6},{8,9},{9,8},{10,11... | collective-permute-start | bytes 4718600 | tf_op jit(solution)/shard_map/ppermute | solution.py:272
  55.6 5.8 %collective-permute-start.6 = (bf16[384,2048]{1,0:T(8,128)(2,1)}, bf16[384,2048]{1,0:T(8,128)(2,1)S(1)}, u32[]{:S(2)}, u32[]{:S(2)}) collective-permute-start(bf16[384,2048]{1,0:T(8,128)(2,1)} %collective-permute-done.5.refs_6_.refs_2_), channel_id=1, source_target_pairs={{0,1},{1,0},{2,3},{3,2},{4,5},{5,4},{6,7},{7,6},{8,9},{9,8},{10,11... | collective-permute-start | bytes 4718600 | tf_op jit(solution)/shard_map/ppermute | solution.py:272
  56.7 20.7 %collective-permute-start = (bf16[192,2048]{1,0:T(8,128)(2,1)S(1)}, bf16[192,2048]{1,0:T(8,128)(2,1)S(1)}, u32[]{:S(2)}, u32[]{:S(2)}) collective-permute-start(bf16[192,2048]{1,0:T(8,128)(2,1)S(1)} %bitcast.25), channel_id=1, source_target_pairs={{0,16},{16,0},{1,17},{17,1},{2,18},{18,2},{3,19},{19,3},{4,20},{20... | collective-permute-start | bytes 2359304 | tf_op jit(solution)/shard_map/ppermute | solution.py:297
  60.3 0.9 copy-start.1
  61.2 16.2 %copy-start.8 = (bf16[2048,384]{1,0:T(8,128)(2,1)}, bf16[2048,384]{1,0:T(8,128)(2,1)S(1)}, u32[]{:S(2)}) copy-start(bf16[2048,384]{1,0:T(8,128)(2,1)S(1)} %collective-permute-done.2.refs_3_.refs_7_) | copy-start | bytes 4718596
  61.2 16.2 %copy-start.9 = (bf16[2048,384]{1,0:T(8,128)(2,1)}, bf16[2048,384]{1,0:T(8,128)(2,1)S(1)}, u32[]{:S(2)}) copy-start(bf16[2048,384]{1,0:T(8,128)(2,1)S(1)} %collective-permute-done.4.refs_5_.refs_9_) | copy-start | bytes 4718596
  61.4 16.0 %copy-start.10 = (bf16[384,2048]{1,0:T(8,128)(2,1)}, bf16[384,2048]{1,0:T(8,128)(2,1)S(1)}, u32[]{:S(2)}) copy-start(bf16[384,2048]{1,0:T(8,128)(2,1)S(1)} %collective-permute-done.6.refs_7_.refs_3_) | copy-start | bytes 4718596
  77.4 0.9 copy-start.11
  91.3 30.3 %collective-permute-start.7 = (bf16[192,2048]{1,0:T(8,128)(2,1)}, bf16[192,2048]{1,0:T(8,128)(2,1)}, u32[]{:S(2)}, u32[]{:S(2)}) collective-permute-start(bf16[192,2048]{1,0:T(8,128)(2,1)} %bitcast.14), channel_id=1, source_target_pairs={{0,16},{16,0},{1,17},{17,1},{2,18},{18,2},{3,19},{19,3},{4,20},{20... | collective-permute-start | bytes 2359304 | tf_op jit(solution)/shard_map/ppermute | solution.py:297
  92.5 41.3 %all-to-all-start.1 = ((bf16[16,24,2048]{2,1,0:T(8,128)(2,1)}), bf16[16,24,2048]{2,1,0:T(8,128)(2,1)S(1)}, u32[]{:S(2)}, u32[]{:S(2)}) async-start(bf16[16,24,2048]{2,1,0:T(8,128)(2,1)} %bitcast.9), calls=%async_computation.1 | async-start | bytes 3145728 | tf_op jit(solution)/shard_map/all_to_all | solution.py:303
  97.7 0.9 copy-start.2
  133.8 4.1 %copy-start.7 = (f32[128,2]{0,1:T(2,128)S(1)}, f32[128,2]{0,1:T(2,128)}, u32[]{:S(2)}) copy-start(f32[128,2]{0,1:T(2,128)} %param.10) | copy-start | bytes 3076
  133.8 41.0 %all-to-all-start.3 = ((bf16[16,24,2048]{2,1,0:T(8,128)(2,1)}), bf16[16,24,2048]{2,1,0:T(8,128)(2,1)S(1)}, u32[]{:S(2)}, u32[]{:S(2)}) async-start(bf16[16,24,2048]{2,1,0:T(8,128)(2,1)} %bitcast.28), calls=%async_computation.3 | async-start | bytes 3145728 | tf_op jit(solution)/shard_map/all_to_all | solution.py:303
  138.0 1.0 copy-start.4
